TPU v7x, 32 devices: a whole 2x2x4 slice. The times are simulated.
32 devices in a mesh: gx: 8 (over z, x), gy: 4 (over y, core).
Axes of the slice: x: 2, y: 2, z: 4, core: 2. Of those that a mesh axis runs over, the one named last changes fastest.
Arguments:
- features: bfloat16 [8, 4, 16, 48, 512], P('gx', 'gy'), may hold values from -6 to 6
- block_slots: int32 [8, 4, 16], P('gx', 'gy'), may hold values from 0 to 15, as said below
- block_count: int32 [8, 4], P('gx', 'gy'), may hold values from 2 to 16
- cotangent: bfloat16 [8, 4, 16, 48, 512], P('gx', 'gy'), may hold values from -6 to 6
- fine_weight: bfloat16 [48, 27, 48], replicated, may hold values from -0.15625 to 0.15625
- down_weight: bfloat16 [48, 8, 48], replicated, may hold values from -0.3125 to 0.3125
- coarse_weight: bfloat16 [48, 27, 48], replicated, may hold values from -0.15625 to 0.15625
- up_weight: bfloat16 [8, 48, 48], replicated, may hold values from -0.875 to 0.875
Outputs:
- output: bfloat16 [8, 4, 16, 48, 512], P('gx', 'gy')
- input_grad: bfloat16 [8, 4, 16, 48, 512], P('gx', 'gy')
- fine_weight_grad: float32 [48, 27, 48], replicated
- down_weight_grad: float32 [48, 8, 48], replicated
- coarse_weight_grad: float32 [48, 27, 48], replicated
- up_weight_grad: float32 [8, 48, 48], replicated
Inputs may be any that keep to these rules, and one draw needn't show every extreme that they name: `block_slots`: on each device the 16 entries are distinct, so every block position of the region appears once.
All inputs are finite; a program needn't handle non-finite values.
Results may differ from a plain program's by a relative error of at most 0.008.
Values may be sent and summed in bfloat16 or wider, within the bound.
No kernel may reach another device: no remote copies, remote signals or barrier semaphores. Data moves between devices by JAX's collectives and lax.ppermute only.
A program may use at most 192 MiB of HBM per device.

v0:
```python
import math

import jax
import jax.numpy as jnp
from jax import lax
from jax.sharding import PartitionSpec as P

BLOCK = 8
VOX = 512
BX = 1
BY = 16


def with_halo(array, sides, width):
    for axis, dim in sides:
        devices, length = (lax.axis_size(axis), array.shape[dim])
        up = [(i, (i + 1) % devices) for i in range(devices - 1)]
        down = [(j, i) for i, j in up]
        last = lax.slice_in_dim(array, length - width, length, axis=dim)
        first = lax.slice_in_dim(array, 0, width, axis=dim)
        before = lax.ppermute(last, axis, up)
        after = lax.ppermute(first, axis, down)
        array = jnp.concatenate([before, array, after], axis=dim)
    return array


def split_parity(fine):
    lead = fine.shape[:-2]
    chans = fine.shape[-2]
    count = len(lead)
    shaped = fine.reshape(lead + (chans, 4, 2, 4, 2, 4, 2))
    order = tuple(range(count)) + (
        count + 2,
        count + 4,
        count + 6,
        count,
        count + 1,
        count + 3,
        count + 5,
    )
    return shaped.transpose(order).reshape(lead + (8, chans, 64))


def join_parity(parts):
    lead = parts.shape[:-3]
    chans = parts.shape[-2]
    count = len(lead)
    shaped = parts.reshape(lead + (2, 2, 2, chans, 4, 4, 4))
    order = tuple(range(count)) + (
        count + 3,
        count + 4,
        count,
        count + 5,
        count + 1,
        count + 6,
        count + 2,
    )
    return shaped.transpose(order).reshape(lead + (chans, 512))


def smooth_gate(value):
    return value * jax.nn.sigmoid(value)


def gate_slope(value):
    sigma = jax.nn.sigmoid(value)
    return sigma * (1.0 + value * (1.0 - sigma))


def block_grid(blocks, places, edge):
    chans = blocks.shape[1]
    dense = jnp.zeros((BX * BY, chans, edge**3), blocks.dtype).at[places].set(blocks)
    dense = dense.reshape(BX, BY, chans, edge, edge, edge)
    dense = dense.transpose(2, 3, 0, 4, 1, 5)
    return dense.reshape(chans, edge, BX * edge, BY * edge)


def grid_blocks(grid, places, edge):
    chans = grid.shape[0]
    shaped = grid.reshape(chans, edge, BX, edge, BY, edge).transpose(2, 4, 0, 1, 3, 5)
    return shaped.reshape(BX * BY, chans, edge**3)[places]


def depth_pad(grid):
    return jnp.pad(grid, ((0, 0), (1, 1), (0, 0), (0, 0)))


def conv_forward(padded, weight, edge):
    width_x = padded.shape[2] - 2
    width_y = padded.shape[3] - 2
    total = jnp.zeros((weight.shape[0], edge, width_x, width_y), jnp.float32)
    for depth in range(3):
        for across in range(3):
            for along in range(3):
                index = 9 * depth + 3 * across + along
                piece = padded[
                    :, depth : depth + edge, across : across + width_x, along : along + width_y
                ]
                total = total + jnp.einsum(
                    "oc,czxy->ozxy", weight[:, index, :], piece, preferred_element_type=jnp.float32
                )
    return total


def conv_backward(padded, weight, edge):
    width_x = padded.shape[2] - 2
    width_y = padded.shape[3] - 2
    total = jnp.zeros((weight.shape[2], edge, width_x, width_y), jnp.float32)
    for depth in range(3):
        for across in range(3):
            for along in range(3):
                index = 9 * depth + 3 * across + along
                piece = padded[
                    :,
                    2 - depth : 2 - depth + edge,
                    2 - across : 2 - across + width_x,
                    2 - along : 2 - along + width_y,
                ]
                total = total + jnp.einsum(
                    "oc,ozxy->czxy", weight[:, index, :], piece, preferred_element_type=jnp.float32
                )
    return total


def kernel_terms(grad_grid, padded, edge):
    width_x = padded.shape[2] - 2
    width_y = padded.shape[3] - 2
    terms = []
    for depth in range(3):
        for across in range(3):
            for along in range(3):
                piece = padded[
                    :, depth : depth + edge, across : across + width_x, along : along + width_y
                ]
                terms.append(
                    jnp.einsum(
                        "ozxy,czxy->oc", grad_grid, piece, preferred_element_type=jnp.float32
                    )
                )
    return jnp.stack(terms, axis=1)


def on_device(
    features,
    block_slots,
    block_count,
    cotangent,
    fine_weight,
    down_weight,
    coarse_weight,
    up_weight,
):
    slot_count = features.shape[2]
    chans = features.shape[3]
    half = BLOCK // 2
    places = block_slots.reshape(slot_count)
    live_count = block_count.reshape(())
    live = lax.iota(jnp.int32, slot_count) < live_count
    live_blocks = live[:, None, None]
    zero_half = jnp.zeros((), jnp.bfloat16)
    inputs = jnp.where(live_blocks, features.reshape(slot_count, chans, VOX), zero_half)
    grad_out = jnp.where(live_blocks, cotangent.reshape(slot_count, chans, VOX), zero_half)
    fine_pad = depth_pad(with_halo(block_grid(inputs, places, BLOCK), (("gx", 2), ("gy", 3)), 1))
    hidden_all = jnp.where(
        live_blocks, grid_blocks(conv_forward(fine_pad, fine_weight, BLOCK), places, BLOCK), 0.0
    )
    active_all = smooth_gate(hidden_all).astype(jnp.bfloat16)
    lowered_all = jnp.einsum(
        "oqc,sqcv->sov", down_weight, split_parity(active_all), preferred_element_type=jnp.float32
    )
    lowered_all = jnp.where(live_blocks, lowered_all, 0.0).astype(jnp.bfloat16)
    coarse_pad = depth_pad(
        with_halo(block_grid(lowered_all, places, half), (("gx", 2), ("gy", 3)), 1)
    )
    coarse = grid_blocks(conv_forward(coarse_pad, coarse_weight, half), places, half)
    rect = smooth_gate(coarse).astype(jnp.bfloat16)
    upward = join_parity(
        jnp.einsum("qoc,scv->sqov", up_weight, rect, preferred_element_type=jnp.float32)
    )
    output = jnp.where(live_blocks, hidden_all + upward, 0.0).astype(jnp.bfloat16)
    grad_parts = split_parity(grad_out)
    grad_rect = jnp.einsum(
        "qoc,sqov->scv", up_weight, grad_parts, preferred_element_type=jnp.float32
    )
    grad_coarse = jnp.where(live_blocks, grad_rect * gate_slope(coarse), 0.0).astype(jnp.bfloat16)
    up_local = jnp.einsum("sqov,scv->qoc", grad_parts, rect, preferred_element_type=jnp.float32)
    grad_coarse_grid = block_grid(grad_coarse, places, half)
    coarse_local = kernel_terms(grad_coarse_grid, coarse_pad, half)
    grad_coarse_pad = depth_pad(with_halo(grad_coarse_grid, (("gx", 2), ("gy", 3)), 1))
    grad_down = grid_blocks(conv_backward(grad_coarse_pad, coarse_weight, half), places, half)
    grad_down = jnp.where(live_blocks, grad_down, 0.0).astype(jnp.bfloat16)
    down_local = jnp.einsum(
        "sov,sqcv->oqc", grad_down, split_parity(active_all), preferred_element_type=jnp.float32
    )
    grad_act = join_parity(
        jnp.einsum("oqc,sov->sqcv", down_weight, grad_down, preferred_element_type=jnp.float32)
    )
    grad_hidden = grad_out.astype(jnp.float32) + grad_act * gate_slope(hidden_all)
    grad_hidden = jnp.where(live_blocks, grad_hidden, 0.0).astype(jnp.bfloat16)
    grad_hidden_grid = block_grid(grad_hidden, places, BLOCK)
    grad_hidden_pad = depth_pad(with_halo(grad_hidden_grid, (("gx", 2), ("gy", 3)), 1))
    fine_local = kernel_terms(grad_hidden_grid, fine_pad, BLOCK)
    input_grad = grid_blocks(conv_backward(grad_hidden_pad, fine_weight, BLOCK), places, BLOCK)
    input_grad = jnp.where(live_blocks, input_grad, 0.0).astype(jnp.bfloat16)
    fine_total, down_total, coarse_total, up_total = lax.psum(
        (fine_local, down_local, coarse_local, up_local), ("gx", "gy")
    )
    scale = 1.0 / math.sqrt(slot_count * VOX * lax.axis_size("gx") * lax.axis_size("gy"))
    shape_out = (1, 1, slot_count, chans, VOX)
    return (
        output.reshape(shape_out),
        input_grad.reshape(shape_out),
        fine_total * scale,
        down_total * scale,
        coarse_total * scale,
        up_total * scale,
    )


def solution(mesh):
    return jax.shard_map(
        on_device,
        mesh=mesh,
        in_specs=(
            P("gx", "gy", None, None, None),
            P("gx", "gy", None),
            P("gx", "gy"),
            P("gx", "gy", None, None, None),
            P(),
            P(),
            P(),
            P(),
        ),
        out_specs=(
            P("gx", "gy", None, None, None),
            P("gx", "gy", None, None, None),
            P(),
            P(),
            P(),
            P(),
        ),
        check_vma=False,
    )
```

profile of v0, /device:TPU:0, one launch (start us, length us, event | category | flops | bytes accessed | tf_op | source)
XLA Modules:
  0.0 446.1 jit_solution(6721761241236702699)
XLA Ops:
  16.8 4.8 %collective-permute-start = (bf16[48,8,1,128]{3,0,2,1:T(8,128)(2,1)}, bf16[48,8,1,128]{3,0,2,1:T(8,128)(2,1)S(1)}, u32[]{:S(2)}, u32[]{:S(2)}) collective-permute-start(bf16[48,8,1,128]{3,0,2,1:T(8,128)(2,1)} %get-tuple-element.76), channel_id=1, source_target_pairs={{0,4},{4,8},{8,12},{12,16},{16,20},{20,24},{24,28},{1,5},{5,9},{9,... | collective-permute-start | bytes 294920 | tf_op jit(solution)/shard_map/ppermute | solution.py:21
  25.0 2.9 copy.893
  39.8 2.3 select_maximum_fusion.4
  79.8 6.5 %fusion.661 = (bf16[48,8,8,128]{3,0,2,1:T(8,128)(2,1)}, bf16[48,8,8,128]{3,0,2,1:T(8,128)(2,1)}, bf16[48,8,8,128]{3,0,2,1:T(8,128)(2,1)}, bf16[48,8,8,128]{3,0,2...) fusion(bf16[48,10,10,130]{3,0,2,1:T(8,128)(2,1)S(1)} %select_ma, ...), kind=kLoop, calls=%fused_computation.811 | loop fusion | bytes 28311552 | tf_op jit(solution)/shard_map/slice | solution.py:96
  86.4 3.1 fusion.662
  90.1 13.9 %bitcast_add_fusion.10 = f32[48,8,8,128]{3,0,2,1:T(8,128)} fusion(f32[8,8,128,48]{2,3,1,0:T(8,128)} %fusion.368, f32[8,8,128,48]{2,3,1,0:T(8,128)} %fusion.371, f32[8,8,128,48]{2,3,1,0:T(8,128)} %fusion.374, f32[8,8,128,48]{2,3,1,0:T(8,128)} %fusion.377, f32[8,8,128,48]{2,3,1,0:T(8,128)} %fusion.380, f32[8,8,128,48]{2,3,1,0:T(8,128)} %fusion.383, ...), kind=kOutput, calls=%fused_computation.59 | convolution fusion | flops 47972352 | bytes 43266048 | tf_op jit(solution)/shard_map/oc,czxy->ozxy/dot_general | solution.py:99
  104.0 3.8 copy.872
  107.8 4.7 %copy.873 = f32[1,16,48,8,8,8]{2,5,4,3,1,0:T(8,128)} copy(f32[1,16,48,8,8,8]{2,5,1,4,3,0:T(8,128)} %bitcast.1422) | data formatting | bytes 3145728 | tf_op jit(solution)/shard_map/transpose | solution.py:80
  112.5 2.8 copy.874
  116.0 3.8 copy.875
  119.8 3.3 fusion.16
  126.9 4.4 collective-permute-start.4
  133.1 4.7 %collective-permute-done.5 = bf16[48,4,1,64]{3,0,2,1:T(8,128)(2,1)S(1)} collective-permute-done((bf16[48,4,1,64]{3,0,2,1:T(8,128)(2,1)S(1)}, bf16[48,4,1,64]{3,0,2,1:T(8,128)(2,1)S(1)}, u32[]{:S(2)}, u32[]{:S(2)}) %collective-permute-start.5) | collective-permute-done | bytes 24608 | tf_op jit(solution)/shard_map/ppermute | solution.py:22
  138.0 3.7 collective-permute-start.6
  143.6 3.9 collective-permute-done.7
  149.3 2.5 fusion.668
  160.5 2.7 fusion.67
  166.2 3.0 fusion.82
  175.9 4.8 %collective-permute-start.8 = (bf16[48,4,1,64]{3,0,2,1:T(8,128)(2,1)S(1)}, bf16[48,4,1,64]{3,0,2,1:T(8,128)(2,1)S(1)}, u32[]{:S(2)}, u32[]{:S(2)}) collective-permute-start(bf16[48,4,1,64]{3,0,2,1:T(8,128)(2,1)S(1)} %get-tuple-element.110), channel_id=1, source_target_pairs={{0,4},{4,8},{8,12},{12,16},{16,20},{20,24},{24,28},{1,5},{5,9},{9,... | collective-permute-start | bytes 73736 | tf_op jit(solution)/shard_map/ppermute | solution.py:21
  182.4 5.2 %copy.890 = f32[16,8,48,64]{2,0,3,1:T(8,128)} copy(f32[16,8,48,64]{3,2,1,0:T(8,128)} %convolution_bitcast_fusion.1) | data formatting | bytes 3145728 | tf_op jit(solution)/shard_map/qoc,scv->sqov/transpose | solution.py:178
  187.6 4.7 %copy.891 = f32[16,48,4,2,4,2,4,2]{1,0,7,6,5,4,3,2:T(8,128)} copy(f32[16,48,4,2,4,2,4,2]{1,0,6,4,2,7,5,3:T(8,128)} %bitcast.1420) | data formatting | bytes 3145728 | tf_op jit(solution)/shard_map/transpose | solution.py:58
  192.4 2.8 copy.892
  205.5 6.7 %collective-permute-start.10 = (bf16[48,4,6,1]{3,0,2,1:T(8,128)(2,1)S(1)}, bf16[48,4,6,1]{3,0,2,1:T(8,128)(2,1)S(1)}, u32[]{:S(2)}, u32[]{:S(2)}) collective-permute-start(bf16[48,4,6,1]{3,0,2,1:T(8,128)(2,1)S(1)} %get-tuple-element.105), channel_id=1, source_target_pairs={{0,1},{1,2},{2,3},{4,5},{5,6},{6,7},{8,9},{9,10},{10,11},{12,13},{... | collective-permute-start | bytes 6920 | tf_op jit(solution)/shard_map/ppermute | solution.py:21
  226.5 5.2 %copy.936 = f32[16,8,48,64]{2,0,3,1:T(8,128)} copy(f32[16,8,48,64]{3,2,1,0:T(8,128)} %convolution_bitcast_fusion) | data formatting | bytes 3145728 | tf_op jit(solution)/shard_map/oqc,sov->sqcv/transpose | solution.py:196
  231.7 4.7 %copy.937 = f32[16,48,4,2,4,2,4,2]{1,0,7,6,5,4,3,2:T(8,128)} copy(f32[16,48,4,2,4,2,4,2]{1,0,6,4,2,7,5,3:T(8,128)} %bitcast.1421) | data formatting | bytes 3145728 | tf_op jit(solution)/shard_map/transpose | solution.py:58
  236.4 2.8 copy.938
  239.2 2.8 select_convert_fusion
  273.7 5.1 %collective-permute-start.12 = (bf16[48,8,1,128]{3,0,2,1:T(8,128)(2,1)S(1)}, bf16[48,8,1,128]{3,0,2,1:T(8,128)(2,1)S(1)}, u32[]{:S(2)}, u32[]{:S(2)}) collective-permute-start(bf16[48,8,1,128]{3,0,2,1:T(8,128)(2,1)S(1)} %get-tuple-element.72), channel_id=1, source_target_pairs={{0,4},{4,8},{8,12},{12,16},{16,20},{20,24},{24,28},{1,5},{5,9},{9,... | collective-permute-start | bytes 294920 | tf_op jit(solution)/shard_map/ppermute | solution.py:21
  278.8 2.5 fusion.100
  296.2 6.6 %collective-permute-start.14 = (bf16[48,8,10,1]{0,1,3,2:T(8,128)(2,1)S(1)}, bf16[48,8,10,1]{0,1,3,2:T(8,128)(2,1)S(1)}, u32[]{:S(2)}, u32[]{:S(2)}) collective-permute-start(bf16[48,8,10,1]{0,1,3,2:T(8,128)(2,1)S(1)} %copy.944), channel_id=1, source_target_pairs={{0,1},{1,2},{2,3},{4,5},{5,6},{6,7},{8,9},{9,10},{10,11},{12,13},{... | collective-permute-start | bytes 23048 | tf_op jit(solution)/shard_map/ppermute | solution.py:21
  349.8 12.0 %bitcast_add_fusion = bf16[48,8,8,128]{3,0,2,1:T(8,128)(2,1)S(1)} fusion(f32[8,8,128,48]{2,3,1,0:T(8,128)} %fusion.154, f32[8,8,128,48]{2,3,1,0:T(8,128)} %fusion.156, f32[8,8,128,48]{2,3,1,0:T(8,128)} %fusion.158, f32[8,8,128,48]{2,3,1,0:T(8,128)} %fusion.160, f32[8,8,128,48]{2,3,1,0:T(8,128)} %fusion.162, f32[8,8,128,48]{2,3,1,0:T(8,128)} %fusion.164, ...), kind=kOutput, calls=%fused_computation.45 | convolution fusion | flops 48365568 | bytes 42479616 | tf_op jit(solution)/shard_map/oc,ozxy->czxy/dot_general | solution.py:119
  368.6 64.8 %all-reduce.7.cloned.1.call-done = (f32[48,27,48]{2,0,1:T(8,128)}, f32[48,8,48]{2,0,1:T(8,128)}, f32[48,27,48]{2,0,1:T(8,128)}, f32[8,48,48]{2,1,0:T(8,128)}) async-done(((f32[48,27,48]{2,0,1:T(8,128)}, f32[48,8,48]{2,0,1:T(8,128)}, f32[48,27,48]{2,0,1:T(8,128)}, f32[8,48,48]{2,1,0:T(8,128)}), (f32[48,27,48]{2,0,1:T(8,128)}, f32[48,8,48]{2,0,1:T(8,128)}, f32[48,27,48]{2,0,1:T(8,128)}, ...) | async-done | bytes 645136 | tf_op jit(solution)/shard_map/psum | solution.py:205
  (436 shorter events, 221.7 us)
Async XLA Ops:
  7.2 153.3 %copy-start = (bf16[8,48,48]{2,1,0:T(8,128)(2,1)S(1)}, bf16[8,48,48]{2,1,0:T(8,128)(2,1)}, u32[]{:S(2)}) copy-start(bf16[8,48,48]{2,1,0:T(8,128)(2,1)} %param.15) | copy-start | bytes 110596
  7.2 426.1 %all-reduce.7.cloned.1.call-start = ((), (), s32[]{:S(2)}) async-start(), calls=%async_computation | async-start | bytes 3440640 | tf_op jit(solution)/shard_map/psum | solution.py:205
  12.1 10.9 %copy-start.2 = (bf16[16,48,512]{1,2,0:T(8,128)(2,1)}, bf16[16,48,512]{1,2,0:T(8,128)(2,1)S(1)}, u32[]{:S(2)}) copy-start(bf16[16,48,512]{1,2,0:T(8,128)(2,1)S(1)} %copy.858) | copy-start | bytes 2359300
  14.1 8.9 %copy-start.21 = (bf16[48,27,48]{2,0,1:T(8,128)(2,1)S(1)}, bf16[48,27,48]{2,0,1:T(8,128)(2,1)}, u32[]{:S(2)}) copy-start(bf16[48,27,48]{2,0,1:T(8,128)(2,1)} %param.12) | copy-start | bytes 373252
  16.8 14.2 %collective-permute-start = (bf16[48,8,1,128]{3,0,2,1:T(8,128)(2,1)}, bf16[48,8,1,128]{3,0,2,1:T(8,128)(2,1)S(1)}, u32[]{:S(2)}, u32[]{:S(2)}) collective-permute-start(bf16[48,8,1,128]{3,0,2,1:T(8,128)(2,1)} %get-tuple-element.76), channel_id=1, source_target_pairs={{0,4},{4,8},{8,12},{12,16},{16,20},{20,24},{24,28},{1,5},{5,9},{9,... | collective-permute-start | bytes 294920 | tf_op jit(solution)/shard_map/ppermute | solution.py:21
  21.6 9.3 %collective-permute-start.1 = (bf16[48,8,1,128]{3,0,2,1:T(8,128)(2,1)}, bf16[48,8,1,128]{3,0,2,1:T(8,128)(2,1)S(1)}, u32[]{:S(2)}, u32[]{:S(2)}) collective-permute-start(bf16[48,8,1,128]{3,0,2,1:T(8,128)(2,1)} %get-tuple-element.77), channel_id=1, source_target_pairs={{4,0},{8,4},{12,8},{16,12},{20,16},{24,20},{28,24},{5,1},{9,5},{13... | collective-permute-start | bytes 294920 | tf_op jit(solution)/shard_map/ppermute | solution.py:22
  32.0 6.6 %collective-permute-start.2 = (bf16[48,8,10,1]{0,1,3,2:T(8,128)(2,1)S(1)}, bf16[48,8,10,1]{0,1,3,2:T(8,128)(2,1)S(1)}, u32[]{:S(2)}, u32[]{:S(2)}) collective-permute-start(bf16[48,8,10,1]{0,1,3,2:T(8,128)(2,1)S(1)} %copy.863), channel_id=1, source_target_pairs={{0,1},{1,2},{2,3},{4,5},{5,6},{6,7},{8,9},{9,10},{10,11},{12,13},{... | collective-permute-start | bytes 23048 | tf_op jit(solution)/shard_map/ppermute | solution.py:21
  34.1 5.2 %collective-permute-start.3 = (bf16[48,8,10,1]{0,1,3,2:T(8,128)(2,1)S(1)}, bf16[48,8,10,1]{0,1,3,2:T(8,128)(2,1)S(1)}, u32[]{:S(2)}, u32[]{:S(2)}) collective-permute-start(bf16[48,8,10,1]{0,1,3,2:T(8,128)(2,1)S(1)} %copy.864), channel_id=1, source_target_pairs={{1,0},{2,1},{3,2},{5,4},{6,5},{7,6},{9,8},{10,9},{11,10},{13,12},{... | collective-permute-start | bytes 23048 | tf_op jit(solution)/shard_map/ppermute | solution.py:22
  124.1 8.6 %copy-start.23 = (bf16[48,27,48]{2,0,1:T(8,128)(2,1)S(1)}, bf16[48,27,48]{2,0,1:T(8,128)(2,1)}, u32[]{:S(2)}) copy-start(bf16[48,27,48]{2,0,1:T(8,128)(2,1)} %param.14) | copy-start | bytes 373252
  126.9 6.1 %collective-permute-start.4 = (bf16[48,4,1,64]{3,0,2,1:T(8,128)(2,1)S(1)}, bf16[48,4,1,64]{3,0,2,1:T(8,128)(2,1)S(1)}, u32[]{:S(2)}, u32[]{:S(2)}) collective-permute-start(bf16[48,4,1,64]{3,0,2,1:T(8,128)(2,1)S(1)} %get-tuple-element.114), channel_id=1, source_target_pairs={{0,4},{4,8},{8,12},{12,16},{16,20},{20,24},{24,28},{1,5},{5,9},{9,... | collective-permute-start | bytes 73736 | tf_op jit(solution)/shard_map/ppermute | solution.py:21
  131.3 6.4 %collective-permute-start.5 = (bf16[48,4,1,64]{3,0,2,1:T(8,128)(2,1)S(1)}, bf16[48,4,1,64]{3,0,2,1:T(8,128)(2,1)S(1)}, u32[]{:S(2)}, u32[]{:S(2)}) collective-permute-start(bf16[48,4,1,64]{3,0,2,1:T(8,128)(2,1)S(1)} %get-tuple-element.115), channel_id=1, source_target_pairs={{4,0},{8,4},{12,8},{16,12},{20,16},{24,20},{28,24},{5,1},{9,5},{13... | collective-permute-start | bytes 73736 | tf_op jit(solution)/shard_map/ppermute | solution.py:22
  138.0 5.6 %collective-permute-start.6 = (bf16[48,4,6,1]{3,0,2,1:T(8,128)(2,1)S(1)}, bf16[48,4,6,1]{3,0,2,1:T(8,128)(2,1)S(1)}, u32[]{:S(2)}, u32[]{:S(2)}) collective-permute-start(bf16[48,4,6,1]{3,0,2,1:T(8,128)(2,1)S(1)} %get-tuple-element.108), channel_id=1, source_target_pairs={{0,1},{1,2},{2,3},{4,5},{5,6},{6,7},{8,9},{9,10},{10,11},{12,13},{... | collective-permute-start | bytes 6920 | tf_op jit(solution)/shard_map/ppermute | solution.py:21
  141.6 5.8 %collective-permute-start.7 = (bf16[48,4,6,1]{3,0,2,1:T(8,128)(2,1)S(1)}, bf16[48,4,6,1]{3,0,2,1:T(8,128)(2,1)S(1)}, u32[]{:S(2)}, u32[]{:S(2)}) collective-permute-start(bf16[48,4,6,1]{3,0,2,1:T(8,128)(2,1)S(1)} %get-tuple-element.109), channel_id=1, source_target_pairs={{1,0},{2,1},{3,2},{5,4},{6,5},{7,6},{9,8},{10,9},{11,10},{13,12},{... | collective-permute-start | bytes 6920 | tf_op jit(solution)/shard_map/ppermute | solution.py:22
  143.2 5.3 %copy-start.50 = (bf16[48,4,4,64]{3,0,2,1:T(8,128)(2,1)}, bf16[48,4,4,64]{3,0,2,1:T(8,128)(2,1)S(1)}, u32[]{:S(2)}) copy-start(bf16[48,4,4,64]{3,0,2,1:T(8,128)(2,1)S(1)} %get-tuple-element.113) | copy-start | bytes 294916
  143.2 5.3 %copy-start.52 = (bf16[48,4,4,64]{3,0,2,1:T(8,128)(2,1)}, bf16[48,4,4,64]{3,0,2,1:T(8,128)(2,1)S(1)}, u32[]{:S(2)}) copy-start(bf16[48,4,4,64]{3,0,2,1:T(8,128)(2,1)S(1)} %get-tuple-element.112) | copy-start | bytes 294916
  164.9 10.7 %copy-start.16 = (bf16[48,4,1,4,16,4]{0,5,4,3,1,2:T(4,128)(2,1)}, bf16[48,4,1,4,16,4]{0,5,4,3,1,2:T(4,128)(2,1)S(1)}, u32[]{:S(2)}) copy-start(bf16[48,4,1,4,16,4]{0,5,4,3,1,2:T(4,128)(2,1)S(1)} %copy.898) | copy-start | bytes 294916
  175.9 29.3 %collective-permute-start.8 = (bf16[48,4,1,64]{3,0,2,1:T(8,128)(2,1)S(1)}, bf16[48,4,1,64]{3,0,2,1:T(8,128)(2,1)S(1)}, u32[]{:S(2)}, u32[]{:S(2)}) collective-permute-start(bf16[48,4,1,64]{3,0,2,1:T(8,128)(2,1)S(1)} %get-tuple-element.110), channel_id=1, source_target_pairs={{0,4},{4,8},{8,12},{12,16},{16,20},{20,24},{24,28},{1,5},{5,9},{9,... | collective-permute-start | bytes 73736 | tf_op jit(solution)/shard_map/ppermute | solution.py:21
  180.7 24.5 %collective-permute-start.9 = (bf16[48,4,1,64]{3,0,2,1:T(8,128)(2,1)S(1)}, bf16[48,4,1,64]{3,0,2,1:T(8,128)(2,1)S(1)}, u32[]{:S(2)}, u32[]{:S(2)}) collective-permute-start(bf16[48,4,1,64]{3,0,2,1:T(8,128)(2,1)S(1)} %get-tuple-element.111), channel_id=1, source_target_pairs={{4,0},{8,4},{12,8},{16,12},{20,16},{24,20},{28,24},{5,1},{9,5},{13... | collective-permute-start | bytes 73736 | tf_op jit(solution)/shard_map/ppermute | solution.py:22
  196.6 5.2 %copy-start.60 = (bf16[48,4,4,64]{3,0,2,1:T(8,128)(2,1)S(1)}, bf16[48,4,4,64]{3,0,2,1:T(8,128)(2,1)}, u32[]{:S(2)}) copy-start(bf16[48,4,4,64]{3,0,2,1:T(8,128)(2,1)} %get-tuple-element.81) | copy-start | bytes 294916
  196.6 6.1 %copy-start.59 = (bf16[48,4,4,64]{3,0,2,1:T(8,128)(2,1)S(1)}, bf16[48,4,4,64]{3,0,2,1:T(8,128)(2,1)}, u32[]{:S(2)}) copy-start(bf16[48,4,4,64]{3,0,2,1:T(8,128)(2,1)} %get-tuple-element.80) | copy-start | bytes 294916
  197.5 6.0 %copy-start.58 = (bf16[48,4,4,64]{3,0,2,1:T(8,128)(2,1)S(1)}, bf16[48,4,4,64]{3,0,2,1:T(8,128)(2,1)}, u32[]{:S(2)}) copy-start(bf16[48,4,4,64]{3,0,2,1:T(8,128)(2,1)} %get-tuple-element.79) | copy-start | bytes 294916
  198.3 6.0 %copy-start.57 = (bf16[48,4,4,64]{3,0,2,1:T(8,128)(2,1)S(1)}, bf16[48,4,4,64]{3,0,2,1:T(8,128)(2,1)}, u32[]{:S(2)}) copy-start(bf16[48,4,4,64]{3,0,2,1:T(8,128)(2,1)} %get-tuple-element.78) | copy-start | bytes 294916
  201.8 11.7 %copy-start.24 = (bf16[48,27,48]{2,0,1:T(8,128)(2,1)S(1)}, bf16[48,27,48]{2,0,1:T(8,128)(2,1)}, u32[]{:S(2)}) copy-start(bf16[48,27,48]{2,0,1:T(8,128)(2,1)} %param.14) | copy-start | bytes 373252
  205.5 8.5 %collective-permute-start.10 = (bf16[48,4,6,1]{3,0,2,1:T(8,128)(2,1)S(1)}, bf16[48,4,6,1]{3,0,2,1:T(8,128)(2,1)S(1)}, u32[]{:S(2)}, u32[]{:S(2)}) collective-permute-start(bf16[48,4,6,1]{3,0,2,1:T(8,128)(2,1)S(1)} %get-tuple-element.105), channel_id=1, source_target_pairs={{0,1},{1,2},{2,3},{4,5},{5,6},{6,7},{8,9},{9,10},{10,11},{12,13},{... | collective-permute-start | bytes 6920 | tf_op jit(solution)/shard_map/ppermute | solution.py:21
  212.2 3.5 collective-permute-start.11
  224.3 7.4 %copy-start.48 = (bf16[16,48,64]{2,1,0:T(8,128)(2,1)}, bf16[16,48,64]{2,1,0:T(8,128)(2,1)S(1)}, u32[]{:S(2)}) copy-start(bf16[16,48,64]{2,1,0:T(8,128)(2,1)S(1)} %gather_fusion.2) | copy-start | bytes 294916
  272.4 22.7 %collective-permute-start.13 = (bf16[48,8,1,128]{3,0,2,1:T(8,128)(2,1)}, bf16[48,8,1,128]{3,0,2,1:T(8,128)(2,1)S(1)}, u32[]{:S(2)}, u32[]{:S(2)}) collective-permute-start(bf16[48,8,1,128]{3,0,2,1:T(8,128)(2,1)} %get-tuple-element.73), channel_id=1, source_target_pairs={{4,0},{8,4},{12,8},{16,12},{20,16},{24,20},{28,24},{5,1},{9,5},{13... | collective-permute-start | bytes 294920 | tf_op jit(solution)/shard_map/ppermute | solution.py:22
  273.7 21.5 %collective-permute-start.12 = (bf16[48,8,1,128]{3,0,2,1:T(8,128)(2,1)S(1)}, bf16[48,8,1,128]{3,0,2,1:T(8,128)(2,1)S(1)}, u32[]{:S(2)}, u32[]{:S(2)}) collective-permute-start(bf16[48,8,1,128]{3,0,2,1:T(8,128)(2,1)S(1)} %get-tuple-element.72), channel_id=1, source_target_pairs={{0,4},{4,8},{8,12},{12,16},{16,20},{20,24},{24,28},{1,5},{5,9},{9,... | collective-permute-start | bytes 294920 | tf_op jit(solution)/shard_map/ppermute | solution.py:21
  296.2 11.6 %collective-permute-start.14 = (bf16[48,8,10,1]{0,1,3,2:T(8,128)(2,1)S(1)}, bf16[48,8,10,1]{0,1,3,2:T(8,128)(2,1)S(1)}, u32[]{:S(2)}, u32[]{:S(2)}) collective-permute-start(bf16[48,8,10,1]{0,1,3,2:T(8,128)(2,1)S(1)} %copy.944), channel_id=1, source_target_pairs={{0,1},{1,2},{2,3},{4,5},{5,6},{6,7},{8,9},{9,10},{10,11},{12,13},{... | collective-permute-start | bytes 23048 | tf_op jit(solution)/shard_map/ppermute | solution.py:21
  303.3 5.1 %collective-permute-start.15 = (bf16[48,8,10,1]{0,1,3,2:T(8,128)(2,1)S(1)}, bf16[48,8,10,1]{0,1,3,2:T(8,128)(2,1)S(1)}, u32[]{:S(2)}, u32[]{:S(2)}) collective-permute-start(bf16[48,8,10,1]{0,1,3,2:T(8,128)(2,1)S(1)} %copy.945), channel_id=1, source_target_pairs={{1,0},{2,1},{3,2},{5,4},{6,5},{7,6},{9,8},{10,9},{11,10},{13,12},{... | collective-permute-start | bytes 23048 | tf_op jit(solution)/shard_map/ppermute | solution.py:22
  343.4 6.5 %copy-start.11 = (f32[8,8,128,48]{2,3,1,0:T(8,128)S(1)}, f32[8,8,128,48]{2,3,1,0:T(8,128)}, u32[]{:S(2)}) copy-start(f32[8,8,128,48]{2,3,1,0:T(8,128)} %fusion.174) | copy-start | bytes 4718596
  367.4 71.4 %copy-start.1 = (bf16[8,48,48]{2,1,0:T(8,128)(2,1)S(1)}, bf16[8,48,48]{2,1,0:T(8,128)(2,1)}, u32[]{:S(2)}) copy-start(bf16[8,48,48]{2,1,0:T(8,128)(2,1)} %param.15) | copy-start | bytes 110596
  (70 other events, 145.0 us)
Sparse Core Ops, SparseCore 0:
  295.3 137.9 all-reduce.6
where the time goes:
time: 453 us; the launch traced here: 446 us
  matrix products  176 us (39%)
  local copies, waits for them, and re-layouts  104 us (23%)
  waiting for transfers between devices  75.1 us (17%)
  starting transfers between devices  48.5 us (11%)
  other arithmetic  25.1 us (6%)
  between operations  16.8 us (4%)
    psum x1, waiting for transfers between devices, on_device(): lax.psum((fine_local, down_local, coarse_local, up_local), ('gx', 'gy'))  64.8 us
    dot_general x54, matrix products, conv_backward(): jnp.einsum('oc,ozxy->czxy', weight[:, index, :], piece, preferred_element...  62.6 us
    dot_general x54, matrix products, conv_forward(): jnp.einsum('oc,czxy->ozxy', weight[:, index, :], piece, preferred_element...  61.4 us
    dot_general x54, matrix products, kernel_terms(): jnp.einsum('ozxy,czxy->oc', grad_grid, piece, preferred_element_type=jnp....  39.8 us
    ppermute x8, starting transfers between devices, with_halo(): before = lax.ppermute(last, axis, up)  37.5 us
    unnamed x173, local copies, waits for them, and re-layouts  13.5 us
    slice x4, local copies, waits for them, and re-layouts, conv_forward(): padded[:, depth:depth + edge, across:across + width_x, along:along + widt...  13.3 us
    ppermute x8, starting transfers between devices, with_halo(): after = lax.ppermute(first, axis, down)  10.9 us
  transfers between devices with their start and end apart: 17, of which 5 were waited for; matrix products, arithmetic and copies ran while one was open for 26% of the time, Pallas kernels for 0%

commit v1 on v0

v1 whole, which is shorter than its diff:
```python
import math

import jax
import jax.numpy as jnp
import numpy as np
from jax import lax
from jax.experimental import pallas as pl
from jax.experimental.pallas import tpu as pltpu
from jax.sharding import PartitionSpec as P

C = 48
EDGE = 8
VOX = 512
LANES = 128
F32 = jnp.float32
BF16 = jnp.bfloat16
VMEM_LIMIT = 58 * 1024 * 1024
SHIFTS = (0, 1, 16, 17)


def placing_matrix():
    place = np.zeros((1024, 8 * LANES), np.float32)
    for z in range(8):
        for y in range(8):
            for x in range(8):
                place[64 * z + 8 * x + y, LANES * y + 16 * z + x + 4] = 1.0
            for x in range(4):
                place[512 + 32 * z + 8 * x + y, LANES * y + 16 * z + x] = 1.0
                place[768 + 32 * z + 8 * x + y, LANES * y + 16 * z + x + 12] = 1.0
    return place


def edge_matrix():
    pick = np.zeros((512, 512), np.float32)
    for z in range(8):
        for y in range(8):
            for x in range(8):
                pick[64 * z + 8 * x + y, 256 * (x // 4) + 32 * z + 8 * (x % 4) + y] = 1.0
    return pick


def dot(left, right, contract=(1, 0)):
    dims = (((contract[0],), (contract[1],)), ((), ()))
    return lax.dot_general(left, right, dims, preferred_element_type=F32)


def roll(value, shift):
    return pltpu.roll(value, shift % LANES, 1)


def lane_ids(rows):
    return lax.broadcasted_iota(jnp.int32, (rows, LANES), 1)


def silu_parts(value):
    sigma = 1.0 / (1.0 + jnp.exp(-value))
    return value * sigma, sigma * (1.0 + value * (1.0 - sigma))


def columns(tile, low, high, z_step, x_step):
    zero = jnp.zeros_like(tile)
    below = jnp.where(low, zero, roll(tile, z_step))
    above = jnp.where(high, zero, roll(tile, -z_step))
    base = jnp.concatenate([below, tile, above], axis=0)
    return jnp.concatenate([roll(base, x_step), base, roll(base, -x_step)], axis=0)


def z_masks(z_step):
    ids = lane_ids(C)
    return ids < z_step, ids >= LANES - z_step


def gather_sub(parts):
    total = parts[:C]
    for index in range(1, 4):
        total = total + roll(parts[index * C : (index + 1) * C], -SHIFTS[index])
    return total


def spread_sub(anchored):
    return jnp.concatenate([anchored] + [roll(anchored, step) for step in SHIFTS[1:]], axis=0)


def anchor_mask(own):
    ids = lane_ids(C)
    across = ids % 16
    keep = ((ids // 16) % 2 == 0) & (across % 2 == 0)
    if own:
        keep = keep & (across >= 4) & (across < 12)
    return keep.astype(F32)


def loop(low, high, body, unroll=1):
    def step(index, carry):
        body(index)
        return carry

    lax.fori_loop(low, high, step, 0, unroll=unroll)


def prepare_kernel(
    slots, count, feats, cots, pick, own, cot, x_low, x_high, y_low, y_high, d_ll, d_lh, d_hl, d_hh
):
    number = feats.shape[0]
    rows = lax.broadcasted_iota(jnp.int32, (C, VOX), 0)
    flags = jnp.zeros((C, VOX), F32)
    first = jnp.zeros((), F32)
    last = jnp.zeros((), F32)
    zero = jnp.zeros((C, VOX), BF16)
    for slot in range(number):
        live = slot < count[0]
        alive = jnp.where(live, 1.0, 0.0)
        place = slots[slot]
        own[place] = jnp.where(live, feats[slot], zero)
        cot[place] = jnp.where(live, cots[slot], zero)
        flags = jnp.where(rows == place + 1, alive, flags)
        first = first + jnp.where(place == 0, alive, 0.0)
        last = last + jnp.where(place == number - 1, alive, 0.0)
    own[number] = flags.astype(BF16)
    first_flag = jnp.where(rows == number + 1, first, 0.0).astype(BF16)
    last_flag = jnp.where(rows == 0, last, 0.0).astype(BF16)
    packed = dot(own[...].reshape((number + 1) * C, VOX), pick[...]).astype(BF16)
    packed = packed.reshape(number + 1, C, VOX)
    x_low[...] = packed[:, :, :256]
    x_high[...] = packed[:, :, 256:]
    for out, index, flag in ((y_low, 0, first_flag), (y_high, number - 1, last_flag)):
        out[0] = own[index]
        out[1] = cot[index]
        out[2] = flag
    for out, index, flag, at in (
        (d_ll, 0, first_flag, 0),
        (d_lh, number - 1, last_flag, 0),
        (d_hl, 0, first_flag, 256),
        (d_hh, number - 1, last_flag, 256),
    ):
        out[0] = packed[index, :, at : at + 256]
        out[1] = flag[:, :256]


def forward_kernel(
    own, cot, x_left, x_right, y_left, y_right, d_ll, d_lr, d_rl, d_rr, place, fine_w, down_w,
    coarse_w, up_w,
    grid, cot_grid, hidden, lowered, rects, grad_c, live, pack_low, pack_high,
    rows_in, rows_cot, fine_p, coarse_p,
):
    number = cot.shape[0]
    last = number + 1
    for block in range(number):
        at = (block + 1) * C
        rows_in[at : at + C, 0:512] = own[block]
        rows_in[at : at + C, 512:768] = x_left[block]
        rows_in[at : at + C, 768:1024] = x_right[block]
        rows_cot[at : at + C, :] = cot[block]
    for at, middle, left, right in (
        (0, y_left, d_ll, d_rl),
        (last * C, y_right, d_lr, d_rr),
    ):
        rows_in[at : at + C, 0:512] = middle[0]
        rows_in[at : at + C, 512:768] = left[0]
        rows_in[at : at + C, 768:1024] = right[0]
        rows_cot[at : at + C, :] = middle[1]
    at = (last + 1) * C
    rows_in[at : at + C, 0:512] = own[number] + y_left[2] + y_right[2]
    rows_in[at : at + C, 512:768] = x_left[number] + d_ll[1] + d_lr[1]
    rows_in[at : at + C, 768:1024] = x_right[number] + d_rl[1] + d_rr[1]
    for pair in range(4):
        lanes = slice(256 * pair, 256 * pair + 256)
        placed = dot(rows_in[...], place[:, lanes])
        placed_cot = dot(rows_cot[...], place[0:512, lanes])
        for half in range(2):
            span = slice(LANES * half, LANES * (half + 1))
            for block in range(last + 1):
                tile = EDGE * block + 2 * pair + half
                grid[tile] = placed[block * C : (block + 1) * C, span].astype(BF16)
                cot_grid[tile] = placed_cot[block * C : (block + 1) * C, span].astype(BF16)
        if pair == 0:
            live[...] = placed[(last + 1) * C :, 0:LANES]
    tiles = grid.shape[0]
    coarse_tiles = lowered.shape[0]
    low, high = z_masks(16)

    def fine_step(index):
        tile = 1 + 2 * index
        cols = jnp.concatenate(
            [columns(grid[tile], low, high, 16, 1), columns(grid[tile + 1], low, high, 16, 1)],
            axis=1,
        )
        out = dot(fine_w[...], cols)
        fine_p[tile] = out[:, :LANES]
        fine_p[tile + 1] = out[:, LANES:]

    loop(0, (tiles - 2) // 2, fine_step, 2)
    anchors = anchor_mask(False)

    def lower_step(coarse):
        alive = jnp.broadcast_to(live[pl.ds(coarse // 4, 1), :], (C, LANES))
        actives = []
        for half in range(2):
            tile = 2 * coarse + half
            value = fine_p[tile - 1, 0:C] + fine_p[tile, C : 2 * C] + fine_p[tile + 1, 2 * C :]
            value = value * alive
            hidden[tile] = value
            actives.append(silu_parts(value)[0].astype(BF16))
        parts = dot(down_w[...], jnp.concatenate(actives, axis=0))
        lowered[coarse] = (gather_sub(parts) * (alive * anchors)).astype(BF16)

    loop(1, coarse_tiles - 1, lower_step, 2)
    low_c, high_c = z_masks(32)

    def coarse_step(index):
        coarse = 1 + 2 * index
        cols = jnp.concatenate(
            [
                columns(lowered[coarse], low_c, high_c, 32, 2),
                columns(lowered[coarse + 1], low_c, high_c, 32, 2),
            ],
            axis=1,
        )
        out = dot(coarse_w[...], cols)
        coarse_p[coarse] = out[:, :LANES]
        coarse_p[coarse + 1] = out[:, LANES:]

    loop(0, (coarse_tiles - 2) // 2, coarse_step, 2)
    own_anchors = anchor_mask(True)

    def grad_step(coarse):
        alive = jnp.broadcast_to(live[pl.ds(coarse // 4, 1), :], (C, LANES))
        value = (
            coarse_p[coarse - 1, 0:C] + coarse_p[coarse, C : 2 * C] + coarse_p[coarse + 1, 2 * C :]
        )
        smooth, slope = silu_parts(value)
        rects[coarse] = (smooth * own_anchors).astype(BF16)
        pair = jnp.concatenate([cot_grid[2 * coarse], cot_grid[2 * coarse + 1]], axis=0)
        grad_rect = gather_sub(dot(up_w[...], pair, (0, 0)))
        grad_c[coarse] = (grad_rect * slope * (alive * own_anchors)).astype(BF16)

    loop(2, coarse_tiles - 2, grad_step, 2)
    ids = lane_ids(C)
    zero = jnp.zeros((C, LANES), BF16)
    for out, lane in ((pack_low, 4), (pack_high, 10)):
        for group in range(out.shape[0]):
            total = zero
            for coarse in range(max(2, 32 * group), min(coarse_tiles - 2, 32 * group + 32)):
                picked = jnp.where(ids % 32 == lane, grad_c[coarse], zero)
                total = total + roll(picked, coarse % 32 - lane)
            out[group] = total


def to_blocks(slots, rows_out, place, out):
    flat = dot(rows_out[...], place[...], (1, 1)).astype(BF16)
    rows_out[:, 0:512] = flat
    for slot in range(out.shape[0]):
        start = pl.multiple_of(slots[slot] * C, 16)
        out[slot] = rows_out[pl.ds(start, C), 0:512]


def side_kernel(
    slots, hidden, rects, cot_grid, lowered, grad_c, live, place, up_w, out, up_g, coarse_g,
    rows_out, grad_own,
):
    number = out.shape[0]
    coarse_tiles = lowered.shape[0]
    up_g[...] = jnp.zeros_like(up_g)
    coarse_g[...] = jnp.zeros_like(coarse_g)

    def block_step(block):
        alive = jnp.broadcast_to(live[pl.ds(block + 1, 1), :], (C, LANES))
        spreads = []
        pairs = []
        start = pl.multiple_of(block * C, 16)
        for inner in range(4):
            coarse = 4 * (block + 1) + inner
            spread = spread_sub(rects[coarse])
            spreads.append(spread)
            pairs.append(
                jnp.concatenate([cot_grid[2 * coarse], cot_grid[2 * coarse + 1]], axis=0)
            )
            upward = dot(up_w[...], spread)
            for half in range(2):
                value = hidden[2 * coarse + half] + upward[half * C : (half + 1) * C]
                at = LANES * (2 * inner + half)
                rows_out[pl.ds(start, C), at : at + LANES] = (value * alive).astype(BF16)
        up_g[...] += dot(
            jnp.concatenate(pairs, axis=1), jnp.concatenate(spreads, axis=1), (1, 1)
        )

    loop(0, number, block_step)
    to_blocks(slots, rows_out, place, out)
    zero = jnp.zeros((C, LANES), BF16)
    for coarse in (2, 3, coarse_tiles - 4, coarse_tiles - 3):
        grad_own[coarse] = zero

    def copy_step(coarse):
        grad_own[coarse] = grad_c[coarse]

    loop(4, coarse_tiles - 4, copy_step, 4)
    low, high = z_masks(32)

    def weight_step(index):
        lefts = []
        rights = []
        for inner in range(2):
            coarse = 3 + 2 * index + inner
            lefts.append(
                jnp.concatenate(
                    [grad_own[coarse + 1], grad_own[coarse], grad_own[coarse - 1]], axis=0
                )
            )
            rights.append(columns(lowered[coarse], low, high, 32, 2))
        coarse_g[...] += dot(
            jnp.concatenate(lefts, axis=1), jnp.concatenate(rights, axis=1), (1, 1)
        )

    loop(0, (coarse_tiles - 6) // 2, weight_step)


def backward_kernel(
    grad_c, from_left, from_right, hidden, cot_grid, live, coarse_w, down_w,
    grad_h, grad_d, pack_low, pack_high, coarse_p,
):
    coarse_tiles = grad_c.shape[0]
    ids = lane_ids(C)
    even = (ids // 16) % 2 == 0
    at_left = even & (ids % 16 == 2)
    at_right = even & (ids % 16 == 12)
    zero = jnp.zeros((C, LANES), BF16)
    low, high = z_masks(32)
    for index in range((coarse_tiles - 4) // 2):
        cols = []
        for coarse in (2 + 2 * index, 3 + 2 * index):
            group, place = coarse // 32, coarse % 32
            tile = jnp.where(at_left, roll(from_left[group], 2 - place), grad_c[coarse])
            tile = jnp.where(at_right, roll(from_right[group], 12 - place), tile)
            cols.append(columns(tile, low, high, 32, 2))
        out = dot(coarse_w[...], jnp.concatenate(cols, axis=1))
        coarse_p[2 + 2 * index] = out[:, :LANES]
        coarse_p[3 + 2 * index] = out[:, LANES:]
    own_anchors = anchor_mask(True)
    across = lane_ids(C) % 16
    inside = ((across >= 4) & (across < 12)).astype(F32)

    def step(coarse):
        alive = jnp.broadcast_to(live[pl.ds(coarse // 4, 1), :], (C, LANES)) * inside
        value = (
            coarse_p[coarse - 1, 0:C] + coarse_p[coarse, C : 2 * C] + coarse_p[coarse + 1, 2 * C :]
        )
        down = (value * (alive * own_anchors)).astype(BF16)
        grad_d[coarse] = down
        acts = dot(down_w[...], spread_sub(down), (0, 0))
        for half in range(2):
            tile = 2 * coarse + half
            slope = silu_parts(hidden[tile])[1]
            grad = cot_grid[tile].astype(F32) + acts[half * C : (half + 1) * C] * slope
            grad_h[tile] = (grad * alive).astype(BF16)

    loop(3, coarse_tiles - 3, step, 2)
    tiles = grad_h.shape[0]
    for out, lane in ((pack_low, 4), (pack_high, 11)):
        for group in range(out.shape[0]):
            total = zero
            for tile in range(max(6, 16 * group), min(tiles - 6, 16 * group + 16)):
                picked = jnp.where(ids % 16 == lane, grad_h[tile], zero)
                total = total + roll(picked, tile % 16 - lane)
            out[group] = total


def weight_kernel(grid, grad_h, grad_d, hidden, fine_g, down_g, grad_own):
    tiles = grid.shape[0]
    coarse_tiles = grad_d.shape[0]
    fine_g[...] = jnp.zeros_like(fine_g)
    down_g[...] = jnp.zeros_like(down_g)
    zero = jnp.zeros((C, LANES), BF16)
    for tile in (5, 6, 7, tiles - 8, tiles - 7, tiles - 6):
        grad_own[tile] = zero

    def copy_step(tile):
        grad_own[tile] = grad_h[tile]

    loop(8, tiles - 8, copy_step, 8)
    low, high = z_masks(16)

    def fine_step(index):
        lefts = []
        rights = []
        for inner in range(4):
            tile = 6 + 4 * index + inner
            lefts.append(
                jnp.concatenate([grad_own[tile + 1], grad_own[tile], grad_own[tile - 1]], axis=0)
            )
            rights.append(columns(grid[tile], low, high, 16, 1))
        fine_g[...] += dot(
            jnp.concatenate(lefts, axis=1), jnp.concatenate(rights, axis=1), (1, 1)
        )

    loop(0, (tiles - 12) // 4, fine_step)

    def down_step(index):
        lefts = []
        rights = []
        for inner in range(4):
            coarse = 4 + 4 * index + inner
            lefts.append(spread_sub(grad_d[coarse]))
            rights.append(
                jnp.concatenate(
                    [
                        silu_parts(hidden[2 * coarse])[0].astype(BF16),
                        silu_parts(hidden[2 * coarse + 1])[0].astype(BF16),
                    ],
                    axis=0,
                )
            )
        down_g[...] += dot(
            jnp.concatenate(lefts, axis=1), jnp.concatenate(rights, axis=1), (1, 1)
        )

    loop(0, (coarse_tiles - 8) // 4, down_step)


def input_kernel(slots, grad_h, from_left, from_right, live, place, fine_w, out, fine_p, rows_out):
    tiles = grad_h.shape[0]
    number = out.shape[0]
    ids = lane_ids(C)
    at_left = ids % 16 == 3
    at_right = ids % 16 == 12
    low, high = z_masks(16)

    def group_step(group):
        packed_left = from_left[group]
        packed_right = from_right[group]
        for pair in range(8):
            cols = []
            for inner in (2 * pair, 2 * pair + 1):
                tile = grad_h[16 * group + inner]
                tile = jnp.where(at_left, roll(packed_left, 3 - inner), tile)
                tile = jnp.where(at_right, roll(packed_right, 12 - inner), tile)
                cols.append(columns(tile, low, high, 16, 1))
            res = dot(fine_w[...], jnp.concatenate(cols, axis=1))
            fine_p[16 * group + 2 * pair] = res[:, :LANES]
            fine_p[16 * group + 2 * pair + 1] = res[:, LANES:]

    loop(0, tiles // 16, group_step)

    def block_step(block):
        alive = jnp.broadcast_to(live[pl.ds(block + 1, 1), :], (C, LANES))
        start = pl.multiple_of(block * C, 16)
        for inner in range(EDGE):
            tile = EDGE * (block + 1) + inner
            value = fine_p[tile - 1, 0:C] + fine_p[tile, C : 2 * C] + fine_p[tile + 1, 2 * C :]
            rows_out[pl.ds(start, C), LANES * inner : LANES * (inner + 1)] = (
                value * alive
            ).astype(BF16)

    loop(0, number, block_step)
    to_blocks(slots, rows_out, place, out)


def call(kernel, inputs, outs, scratch=(), scalars=0, flops=0):
    vmem = pl.BlockSpec(memory_space=pltpu.VMEM)
    smem = pl.BlockSpec(memory_space=pltpu.SMEM)
    moved = sum(math.prod(s) * jnp.dtype(d).itemsize for s, d in outs)
    moved += sum(math.prod(a.shape) * a.dtype.itemsize for a in inputs)
    return pl.pallas_call(
        kernel,
        out_shape=tuple(jax.ShapeDtypeStruct(s, d) for s, d in outs),
        in_specs=[smem] * scalars + [vmem] * (len(inputs) - scalars),
        out_specs=tuple(vmem for _ in outs),
        scratch_shapes=[pltpu.VMEM(s, d) for s, d in scratch],
        compiler_params=pltpu.CompilerParams(vmem_limit_bytes=VMEM_LIMIT),
        cost_estimate=pl.CostEstimate(flops=flops, bytes_accessed=moved, transcendentals=0),
        name=kernel.__name__,
    )(*inputs)


def send(array, step_x, step_y):
    number_x, number_y = lax.axis_size("gx"), lax.axis_size("gy")
    pairs = []
    for i in range(number_x):
        for j in range(number_y):
            to_x, to_y = i + step_x, j + step_y
            if 0 <= to_x < number_x and 0 <= to_y < number_y:
                pairs.append((i * number_y + j, to_x * number_y + to_y))
    return lax.ppermute(array, ("gx", "gy"), pairs)


def reduce_all(parts):
    axes = ("gx", "gy")
    devices = lax.axis_size("gx") * lax.axis_size("gy")
    sizes = [part.shape[0] for part in parts]
    rows = sum(sizes)
    share = -(-rows // (16 * devices)) * 16
    joined = jnp.concatenate(parts, axis=0).astype(BF16)
    joined = jnp.pad(joined, ((0, share * devices - rows), (0, 0)))
    mine = lax.all_to_all(joined.reshape(devices, share, LANES), axes, 0, 0)
    mine = jnp.sum(mine.astype(F32), axis=0).astype(BF16)
    full = lax.all_gather(mine, axes, axis=0, tiled=True)
    outs = []
    at = 0
    for size in sizes:
        outs.append(full[at : at + size].astype(F32))
        at += size
    return outs


def lane_split(array):
    rows, width = array.shape
    padded = -(-width // LANES) * LANES
    array = jnp.pad(array, ((0, 0), (0, padded - width)))
    return array.reshape(rows, padded // LANES, LANES).transpose(1, 0, 2).reshape(-1, LANES)


def lane_join(flat, rows, width):
    parts = flat.shape[0] // rows
    array = flat.reshape(parts, rows, LANES).transpose(1, 0, 2).reshape(rows, parts * LANES)
    return array[:, :width]


def on_device(
    features, block_slots, block_count, cotangent, fine_weight, down_weight, coarse_weight,
    up_weight,
):
    number = features.shape[2]
    slots = block_slots.reshape(number)
    count = block_count.reshape(1)
    feats = features.reshape(number, C, VOX)
    cots = cotangent.reshape(number, C, VOX)
    place = jnp.asarray(placing_matrix(), BF16)
    place_own = jnp.asarray(placing_matrix()[:512], BF16)
    pick = jnp.asarray(edge_matrix(), BF16)
    tiles = EDGE * (number + 2)
    coarse_tiles = tiles // 2
    groups = -(-coarse_tiles // 32)
    fine_groups = tiles // 16

    fine_5 = fine_weight.reshape(C, 3, 3, 3, C)
    coarse_5 = coarse_weight.reshape(C, 3, 3, 3, C)
    fine_fore = fine_5.transpose(3, 0, 2, 1, 4).reshape(3 * C, 9 * C)
    fine_back = fine_5[:, ::-1, ::-1, ::-1].transpose(3, 4, 2, 1, 0).reshape(3 * C, 9 * C)
    coarse_fore = coarse_5.transpose(3, 0, 2, 1, 4).reshape(3 * C, 9 * C)
    coarse_back = coarse_5[:, ::-1, ::-1, ::-1].transpose(3, 4, 2, 1, 0).reshape(3 * C, 9 * C)
    down_w = down_weight.reshape(C, 2, 2, 2, C).transpose(1, 2, 0, 3, 4).reshape(4 * C, 2 * C)
    up_w = up_weight.reshape(2, 2, 2, C, C).transpose(2, 3, 0, 1, 4).reshape(2 * C, 4 * C)

    own, cot, x_low, x_high, y_low, y_high, d_ll, d_lh, d_hl, d_hh = call(
        prepare_kernel,
        (slots, count, feats, cots, pick),
        [((number + 1, C, VOX), BF16), ((number, C, VOX), BF16)]
        + [((number + 1, C, 256), BF16)] * 2
        + [((3, C, VOX), BF16)] * 2
        + [((2, C, 256), BF16)] * 4,
        scalars=2,
    )
    x_left = send(x_high, 1, 0)
    x_right = send(x_low, -1, 0)
    y_left = send(y_high, 0, 1)
    y_right = send(y_low, 0, -1)
    c_ll = send(d_hh, 1, 1)
    c_lr = send(d_hl, 1, -1)
    c_rl = send(d_lh, -1, 1)
    c_rr = send(d_ll, -1, -1)
    grid, cot_grid, hidden, lowered, rects, grad_c, live, pack_low, pack_high = call(
        forward_kernel,
        (own, cot, x_left, x_right, y_left, y_right, c_ll, c_lr, c_rl, c_rr, place, fine_fore,
         down_w, coarse_fore, up_w),
        [
            ((tiles, C, LANES), BF16),
            ((tiles, C, LANES), BF16),
            ((tiles, C, LANES), F32),
            ((coarse_tiles, C, LANES), BF16),
            ((coarse_tiles, C, LANES), BF16),
            ((coarse_tiles, C, LANES), BF16),
            ((C, LANES), F32),
            ((groups, C, LANES), BF16),
            ((groups, C, LANES), BF16),
        ],
        [
            (((number + 3) * C, 1024), BF16),
            (((number + 2) * C, VOX), BF16),
            ((tiles, 3 * C, LANES), F32),
            ((coarse_tiles, 3 * C, LANES), F32),
        ],
        flops=3 * 10**9,
    )
    grad_left = send(pack_high, 1, 0)
    grad_right = send(pack_low, -1, 0)
    output, up_part, coarse_part = call(
        side_kernel,
        (slots, hidden, rects, cot_grid, lowered, grad_c, live, place_own, up_w),
        [((number, C, VOX), BF16), ((2 * C, 4 * C), F32), ((3 * C, 9 * C), F32)],
        [((number * C, 1024), BF16), ((coarse_tiles, C, LANES), BF16)],
        scalars=1,
        flops=10**9,
    )
    grad_h, grad_d, edge_low, edge_high = call(
        backward_kernel,
        (grad_c, grad_left, grad_right, hidden, cot_grid, live, coarse_back, down_w),
        [
            ((tiles, C, LANES), BF16),
            ((coarse_tiles, C, LANES), BF16),
            ((fine_groups, C, LANES), BF16),
            ((fine_groups, C, LANES), BF16),
        ],
        [((coarse_tiles, 3 * C, LANES), F32)],
        flops=10**9,
    )
    edge_left = send(edge_high, 1, 0)
    edge_right = send(edge_low, -1, 0)
    fine_part, down_part = call(
        weight_kernel,
        (grid, grad_h, grad_d, hidden),
        [((3 * C, 9 * C), F32), ((4 * C, 2 * C), F32)],
        [((tiles, C, LANES), BF16)],
        flops=3 * 10**9,
    )
    (input_grad,) = call(
        input_kernel,
        (slots, grad_h, edge_left, edge_right, live, place_own, fine_back),
        [((number, C, VOX), BF16)],
        [((tiles, 3 * C, LANES), F32), ((number * C, 1024), BF16)],
        scalars=1,
        flops=3 * 10**9,
    )
    fine_sum, down_sum, coarse_sum, up_sum = reduce_all(
        [lane_split(part) for part in (fine_part, down_part, coarse_part, up_part)]
    )
    scale = 1.0 / math.sqrt(number * VOX * lax.axis_size("gx") * lax.axis_size("gy"))
    fine_total = lane_join(fine_sum, 3 * C, 9 * C).reshape(3, C, 3, 3, C) * scale
    coarse_total = lane_join(coarse_sum, 3 * C, 9 * C).reshape(3, C, 3, 3, C) * scale
    down_total = lane_join(down_sum, 4 * C, 2 * C).reshape(2, 2, C, 2, C) * scale
    up_total = lane_join(up_sum, 2 * C, 4 * C).reshape(2, C, 2, 2, C) * scale
    shape_out = (1, 1, number, C, VOX)
    return (
        output.reshape(shape_out),
        input_grad.reshape(shape_out),
        fine_total.transpose(1, 3, 2, 0, 4).reshape(C, 27, C),
        down_total.transpose(2, 0, 1, 3, 4).reshape(C, 8, C),
        coarse_total.transpose(1, 3, 2, 0, 4).reshape(C, 27, C),
        up_total.transpose(2, 3, 0, 1, 4).reshape(8, C, C),
    )


def solution(mesh):
    split = P("gx", "gy", None, None, None)
    return jax.shard_map(
        on_device,
        mesh=mesh,
        in_specs=(split, P("gx", "gy", None), P("gx", "gy"), split, P(), P(), P(), P()),
        out_specs=(split, split, P(), P(), P(), P()),
        check_vma=False,
    )
```

time: 453 us -> 261 us (0.58); the launches traced: 446 us -> 261 us
  matrix products: 176 us -> 0 us
  Pallas kernels: 0 us -> 137 us
  local copies, waits for them, and re-layouts: 104 us -> 18.4 us
  waiting for transfers between devices: 75.1 us -> 14.7 us
  blocking collectives: 0 us -> 42.5 us
  other arithmetic: 25.1 us -> 4.72 us
  between operations: 16.8 us -> 1.82 us
  starting transfers between devices: 48.5 us -> 42 us
    dot_general x168 -> x0, matrix products: 176 us -> none  [the longest x54 62.6 us: conv_backward(): jnp.einsum('oc,ozxy->czxy', weight[:, index, :], piece, preferred_element...]
    pallas_call x0 -> x6, Pallas kernels: none -> 137 us  [call(): pl.pallas_call(kernel, out_shape=tuple((jax.ShapeDtypeStruct(s, d) for s,...]
    psum x1 -> x0, waiting for transfers between devices: 64.8 us -> none  [on_device(): lax.psum((fine_local, down_local, coarse_local, up_local), ('gx', 'gy'))]
    all_gather x0 -> x1, blocking collectives: none -> 42.5 us  [reduce_all(): full = lax.all_gather(mine, axes, axis=0, tiled=True)]
    transpose x14 -> x4, local copies, waits for them, and re-layouts: 33.4 us -> 2.47 us  [the longest x1 0.88 us: on_device(): fine_total.transpose(1, 3, 2, 0, 4).reshape(C, 27, C)]
    ppermute x16 -> x12, starting transfers between devices: 48.5 us -> 30.4 us  [send(): return lax.ppermute(array, ('gx', 'gy'), pairs)]
    slice x16 -> x3, local copies, waits for them, and re-layouts: 17.9 us -> 0.02 us  [reduce_all(): outs.append(full[at:at + size].astype(F32))]
    all_to_all x0 -> x1, starting transfers between devices: none -> 11.6 us  [reduce_all(): mine = lax.all_to_all(joined.reshape(devices, share, LANES), axes, 0, 0)]
  transfers between devices with their start and end apart: 17 -> 13, of which waited for: 5 -> 3; matrix products, arithmetic and copies ran while one was open for 26% -> 5% of each run, Pallas kernels for 0% -> 14%
where the time goes in v1:
time: 261 us
  Pallas kernels  137 us (52%)
  blocking collectives  42.5 us (16%)
  starting transfers between devices  42 us (16%)
  local copies, waits for them, and re-layouts  18.4 us (7%)
  waiting for transfers between devices  14.7 us (6%)
  other arithmetic  4.72 us (2%)
    pallas_call x6, Pallas kernels, call(): pl.pallas_call(kernel, out_shape=tuple((jax.ShapeDtypeStruct(s, d) for s,...  137 us
    all_gather x1, blocking collectives, reduce_all(): full = lax.all_gather(mine, axes, axis=0, tiled=True)  42.5 us
    ppermute x12, starting transfers between devices, send(): return lax.ppermute(array, ('gx', 'gy'), pairs)  30.4 us
    ppermute x12, waiting for transfers between devices, send(): return lax.ppermute(array, ('gx', 'gy'), pairs)  14.7 us
    all_to_all x1, starting transfers between devices, reduce_all(): mine = lax.all_to_all(joined.reshape(devices, share, LANES), axes, 0, 0)  11.6 us
  transfers between devices with their start and end apart: 13, of which 3 were waited for; matrix products, arithmetic and copies ran while one was open for 5% of the time, Pallas kernels for 14%

profile of v1, /device:TPU:0, one launch (start us, length us, event | category | flops | bytes accessed | tf_op | source)
XLA Modules:
  0.0 260.7 jit_solution(4939531703774615066)
XLA Ops:
  1.3 3.3 %prepare_kernel.1 = (bf16[17,48,512]{2,1,0:T(8,128)(2,1)}, bf16[16,48,512]{2,1,0:T(8,128)(2,1)}, bf16[17,48,256]{2,1,0:T(8,128)(2,1)}, bf16[17,48,256]{2,1,0:T(8...) custom-call(s32[16]{0:T(128)} %bitcast.110, ...), custom_call_target="tpu_custom_call" | custom-call | bytes 5046340 | tf_op jit(solution)/shard_map/prepare_kernel/pallas_call | solution.py:462
  4.7 5.0 %collective-permute-start = (bf16[17,48,256]{2,1,0:T(8,128)(2,1)}, bf16[17,48,256]{2,1,0:T(8,128)(2,1)S(1)}, u32[]{:S(2)}, u32[]{:S(2)}) collective-permute-start(bf16[17,48,256]{2,1,0:T(8,128)(2,1)} %get-tuple-element.36), channel_id=1, source_target_pairs={{0,4},{1,5},{2,6},{3,7},{4,8},{5,9},{6,10},{7,11},{8,12},{9,13},{1... | collective-permute-start | bytes 1253384 | tf_op jit(solution)/shard_map/ppermute | solution.py:482
  9.7 1.3 collective-permute-start.1
  11.0 3.4 %collective-permute-start.4 = (bf16[2,48,256]{2,1,0:T(8,128)(2,1)}, bf16[2,48,256]{2,1,0:T(8,128)(2,1)S(1)}, u32[]{:S(2)}, u32[]{:S(2)}) collective-permute-start(bf16[2,48,256]{2,1,0:T(8,128)(2,1)} %get-tuple-element.40), channel_id=1, source_target_pairs={{0,5},{1,6},{2,7},{4,9},{5,10},{6,11},{8,13},{9,14},{10,15},{12,17... | collective-permute-start | bytes 147464 | tf_op jit(solution)/shard_map/ppermute | solution.py:482
  15.1 5.7 %collective-permute-start.2 = (bf16[3,48,512]{2,1,0:T(8,128)(2,1)}, bf16[3,48,512]{2,1,0:T(8,128)(2,1)S(1)}, u32[]{:S(2)}, u32[]{:S(2)}) collective-permute-start(bf16[3,48,512]{2,1,0:T(8,128)(2,1)} %get-tuple-element.38), channel_id=1, source_target_pairs={{0,1},{1,2},{2,3},{4,5},{5,6},{6,7},{8,9},{9,10},{10,11},{12,13},{... | collective-permute-start | bytes 442376 | tf_op jit(solution)/shard_map/ppermute | solution.py:482
  20.8 8.6 %collective-permute-done.4.d_ll = bf16[2,48,256]{2,1,0:T(8,128)(2,1)S(1)} collective-permute-done((bf16[2,48,256]{2,1,0:T(8,128)(2,1)}, bf16[2,48,256]{2,1,0:T(8,128)(2,1)S(1)}, u32[]{:S(2)}, u32[]{:S(2)}) %collective-permute-start.4) | collective-permute-done | bytes 49184 | tf_op jit(solution)/shard_map/ppermute | solution.py:482
  29.4 1.3 collective-permute-start.3
  31.4 1.3 collective-permute-start.7
  33.3 0.9 reshape.140.fine_w
  34.2 0.9 reshape.144.coarse_w
  36.8 2.4 rev.6
  39.2 0.9 reshape.148.coarse_w
  40.1 3.4 %collective-permute-done.7.d_rr = bf16[2,48,256]{2,1,0:T(8,128)(2,1)S(1)} collective-permute-done((bf16[2,48,256]{2,1,0:T(8,128)(2,1)}, bf16[2,48,256]{2,1,0:T(8,128)(2,1)S(1)}, u32[]{:S(2)}, u32[]{:S(2)}) %collective-permute-start.7) | collective-permute-done | bytes 49184 | tf_op jit(solution)/shard_map/ppermute | solution.py:482
  44.5 50.5 %forward_kernel.1 = (bf16[144,48,128]{2,1,0:T(8,128)(2,1)}, bf16[144,48,128]{2,1,0:T(8,128)(2,1)}, f32[144,48,128]{2,1,0:T(8,128)}, bf16[72,48,128]{2,1,0:T(8,12...) custom-call(bf16[17,48,512]{2,1,0:T(8,128)(2,1)} %get-tuple-element., ...), custom_call_target="tpu_custom_call" | custom-call | flops 3000000000 | bytes 15199232 | tf_op jit(solution)/shard_map/forward_kernel/pallas_call | solution.py:462
  95.1 4.7 %collective-permute-start.8 = (bf16[3,48,128]{2,1,0:T(8,128)(2,1)}, bf16[3,48,128]{2,1,0:T(8,128)(2,1)S(1)}, u32[]{:S(2)}, u32[]{:S(2)}) collective-permute-start(bf16[3,48,128]{2,1,0:T(8,128)(2,1)} %get-tuple-element.51), channel_id=1, source_target_pairs={{0,4},{1,5},{2,6},{3,7},{4,8},{5,9},{6,10},{7,11},{8,12},{9,13},{1... | collective-permute-start | bytes 110600 | tf_op jit(solution)/shard_map/ppermute | solution.py:482
  99.7 1.5 collective-permute-start.9
  101.2 22.8 %side_kernel.1 = (bf16[16,48,512]{2,1,0:T(8,128)(2,1)}, f32[96,192]{1,0:T(8,128)}, f32[144,432]{1,0:T(8,128)}) custom-call(s32[16]{0:T(128)} %bitcast.111, f32[144,48,128]{2,1,0:T(8,128)} %get-tuple-element.44.hidden, bf16[72,48,128]{2,1,0:T(8,128)(2,1)} %get-tuple-element.45.rects, bf16[144,48,128]{2,1,0:T(8,128)(2,1)} %get-tuple-element.46.cot_grid, ...), custom_call_target="tpu_custom_call" | custom-call | flops 1000000000 | bytes 10181696 | tf_op jit(solution)/shard_map/side_kernel/pallas_call | solution.py:462
  124.0 1.0 convert.45
  125.1 0.9 convert.46
  127.2 22.7 %backward_kernel.1 = (bf16[144,48,128]{2,1,0:T(8,128)(2,1)}, bf16[72,48,128]{2,1,0:T(8,128)(2,1)}, bf16[9,48,128]{2,1,0:T(8,128)(2,1)}, bf16[9,48,128]{2,1,0:T(8,128)(2,1)}) custom-call(bf16[72,48,128]{2,1,0:T(8,128)(2,1)} %get-tuple-element.48.grad_c, bf16[3,48,128]{2,1,0:T(8,128)(2,1)} %copy-done.5, bf16[3,48,128]{2,1,0:T(8,128)(2,1)} %copy-done.6, ...), custom_call_target="tpu_custom_call" | custom-call | flops 1000000000 | bytes 9328128 | tf_op jit(solution)/shard_map/backward_kernel/pallas_call | solution.py:462
  149.9 23.5 %weight_kernel.1 = (f32[144,432]{1,0:T(8,128)}, f32[192,96]{1,0:T(8,128)}) custom-call(bf16[144,48,128]{2,1,0:T(8,128)(2,1)} %get-tuple-element.56.grid, bf16[144,48,128]{2,1,0:T(8,128)(2,1)} %get-tuple-element.53.grad_h, bf16[72,48,128]{2,1,0:T(8,128)(2,1)} %get-tuple-element.57.grad_d, f32[144,48,128]{2,1,0:T(8,128)} %get-tuple-element.44.hidden), custom_call_target="tpu_custom_call" | custom-call | flops 3000000000 | bytes 8285184 | tf_op jit(solution)/shard_map/weight_kernel/pallas_call | solution.py:462
  173.4 1.0 convert.43
  174.5 0.9 convert.44
  176.2 11.6 %all-to-all-start = ((bf16[32,48,128]{2,1,0:T(8,128)(2,1)}), bf16[32,48,128]{2,1,0:T(8,128)(2,1)S(1)}, u32[]{:S(2)}, u32[]{:S(2)}) async-start(bf16[32,48,128]{2,1,0:T(8,128)(2,1)} %bitcast.22), calls=%async_computation | async-start | bytes 786432 | tf_op jit(solution)/shard_map/all_to_all | solution.py:493
  187.8 3.7 %collective-permute-start.10 = (bf16[9,48,128]{2,1,0:T(8,128)(2,1)S(1)}, bf16[9,48,128]{2,1,0:T(8,128)(2,1)S(1)}, u32[]{:S(2)}, u32[]{:S(2)}) collective-permute-start(bf16[9,48,128]{2,1,0:T(8,128)(2,1)S(1)} %copy-done.12), channel_id=1, source_target_pairs={{0,4},{1,5},{2,6},{3,7},{4,8},{5,9},{6,10},{7,11},{8,12},{9,13},{1... | collective-permute-start | bytes 331784 | tf_op jit(solution)/shard_map/ppermute | solution.py:482
  191.5 1.3 collective-permute-start.11
  193.0 2.4 rev.7
  195.4 0.9 reshape.149.fine_w
  196.4 2.7 %collective-permute-done.11.from_right = bf16[9,48,128]{2,1,0:T(8,128)(2,1)S(1)} collective-permute-done((bf16[9,48,128]{2,1,0:T(8,128)(2,1)S(1)}, bf16[9,48,128]{2,1,0:T(8,128)(2,1)S(1)}, u32[]{:S(2)}, u32[]{:S(2)}) %collective-permute-start.11) | collective-permute-done | bytes 110624 | tf_op jit(solution)/shard_map/ppermute | solution.py:482
  199.7 13.6 %input_kernel.1 = bf16[16,48,512]{2,1,0:T(8,128)(2,1)} custom-call(s32[16]{0:T(128)} %bitcast.112, bf16[144,48,128]{2,1,0:T(8,128)(2,1)} %get-tuple-element.53.grad_h, bf16[9,48,128]{2,1,0:T(8,128)(2,1)} %copy-done.13, bf16[9,48,128]{2,1,0:T(8,128)(2,1)} %copy-done.14, f32[48,128]{1,0:T(8,128)} %get-tuple-element.49.live, ...), custom_call_target="tpu_custom_call" | custom-call | flops 3000000000 | bytes 3974720 | tf_op jit(solution)/shard_map/input_kernel/pallas_call | solution.py:462
  213.4 42.5 %all_gather.3 = bf16[1536,128]{1,0:T(8,128)(2,1)S(1)} all-gather(bf16[48,128]{1,0:T(8,128)(2,1)S(1)} %reduce_sum.12), channel_id=1, replica_groups=mesh['gx'=8,'gy'=4] {'gx','gy'}, dimensions={0}, use_global_device_ids=true | all-gather | bytes 405504 | tf_op jit(solution)/shard_map/all_gather | solution.py:495
  256.5 0.9 copy.43
  (82 shorter events, 11.3 us)
Async XLA Ops:
  0.6 32.1 %copy-start.1 = (bf16[48,27,48]{2,0,1:T(8,128)(2,1)S(1)}, bf16[48,27,48]{2,0,1:T(8,128)(2,1)}, u32[]{:S(2)}) copy-start(bf16[48,27,48]{2,0,1:T(8,128)(2,1)} %param.17) | copy-start | bytes 373252
  1.3 31.8 %copy-start.2 = (bf16[48,27,48]{2,0,1:T(8,128)(2,1)S(1)}, bf16[48,27,48]{2,0,1:T(8,128)(2,1)}, u32[]{:S(2)}) copy-start(bf16[48,27,48]{2,0,1:T(8,128)(2,1)} %param.15) | copy-start | bytes 373252
  4.7 30.5 %copy-start.3 = (bf16[48,8,48]{2,1,0:T(8,128)(2,1)S(1)}, bf16[48,8,48]{2,1,0:T(8,128)(2,1)}, u32[]{:S(2)}) copy-start(bf16[48,8,48]{2,1,0:T(8,128)(2,1)} %param.16) | copy-start | bytes 110596
  4.7 38.9 %collective-permute-start = (bf16[17,48,256]{2,1,0:T(8,128)(2,1)}, bf16[17,48,256]{2,1,0:T(8,128)(2,1)S(1)}, u32[]{:S(2)}, u32[]{:S(2)}) collective-permute-start(bf16[17,48,256]{2,1,0:T(8,128)(2,1)} %get-tuple-element.36), channel_id=1, source_target_pairs={{0,4},{1,5},{2,6},{3,7},{4,8},{5,9},{6,10},{7,11},{8,12},{9,13},{1... | collective-permute-start | bytes 1253384 | tf_op jit(solution)/shard_map/ppermute | solution.py:482
  9.7 33.9 %collective-permute-start.1 = (bf16[17,48,256]{2,1,0:T(8,128)(2,1)}, bf16[17,48,256]{2,1,0:T(8,128)(2,1)S(1)}, u32[]{:S(2)}, u32[]{:S(2)}) collective-permute-start(bf16[17,48,256]{2,1,0:T(8,128)(2,1)} %get-tuple-element.37), channel_id=1, source_target_pairs={{4,0},{5,1},{6,2},{7,3},{8,4},{9,5},{10,6},{11,7},{12,8},{13,9},{1... | collective-permute-start | bytes 1253384 | tf_op jit(solution)/shard_map/ppermute | solution.py:482
  11.0 18.4 %collective-permute-start.4 = (bf16[2,48,256]{2,1,0:T(8,128)(2,1)}, bf16[2,48,256]{2,1,0:T(8,128)(2,1)S(1)}, u32[]{:S(2)}, u32[]{:S(2)}) collective-permute-start(bf16[2,48,256]{2,1,0:T(8,128)(2,1)} %get-tuple-element.40), channel_id=1, source_target_pairs={{0,5},{1,6},{2,7},{4,9},{5,10},{6,11},{8,13},{9,14},{10,15},{12,17... | collective-permute-start | bytes 147464 | tf_op jit(solution)/shard_map/ppermute | solution.py:482
  14.4 16.3 %collective-permute-start.5 = (bf16[2,48,256]{2,1,0:T(8,128)(2,1)}, bf16[2,48,256]{2,1,0:T(8,128)(2,1)S(1)}, u32[]{:S(2)}, u32[]{:S(2)}) collective-permute-start(bf16[2,48,256]{2,1,0:T(8,128)(2,1)} %get-tuple-element.41), channel_id=1, source_target_pairs={{1,4},{2,5},{3,6},{5,8},{6,9},{7,10},{9,12},{10,13},{11,14},{13,16... | collective-permute-start | bytes 147464 | tf_op jit(solution)/shard_map/ppermute | solution.py:482
  15.1 28.4 %collective-permute-start.2 = (bf16[3,48,512]{2,1,0:T(8,128)(2,1)}, bf16[3,48,512]{2,1,0:T(8,128)(2,1)S(1)}, u32[]{:S(2)}, u32[]{:S(2)}) collective-permute-start(bf16[3,48,512]{2,1,0:T(8,128)(2,1)} %get-tuple-element.38), channel_id=1, source_target_pairs={{0,1},{1,2},{2,3},{4,5},{5,6},{6,7},{8,9},{9,10},{10,11},{12,13},{... | collective-permute-start | bytes 442376 | tf_op jit(solution)/shard_map/ppermute | solution.py:482
  29.4 5.9 %copy-start.15 = (bf16[2,48,256]{2,1,0:T(8,128)(2,1)}, bf16[2,48,256]{2,1,0:T(8,128)(2,1)S(1)}, u32[]{:S(2)}) copy-start(bf16[2,48,256]{2,1,0:T(8,128)(2,1)S(1)} %collective-permute-done.4.d_ll) | copy-start | bytes 147460
  29.4 14.1 %collective-permute-start.3 = (bf16[3,48,512]{2,1,0:T(8,128)(2,1)}, bf16[3,48,512]{2,1,0:T(8,128)(2,1)S(1)}, u32[]{:S(2)}, u32[]{:S(2)}) collective-permute-start(bf16[3,48,512]{2,1,0:T(8,128)(2,1)} %get-tuple-element.39), channel_id=1, source_target_pairs={{1,0},{2,1},{3,2},{5,4},{6,5},{7,6},{9,8},{10,9},{11,10},{13,12},{... | collective-permute-start | bytes 442376 | tf_op jit(solution)/shard_map/ppermute | solution.py:482
  30.7 4.6 %copy-start.16 = (bf16[2,48,256]{2,1,0:T(8,128)(2,1)}, bf16[2,48,256]{2,1,0:T(8,128)(2,1)S(1)}, u32[]{:S(2)}) copy-start(bf16[2,48,256]{2,1,0:T(8,128)(2,1)S(1)} %collective-permute-done.5.d_lr) | copy-start | bytes 147460
  30.7 0.7 collective-permute-start.6
  31.4 3.9 %copy-start.17 = (bf16[2,48,256]{2,1,0:T(8,128)(2,1)}, bf16[2,48,256]{2,1,0:T(8,128)(2,1)S(1)}, u32[]{:S(2)}) copy-start(bf16[2,48,256]{2,1,0:T(8,128)(2,1)S(1)} %collective-permute-done.6.d_rl) | copy-start | bytes 147460
  31.4 12.1 %collective-permute-start.7 = (bf16[2,48,256]{2,1,0:T(8,128)(2,1)}, bf16[2,48,256]{2,1,0:T(8,128)(2,1)S(1)}, u32[]{:S(2)}, u32[]{:S(2)}) collective-permute-start(bf16[2,48,256]{2,1,0:T(8,128)(2,1)} %get-tuple-element.43), channel_id=1, source_target_pairs={{5,0},{6,1},{7,2},{9,4},{10,5},{11,6},{13,8},{14,9},{15,10},{17,12... | collective-permute-start | bytes 147464 | tf_op jit(solution)/shard_map/ppermute | solution.py:482
  32.7 3.3 %copy-start.4 = (bf16[8,48,48]{2,1,0:T(8,128)(2,1)S(1)}, bf16[8,48,48]{2,1,0:T(8,128)(2,1)}, u32[]{:S(2)}) copy-start(bf16[8,48,48]{2,1,0:T(8,128)(2,1)} %param.18) | copy-start | bytes 110596
  43.5 0.7 copy-start.9
  43.5 0.7 copy-start.10
  43.6 0.8 copy-start.7
  43.6 0.9 copy-start.8
  95.1 30.9 %collective-permute-start.8 = (bf16[3,48,128]{2,1,0:T(8,128)(2,1)}, bf16[3,48,128]{2,1,0:T(8,128)(2,1)S(1)}, u32[]{:S(2)}, u32[]{:S(2)}) collective-permute-start(bf16[3,48,128]{2,1,0:T(8,128)(2,1)} %get-tuple-element.51), channel_id=1, source_target_pairs={{0,4},{1,5},{2,6},{3,7},{4,8},{5,9},{6,10},{7,11},{8,12},{9,13},{1... | collective-permute-start | bytes 110600 | tf_op jit(solution)/shard_map/ppermute | solution.py:482
  99.7 26.3 %collective-permute-start.9 = (bf16[3,48,128]{2,1,0:T(8,128)(2,1)}, bf16[3,48,128]{2,1,0:T(8,128)(2,1)S(1)}, u32[]{:S(2)}, u32[]{:S(2)}) collective-permute-start(bf16[3,48,128]{2,1,0:T(8,128)(2,1)} %get-tuple-element.52), channel_id=1, source_target_pairs={{4,0},{5,1},{6,2},{7,3},{8,4},{9,5},{10,6},{11,7},{12,8},{13,9},{1... | collective-permute-start | bytes 110600 | tf_op jit(solution)/shard_map/ppermute | solution.py:482
  126.0 0.6 copy-start.5
  126.6 0.6 copy-start.6
  173.4 14.4 %copy-start.12 = (bf16[9,48,128]{2,1,0:T(8,128)(2,1)S(1)}, bf16[9,48,128]{2,1,0:T(8,128)(2,1)}, u32[]{:S(2)}) copy-start(bf16[9,48,128]{2,1,0:T(8,128)(2,1)} %get-tuple-element.54) | copy-start | bytes 331780
  173.4 18.1 %copy-start.11 = (bf16[9,48,128]{2,1,0:T(8,128)(2,1)S(1)}, bf16[9,48,128]{2,1,0:T(8,128)(2,1)}, u32[]{:S(2)}) copy-start(bf16[9,48,128]{2,1,0:T(8,128)(2,1)} %get-tuple-element.55) | copy-start | bytes 331780
  176.2 37.2 %all-to-all-start = ((bf16[32,48,128]{2,1,0:T(8,128)(2,1)}), bf16[32,48,128]{2,1,0:T(8,128)(2,1)S(1)}, u32[]{:S(2)}, u32[]{:S(2)}) async-start(bf16[32,48,128]{2,1,0:T(8,128)(2,1)} %bitcast.22), calls=%async_computation | async-start | bytes 786432 | tf_op jit(solution)/shard_map/all_to_all | solution.py:493
  187.8 8.6 %collective-permute-start.10 = (bf16[9,48,128]{2,1,0:T(8,128)(2,1)S(1)}, bf16[9,48,128]{2,1,0:T(8,128)(2,1)S(1)}, u32[]{:S(2)}, u32[]{:S(2)}) collective-permute-start(bf16[9,48,128]{2,1,0:T(8,128)(2,1)S(1)} %copy-done.12), channel_id=1, source_target_pairs={{0,4},{1,5},{2,6},{3,7},{4,8},{5,9},{6,10},{7,11},{8,12},{9,13},{1... | collective-permute-start | bytes 331784 | tf_op jit(solution)/shard_map/ppermute | solution.py:482
  191.5 7.6 %collective-permute-start.11 = (bf16[9,48,128]{2,1,0:T(8,128)(2,1)S(1)}, bf16[9,48,128]{2,1,0:T(8,128)(2,1)S(1)}, u32[]{:S(2)}, u32[]{:S(2)}) collective-permute-start(bf16[9,48,128]{2,1,0:T(8,128)(2,1)S(1)} %copy-done.11), channel_id=1, source_target_pairs={{4,0},{5,1},{6,2},{7,3},{8,4},{9,5},{10,6},{11,7},{12,8},{13,9},{1... | collective-permute-start | bytes 331784 | tf_op jit(solution)/shard_map/ppermute | solution.py:482
  196.4 2.7 %copy-start.13 = (bf16[9,48,128]{2,1,0:T(8,128)(2,1)}, bf16[9,48,128]{2,1,0:T(8,128)(2,1)S(1)}, u32[]{:S(2)}) copy-start(bf16[9,48,128]{2,1,0:T(8,128)(2,1)S(1)} %collective-permute-done.10.from_left) | copy-start | bytes 331780
  199.1 0.6 copy-start.14
  255.9 1.5 copy-start
  257.5 2.2 slice-start
  (1 other events, 0.6 us)

commit v2 on v1

v2 whole, which is shorter than its diff:
```python
import math

import jax
import jax.numpy as jnp
import numpy as np
from jax import lax
from jax.experimental import pallas as pl
from jax.experimental.pallas import tpu as pltpu
from jax.sharding import PartitionSpec as P

C = 48
EDGE = 8
VOX = 512
LANES = 128
F32 = jnp.float32
BF16 = jnp.bfloat16
VMEM_LIMIT = 58 * 1024 * 1024
SHIFTS = (0, 1, 16, 17)


def placing_matrix():
    place = np.zeros((1024, 8 * LANES), np.float32)
    for z in range(8):
        for y in range(8):
            for x in range(8):
                place[64 * z + 8 * x + y, LANES * y + 16 * z + x + 4] = 1.0
            for x in range(4):
                place[512 + 32 * z + 8 * x + y, LANES * y + 16 * z + x] = 1.0
                place[768 + 32 * z + 8 * x + y, LANES * y + 16 * z + x + 12] = 1.0
    return place


def edge_matrix():
    pick = np.zeros((512, 512), np.float32)
    for z in range(8):
        for y in range(8):
            for x in range(8):
                pick[64 * z + 8 * x + y, 256 * (x // 4) + 32 * z + 8 * (x % 4) + y] = 1.0
    return pick


def dot(left, right, contract=(1, 0)):
    dims = (((contract[0],), (contract[1],)), ((), ()))
    return lax.dot_general(left, right, dims, preferred_element_type=F32)


def roll(value, shift):
    return pltpu.roll(value, shift % LANES, 1)


def lane_ids(rows):
    return lax.broadcasted_iota(jnp.int32, (rows, LANES), 1)


def silu_parts(value):
    sigma = 1.0 / (1.0 + jnp.exp(-value))
    return value * sigma, sigma * (1.0 + value * (1.0 - sigma))


def columns(tile, low, high, z_step, x_step):
    zero = jnp.zeros_like(tile)
    below = jnp.where(low, zero, roll(tile, z_step))
    above = jnp.where(high, zero, roll(tile, -z_step))
    base = jnp.concatenate([below, tile, above], axis=0)
    return jnp.concatenate([roll(base, x_step), base, roll(base, -x_step)], axis=0)


def z_masks(z_step):
    ids = lane_ids(C)
    return ids < z_step, ids >= LANES - z_step


def gather_sub(parts):
    total = parts[:C]
    for index in range(1, 4):
        total = total + roll(parts[index * C : (index + 1) * C], -SHIFTS[index])
    return total


def spread_sub(anchored):
    return jnp.concatenate([anchored] + [roll(anchored, step) for step in SHIFTS[1:]], axis=0)


def anchor_mask(own):
    ids = lane_ids(C)
    across = ids % 16
    keep = ((ids // 16) % 2 == 0) & (across % 2 == 0)
    if own:
        keep = keep & (across >= 4) & (across < 12)
    return keep.astype(F32)


def loop(low, high, body, unroll=1):
    def step(index, carry):
        body(index)
        return carry

    lax.fori_loop(low, high, step, 0, unroll=unroll)


def prepare_kernel(slots, count, feats, cots, pick, own, cot, x_low, x_high, y_low, y_high):
    number = feats.shape[0]
    rows = lax.broadcasted_iota(jnp.int32, (C, VOX), 0)
    flags = jnp.zeros((C, VOX), F32)
    first = jnp.zeros((), F32)
    last = jnp.zeros((), F32)
    zero = jnp.zeros((C, VOX), BF16)
    for slot in range(number):
        live = slot < count[0]
        alive = jnp.where(live, 1.0, 0.0)
        place = slots[slot]
        own[place] = jnp.where(live, feats[slot], zero)
        cot[place] = jnp.where(live, cots[slot], zero)
        flags = jnp.where(rows == place + 1, alive, flags)
        first = first + jnp.where(place == 0, alive, 0.0)
        last = last + jnp.where(place == number - 1, alive, 0.0)
    own[number] = flags.astype(BF16)
    first_flag = jnp.where(rows == number + 1, first, 0.0).astype(BF16)
    last_flag = jnp.where(rows == 0, last, 0.0).astype(BF16)
    packed = dot(own[...].reshape((number + 1) * C, VOX), pick[...]).astype(BF16)
    packed = packed.reshape(number + 1, C, VOX)
    x_low[...] = packed[:, :, :256]
    x_high[...] = packed[:, :, 256:]
    for out, index, flag in ((y_low, 0, first_flag), (y_high, number - 1, last_flag)):
        out[0] = own[index]
        out[1] = cot[index]
        out[2] = flag


def corner_kernel(y_left, y_right, own, pick, low, high, flags):
    extra = y_left[2] + y_right[2]
    rows = jnp.concatenate([y_left[0], y_right[0], extra], axis=0)
    packed = dot(rows, pick[...]).astype(BF16).reshape(3, C, VOX)
    low[...] = packed[:, :, :256]
    high[...] = packed[:, :, 256:]
    flags[...] = own[0] + extra


def place_kernel(
    own, cot, y_left, y_right, flags, place, up_w, grid, cot_grid, grad_r, live, rows_in, rows_cot
):
    number = cot.shape[0]
    last = number + 1
    for block in range(number):
        at = (block + 1) * C
        rows_in[at : at + C, :] = own[block]
        rows_cot[at : at + C, :] = cot[block]
    for at, middle in ((0, y_left), (last * C, y_right)):
        rows_in[at : at + C, :] = middle[0]
        rows_cot[at : at + C, :] = middle[1]
    rows_in[(last + 1) * C :, :] = flags[...]
    for pair in range(4):
        lanes = slice(256 * pair, 256 * pair + 256)
        placed_cot = dot(rows_cot[...], place[:, lanes])
        placed = dot(rows_in[...], place[:, lanes])
        for half in range(2):
            span = slice(LANES * half, LANES * (half + 1))
            for block in range(last + 1):
                tile = EDGE * block + 2 * pair + half
                grid[tile] = placed[block * C : (block + 1) * C, span].astype(BF16)
                cot_grid[tile] = placed_cot[block * C : (block + 1) * C, span].astype(BF16)
        if pair == 0:
            live[...] = placed[(last + 1) * C :, 0:LANES]

    def rect_step(block):
        pairs = []
        for inner in range(4):
            tile = EDGE * block + 2 * inner
            pairs.append(jnp.concatenate([cot_grid[tile], cot_grid[tile + 1]], axis=0))
        parts = dot(up_w[...], jnp.concatenate(pairs, axis=1), (0, 0))
        for inner in range(4):
            grad_r[4 * block + inner] = gather_sub(parts[:, LANES * inner : LANES * (inner + 1)])

    loop(0, number + 2, rect_step, 2)


def conv_sum(parts, tile):
    return parts[tile, 0:C] + parts[tile + 1, C : 2 * C] + parts[tile + 2, 2 * C :]


def conv_steps(parts, weight, load, tiles, z_step, x_step, unroll):
    low, high = z_masks(z_step)
    spare = jnp.zeros((3 * C, LANES), F32)
    parts[0] = spare
    parts[tiles + 1] = spare

    def step(index):
        tile = 4 * index
        for pair in range(2):
            at = tile + 2 * pair
            cols = [columns(load(at + i), low, high, z_step, x_step) for i in range(2)]
            out = dot(weight[...], jnp.concatenate(cols, axis=1))
            parts[at + 1] = out[:, :LANES]
            parts[at + 2] = out[:, LANES:]

    loop(0, tiles // 4, step, unroll)


def forward_kernel(
    grid_own, live_own, grad_r, x_left, x_right, c_left, c_right, place, fine_w, down_w, coarse_w,
    grid, hidden, lowered, rects, grad_c, live, pack_low, pack_high,
    rows_in, fine_p, coarse_p,
):
    number = x_left.shape[0] - 1
    last = number + 1
    for block in range(number):
        at = (block + 1) * C
        rows_in[at : at + C, 0:256] = x_left[block]
        rows_in[at : at + C, 256:512] = x_right[block]
    for at, index in ((0, 0), (last * C, 1)):
        rows_in[at : at + C, 0:256] = c_left[index]
        rows_in[at : at + C, 256:512] = c_right[index]
    at = (last + 1) * C
    rows_in[at : at + C, 0:256] = x_left[number] + c_left[2]
    rows_in[at : at + C, 256:512] = x_right[number] + c_right[2]
    for pair in range(4):
        lanes = slice(256 * pair, 256 * pair + 256)
        placed = dot(rows_in[...], place[:, lanes])
        for half in range(2):
            span = slice(LANES * half, LANES * (half + 1))
            for block in range(last + 1):
                tile = EDGE * block + 2 * pair + half
                halo = placed[block * C : (block + 1) * C, span].astype(BF16)
                grid[tile] = grid_own[tile] + halo
        if pair == 0:
            live[...] = live_own[...] + placed[(last + 1) * C :, 0:LANES]
    tiles = grid.shape[0]
    coarse_tiles = lowered.shape[0]
    conv_steps(fine_p, fine_w, lambda tile: grid[tile], tiles, 16, 1, 2)
    anchors = anchor_mask(False)

    def lower_step(block):
        alive = jnp.broadcast_to(live[pl.ds(block, 1), :], (C, LANES))
        keep = alive * anchors
        pairs = []
        for inner in range(4):
            actives = []
            for half in range(2):
                tile = EDGE * block + 2 * inner + half
                value = conv_sum(fine_p, tile) * alive
                hidden[tile] = value
                actives.append(silu_parts(value)[0].astype(BF16))
            pairs.append(jnp.concatenate(actives, axis=0))
        parts = dot(down_w[...], jnp.concatenate(pairs, axis=1))
        for inner in range(4):
            total = gather_sub(parts[:, LANES * inner : LANES * (inner + 1)])
            lowered[4 * block + inner] = (total * keep).astype(BF16)

    loop(0, last + 1, lower_step, 2)
    conv_steps(coarse_p, coarse_w, lambda tile: lowered[tile], coarse_tiles, 32, 2, 2)
    own_anchors = anchor_mask(True)

    def grad_step(block):
        alive = jnp.broadcast_to(live[pl.ds(block, 1), :], (C, LANES))
        keep = alive * own_anchors
        for inner in range(4):
            coarse = 4 * block + inner
            smooth, slope = silu_parts(conv_sum(coarse_p, coarse))
            rects[coarse] = (smooth * own_anchors).astype(BF16)
            grad_c[coarse] = (grad_r[coarse] * slope * keep).astype(BF16)

    loop(0, last + 1, grad_step, 2)
    ids = lane_ids(C)
    zero = jnp.zeros((C, LANES), BF16)
    for out, lane in ((pack_low, 4), (pack_high, 10)):
        for group in range(out.shape[0]):
            total = zero
            for coarse in range(max(2, 32 * group), min(coarse_tiles - 2, 32 * group + 32)):
                picked = jnp.where(ids % 32 == lane, grad_c[coarse], zero)
                total = total + roll(picked, coarse % 32 - lane)
            out[group] = total


def to_blocks(slots, rows_out, place, out):
    flat = dot(rows_out[...], place[...], (1, 1)).astype(BF16)
    rows_out[:, 0:512] = flat
    for slot in range(out.shape[0]):
        start = pl.multiple_of(slots[slot] * C, 16)
        out[slot] = rows_out[pl.ds(start, C), 0:512]


def stacks(own, tiles):
    parts = [jnp.concatenate([own[t + 1], own[t], own[t - 1]], axis=0) for t in tiles]
    return jnp.concatenate(parts, axis=1)


def flatten_weights(total, out, at):
    turned = total[...].T.astype(BF16)
    for group in range(4):
        out[at + 3 * C * group : at + 3 * C * (group + 1), :] = turned[
            :, LANES * group : LANES * (group + 1)
        ]


def side_kernel(
    slots, hidden, rects, cot_grid, lowered, grad_c, live, place, up_w, out, flat,
    rows_out, grad_own, up_g, coarse_g,
):
    number = out.shape[0]
    coarse_tiles = lowered.shape[0]
    up_g[...] = jnp.zeros_like(up_g)
    coarse_g[...] = jnp.zeros_like(coarse_g)

    def block_step(block):
        alive = jnp.broadcast_to(live[pl.ds(block + 1, 1), :], (C, LANES))
        start = pl.multiple_of(block * C, 16)
        spreads = []
        pairs = []
        for inner in range(4):
            coarse = 4 * (block + 1) + inner
            spreads.append(spread_sub(rects[coarse]))
            pairs.append(
                jnp.concatenate([cot_grid[2 * coarse], cot_grid[2 * coarse + 1]], axis=0)
            )
        spread = jnp.concatenate(spreads, axis=1)
        upward = dot(up_w[...], spread)
        for inner in range(4):
            for half in range(2):
                part = upward[half * C : (half + 1) * C, LANES * inner : LANES * (inner + 1)]
                value = hidden[EDGE * (block + 1) + 2 * inner + half] + part
                at = LANES * (2 * inner + half)
                rows_out[pl.ds(start, C), at : at + LANES] = (value * alive).astype(BF16)
        up_g[:, 0 : 2 * C] += dot(spread, jnp.concatenate(pairs, axis=1), (1, 1))

    loop(0, number, block_step, 2)
    to_blocks(slots, rows_out, place, out)
    zero = jnp.zeros((C, LANES), BF16)
    for coarse in (1, 2, 3, coarse_tiles - 4, coarse_tiles - 3, coarse_tiles - 2):
        grad_own[coarse] = zero

    def copy_step(coarse):
        grad_own[coarse] = grad_c[coarse]

    loop(4, coarse_tiles - 4, copy_step, 8)
    low, high = z_masks(32)

    def weight_step(index):
        tiles = [2 + 4 * index + inner for inner in range(4)]
        rights = [columns(lowered[tile], low, high, 32, 2) for tile in tiles]
        coarse_g[0 : 9 * C, :] += dot(
            jnp.concatenate(rights, axis=1), stacks(grad_own, tiles), (1, 1)
        )

    loop(0, (coarse_tiles - 4) // 4, weight_step)
    flatten_weights(coarse_g, flat, 0)
    flat[12 * C :, :] = up_g[...].astype(BF16)


def backward_kernel(
    grad_c, from_left, from_right, hidden, cot_grid, live, coarse_w, down_w,
    grad_h, grad_d, pack_low, pack_high, coarse_p, grad_x,
):
    coarse_tiles = grad_c.shape[0]
    ids = lane_ids(C)
    even = (ids // 16) % 2 == 0
    at_left = even & (ids % 16 == 2)
    at_right = even & (ids % 16 == 12)
    zero = jnp.zeros((C, LANES), BF16)
    for coarse in range(coarse_tiles):
        group, place = coarse // 32, coarse % 32
        tile = jnp.where(at_left, roll(from_left[group], 2 - place), grad_c[coarse])
        grad_x[coarse] = jnp.where(at_right, roll(from_right[group], 12 - place), tile)
    conv_steps(coarse_p, coarse_w, lambda tile: grad_x[tile], coarse_tiles, 32, 2, 2)
    own_anchors = anchor_mask(True)
    across = lane_ids(C) % 16
    inside = ((across >= 4) & (across < 12)).astype(F32)

    def step(block):
        alive = jnp.broadcast_to(live[pl.ds(block, 1), :], (C, LANES)) * inside
        keep = alive * own_anchors
        spreads = []
        for inner in range(4):
            coarse = 4 * block + inner
            down = (conv_sum(coarse_p, coarse) * keep).astype(BF16)
            grad_d[coarse] = down
            spreads.append(spread_sub(down))
        acts = dot(down_w[...], jnp.concatenate(spreads, axis=1), (0, 0))
        for inner in range(4):
            for half in range(2):
                tile = EDGE * block + 2 * inner + half
                slope = silu_parts(hidden[tile])[1]
                part = acts[half * C : (half + 1) * C, LANES * inner : LANES * (inner + 1)]
                grad = cot_grid[tile].astype(F32) + part * slope
                grad_h[tile] = (grad * alive).astype(BF16)

    loop(0, coarse_tiles // 4, step, 2)
    for out, lane in ((pack_low, 4), (pack_high, 11)):
        def pack_step(group):
            total = zero
            for inner in range(16):
                picked = jnp.where(ids % 16 == lane, grad_h[16 * group + inner], zero)
                total = total + roll(picked, inner - lane)
            out[group] = total

        loop(0, out.shape[0], pack_step)


def weight_kernel(grid, grad_h, grad_d, hidden, early, joined, grad_own, fine_g, down_g):
    tiles = grid.shape[0]
    coarse_tiles = grad_d.shape[0]
    fine_g[...] = jnp.zeros_like(fine_g)
    down_g[...] = jnp.zeros_like(down_g)
    zero = jnp.zeros((C, LANES), BF16)
    for step in range(3, 8):
        grad_own[step] = zero
        grad_own[tiles - 1 - step] = zero

    def copy_step(tile):
        grad_own[tile] = grad_h[tile]

    loop(8, tiles - 8, copy_step, 8)
    low, high = z_masks(16)

    def fine_step(index):
        at = [4 + 8 * index + inner for inner in range(8)]
        rights = [columns(grid[tile], low, high, 16, 1) for tile in at]
        fine_g[0 : 9 * C, :] += dot(
            jnp.concatenate(rights, axis=1), stacks(grad_own, at), (1, 1)
        )

    loop(0, (tiles - 8) // 8, fine_step)

    def down_step(index):
        lefts = []
        rights = []
        for inner in range(4):
            coarse = 4 + 4 * index + inner
            lefts.append(spread_sub(grad_d[coarse]))
            actives = [silu_parts(hidden[2 * coarse + half])[0].astype(BF16) for half in range(2)]
            rights.append(jnp.concatenate(actives, axis=0))
        down_g[:, 0 : 2 * C] += dot(
            jnp.concatenate(lefts, axis=1), jnp.concatenate(rights, axis=1), (1, 1)
        )

    loop(0, (coarse_tiles - 8) // 4, down_step, 2)
    flatten_weights(fine_g, joined, 0)
    joined[12 * C : 16 * C, :] = down_g[...].astype(BF16)
    joined[16 * C :, :] = early[...]


def input_kernel(
    slots, grad_h, from_left, from_right, live, place, fine_w, out, fine_p, rows_out, grad_x
):
    tiles = grad_h.shape[0]
    number = out.shape[0]
    ids = lane_ids(C)
    at_left = ids % 16 == 3
    at_right = ids % 16 == 12

    def fill_step(group):
        packed_left = from_left[group]
        packed_right = from_right[group]
        for inner in range(16):
            tile = jnp.where(at_left, roll(packed_left, 3 - inner), grad_h[16 * group + inner])
            tile = jnp.where(at_right, roll(packed_right, 12 - inner), tile)
            grad_x[16 * group + inner] = tile

    loop(0, tiles // 16, fill_step)
    conv_steps(fine_p, fine_w, lambda tile: grad_x[tile], tiles, 16, 1, 2)

    def block_step(block):
        alive = jnp.broadcast_to(live[pl.ds(block + 1, 1), :], (C, LANES))
        start = pl.multiple_of(block * C, 16)
        for inner in range(EDGE):
            value = conv_sum(fine_p, EDGE * (block + 1) + inner)
            rows_out[pl.ds(start, C), LANES * inner : LANES * (inner + 1)] = (
                value * alive
            ).astype(BF16)

    loop(0, number, block_step, 2)
    to_blocks(slots, rows_out, place, out)


def call(kernel, inputs, outs, scratch=(), scalars=0, flops=0):
    vmem = pl.BlockSpec(memory_space=pltpu.VMEM)
    smem = pl.BlockSpec(memory_space=pltpu.SMEM)
    moved = sum(math.prod(s) * jnp.dtype(d).itemsize for s, d in outs)
    moved += sum(math.prod(a.shape) * a.dtype.itemsize for a in inputs)
    return pl.pallas_call(
        kernel,
        out_shape=tuple(jax.ShapeDtypeStruct(s, d) for s, d in outs),
        in_specs=[smem] * scalars + [vmem] * (len(inputs) - scalars),
        out_specs=tuple(vmem for _ in outs),
        scratch_shapes=[pltpu.VMEM(s, d) for s, d in scratch],
        compiler_params=pltpu.CompilerParams(vmem_limit_bytes=VMEM_LIMIT),
        cost_estimate=pl.CostEstimate(flops=flops, bytes_accessed=moved, transcendentals=0),
        name=kernel.__name__,
    )(*inputs)


def send(array, step_x, step_y):
    number_x, number_y = lax.axis_size("gx"), lax.axis_size("gy")
    pairs = []
    for i in range(number_x):
        for j in range(number_y):
            to_x, to_y = i + step_x, j + step_y
            if 0 <= to_x < number_x and 0 <= to_y < number_y:
                pairs.append((i * number_y + j, to_x * number_y + to_y))
    return lax.ppermute(array, ("gx", "gy"), pairs)


def reduce_all(joined):
    axes = ("gx", "gy")
    devices = lax.axis_size("gx") * lax.axis_size("gy")
    rows = joined.shape[0]
    share = -(-rows // devices)
    joined = jnp.pad(joined, ((0, share * devices - rows), (0, 0)))
    mine = lax.all_to_all(joined.reshape(devices, share, LANES), axes, 0, 0)
    mine = jnp.sum(mine.astype(F32), axis=0).astype(BF16)
    spread = jnp.broadcast_to(mine[None], (devices, share, LANES))
    full = lax.all_to_all(spread, axes, 0, 0)
    return full.reshape(devices * share, LANES)[:rows]


def lane_join(flat, rows, width):
    parts = flat.shape[0] // rows
    array = flat.reshape(parts, rows, LANES).transpose(1, 0, 2).reshape(rows, parts * LANES)
    return array[:, :width]


def on_device(
    features, block_slots, block_count, cotangent, fine_weight, down_weight, coarse_weight,
    up_weight,
):
    number = features.shape[2]
    slots = block_slots.reshape(number)
    count = block_count.reshape(1)
    feats = features.reshape(number, C, VOX)
    cots = cotangent.reshape(number, C, VOX)
    place_own = jnp.asarray(placing_matrix()[:512], BF16)
    place_halo = jnp.asarray(placing_matrix()[512:], BF16)
    pick = jnp.asarray(edge_matrix(), BF16)
    tiles = EDGE * (number + 2)
    coarse_tiles = tiles // 2
    groups = -(-coarse_tiles // 32)
    fine_groups = tiles // 16

    fine_5 = fine_weight.reshape(C, 3, 3, 3, C)
    coarse_5 = coarse_weight.reshape(C, 3, 3, 3, C)
    fine_fore = fine_5.transpose(3, 0, 2, 1, 4).reshape(3 * C, 9 * C)
    fine_back = fine_5[:, ::-1, ::-1, ::-1].transpose(3, 4, 2, 1, 0).reshape(3 * C, 9 * C)
    coarse_fore = coarse_5.transpose(3, 0, 2, 1, 4).reshape(3 * C, 9 * C)
    coarse_back = coarse_5[:, ::-1, ::-1, ::-1].transpose(3, 4, 2, 1, 0).reshape(3 * C, 9 * C)
    down_w = down_weight.reshape(C, 2, 2, 2, C).transpose(1, 2, 0, 3, 4).reshape(4 * C, 2 * C)
    up_w = up_weight.reshape(2, 2, 2, C, C).transpose(2, 3, 0, 1, 4).reshape(2 * C, 4 * C)

    own, cot, x_low, x_high, y_low, y_high = call(
        prepare_kernel,
        (slots, count, feats, cots, pick),
        [((number + 1, C, VOX), BF16), ((number, C, VOX), BF16)]
        + [((number + 1, C, 256), BF16)] * 2
        + [((3, C, VOX), BF16)] * 2,
        scalars=2,
    )
    x_left = send(x_high, 1, 0)
    x_right = send(x_low, -1, 0)
    y_left = send(y_high, 0, 1)
    y_right = send(y_low, 0, -1)
    corner_low, corner_high, flags = call(
        corner_kernel,
        (y_left, y_right, own[number:], pick),
        [((3, C, 256), BF16), ((3, C, 256), BF16), ((C, VOX), BF16)],
    )
    c_left = send(corner_high, 1, 0)
    c_right = send(corner_low, -1, 0)
    grid_own, cot_grid, grad_r, live_own = call(
        place_kernel,
        (own, cot, y_left, y_right, flags, place_own, up_w),
        [
            ((tiles, C, LANES), BF16),
            ((tiles, C, LANES), BF16),
            ((coarse_tiles, C, LANES), F32),
            ((C, LANES), F32),
        ],
        [(((number + 3) * C, VOX), BF16), (((number + 2) * C, VOX), BF16)],
        flops=8 * 10**9,
    )
    fine_fore, fine_back, coarse_fore, coarse_back, down_w, grid_own = lax.optimization_barrier(
        (fine_fore, fine_back, coarse_fore, coarse_back, down_w, grid_own)
    )
    grid, hidden, lowered, rects, grad_c, live, pack_low, pack_high = call(
        forward_kernel,
        (grid_own, live_own, grad_r, x_left, x_right, c_left, c_right, place_halo, fine_fore,
         down_w, coarse_fore),
        [
            ((tiles, C, LANES), BF16),
            ((tiles, C, LANES), F32),
            ((coarse_tiles, C, LANES), BF16),
            ((coarse_tiles, C, LANES), BF16),
            ((coarse_tiles, C, LANES), BF16),
            ((C, LANES), F32),
            ((groups, C, LANES), BF16),
            ((groups, C, LANES), BF16),
        ],
        [
            (((number + 3) * C, VOX), BF16),
            ((tiles + 2, 3 * C, LANES), F32),
            ((coarse_tiles + 2, 3 * C, LANES), F32),
        ],
        flops=8 * 10**9,
    )
    grad_left = send(pack_high, 1, 0)
    grad_right = send(pack_low, -1, 0)
    output, early = call(
        side_kernel,
        (slots, hidden, rects, cot_grid, lowered, grad_c, live, place_own, up_w),
        [((number, C, VOX), BF16), ((16 * C, LANES), BF16)],
        [
            ((number * C, 1024), BF16),
            ((coarse_tiles, C, LANES), BF16),
            ((4 * C, LANES), F32),
            ((VOX, 3 * C), F32),
        ],
        scalars=1,
        flops=8 * 10**9,
    )
    grad_h, grad_d, edge_low, edge_high = call(
        backward_kernel,
        (grad_c, grad_left, grad_right, hidden, cot_grid, live, coarse_back, down_w),
        [
            ((tiles, C, LANES), BF16),
            ((coarse_tiles, C, LANES), BF16),
            ((fine_groups, C, LANES), BF16),
            ((fine_groups, C, LANES), BF16),
        ],
        [((coarse_tiles + 2, 3 * C, LANES), F32), ((coarse_tiles, C, LANES), BF16)],
        flops=8 * 10**9,
    )
    edge_left = send(edge_high, 1, 0)
    edge_right = send(edge_low, -1, 0)
    (joined,) = call(
        weight_kernel,
        (grid, grad_h, grad_d, hidden, early),
        [((32 * C, LANES), BF16)],
        [((tiles, C, LANES), BF16), ((VOX, 3 * C), F32), ((4 * C, LANES), F32)],
        flops=12 * 10**9,
    )
    joined, edge_left, edge_right = lax.optimization_barrier((joined, edge_left, edge_right))
    total = reduce_all(joined)
    (input_grad,) = call(
        input_kernel,
        (slots, grad_h, edge_left, edge_right, live, place_own, fine_back),
        [((number, C, VOX), BF16)],
        [
            ((tiles + 2, 3 * C, LANES), F32),
            ((number * C, 1024), BF16),
            ((tiles, C, LANES), BF16),
        ],
        scalars=1,
        flops=8 * 10**9,
    )
    total = total.astype(F32)
    fine_sum, down_sum = total[: 12 * C], total[12 * C : 16 * C]
    coarse_sum, up_sum = total[16 * C : 28 * C], total[28 * C :]
    scale = 1.0 / math.sqrt(number * VOX * lax.axis_size("gx") * lax.axis_size("gy"))
    fine_total = lane_join(fine_sum, 3 * C, 9 * C).reshape(3, C, 3, 3, C) * scale
    coarse_total = lane_join(coarse_sum, 3 * C, 9 * C).reshape(3, C, 3, 3, C) * scale
    down_total = down_sum[:, : 2 * C].reshape(2, 2, C, 2, C) * scale
    up_total = up_sum[:, : 2 * C].reshape(2, 2, C, 2, C) * scale
    shape_out = (1, 1, number, C, VOX)
    return (
        output.reshape(shape_out),
        input_grad.reshape(shape_out),
        fine_total.transpose(1, 3, 2, 0, 4).reshape(C, 27, C),
        down_total.transpose(2, 0, 1, 3, 4).reshape(C, 8, C),
        coarse_total.transpose(1, 3, 2, 0, 4).reshape(C, 27, C),
        up_total.transpose(0, 1, 3, 4, 2).reshape(8, C, C),
    )


def solution(mesh):
    split = P("gx", "gy", None, None, None)
    return jax.shard_map(
        on_device,
        mesh=mesh,
        in_specs=(split, P("gx", "gy", None), P("gx", "gy"), split, P(), P(), P(), P()),
        out_specs=(split, split, P(), P(), P(), P()),
        check_vma=False,
    )
```

time: 261 us -> 181 us (0.69)
  Pallas kernels: 137 us -> 103 us
  blocking collectives: 42.5 us -> 24 us
  waiting for transfers between devices: 14.7 us -> 0.03 us
  starting transfers between devices: 42 us -> 31 us
  other arithmetic: 4.72 us -> 0.19 us
  local copies, waits for them, and re-layouts: 18.4 us -> 21.1 us
    all_gather x1 -> x0, blocking collectives: 42.5 us -> none  [reduce_all(): full = lax.all_gather(mine, axes, axis=0, tiled=True)]
    pallas_call x6 -> x8, Pallas kernels: 137 us -> 103 us  [call(): pl.pallas_call(kernel, out_shape=tuple((jax.ShapeDtypeStruct(s, d) for s,...]
    all_to_all x0 -> x1, blocking collectives: none -> 24 us  [reduce_all(): mine = lax.all_to_all(joined.reshape(devices, share, LANES), axes, 0, 0)]
    ppermute x12 -> x10, waiting for transfers between devices: 14.7 us -> 0.03 us  [send(): return lax.ppermute(array, ('gx', 'gy'), pairs)]
    all_to_all x1, starting transfers between devices: 11.6 us -> 2.64 us  [reduce_all(): full = lax.all_to_all(spread, axes, 0, 0)]
    another operation x4 -> x0, other arithmetic: 3.81 us -> none
    ppermute x12 -> x10, starting transfers between devices: 30.4 us -> 28.3 us  [send(): return lax.ppermute(array, ('gx', 'gy'), pairs)]
  transfers between devices with their start and end apart: 13 -> 11, of which waited for: 3 -> 0; matrix products, arithmetic and copies ran while one was open for 5% -> 7% of each run, Pallas kernels for 14% -> 32%
where the time goes in v2:
time: 181 us
  Pallas kernels  103 us (57%)
  starting transfers between devices  31 us (17%)
  blocking collectives  24 us (13%)
  local copies, waits for them, and re-layouts  21.1 us (12%)
    pallas_call x8, Pallas kernels, call(): pl.pallas_call(kernel, out_shape=tuple((jax.ShapeDtypeStruct(s, d) for s,...  103 us
    ppermute x10, starting transfers between devices, send(): return lax.ppermute(array, ('gx', 'gy'), pairs)  28.3 us
    all_to_all x1, blocking collectives, reduce_all(): mine = lax.all_to_all(joined.reshape(devices, share, LANES), axes, 0, 0)  24 us
    unnamed x29, local copies, waits for them, and re-layouts  4.18 us
  transfers between devices with their start and end apart: 11, of which 0 were waited for; matrix products, arithmetic and copies ran while one was open for 7% of the time, Pallas kernels for 32%

profile of v2, /device:TPU:0, one launch (start us, length us, event | category | flops | bytes accessed | tf_op | source)
XLA Modules:
  0.0 180.6 jit_solution(11974073131367598659)
XLA Ops:
  1.3 3.2 %prepare_kernel.1 = (bf16[17,48,512]{2,1,0:T(8,128)(2,1)}, bf16[16,48,512]{2,1,0:T(8,128)(2,1)}, bf16[17,48,256]{2,1,0:T(8,128)(2,1)}, bf16[17,48,256]{2,1,0:T(8...) custom-call(s32[16]{0:T(128)} %bitcast.77, s32[1]{0:T(128)} %bitcast.48.count, ...), custom_call_target="tpu_custom_call" | custom-call | bytes 4849732 | tf_op jit(solution)/shard_map/prepare_kernel/pallas_call | solution.py:479
  4.6 2.5 %collective-permute-start = (bf16[3,48,512]{2,1,0:T(8,128)(2,1)}, bf16[3,48,512]{2,1,0:T(8,128)(2,1)S(1)}, u32[]{:S(2)}, u32[]{:S(2)}) collective-permute-start(bf16[3,48,512]{2,1,0:T(8,128)(2,1)} %get-tuple-element.44), channel_id=1, source_target_pairs={{0,1},{1,2},{2,3},{4,5},{5,6},{6,7},{8,9},{9,10},{10,11},{12,13},{... | collective-permute-start | bytes 442376 | tf_op jit(solution)/shard_map/ppermute | solution.py:499
  7.1 1.3 collective-permute-start.1
  8.4 4.2 %collective-permute-start.2 = (bf16[17,48,256]{2,1,0:T(8,128)(2,1)}, bf16[17,48,256]{2,1,0:T(8,128)(2,1)S(1)}, u32[]{:S(2)}, u32[]{:S(2)}) collective-permute-start(bf16[17,48,256]{2,1,0:T(8,128)(2,1)} %get-tuple-element.51), channel_id=1, source_target_pairs={{0,4},{1,5},{2,6},{3,7},{4,8},{5,9},{6,10},{7,11},{8,12},{9,13},{1... | collective-permute-start | bytes 1253384 | tf_op jit(solution)/shard_map/ppermute | solution.py:499
  12.6 1.3 collective-permute-start.3
  16.4 2.4 %rev.6 = bf16[48,3,3,3,48]{0,1,2,4,3:T(4,128)(2,1)S(1)} reverse(bf16[48,3,3,3,48]{0,1,2,4,3:T(4,128)(2,1)S(1)} %copy.30), dimensions={1,2,3} | reverse | bytes 248832 | tf_op jit(solution)/shard_map/rev | solution.py:541
  18.8 0.9 reshape.109.fine_w
  19.8 0.9 reshape.108.fine_w
  20.7 2.4 %rev.7 = bf16[48,3,3,3,48]{0,1,2,4,3:T(4,128)(2,1)S(1)} reverse(bf16[48,3,3,3,48]{0,1,2,4,3:T(4,128)(2,1)S(1)} %copy.32), dimensions={1,2,3} | reverse | bytes 248832 | tf_op jit(solution)/shard_map/rev | solution.py:543
  23.1 0.9 reshape.112.coarse_w
  24.0 0.9 reshape.111.coarse_w
  24.9 1.4 slice.27.own
  27.7 2.2 %corner_kernel.1 = (bf16[3,48,256]{2,1,0:T(8,128)(2,1)}, bf16[3,48,256]{2,1,0:T(8,128)(2,1)}, bf16[48,512]{1,0:T(8,128)(2,1)}) custom-call(bf16[3,48,512]{2,1,0:T(8,128)(2,1)} %copy-done.2, bf16[3,48,512]{2,1,0:T(8,128)(2,1)} %copy-done.3, bf16[1,48,512]{2,1,0:T(8,128)(2,1)} %slice.27.own, bf16[512,512]{1,0:T(8,128)(2,1)} %constant.15.clone.pick), custom_call_target="tpu_custom_call" | custom-call | bytes 1064960 | tf_op jit(solution)/shard_map/corner_kernel/pallas_call | solution.py:479
  29.8 4.5 %collective-permute-start.4 = (bf16[3,48,256]{2,1,0:T(8,128)(2,1)}, bf16[3,48,256]{2,1,0:T(8,128)(2,1)S(1)}, u32[]{:S(2)}, u32[]{:S(2)}) collective-permute-start(bf16[3,48,256]{2,1,0:T(8,128)(2,1)} %get-tuple-element.53), channel_id=1, source_target_pairs={{0,4},{1,5},{2,6},{3,7},{4,8},{5,9},{6,10},{7,11},{8,12},{9,13},{1... | collective-permute-start | bytes 221192 | tf_op jit(solution)/shard_map/ppermute | solution.py:499
  34.4 1.3 collective-permute-start.5
  35.7 9.5 %place_kernel.1 = (bf16[144,48,128]{2,1,0:T(8,128)(2,1)}, bf16[144,48,128]{2,1,0:T(8,128)(2,1)}, f32[72,48,128]{2,1,0:T(8,128)}, f32[48,128]{1,0:T(8,128)}) custom-call(bf16[17,48,512]{2,1,0:T(8,128)(2,1)} %get-tuple-element.42.own, bf16[16,48,512]{2,1,0:T(8,128)(2,1)} %get-tuple-element.43.cot, bf16[3,48,512]{2,1,0:T(8,128)(2,1)} %copy-done.2, ...), custom_call_target="tpu_custom_call" | custom-call | flops 8000000000 | bytes 8384512 | tf_op jit(solution)/shard_map/place_kernel/pallas_call | solution.py:479
  46.1 26.3 %forward_kernel.1 = (bf16[144,48,128]{2,1,0:T(8,128)(2,1)}, f32[144,48,128]{2,1,0:T(8,128)}, bf16[72,48,128]{2,1,0:T(8,128)(2,1)}, bf16[72,48,128]{2,1,0:T(8,128...) custom-call(bf16[144,48,128]{2,1,0:T(8,128)(2,1)} %get-tuple-element, ...), custom_call_target="tpu_custom_call" | custom-call | flops 8000000000 | bytes 13941760 | tf_op jit(solution)/shard_map/forward_kernel/pallas_call | solution.py:479
  72.5 5.0 %collective-permute-start.6 = (bf16[3,48,128]{2,1,0:T(8,128)(2,1)}, bf16[3,48,128]{2,1,0:T(8,128)(2,1)S(1)}, u32[]{:S(2)}, u32[]{:S(2)}) collective-permute-start(bf16[3,48,128]{2,1,0:T(8,128)(2,1)} %get-tuple-element.65), channel_id=1, source_target_pairs={{0,4},{1,5},{2,6},{3,7},{4,8},{5,9},{6,10},{7,11},{8,12},{9,13},{1... | collective-permute-start | bytes 110600 | tf_op jit(solution)/shard_map/ppermute | solution.py:499
  77.4 1.3 collective-permute-start.7
  78.7 15.3 %side_kernel.1 = (bf16[16,48,512]{2,1,0:T(8,128)(2,1)}, bf16[768,128]{1,0:T(8,128)(2,1)}) custom-call(s32[16]{0:T(128)} %bitcast.78, f32[144,48,128]{2,1,0:T(8,128)} %get-tuple-element.58.hidden, bf16[72,48,128]{2,1,0:T(8,128)(2,1)} %get-tuple-element.59.rects, bf16[144,48,128]{2,1,0:T(8,128)(2,1)} %get-tuple-element.60.cot_grid, ...), custom_call_target="tpu_custom_call" | custom-call | flops 8000000000 | bytes 10055744 | tf_op jit(solution)/shard_map/side_kernel/pallas_call | solution.py:479
  95.3 14.9 %backward_kernel.1 = (bf16[144,48,128]{2,1,0:T(8,128)(2,1)}, bf16[72,48,128]{2,1,0:T(8,128)(2,1)}, bf16[9,48,128]{2,1,0:T(8,128)(2,1)}, bf16[9,48,128]{2,1,0:T(8,128)(2,1)}) custom-call(bf16[72,48,128]{2,1,0:T(8,128)(2,1)} %get-tuple-element.62.grad_c, bf16[3,48,128]{2,1,0:T(8,128)(2,1)} %copy-done.12, bf16[3,48,128]{2,1,0:T(8,128)(2,1)} %copy-done.13, ...), custom_call_target="tpu_custom_call" | custom-call | flops 8000000000 | bytes 9328128 | tf_op jit(solution)/shard_map/backward_kernel/pallas_call | solution.py:479
  110.2 5.5 %collective-permute-start.8 = (bf16[9,48,128]{2,1,0:T(8,128)(2,1)}, bf16[9,48,128]{2,1,0:T(8,128)(2,1)S(1)}, u32[]{:S(2)}, u32[]{:S(2)}) collective-permute-start(bf16[9,48,128]{2,1,0:T(8,128)(2,1)} %get-tuple-element.72), channel_id=1, source_target_pairs={{0,4},{1,5},{2,6},{3,7},{4,8},{5,9},{6,10},{7,11},{8,12},{9,13},{1... | collective-permute-start | bytes 331784 | tf_op jit(solution)/shard_map/ppermute | solution.py:499
  115.6 1.5 collective-permute-start.9
  117.1 16.0 %weight_kernel.1 = bf16[1536,128]{1,0:T(8,128)(2,1)} custom-call(bf16[144,48,128]{2,1,0:T(8,128)(2,1)} %get-tuple-element.69.grid, bf16[144,48,128]{2,1,0:T(8,128)(2,1)} %get-tuple-element.68.grad_h, bf16[72,48,128]{2,1,0:T(8,128)(2,1)} %get-tuple-element.70.grad_d, f32[144,48,128]{2,1,0:T(8,128)} %get-tuple-element.58.hidden, ...), custom_call_target="tpu_custom_call" | custom-call | flops 12000000000 | bytes 8552448 | tf_op jit(solution)/shard_map/weight_kernel/pallas_call | solution.py:479
  133.2 24.0 %all_to_all.10 = bf16[32,48,128]{2,1,0:T(8,128)(2,1)S(1)} all-to-all(bf16[32,48,128]{2,1,0:T(8,128)(2,1)} %bitcast.71), channel_id=1, replica_groups=mesh['gx'=8,'gy'=4] {'gx','gy'}, dimensions={0} | all-to-all | bytes 786432 | tf_op jit(solution)/shard_map/all_to_all | solution.py:508
  157.3 0.8 broadcast_in_dim.2
  158.1 2.6 %all-to-all-start.1 = ((bf16[32,48,128]{2,1,0:T(8,128)(2,1)}), bf16[32,48,128]{2,1,0:T(8,128)(2,1)S(1)}, u32[]{:S(2)}, u32[]{:S(2)}) async-start(bf16[32,48,128]{2,1,0:T(8,128)(2,1)} %broadcast_in_dim.2), calls=%async_computation.1 | async-start | bytes 786432 | tf_op jit(solution)/shard_map/all_to_all | solution.py:511
  160.8 15.0 %input_kernel.1 = bf16[16,48,512]{2,1,0:T(8,128)(2,1)} custom-call(s32[16]{0:T(128)} %bitcast.79, bf16[144,48,128]{2,1,0:T(8,128)(2,1)} %get-tuple-element.68.grad_h, bf16[9,48,128]{2,1,0:T(8,128)(2,1)} %copy-done.8, bf16[9,48,128]{2,1,0:T(8,128)(2,1)} %copy-done.9, f32[48,128]{1,0:T(8,128)} %get-tuple-element.63.live, ...), custom_call_target="tpu_custom_call" | custom-call | flops 8000000000 | bytes 3974720 | tf_op jit(solution)/shard_map/input_kernel/pallas_call | solution.py:479
  176.2 0.8 copy.40
  177.2 0.7 copy.41
  178.4 0.9 copy.36
  179.7 0.9 copy.39
  (60 shorter events, 7.3 us)
Async XLA Ops:
  0.6 13.3 %copy-start = (bf16[48,27,48]{2,0,1:T(8,128)(2,1)S(1)}, bf16[48,27,48]{2,0,1:T(8,128)(2,1)}, u32[]{:S(2)}) copy-start(bf16[48,27,48]{2,0,1:T(8,128)(2,1)} %param.15) | copy-start | bytes 373252
  1.3 13.0 %copy-start.1 = (bf16[48,27,48]{2,0,1:T(8,128)(2,1)S(1)}, bf16[48,27,48]{2,0,1:T(8,128)(2,1)}, u32[]{:S(2)}) copy-start(bf16[48,27,48]{2,0,1:T(8,128)(2,1)} %param.17) | copy-start | bytes 373252
  4.6 10.2 %copy-start.4 = (bf16[48,8,48]{2,1,0:T(8,128)(2,1)S(1)}, bf16[48,8,48]{2,1,0:T(8,128)(2,1)}, u32[]{:S(2)}) copy-start(bf16[48,8,48]{2,1,0:T(8,128)(2,1)} %param.16) | copy-start | bytes 110596
  4.6 11.0 %copy-start.5 = (bf16[8,48,48]{2,1,0:T(8,128)(2,1)S(1)}, bf16[8,48,48]{2,1,0:T(8,128)(2,1)}, u32[]{:S(2)}) copy-start(bf16[8,48,48]{2,1,0:T(8,128)(2,1)} %param.18) | copy-start | bytes 110596
  4.6 21.8 %collective-permute-start = (bf16[3,48,512]{2,1,0:T(8,128)(2,1)}, bf16[3,48,512]{2,1,0:T(8,128)(2,1)S(1)}, u32[]{:S(2)}, u32[]{:S(2)}) collective-permute-start(bf16[3,48,512]{2,1,0:T(8,128)(2,1)} %get-tuple-element.44), channel_id=1, source_target_pairs={{0,1},{1,2},{2,3},{4,5},{5,6},{6,7},{8,9},{9,10},{10,11},{12,13},{... | collective-permute-start | bytes 442376 | tf_op jit(solution)/shard_map/ppermute | solution.py:499
  7.1 19.3 %collective-permute-start.1 = (bf16[3,48,512]{2,1,0:T(8,128)(2,1)}, bf16[3,48,512]{2,1,0:T(8,128)(2,1)S(1)}, u32[]{:S(2)}, u32[]{:S(2)}) collective-permute-start(bf16[3,48,512]{2,1,0:T(8,128)(2,1)} %get-tuple-element.45), channel_id=1, source_target_pairs={{1,0},{2,1},{3,2},{5,4},{6,5},{7,6},{9,8},{10,9},{11,10},{13,12},{... | collective-permute-start | bytes 442376 | tf_op jit(solution)/shard_map/ppermute | solution.py:499
  8.4 36.8 %collective-permute-start.2 = (bf16[17,48,256]{2,1,0:T(8,128)(2,1)}, bf16[17,48,256]{2,1,0:T(8,128)(2,1)S(1)}, u32[]{:S(2)}, u32[]{:S(2)}) collective-permute-start(bf16[17,48,256]{2,1,0:T(8,128)(2,1)} %get-tuple-element.51), channel_id=1, source_target_pairs={{0,4},{1,5},{2,6},{3,7},{4,8},{5,9},{6,10},{7,11},{8,12},{9,13},{1... | collective-permute-start | bytes 1253384 | tf_op jit(solution)/shard_map/ppermute | solution.py:499
  12.6 32.6 %collective-permute-start.3 = (bf16[17,48,256]{2,1,0:T(8,128)(2,1)}, bf16[17,48,256]{2,1,0:T(8,128)(2,1)S(1)}, u32[]{:S(2)}, u32[]{:S(2)}) collective-permute-start(bf16[17,48,256]{2,1,0:T(8,128)(2,1)} %get-tuple-element.52), channel_id=1, source_target_pairs={{4,0},{5,1},{6,2},{7,3},{8,4},{9,5},{10,6},{11,7},{12,8},{13,9},{1... | collective-permute-start | bytes 1253384 | tf_op jit(solution)/shard_map/ppermute | solution.py:499
  26.3 0.7 copy-start.2
  27.0 0.7 copy-start.3
  29.8 15.4 %collective-permute-start.4 = (bf16[3,48,256]{2,1,0:T(8,128)(2,1)}, bf16[3,48,256]{2,1,0:T(8,128)(2,1)S(1)}, u32[]{:S(2)}, u32[]{:S(2)}) collective-permute-start(bf16[3,48,256]{2,1,0:T(8,128)(2,1)} %get-tuple-element.53), channel_id=1, source_target_pairs={{0,4},{1,5},{2,6},{3,7},{4,8},{5,9},{6,10},{7,11},{8,12},{9,13},{1... | collective-permute-start | bytes 221192 | tf_op jit(solution)/shard_map/ppermute | solution.py:499
  34.4 10.8 %collective-permute-start.5 = (bf16[3,48,256]{2,1,0:T(8,128)(2,1)}, bf16[3,48,256]{2,1,0:T(8,128)(2,1)S(1)}, u32[]{:S(2)}, u32[]{:S(2)}) collective-permute-start(bf16[3,48,256]{2,1,0:T(8,128)(2,1)} %get-tuple-element.54), channel_id=1, source_target_pairs={{4,0},{5,1},{6,2},{7,3},{8,4},{9,5},{10,6},{11,7},{12,8},{13,9},{1... | collective-permute-start | bytes 221192 | tf_op jit(solution)/shard_map/ppermute | solution.py:499
  45.2 0.6 copy-start.10
  45.2 0.6 copy-start.11
  45.2 0.8 copy-start.6
  45.2 0.9 copy-start.7
  72.5 21.6 %collective-permute-start.6 = (bf16[3,48,128]{2,1,0:T(8,128)(2,1)}, bf16[3,48,128]{2,1,0:T(8,128)(2,1)S(1)}, u32[]{:S(2)}, u32[]{:S(2)}) collective-permute-start(bf16[3,48,128]{2,1,0:T(8,128)(2,1)} %get-tuple-element.65), channel_id=1, source_target_pairs={{0,4},{1,5},{2,6},{3,7},{4,8},{5,9},{6,10},{7,11},{8,12},{9,13},{1... | collective-permute-start | bytes 110600 | tf_op jit(solution)/shard_map/ppermute | solution.py:499
  77.4 16.6 %collective-permute-start.7 = (bf16[3,48,128]{2,1,0:T(8,128)(2,1)}, bf16[3,48,128]{2,1,0:T(8,128)(2,1)S(1)}, u32[]{:S(2)}, u32[]{:S(2)}) collective-permute-start(bf16[3,48,128]{2,1,0:T(8,128)(2,1)} %get-tuple-element.66), channel_id=1, source_target_pairs={{4,0},{5,1},{6,2},{7,3},{8,4},{9,5},{10,6},{11,7},{12,8},{13,9},{1... | collective-permute-start | bytes 110600 | tf_op jit(solution)/shard_map/ppermute | solution.py:499
  94.0 0.6 copy-start.12
  94.7 0.6 copy-start.13
  110.2 23.0 %collective-permute-start.8 = (bf16[9,48,128]{2,1,0:T(8,128)(2,1)}, bf16[9,48,128]{2,1,0:T(8,128)(2,1)S(1)}, u32[]{:S(2)}, u32[]{:S(2)}) collective-permute-start(bf16[9,48,128]{2,1,0:T(8,128)(2,1)} %get-tuple-element.72), channel_id=1, source_target_pairs={{0,4},{1,5},{2,6},{3,7},{4,8},{5,9},{6,10},{7,11},{8,12},{9,13},{1... | collective-permute-start | bytes 331784 | tf_op jit(solution)/shard_map/ppermute | solution.py:499
  115.6 17.5 %collective-permute-start.9 = (bf16[9,48,128]{2,1,0:T(8,128)(2,1)}, bf16[9,48,128]{2,1,0:T(8,128)(2,1)S(1)}, u32[]{:S(2)}, u32[]{:S(2)}) collective-permute-start(bf16[9,48,128]{2,1,0:T(8,128)(2,1)} %get-tuple-element.73), channel_id=1, source_target_pairs={{4,0},{5,1},{6,2},{7,3},{8,4},{9,5},{10,6},{11,7},{12,8},{13,9},{1... | collective-permute-start | bytes 331784 | tf_op jit(solution)/shard_map/ppermute | solution.py:499
  133.2 27.6 %copy-start.8 = (bf16[9,48,128]{2,1,0:T(8,128)(2,1)}, bf16[9,48,128]{2,1,0:T(8,128)(2,1)S(1)}, u32[]{:S(2)}) copy-start(bf16[9,48,128]{2,1,0:T(8,128)(2,1)S(1)} %collective-permute-done.8.from_left) | copy-start | bytes 331780
  133.2 27.6 %copy-start.9 = (bf16[9,48,128]{2,1,0:T(8,128)(2,1)}, bf16[9,48,128]{2,1,0:T(8,128)(2,1)S(1)}, u32[]{:S(2)}) copy-start(bf16[9,48,128]{2,1,0:T(8,128)(2,1)S(1)} %collective-permute-done.9.from_right) | copy-start | bytes 331780
  158.1 17.7 %all-to-all-start.1 = ((bf16[32,48,128]{2,1,0:T(8,128)(2,1)}), bf16[32,48,128]{2,1,0:T(8,128)(2,1)S(1)}, u32[]{:S(2)}, u32[]{:S(2)}) async-start(bf16[32,48,128]{2,1,0:T(8,128)(2,1)} %broadcast_in_dim.2), calls=%async_computation.1 | async-start | bytes 786432 | tf_op jit(solution)/shard_map/all_to_all | solution.py:511

commit v3 on v2

--- a/solution.py
+++ b/solution.py
@@ -1,3 +1,4 @@
+import functools
 import math
 
 import jax
@@ -14,7 +15,7 @@
 LANES = 128
 F32 = jnp.float32
 BF16 = jnp.bfloat16
-VMEM_LIMIT = 58 * 1024 * 1024
+SLACK = 8 * 1024 * 1024
 SHIFTS = (0, 1, 16, 17)
 
 
@@ -98,7 +99,9 @@
     lax.fori_loop(low, high, step, 0, unroll=unroll)
 
 
-def prepare_kernel(slots, count, feats, cots, pick, own, cot, x_low, x_high, y_low, y_high):
+def prepare_kernel(
+    slots, count, feats, cots, pick, own, cot, flag_rows, x_low, x_high, y_low, y_high, rows_in
+):
     number = feats.shape[0]
     rows = lax.broadcasted_iota(jnp.int32, (C, VOX), 0)
     flags = jnp.zeros((C, VOX), F32)
@@ -109,15 +112,18 @@
         live = slot < count[0]
         alive = jnp.where(live, 1.0, 0.0)
         place = slots[slot]
-        own[place] = jnp.where(live, feats[slot], zero)
+        block = jnp.where(live, feats[slot], zero)
+        own[place] = block
+        rows_in[pl.ds(pl.multiple_of(place * C, 16), C), :] = block
         cot[place] = jnp.where(live, cots[slot], zero)
         flags = jnp.where(rows == place + 1, alive, flags)
         first = first + jnp.where(place == 0, alive, 0.0)
         last = last + jnp.where(place == number - 1, alive, 0.0)
-    own[number] = flags.astype(BF16)
+    flag_rows[...] = flags.astype(BF16)
+    rows_in[number * C :, :] = flags.astype(BF16)
     first_flag = jnp.where(rows == number + 1, first, 0.0).astype(BF16)
     last_flag = jnp.where(rows == 0, last, 0.0).astype(BF16)
-    packed = dot(own[...].reshape((number + 1) * C, VOX), pick[...]).astype(BF16)
+    packed = dot(rows_in[...], pick[...]).astype(BF16)
     packed = packed.reshape(number + 1, C, VOX)
     x_low[...] = packed[:, :, :256]
     x_high[...] = packed[:, :, 256:]
@@ -127,18 +133,42 @@
         out[2] = flag
 
 
-def corner_kernel(y_left, y_right, own, pick, low, high, flags):
+def corner_kernel(y_left, y_right, flag_rows, pick, low, high, flags):
     extra = y_left[2] + y_right[2]
     rows = jnp.concatenate([y_left[0], y_right[0], extra], axis=0)
     packed = dot(rows, pick[...]).astype(BF16).reshape(3, C, VOX)
     low[...] = packed[:, :, :256]
     high[...] = packed[:, :, 256:]
-    flags[...] = own[0] + extra
+    flags[...] = flag_rows[...] + extra
+
+
+def arrange_weights(fine, down, coarse, up, fine_w, fine_b, coarse_w, coarse_b, down_w, up_w):
+    for source, fore, back in ((fine, fine_w, fine_b), (coarse, coarse_w, coarse_b)):
+        for along in range(3):
+            rows = slice(C * along, C * (along + 1))
+            turned_rows = slice(C * (2 - along), C * (3 - along))
+            ahead = []
+            behind = []
+            for across in range(3):
+                for depth in range(3):
+                    ahead.append(source[9 * depth + 3 * across + along])
+                    behind.append(source[9 * (2 - depth) + 3 * (2 - across) + along].T)
+            fore[rows, :] = jnp.concatenate(ahead, axis=1)
+            back[turned_rows, :] = jnp.concatenate(behind, axis=1)
+    for index in range(4):
+        pair = [down[2 * index], down[2 * index + 1]]
+        down_w[C * index : C * (index + 1), :] = jnp.concatenate(pair, axis=1)
+    for along in range(2):
+        row = jnp.concatenate([up[2 * index + along] for index in range(4)], axis=1)
+        up_w[C * along : C * (along + 1), :] = row
 
 
 def place_kernel(
-    own, cot, y_left, y_right, flags, place, up_w, grid, cot_grid, grad_r, live, rows_in, rows_cot
+    own, cot, y_left, y_right, flags, place, fine, down, coarse, up,
+    grid, cot_grid, grad_r, live, fine_w, fine_b, coarse_w, coarse_b, down_w, up_w,
+    rows_in, rows_cot,
 ):
+    arrange_weights(fine, down, coarse, up, fine_w, fine_b, coarse_w, coarse_b, down_w, up_w)
     number = cot.shape[0]
     last = number + 1
     for block in range(number):
@@ -272,7 +302,7 @@
 
 
 def to_blocks(slots, rows_out, place, out):
-    flat = dot(rows_out[...], place[...], (1, 1)).astype(BF16)
+    flat = dot(rows_out[...], place[...]).astype(BF16)
     rows_out[:, 0:512] = flat
     for slot in range(out.shape[0]):
         start = pl.multiple_of(slots[slot] * C, 16)
@@ -471,9 +501,29 @@
     to_blocks(slots, rows_out, place, out)
 
 
+def finish_kernel(scale, total, fine, down, coarse, up):
+    for out, at in ((fine, 0), (coarse, 16 * C)):
+        for along in range(3):
+            first = at + C * along
+            rows = [total[first + 3 * C * g : first + 3 * C * g + C, :] for g in range(4)]
+            row = jnp.concatenate(rows, axis=1).astype(F32) * scale
+            for index in range(9):
+                out[9 * (index % 3) + 3 * (index // 3) + along] = row[:, C * index : C * (index + 1)]
+    for out, at, turn in ((down, 12 * C, False), (up, 28 * C, True)):
+        for index in range(4):
+            rows = total[at + C * index : at + C * (index + 1), :].astype(F32) * scale
+            for along in range(2):
+                part = rows[:, C * along : C * (along + 1)]
+                out[2 * index + along] = part.T if turn else part
+
+
 def call(kernel, inputs, outs, scratch=(), scalars=0, flops=0):
     vmem = pl.BlockSpec(memory_space=pltpu.VMEM)
     smem = pl.BlockSpec(memory_space=pltpu.SMEM)
+    held = SLACK
+    for shape, kind in [(a.shape, a.dtype) for a in inputs[scalars:]] + list(outs) + list(scratch):
+        rows, lanes = -(-shape[-2] // 16) * 16, -(-shape[-1] // LANES) * LANES
+        held += math.prod(shape[:-2]) * rows * lanes * jnp.dtype(kind).itemsize
     moved = sum(math.prod(s) * jnp.dtype(d).itemsize for s, d in outs)
     moved += sum(math.prod(a.shape) * a.dtype.itemsize for a in inputs)
     return pl.pallas_call(
@@ -482,9 +532,9 @@
         in_specs=[smem] * scalars + [vmem] * (len(inputs) - scalars),
         out_specs=tuple(vmem for _ in outs),
         scratch_shapes=[pltpu.VMEM(s, d) for s, d in scratch],
-        compiler_params=pltpu.CompilerParams(vmem_limit_bytes=VMEM_LIMIT),
+        compiler_params=pltpu.CompilerParams(vmem_limit_bytes=held),
         cost_estimate=pl.CostEstimate(flops=flops, bytes_accessed=moved, transcendentals=0),
-        name=kernel.__name__,
+        name=getattr(kernel, "func", kernel).__name__,
     )(*inputs)
 
 
@@ -512,12 +562,6 @@
     return full.reshape(devices * share, LANES)[:rows]
 
 
-def lane_join(flat, rows, width):
-    parts = flat.shape[0] // rows
-    array = flat.reshape(parts, rows, LANES).transpose(1, 0, 2).reshape(rows, parts * LANES)
-    return array[:, :width]
-
-
 def on_device(
     features, block_slots, block_count, cotangent, fine_weight, down_weight, coarse_weight,
     up_weight,
@@ -529,27 +573,24 @@
     cots = cotangent.reshape(number, C, VOX)
     place_own = jnp.asarray(placing_matrix()[:512], BF16)
     place_halo = jnp.asarray(placing_matrix()[512:], BF16)
+    place_back = jnp.asarray(placing_matrix()[:512].T, BF16)
     pick = jnp.asarray(edge_matrix(), BF16)
     tiles = EDGE * (number + 2)
     coarse_tiles = tiles // 2
     groups = -(-coarse_tiles // 32)
     fine_groups = tiles // 16
 
-    fine_5 = fine_weight.reshape(C, 3, 3, 3, C)
-    coarse_5 = coarse_weight.reshape(C, 3, 3, 3, C)
-    fine_fore = fine_5.transpose(3, 0, 2, 1, 4).reshape(3 * C, 9 * C)
-    fine_back = fine_5[:, ::-1, ::-1, ::-1].transpose(3, 4, 2, 1, 0).reshape(3 * C, 9 * C)
-    coarse_fore = coarse_5.transpose(3, 0, 2, 1, 4).reshape(3 * C, 9 * C)
-    coarse_back = coarse_5[:, ::-1, ::-1, ::-1].transpose(3, 4, 2, 1, 0).reshape(3 * C, 9 * C)
-    down_w = down_weight.reshape(C, 2, 2, 2, C).transpose(1, 2, 0, 3, 4).reshape(4 * C, 2 * C)
-    up_w = up_weight.reshape(2, 2, 2, C, C).transpose(2, 3, 0, 1, 4).reshape(2 * C, 4 * C)
-
-    own, cot, x_low, x_high, y_low, y_high = call(
+    fine_3, down_3, coarse_3 = (
+        weight.transpose(1, 0, 2) for weight in (fine_weight, down_weight, coarse_weight)
+    )
+    own, cot, flag_rows, x_low, x_high, y_low, y_high = call(
         prepare_kernel,
         (slots, count, feats, cots, pick),
-        [((number + 1, C, VOX), BF16), ((number, C, VOX), BF16)]
+        [((number, C, VOX), BF16)] * 2
+        + [((C, VOX), BF16)]
         + [((number + 1, C, 256), BF16)] * 2
         + [((3, C, VOX), BF16)] * 2,
+        [(((number + 1) * C, VOX), BF16)],
         scalars=2,
     )
     x_left = send(x_high, 1, 0)
@@ -558,25 +599,25 @@
     y_right = send(y_low, 0, -1)
     corner_low, corner_high, flags = call(
         corner_kernel,
-        (y_left, y_right, own[number:], pick),
+        (y_left, y_right, flag_rows, pick),
         [((3, C, 256), BF16), ((3, C, 256), BF16), ((C, VOX), BF16)],
     )
     c_left = send(corner_high, 1, 0)
     c_right = send(corner_low, -1, 0)
-    grid_own, cot_grid, grad_r, live_own = call(
+    (grid_own, cot_grid, grad_r, live_own, fine_fore, fine_back, coarse_fore, coarse_back, down_w,
+     up_w) = call(
         place_kernel,
-        (own, cot, y_left, y_right, flags, place_own, up_w),
+        (own, cot, y_left, y_right, flags, place_own, fine_3, down_3, coarse_3, up_weight),
         [
             ((tiles, C, LANES), BF16),
             ((tiles, C, LANES), BF16),
             ((coarse_tiles, C, LANES), F32),
             ((C, LANES), F32),
-        ],
+        ]
+        + [((3 * C, 9 * C), BF16)] * 4
+        + [((4 * C, 2 * C), BF16), ((2 * C, 4 * C), BF16)],
         [(((number + 3) * C, VOX), BF16), (((number + 2) * C, VOX), BF16)],
         flops=8 * 10**9,
-    )
-    fine_fore, fine_back, coarse_fore, coarse_back, down_w, grid_own = lax.optimization_barrier(
-        (fine_fore, fine_back, coarse_fore, coarse_back, down_w, grid_own)
     )
     grid, hidden, lowered, rects, grad_c, live, pack_low, pack_high = call(
         forward_kernel,
@@ -603,7 +644,7 @@
     grad_right = send(pack_low, -1, 0)
     output, early = call(
         side_kernel,
-        (slots, hidden, rects, cot_grid, lowered, grad_c, live, place_own, up_w),
+        (slots, hidden, rects, cot_grid, lowered, grad_c, live, place_back, up_w),
         [((number, C, VOX), BF16), ((16 * C, LANES), BF16)],
         [
             ((number * C, 1024), BF16),
@@ -639,7 +680,7 @@
     total = reduce_all(joined)
     (input_grad,) = call(
         input_kernel,
-        (slots, grad_h, edge_left, edge_right, live, place_own, fine_back),
+        (slots, grad_h, edge_left, edge_right, live, place_back, fine_back),
         [((number, C, VOX), BF16)],
         [
             ((tiles + 2, 3 * C, LANES), F32),
@@ -649,22 +690,20 @@
         scalars=1,
         flops=8 * 10**9,
     )
-    total = total.astype(F32)
-    fine_sum, down_sum = total[: 12 * C], total[12 * C : 16 * C]
-    coarse_sum, up_sum = total[16 * C : 28 * C], total[28 * C :]
     scale = 1.0 / math.sqrt(number * VOX * lax.axis_size("gx") * lax.axis_size("gy"))
-    fine_total = lane_join(fine_sum, 3 * C, 9 * C).reshape(3, C, 3, 3, C) * scale
-    coarse_total = lane_join(coarse_sum, 3 * C, 9 * C).reshape(3, C, 3, 3, C) * scale
-    down_total = down_sum[:, : 2 * C].reshape(2, 2, C, 2, C) * scale
-    up_total = up_sum[:, : 2 * C].reshape(2, 2, C, 2, C) * scale
+    fine_total, down_total, coarse_total, up_total = call(
+        functools.partial(finish_kernel, scale),
+        (total,),
+        [((27, C, C), F32), ((8, C, C), F32), ((27, C, C), F32), ((8, C, C), F32)],
+    )
     shape_out = (1, 1, number, C, VOX)
     return (
         output.reshape(shape_out),
         input_grad.reshape(shape_out),
-        fine_total.transpose(1, 3, 2, 0, 4).reshape(C, 27, C),
-        down_total.transpose(2, 0, 1, 3, 4).reshape(C, 8, C),
-        coarse_total.transpose(1, 3, 2, 0, 4).reshape(C, 27, C),
-        up_total.transpose(0, 1, 3, 4, 2).reshape(8, C, C),
+        fine_total.transpose(1, 0, 2),
+        down_total.transpose(1, 0, 2),
+        coarse_total.transpose(1, 0, 2),
+        up_total,
     )
 
 

time: 181 us -> 146 us (0.81)
  Pallas kernels: 103 us -> 77.7 us
  local copies, waits for them, and re-layouts: 21.1 us -> 7.11 us
  waiting for transfers between devices: 0.03 us -> 6.56 us
  blocking collectives: 24 us -> 21.8 us
    pallas_call x8 -> x9, Pallas kernels: 103 us -> 77.7 us  [call(): pl.pallas_call(kernel, out_shape=tuple((jax.ShapeDtypeStruct(s, d) for s,...]
    ppermute x10, waiting for transfers between devices: 0.03 us -> 6.56 us  [send(): return lax.ppermute(array, ('gx', 'gy'), pairs)]
    reshape x14 -> x0, local copies, waits for them, and re-layouts: 6.18 us -> none  [the longest x1 0.94 us: on_device(): fine_5[:, ::-1, ::-1, ::-1].transpose(3, 4, 2, 1, 0).reshape(3 * C, 9 * C)]
    rev x2 -> x0, local copies, waits for them, and re-layouts: 4.76 us -> none  [the longest x1 2.38 us: on_device(): fine_5[:, ::-1, ::-1, ::-1].transpose(3, 4, 2, 1, 0).reshape(3 * C, 9 * C)]
    transpose x4 -> x0, local copies, waits for them, and re-layouts: 2.58 us -> none  [the longest x1 0.88 us: on_device(): fine_total.transpose(1, 3, 2, 0, 4).reshape(C, 27, C)]
    all_to_all x1, blocking collectives: 24 us -> 21.8 us  [reduce_all(): mine = lax.all_to_all(joined.reshape(devices, share, LANES), axes, 0, 0)]
    unnamed x29 -> x30, local copies, waits for them, and re-layouts: 4.18 us -> 6.31 us
  transfers between devices with their start and end apart: 11 -> 11, of which waited for: 0 -> 1; matrix products, arithmetic and copies ran while one was open for 7% -> 0% of each run, Pallas kernels for 32% -> 30%
where the time goes in v3:
time: 146 us
  Pallas kernels  77.7 us (53%)
  starting transfers between devices  31 us (21%)
  blocking collectives  21.8 us (15%)
  local copies, waits for them, and re-layouts  7.11 us (5%)
  waiting for transfers between devices  6.56 us (4%)
  between operations  1.58 us (1%)
    pallas_call x9, Pallas kernels, call(): pl.pallas_call(kernel, out_shape=tuple((jax.ShapeDtypeStruct(s, d) for s,...  77.7 us
    ppermute x10, starting transfers between devices, send(): return lax.ppermute(array, ('gx', 'gy'), pairs)  28.4 us
    all_to_all x1, blocking collectives, reduce_all(): mine = lax.all_to_all(joined.reshape(devices, share, LANES), axes, 0, 0)  21.8 us
    ppermute x10, waiting for transfers between devices, send(): return lax.ppermute(array, ('gx', 'gy'), pairs)  6.56 us
    unnamed x30, local copies, waits for them, and re-layouts  6.31 us
  transfers between devices with their start and end apart: 11, of which 1 were waited for; matrix products, arithmetic and copies ran while one was open for 0% of the time, Pallas kernels for 30%

profile of v3, /device:TPU:0, one launch (start us, length us, event | category | flops | bytes accessed | tf_op | source)
XLA Modules:
  0.0 145.9 jit_solution(17550605306116588468)
XLA Ops:
  1.3 0.0 copy-start
  1.3 1.0 copy-done
  2.3 1.1 copy-done.1
  3.5 1.1 copy-done.2
  4.6 0.7 copy-done.3
  5.3 1.3 prepare_kernel.1
  6.6 2.4 %collective-permute-start = (bf16[3,48,512]{2,1,0:T(8,128)(2,1)S(1)}, bf16[3,48,512]{2,1,0:T(8,128)(2,1)S(1)}, u32[]{:S(2)}, u32[]{:S(2)}) collective-permute-start(bf16[3,48,512]{2,1,0:T(8,128)(2,1)S(1)} %get-tuple-element.49), channel_id=1, source_target_pairs={{0,1},{1,2},{2,3},{4,5},{5,6},{6,7},{8,9},{9,10},{10,11},{12,13},{... | collective-permute-start | bytes 442376 | tf_op jit(solution)/shard_map/ppermute | solution.py:549
  9.0 1.3 collective-permute-start.1
  10.3 4.2 %collective-permute-start.2 = (bf16[17,48,256]{2,1,0:T(8,128)(2,1)S(1)}, bf16[17,48,256]{2,1,0:T(8,128)(2,1)S(1)}, u32[]{:S(2)}, u32[]{:S(2)}) collective-permute-start(bf16[17,48,256]{2,1,0:T(8,128)(2,1)S(1)} %get-tuple-element.56), channel_id=1, source_target_pairs={{0,4},{1,5},{2,6},{3,7},{4,8},{5,9},{6,10},{7,11},{8,12},{9,13},{1... | collective-permute-start | bytes 1253384 | tf_op jit(solution)/shard_map/ppermute | solution.py:549
  14.5 1.3 collective-permute-start.3
  15.9 0.2 corner_kernel.1
  16.1 4.5 %collective-permute-start.4 = (bf16[3,48,256]{2,1,0:T(8,128)(2,1)S(1)}, bf16[3,48,256]{2,1,0:T(8,128)(2,1)S(1)}, u32[]{:S(2)}, u32[]{:S(2)}) collective-permute-start(bf16[3,48,256]{2,1,0:T(8,128)(2,1)S(1)} %get-tuple-element.58), channel_id=1, source_target_pairs={{0,4},{1,5},{2,6},{3,7},{4,8},{5,9},{6,10},{7,11},{8,12},{9,13},{1... | collective-permute-start | bytes 221192 | tf_op jit(solution)/shard_map/ppermute | solution.py:549
  20.7 1.3 collective-permute-start.5
  22.0 5.9 %place_kernel.1 = (bf16[144,48,128]{2,1,0:T(8,128)(2,1)S(1)}, bf16[144,48,128]{2,1,0:T(8,128)(2,1)S(1)}, f32[72,48,128]{2,1,0:T(8,128)S(1)}, f32[48,128]{1,0:T(8...) custom-call(bf16[16,48,512]{2,1,0:T(8,128)(2,1)S(1)} %get-tuple-elem, ...), custom_call_target="tpu_custom_call" | custom-call | flops 8000000000 | bytes 9192448 | tf_op jit(solution)/shard_map/place_kernel/pallas_call | solution.py:529
  27.9 0.7 copy-done.11
  28.6 6.5 %collective-permute-done.4.c_left = bf16[3,48,256]{2,1,0:T(8,128)(2,1)S(1)} collective-permute-done((bf16[3,48,256]{2,1,0:T(8,128)(2,1)S(1)}, bf16[3,48,256]{2,1,0:T(8,128)(2,1)S(1)}, u32[]{:S(2)}, u32[]{:S(2)}) %collective-permute-start.4) | collective-permute-done | bytes 73760 | tf_op jit(solution)/shard_map/ppermute | solution.py:549
  35.1 20.6 %forward_kernel.1 = (bf16[144,48,128]{2,1,0:T(8,128)(2,1)S(1)}, f32[144,48,128]{2,1,0:T(8,128)S(1)}, bf16[72,48,128]{2,1,0:T(8,128)(2,1)S(1)}, bf16[72,48,128]{2...) custom-call(bf16[144,48,128]{2,1,0:T(8,128)(2,1)S(1)} %get-tuple-ele, ...), custom_call_target="tpu_custom_call" | custom-call | flops 8000000000 | bytes 13941760 | tf_op jit(solution)/shard_map/forward_kernel/pallas_call | solution.py:529
  55.7 4.4 %collective-permute-start.6 = (bf16[3,48,128]{2,1,0:T(8,128)(2,1)S(1)}, bf16[3,48,128]{2,1,0:T(8,128)(2,1)S(1)}, u32[]{:S(2)}, u32[]{:S(2)}) collective-permute-start(bf16[3,48,128]{2,1,0:T(8,128)(2,1)S(1)} %get-tuple-element.71), channel_id=1, source_target_pairs={{0,4},{1,5},{2,6},{3,7},{4,8},{5,9},{6,10},{7,11},{8,12},{9,13},{1... | collective-permute-start | bytes 110600 | tf_op jit(solution)/shard_map/ppermute | solution.py:549
  60.1 1.3 collective-permute-start.7
  61.4 12.0 %side_kernel.1 = (bf16[16,48,512]{2,1,0:T(8,128)(2,1)}, bf16[768,128]{1,0:T(8,128)(2,1)S(1)}) custom-call(s32[16]{0:T(128)S(1)} %bitcast.24, f32[144,48,128]{2,1,0:T(8,128)S(1)} %get-tuple-element.63.hidden, bf16[72,48,128]{2,1,0:T(8,128)(2,1)S(1)} %get-tuple-element.64.rects, bf16[144,48,128]{2,1,0:T(8,128)(2,1)S(1)} %get-tuple-element.65.cot_grid, ...), custom_call_target="tpu_custom_call" | custom-call | flops 8000000000 | bytes 10055744 | tf_op jit(solution)/shard_map/side_kernel/pallas_call | solution.py:529
  73.4 10.6 %backward_kernel.1 = (bf16[144,48,128]{2,1,0:T(8,128)(2,1)S(1)}, bf16[72,48,128]{2,1,0:T(8,128)(2,1)S(1)}, bf16[9,48,128]{2,1,0:T(8,128)(2,1)S(1)}, bf16[9,48,128]{2,1,0:T(8,128)(2,1)S(1)}) custom-call(bf16[72,48,128]{2,1,0:T(8,128)(2,1)S(1)} %get-tuple-element.67.grad_c, bf16[3,48,128]{2,1,0:T(8,128)(2,1)S(1)} %collective-permute-done.6.from_left, ...), custom_call_target="tpu_custom_call" | custom-call | flops 8000000000 | bytes 9328128 | tf_op jit(solution)/shard_map/backward_kernel/pallas_call | solution.py:529
  84.0 6.4 %collective-permute-start.8 = (bf16[9,48,128]{2,1,0:T(8,128)(2,1)S(1)}, bf16[9,48,128]{2,1,0:T(8,128)(2,1)S(1)}, u32[]{:S(2)}, u32[]{:S(2)}) collective-permute-start(bf16[9,48,128]{2,1,0:T(8,128)(2,1)S(1)} %get-tuple-element.78), channel_id=1, source_target_pairs={{0,4},{1,5},{2,6},{3,7},{4,8},{5,9},{6,10},{7,11},{8,12},{9,13},{1... | collective-permute-start | bytes 331784 | tf_op jit(solution)/shard_map/ppermute | solution.py:549
  90.4 1.3 collective-permute-start.9
  91.7 12.0 %weight_kernel.1 = bf16[1536,128]{1,0:T(8,128)(2,1)S(1)} custom-call(bf16[144,48,128]{2,1,0:T(8,128)(2,1)S(1)} %get-tuple-element.75.grid, bf16[144,48,128]{2,1,0:T(8,128)(2,1)S(1)} %get-tuple-element.74.grad_h, bf16[72,48,128]{2,1,0:T(8,128)(2,1)S(1)} %get-tuple-element.76.grad_d, f32[144,48,128]{2,1,0:T(8,128)S(1)} %get-tuple-element.63.hidden, ...), custom_call_target="tpu_custom_call" | custom-call | flops 12000000000 | bytes 8552448 | tf_op jit(solution)/shard_map/weight_kernel/pallas_call | solution.py:529
  103.7 21.8 %all_to_all.10 = bf16[32,48,128]{2,1,0:T(8,128)(2,1)S(1)} all-to-all(bf16[32,48,128]{2,1,0:T(8,128)(2,1)S(1)} %bitcast.20), channel_id=1, replica_groups=mesh['gx'=8,'gy'=4] {'gx','gy'}, dimensions={0} | all-to-all | bytes 786432 | tf_op jit(solution)/shard_map/all_to_all | solution.py:558
  125.5 0.1 reduce_sum.12
  125.6 0.8 broadcast_in_dim.2
  126.4 2.6 %all-to-all-start.1 = ((bf16[32,48,128]{2,1,0:T(8,128)(2,1)}), bf16[32,48,128]{2,1,0:T(8,128)(2,1)S(1)}, u32[]{:S(2)}, u32[]{:S(2)}) async-start(bf16[32,48,128]{2,1,0:T(8,128)(2,1)} %broadcast_in_dim.2), calls=%async_computation.1 | async-start | bytes 786432 | tf_op jit(solution)/shard_map/all_to_all | solution.py:561
  129.0 0.9 copy-done.12
  129.9 13.7 %input_kernel.1 = bf16[16,48,512]{2,1,0:T(8,128)(2,1)} custom-call(s32[16]{0:T(128)S(1)} %bitcast.25, bf16[144,48,128]{2,1,0:T(8,128)(2,1)S(1)} %get-tuple-element.74.grad_h, bf16[9,48,128]{2,1,0:T(8,128)(2,1)S(1)} %collective-permute-done.8.from_left, bf16[9,48,128]{2,1,0:T(8,128)(2,1)S(1)} %collective-permute-done.9.from_right, ...), custom_call_target="tpu_custom_call" | custom-call | flops 8000000000 | bytes 3974720 | tf_op jit(solution)/shard_map/input_kernel/pallas_call | solution.py:529
  143.6 1.6 %finish_kernel.1 = (f32[27,48,48]{2,1,0:T(8,128)}, f32[8,48,48]{2,1,0:T(8,128)S(1)}, f32[27,48,48]{2,1,0:T(8,128)}, f32[8,48,48]{2,1,0:T(8,128)}) custom-call(bf16[1536,128]{1,0:T(8,128)(2,1)S(1)} %bitcast.17), custom_call_target="tpu_custom_call" | custom-call | bytes 1038336 | tf_op jit(solution)/shard_map/finish_kernel/pallas_call | solution.py:529
  145.2 0.7 copy.19
  (32 shorter events, 0.1 us)
Async XLA Ops:
  1.3 1.0 copy-start
  2.3 1.1 copy-start.1
  3.5 1.1 copy-start.2
  4.6 0.7 copy-start.3
  5.2 10.6 %copy-start.13 = (bf16[48,8,48]{2,1,0:T(8,128)(2,1)S(1)}, bf16[48,8,48]{2,1,0:T(8,128)(2,1)}, u32[]{:S(2)}) copy-start(bf16[48,8,48]{2,1,0:T(8,128)(2,1)} %param.17) | copy-start | bytes 110596
  5.2 16.7 %copy-start.5 = (bf16[48,27,48]{2,0,1:T(8,128)(2,1)S(1)}, bf16[48,27,48]{2,0,1:T(8,128)(2,1)}, u32[]{:S(2)}) copy-start(bf16[48,27,48]{2,0,1:T(8,128)(2,1)} %param.16) | copy-start | bytes 373252
  5.3 16.7 %copy-start.6 = (bf16[48,27,48]{2,0,1:T(8,128)(2,1)S(1)}, bf16[48,27,48]{2,0,1:T(8,128)(2,1)}, u32[]{:S(2)}) copy-start(bf16[48,27,48]{2,0,1:T(8,128)(2,1)} %param.18) | copy-start | bytes 373252
  5.3 16.7 %copy-start.7 = (bf16[8,48,48]{2,1,0:T(8,128)(2,1)S(1)}, bf16[8,48,48]{2,1,0:T(8,128)(2,1)}, u32[]{:S(2)}) copy-start(bf16[8,48,48]{2,1,0:T(8,128)(2,1)} %up.1) | copy-start | bytes 110596
  5.3 16.7 %copy-start.10 = (bf16[512,1024]{1,0:T(8,128)(2,1)S(1)}, bf16[512,1024]{1,0:T(8,128)(2,1)}, u32[]{:S(2)}) copy-start(bf16[512,1024]{1,0:T(8,128)(2,1)} %constant.12.clone.place) | copy-start | bytes 3145732
  6.6 9.3 %collective-permute-start = (bf16[3,48,512]{2,1,0:T(8,128)(2,1)S(1)}, bf16[3,48,512]{2,1,0:T(8,128)(2,1)S(1)}, u32[]{:S(2)}, u32[]{:S(2)}) collective-permute-start(bf16[3,48,512]{2,1,0:T(8,128)(2,1)S(1)} %get-tuple-element.49), channel_id=1, source_target_pairs={{0,1},{1,2},{2,3},{4,5},{5,6},{6,7},{8,9},{9,10},{10,11},{12,13},{... | collective-permute-start | bytes 442376 | tf_op jit(solution)/shard_map/ppermute | solution.py:549
  9.0 6.9 %collective-permute-start.1 = (bf16[3,48,512]{2,1,0:T(8,128)(2,1)S(1)}, bf16[3,48,512]{2,1,0:T(8,128)(2,1)S(1)}, u32[]{:S(2)}, u32[]{:S(2)}) collective-permute-start(bf16[3,48,512]{2,1,0:T(8,128)(2,1)S(1)} %get-tuple-element.50), channel_id=1, source_target_pairs={{1,0},{2,1},{3,2},{5,4},{6,5},{7,6},{9,8},{10,9},{11,10},{13,12},{... | collective-permute-start | bytes 442376 | tf_op jit(solution)/shard_map/ppermute | solution.py:549
  10.3 24.8 %collective-permute-start.2 = (bf16[17,48,256]{2,1,0:T(8,128)(2,1)S(1)}, bf16[17,48,256]{2,1,0:T(8,128)(2,1)S(1)}, u32[]{:S(2)}, u32[]{:S(2)}) collective-permute-start(bf16[17,48,256]{2,1,0:T(8,128)(2,1)S(1)} %get-tuple-element.56), channel_id=1, source_target_pairs={{0,4},{1,5},{2,6},{3,7},{4,8},{5,9},{6,10},{7,11},{8,12},{9,13},{1... | collective-permute-start | bytes 1253384 | tf_op jit(solution)/shard_map/ppermute | solution.py:549
  14.5 20.6 %collective-permute-start.3 = (bf16[17,48,256]{2,1,0:T(8,128)(2,1)S(1)}, bf16[17,48,256]{2,1,0:T(8,128)(2,1)S(1)}, u32[]{:S(2)}, u32[]{:S(2)}) collective-permute-start(bf16[17,48,256]{2,1,0:T(8,128)(2,1)S(1)} %get-tuple-element.57), channel_id=1, source_target_pairs={{4,0},{5,1},{6,2},{7,3},{8,4},{9,5},{10,6},{11,7},{12,8},{13,9},{1... | collective-permute-start | bytes 1253384 | tf_op jit(solution)/shard_map/ppermute | solution.py:549
  16.1 19.0 %collective-permute-start.4 = (bf16[3,48,256]{2,1,0:T(8,128)(2,1)S(1)}, bf16[3,48,256]{2,1,0:T(8,128)(2,1)S(1)}, u32[]{:S(2)}, u32[]{:S(2)}) collective-permute-start(bf16[3,48,256]{2,1,0:T(8,128)(2,1)S(1)} %get-tuple-element.58), channel_id=1, source_target_pairs={{0,4},{1,5},{2,6},{3,7},{4,8},{5,9},{6,10},{7,11},{8,12},{9,13},{1... | collective-permute-start | bytes 221192 | tf_op jit(solution)/shard_map/ppermute | solution.py:549
  20.7 14.4 %collective-permute-start.5 = (bf16[3,48,256]{2,1,0:T(8,128)(2,1)S(1)}, bf16[3,48,256]{2,1,0:T(8,128)(2,1)S(1)}, u32[]{:S(2)}, u32[]{:S(2)}) collective-permute-start(bf16[3,48,256]{2,1,0:T(8,128)(2,1)S(1)} %get-tuple-element.59), channel_id=1, source_target_pairs={{4,0},{5,1},{6,2},{7,3},{8,4},{9,5},{10,6},{11,7},{12,8},{13,9},{1... | collective-permute-start | bytes 221192 | tf_op jit(solution)/shard_map/ppermute | solution.py:549
  22.0 13.1 %copy-start.9 = (bf16[512,1024]{1,0:T(8,128)(2,1)S(1)}, bf16[512,1024]{1,0:T(8,128)(2,1)}, u32[]{:S(2)}) copy-start(bf16[512,1024]{1,0:T(8,128)(2,1)} %constant.13.clone.place) | copy-start | bytes 3145732
  27.9 0.7 copy-start.11
  35.1 26.3 %copy-start.4 = (s32[1,1,16]{2,1,0:T(1,128)S(1)}, s32[1,1,16]{2,1,0:T(1,128)}, u32[]{:S(2)}) copy-start(s32[1,1,16]{2,1,0:T(1,128)} %param.13) | copy-start | bytes 196
  35.1 26.3 %copy-start.8 = (bf16[1024,512]{1,0:T(8,128)(2,1)S(1)}, bf16[1024,512]{1,0:T(8,128)(2,1)}, u32[]{:S(2)}) copy-start(bf16[1024,512]{1,0:T(8,128)(2,1)} %constant.14.clone.place) | copy-start | bytes 3145732
  55.7 17.6 %collective-permute-start.6 = (bf16[3,48,128]{2,1,0:T(8,128)(2,1)S(1)}, bf16[3,48,128]{2,1,0:T(8,128)(2,1)S(1)}, u32[]{:S(2)}, u32[]{:S(2)}) collective-permute-start(bf16[3,48,128]{2,1,0:T(8,128)(2,1)S(1)} %get-tuple-element.71), channel_id=1, source_target_pairs={{0,4},{1,5},{2,6},{3,7},{4,8},{5,9},{6,10},{7,11},{8,12},{9,13},{1... | collective-permute-start | bytes 110600 | tf_op jit(solution)/shard_map/ppermute | solution.py:549
  60.1 13.3 %collective-permute-start.7 = (bf16[3,48,128]{2,1,0:T(8,128)(2,1)S(1)}, bf16[3,48,128]{2,1,0:T(8,128)(2,1)S(1)}, u32[]{:S(2)}, u32[]{:S(2)}) collective-permute-start(bf16[3,48,128]{2,1,0:T(8,128)(2,1)S(1)} %get-tuple-element.72), channel_id=1, source_target_pairs={{4,0},{5,1},{6,2},{7,3},{8,4},{9,5},{10,6},{11,7},{12,8},{13,9},{1... | collective-permute-start | bytes 110600 | tf_op jit(solution)/shard_map/ppermute | solution.py:549
  84.0 19.7 %collective-permute-start.8 = (bf16[9,48,128]{2,1,0:T(8,128)(2,1)S(1)}, bf16[9,48,128]{2,1,0:T(8,128)(2,1)S(1)}, u32[]{:S(2)}, u32[]{:S(2)}) collective-permute-start(bf16[9,48,128]{2,1,0:T(8,128)(2,1)S(1)} %get-tuple-element.78), channel_id=1, source_target_pairs={{0,4},{1,5},{2,6},{3,7},{4,8},{5,9},{6,10},{7,11},{8,12},{9,13},{1... | collective-permute-start | bytes 331784 | tf_op jit(solution)/shard_map/ppermute | solution.py:549
  90.4 13.3 %collective-permute-start.9 = (bf16[9,48,128]{2,1,0:T(8,128)(2,1)S(1)}, bf16[9,48,128]{2,1,0:T(8,128)(2,1)S(1)}, u32[]{:S(2)}, u32[]{:S(2)}) collective-permute-start(bf16[9,48,128]{2,1,0:T(8,128)(2,1)S(1)} %get-tuple-element.79), channel_id=1, source_target_pairs={{4,0},{5,1},{6,2},{7,3},{8,4},{9,5},{10,6},{11,7},{12,8},{13,9},{1... | collective-permute-start | bytes 331784 | tf_op jit(solution)/shard_map/ppermute | solution.py:549
  126.4 17.2 %all-to-all-start.1 = ((bf16[32,48,128]{2,1,0:T(8,128)(2,1)}), bf16[32,48,128]{2,1,0:T(8,128)(2,1)S(1)}, u32[]{:S(2)}, u32[]{:S(2)}) async-start(bf16[32,48,128]{2,1,0:T(8,128)(2,1)} %broadcast_in_dim.2), calls=%async_computation.1 | async-start | bytes 786432 | tf_op jit(solution)/shard_map/all_to_all | solution.py:561
  129.0 0.9 copy-start.12

commit v4 on v3

--- a/solution.py
+++ b/solution.py
@@ -100,22 +100,26 @@
 
 
 def prepare_kernel(
-    slots, count, feats, cots, pick, own, cot, flag_rows, x_low, x_high, y_low, y_high, rows_in
+    slots, count, pick, feats, cots, own, cot, flag_rows, x_low, x_high, y_low, y_high,
+    rows_in, feat_sems, cot_sems,
 ):
     number = feats.shape[0]
+    copies = []
+    for source, target, sems in ((feats, own, feat_sems), (cots, cot, cot_sems)):
+        group = []
+        for slot in range(number):
+            copy = pltpu.make_async_copy(source.at[slot], target.at[slots[slot]], sems.at[slot])
+            copy.start()
+            group.append(copy)
+        copies.append(group)
     rows = lax.broadcasted_iota(jnp.int32, (C, VOX), 0)
     flags = jnp.zeros((C, VOX), F32)
     first = jnp.zeros((), F32)
     last = jnp.zeros((), F32)
     zero = jnp.zeros((C, VOX), BF16)
     for slot in range(number):
-        live = slot < count[0]
-        alive = jnp.where(live, 1.0, 0.0)
+        alive = jnp.where(slot < count[0], 1.0, 0.0)
         place = slots[slot]
-        block = jnp.where(live, feats[slot], zero)
-        own[place] = block
-        rows_in[pl.ds(pl.multiple_of(place * C, 16), C), :] = block
-        cot[place] = jnp.where(live, cots[slot], zero)
         flags = jnp.where(rows == place + 1, alive, flags)
         first = first + jnp.where(place == 0, alive, 0.0)
         last = last + jnp.where(place == number - 1, alive, 0.0)
@@ -123,6 +127,17 @@
     rows_in[number * C :, :] = flags.astype(BF16)
     first_flag = jnp.where(rows == number + 1, first, 0.0).astype(BF16)
     last_flag = jnp.where(rows == 0, last, 0.0).astype(BF16)
+    for target, group in ((own, copies[0]), (cot, copies[1])):
+        for slot in range(number):
+            group[slot].wait()
+        for slot in range(number):
+
+            @pl.when(slot >= count[0])
+            def _():
+                target[slots[slot]] = zero
+
+    for block in range(number):
+        rows_in[block * C : (block + 1) * C, :] = own[block]
     packed = dot(rows_in[...], pick[...]).astype(BF16)
     packed = packed.reshape(number + 1, C, VOX)
     x_low[...] = packed[:, :, :256]
@@ -315,7 +330,7 @@
 
 
 def flatten_weights(total, out, at):
-    turned = total[...].T.astype(BF16)
+    turned = total[...].T
     for group in range(4):
         out[at + 3 * C * group : at + 3 * C * (group + 1), :] = turned[
             :, LANES * group : LANES * (group + 1)
@@ -373,7 +388,7 @@
 
     loop(0, (coarse_tiles - 4) // 4, weight_step)
     flatten_weights(coarse_g, flat, 0)
-    flat[12 * C :, :] = up_g[...].astype(BF16)
+    flat[12 * C :, :] = up_g[...]
 
 
 def backward_kernel(
@@ -425,7 +440,7 @@
         loop(0, out.shape[0], pack_step)
 
 
-def weight_kernel(grid, grad_h, grad_d, hidden, early, joined, grad_own, fine_g, down_g):
+def weight_kernel(grid, grad_h, grad_d, hidden, flat, grad_own, fine_g, down_g):
     tiles = grid.shape[0]
     coarse_tiles = grad_d.shape[0]
     fine_g[...] = jnp.zeros_like(fine_g)
@@ -463,9 +478,8 @@
         )
 
     loop(0, (coarse_tiles - 8) // 4, down_step, 2)
-    flatten_weights(fine_g, joined, 0)
-    joined[12 * C : 16 * C, :] = down_g[...].astype(BF16)
-    joined[16 * C :, :] = early[...]
+    flatten_weights(fine_g, flat, 0)
+    flat[12 * C :, :] = down_g[...]
 
 
 def input_kernel(
@@ -501,27 +515,32 @@
     to_blocks(slots, rows_out, place, out)
 
 
-def finish_kernel(scale, total, fine, down, coarse, up):
-    for out, at in ((fine, 0), (coarse, 16 * C)):
+def finish_kernel(scale, late, early, fine, down, coarse, up):
+    for out, total in ((fine, late), (coarse, early)):
         for along in range(3):
-            first = at + C * along
+            first = C * along
             rows = [total[first + 3 * C * g : first + 3 * C * g + C, :] for g in range(4)]
-            row = jnp.concatenate(rows, axis=1).astype(F32) * scale
+            row = jnp.concatenate(rows, axis=1) * scale
             for index in range(9):
                 out[9 * (index % 3) + 3 * (index // 3) + along] = row[:, C * index : C * (index + 1)]
-    for out, at, turn in ((down, 12 * C, False), (up, 28 * C, True)):
+    for out, total, turn in ((down, late, False), (up, early, True)):
         for index in range(4):
-            rows = total[at + C * index : at + C * (index + 1), :].astype(F32) * scale
+            rows = total[C * (12 + index) : C * (13 + index), :] * scale
             for along in range(2):
                 part = rows[:, C * along : C * (along + 1)]
                 out[2 * index + along] = part.T if turn else part
 
 
-def call(kernel, inputs, outs, scratch=(), scalars=0, flops=0):
+def call(kernel, inputs, outs, scratch=(), scalars=0, flops=0, far=0):
     vmem = pl.BlockSpec(memory_space=pltpu.VMEM)
     smem = pl.BlockSpec(memory_space=pltpu.SMEM)
+    far_space = pl.BlockSpec(memory_space=pltpu.HBM)
+    near = len(inputs) - scalars - far
+    sems = [number for number in scratch if isinstance(number, int)]
+    scratch = [entry for entry in scratch if not isinstance(entry, int)]
     held = SLACK
-    for shape, kind in [(a.shape, a.dtype) for a in inputs[scalars:]] + list(outs) + list(scratch):
+    near_kinds = [(a.shape, a.dtype) for a in inputs[scalars : scalars + near]]
+    for shape, kind in near_kinds + list(outs) + scratch:
         rows, lanes = -(-shape[-2] // 16) * 16, -(-shape[-1] // LANES) * LANES
         held += math.prod(shape[:-2]) * rows * lanes * jnp.dtype(kind).itemsize
     moved = sum(math.prod(s) * jnp.dtype(d).itemsize for s, d in outs)
@@ -529,9 +548,10 @@
     return pl.pallas_call(
         kernel,
         out_shape=tuple(jax.ShapeDtypeStruct(s, d) for s, d in outs),
-        in_specs=[smem] * scalars + [vmem] * (len(inputs) - scalars),
+        in_specs=[smem] * scalars + [vmem] * near + [far_space] * far,
         out_specs=tuple(vmem for _ in outs),
-        scratch_shapes=[pltpu.VMEM(s, d) for s, d in scratch],
+        scratch_shapes=[pltpu.VMEM(s, d) for s, d in scratch]
+        + [pltpu.SemaphoreType.DMA((number,)) for number in sems],
         compiler_params=pltpu.CompilerParams(vmem_limit_bytes=held),
         cost_estimate=pl.CostEstimate(flops=flops, bytes_accessed=moved, transcendentals=0),
         name=getattr(kernel, "func", kernel).__name__,
@@ -549,17 +569,8 @@
     return lax.ppermute(array, ("gx", "gy"), pairs)
 
 
-def reduce_all(joined):
-    axes = ("gx", "gy")
-    devices = lax.axis_size("gx") * lax.axis_size("gy")
-    rows = joined.shape[0]
-    share = -(-rows // devices)
-    joined = jnp.pad(joined, ((0, share * devices - rows), (0, 0)))
-    mine = lax.all_to_all(joined.reshape(devices, share, LANES), axes, 0, 0)
-    mine = jnp.sum(mine.astype(F32), axis=0).astype(BF16)
-    spread = jnp.broadcast_to(mine[None], (devices, share, LANES))
-    full = lax.all_to_all(spread, axes, 0, 0)
-    return full.reshape(devices * share, LANES)[:rows]
+def reduce_all(part):
+    return lax.psum(lax.psum(part, "gx"), "gy")
 
 
 def on_device(
@@ -585,13 +596,14 @@
     )
     own, cot, flag_rows, x_low, x_high, y_low, y_high = call(
         prepare_kernel,
-        (slots, count, feats, cots, pick),
+        (slots, count, pick, feats, cots),
         [((number, C, VOX), BF16)] * 2
         + [((C, VOX), BF16)]
         + [((number + 1, C, 256), BF16)] * 2
         + [((3, C, VOX), BF16)] * 2,
-        [(((number + 1) * C, VOX), BF16)],
+        [(((number + 1) * C, VOX), BF16), number, number],
         scalars=2,
+        far=2,
     )
     x_left = send(x_high, 1, 0)
     x_right = send(x_low, -1, 0)
@@ -645,7 +657,7 @@
     output, early = call(
         side_kernel,
         (slots, hidden, rects, cot_grid, lowered, grad_c, live, place_back, up_w),
-        [((number, C, VOX), BF16), ((16 * C, LANES), BF16)],
+        [((number, C, VOX), BF16), ((16 * C, LANES), F32)],
         [
             ((number * C, 1024), BF16),
             ((coarse_tiles, C, LANES), BF16),
@@ -655,6 +667,7 @@
         scalars=1,
         flops=8 * 10**9,
     )
+    early_sum = reduce_all(early)
     grad_h, grad_d, edge_low, edge_high = call(
         backward_kernel,
         (grad_c, grad_left, grad_right, hidden, cot_grid, live, coarse_back, down_w),
@@ -669,15 +682,15 @@
     )
     edge_left = send(edge_high, 1, 0)
     edge_right = send(edge_low, -1, 0)
-    (joined,) = call(
+    (late,) = call(
         weight_kernel,
-        (grid, grad_h, grad_d, hidden, early),
-        [((32 * C, LANES), BF16)],
+        (grid, grad_h, grad_d, hidden),
+        [((16 * C, LANES), F32)],
         [((tiles, C, LANES), BF16), ((VOX, 3 * C), F32), ((4 * C, LANES), F32)],
         flops=12 * 10**9,
     )
-    joined, edge_left, edge_right = lax.optimization_barrier((joined, edge_left, edge_right))
-    total = reduce_all(joined)
+    late, edge_left, edge_right = lax.optimization_barrier((late, edge_left, edge_right))
+    late_sum = reduce_all(late)
     (input_grad,) = call(
         input_kernel,
         (slots, grad_h, edge_left, edge_right, live, place_back, fine_back),
@@ -693,7 +706,7 @@
     scale = 1.0 / math.sqrt(number * VOX * lax.axis_size("gx") * lax.axis_size("gy"))
     fine_total, down_total, coarse_total, up_total = call(
         functools.partial(finish_kernel, scale),
-        (total,),
+        (late_sum, early_sum),
         [((27, C, C), F32), ((8, C, C), F32), ((27, C, C), F32), ((8, C, C), F32)],
     )
     shape_out = (1, 1, number, C, VOX)

time: 146 us -> 241 us (1.65)
  waiting for transfers between devices: 6.56 us -> 109 us
  blocking collectives: 21.8 us -> 0 us
  between operations: 1.58 us -> 14.9 us
  Pallas kernels: 77.7 us -> 81.7 us
    psum x0 -> x2, waiting for transfers between devices: none -> 102 us  [reduce_all(): return lax.psum(lax.psum(part, 'gx'), 'gy')]
    all_to_all x1 -> x0, blocking collectives: 21.8 us -> none  [reduce_all(): mine = lax.all_to_all(joined.reshape(devices, share, LANES), axes, 0, 0)]
    pallas_call x9, Pallas kernels: 77.7 us -> 81.7 us  [call(): pl.pallas_call(kernel, out_shape=tuple((jax.ShapeDtypeStruct(s, d) for s,...]
    all_to_all x1 -> x0, starting transfers between devices: 2.64 us -> none  [reduce_all(): full = lax.all_to_all(spread, axes, 0, 0)]
  transfers between devices with their start and end apart: 11 -> 12, of which waited for: 1 -> 3; matrix products, arithmetic and copies ran while one was open for 0% -> 0% of each run, Pallas kernels for 30% -> 19%
where the time goes in v4:
time: 241 us
  waiting for transfers between devices  109 us (45%)
  Pallas kernels  81.7 us (34%)
  starting transfers between devices  28.6 us (12%)
  between operations  14.9 us (6%)
  local copies, waits for them, and re-layouts  6.74 us (3%)
    psum x2, waiting for transfers between devices, reduce_all(): return lax.psum(lax.psum(part, 'gx'), 'gy')  102 us
    pallas_call x9, Pallas kernels, call(): pl.pallas_call(kernel, out_shape=tuple((jax.ShapeDtypeStruct(s, d) for s,...  81.7 us
    ppermute x10, starting transfers between devices, send(): return lax.ppermute(array, ('gx', 'gy'), pairs)  28.5 us
    ppermute x10, waiting for transfers between devices, send(): return lax.ppermute(array, ('gx', 'gy'), pairs)  7.17 us
    unnamed x30, local copies, waits for them, and re-layouts  6.74 us
  transfers between devices with their start and end apart: 12, of which 3 were waited for; matrix products, arithmetic and copies ran while one was open for 0% of the time, Pallas kernels for 19%

profile of v4, /device:TPU:0, one launch (start us, length us, event | category | flops | bytes accessed | tf_op | source)
XLA Modules:
  0.0 240.8 jit_solution(9950179305465394874)
XLA Ops:
  7.2 0.0 all-reduce.5.cloned.1.call-start
  7.9 1.0 copy-done
  8.9 1.1 copy-done.1
  10.0 1.1 copy-done.2
  11.2 0.7 copy-done.5
  11.9 4.0 %prepare_kernel.1 = (bf16[16,48,512]{2,1,0:T(8,128)(2,1)S(1)}, bf16[16,48,512]{2,1,0:T(8,128)(2,1)S(1)}, bf16[48,512]{1,0:T(8,128)(2,1)S(1)}, bf16[17,48,256]{2,...) custom-call(s32[16]{0:T(128)S(1)} %bitcast.19, ...), custom_call_target="tpu_custom_call" | custom-call | bytes 4849732 | tf_op jit(solution)/shard_map/prepare_kernel/pallas_call | solution.py:548
  15.9 2.3 collective-permute-start
  18.2 1.3 collective-permute-start.1
  19.5 4.2 %collective-permute-start.2 = (bf16[17,48,256]{2,1,0:T(8,128)(2,1)S(1)}, bf16[17,48,256]{2,1,0:T(8,128)(2,1)S(1)}, u32[]{:S(2)}, u32[]{:S(2)}) collective-permute-start(bf16[17,48,256]{2,1,0:T(8,128)(2,1)S(1)} %get-tuple-element.56), channel_id=1, source_target_pairs={{0,4},{1,5},{2,6},{3,7},{4,8},{5,9},{6,10},{7,11},{8,12},{9,13},{1... | collective-permute-start | bytes 1253384 | tf_op jit(solution)/shard_map/ppermute | solution.py:569
  23.8 1.3 collective-permute-start.3
  25.1 0.2 corner_kernel.1
  25.4 4.5 %collective-permute-start.4 = (bf16[3,48,256]{2,1,0:T(8,128)(2,1)S(1)}, bf16[3,48,256]{2,1,0:T(8,128)(2,1)S(1)}, u32[]{:S(2)}, u32[]{:S(2)}) collective-permute-start(bf16[3,48,256]{2,1,0:T(8,128)(2,1)S(1)} %get-tuple-element.58), channel_id=1, source_target_pairs={{0,4},{1,5},{2,6},{3,7},{4,8},{5,9},{6,10},{7,11},{8,12},{9,13},{1... | collective-permute-start | bytes 221192 | tf_op jit(solution)/shard_map/ppermute | solution.py:569
  29.9 1.3 collective-permute-start.5
  31.3 5.9 %place_kernel.1 = (bf16[144,48,128]{2,1,0:T(8,128)(2,1)S(1)}, bf16[144,48,128]{2,1,0:T(8,128)(2,1)S(1)}, f32[72,48,128]{2,1,0:T(8,128)S(1)}, f32[48,128]{1,0:T(8...) custom-call(bf16[16,48,512]{2,1,0:T(8,128)(2,1)S(1)} %get-tuple-elem, ...), custom_call_target="tpu_custom_call" | custom-call | flops 8000000000 | bytes 9192448 | tf_op jit(solution)/shard_map/place_kernel/pallas_call | solution.py:548
  37.2 7.1 %collective-permute-done.4.c_left = bf16[3,48,256]{2,1,0:T(8,128)(2,1)S(1)} collective-permute-done((bf16[3,48,256]{2,1,0:T(8,128)(2,1)S(1)}, bf16[3,48,256]{2,1,0:T(8,128)(2,1)S(1)}, u32[]{:S(2)}, u32[]{:S(2)}) %collective-permute-start.4) | collective-permute-done | bytes 73760 | tf_op jit(solution)/shard_map/ppermute | solution.py:569
  44.3 20.6 %forward_kernel.1 = (bf16[144,48,128]{2,1,0:T(8,128)(2,1)S(1)}, f32[144,48,128]{2,1,0:T(8,128)S(1)}, bf16[72,48,128]{2,1,0:T(8,128)(2,1)S(1)}, bf16[72,48,128]{2...) custom-call(bf16[144,48,128]{2,1,0:T(8,128)(2,1)S(1)} %get-tuple-ele, ...), custom_call_target="tpu_custom_call" | custom-call | flops 8000000000 | bytes 13941760 | tf_op jit(solution)/shard_map/forward_kernel/pallas_call | solution.py:548
  65.0 4.4 %collective-permute-start.6 = (bf16[3,48,128]{2,1,0:T(8,128)(2,1)S(1)}, bf16[3,48,128]{2,1,0:T(8,128)(2,1)S(1)}, u32[]{:S(2)}, u32[]{:S(2)}) collective-permute-start(bf16[3,48,128]{2,1,0:T(8,128)(2,1)S(1)} %get-tuple-element.71), channel_id=1, source_target_pairs={{0,4},{1,5},{2,6},{3,7},{4,8},{5,9},{6,10},{7,11},{8,12},{9,13},{1... | collective-permute-start | bytes 110600 | tf_op jit(solution)/shard_map/ppermute | solution.py:569
  69.4 1.3 collective-permute-start.7
  70.7 12.4 %side_kernel.1 = (bf16[16,48,512]{2,1,0:T(8,128)(2,1)}, f32[768,128]{1,0:T(8,128)}) custom-call(s32[16]{0:T(128)S(1)} %bitcast.20, f32[144,48,128]{2,1,0:T(8,128)S(1)} %get-tuple-element.63.hidden, bf16[72,48,128]{2,1,0:T(8,128)(2,1)S(1)} %get-tuple-element.64.rects, bf16[144,48,128]{2,1,0:T(8,128)(2,1)S(1)} %get-tuple-element.65.cot_grid, ...), custom_call_target="tpu_custom_call" | custom-call | flops 8000000000 | bytes 10252352 | tf_op jit(solution)/shard_map/side_kernel/pallas_call | solution.py:548
  83.1 10.5 %backward_kernel.1 = (bf16[144,48,128]{2,1,0:T(8,128)(2,1)S(1)}, bf16[72,48,128]{2,1,0:T(8,128)(2,1)S(1)}, bf16[9,48,128]{2,1,0:T(8,128)(2,1)S(1)}, bf16[9,48,128]{2,1,0:T(8,128)(2,1)S(1)}) custom-call(bf16[72,48,128]{2,1,0:T(8,128)(2,1)S(1)} %get-tuple-element.67.grad_c, bf16[3,48,128]{2,1,0:T(8,128)(2,1)S(1)} %collective-permute-done.6.from_left, ...), custom_call_target="tpu_custom_call" | custom-call | flops 8000000000 | bytes 9328128 | tf_op jit(solution)/shard_map/backward_kernel/pallas_call | solution.py:548
  93.7 6.5 %collective-permute-start.8 = (bf16[9,48,128]{2,1,0:T(8,128)(2,1)S(1)}, bf16[9,48,128]{2,1,0:T(8,128)(2,1)S(1)}, u32[]{:S(2)}, u32[]{:S(2)}) collective-permute-start(bf16[9,48,128]{2,1,0:T(8,128)(2,1)S(1)} %get-tuple-element.77), channel_id=1, source_target_pairs={{0,4},{1,5},{2,6},{3,7},{4,8},{5,9},{6,10},{7,11},{8,12},{9,13},{1... | collective-permute-start | bytes 331784 | tf_op jit(solution)/shard_map/ppermute | solution.py:569
  100.2 1.3 collective-permute-start.9
  101.5 12.8 %weight_kernel.1 = f32[768,128]{1,0:T(8,128)} custom-call(bf16[144,48,128]{2,1,0:T(8,128)(2,1)S(1)} %get-tuple-element.75.grid, bf16[144,48,128]{2,1,0:T(8,128)(2,1)S(1)} %get-tuple-element.74.grad_h, bf16[72,48,128]{2,1,0:T(8,128)(2,1)S(1)} %get-tuple-element.76.grad_d, f32[144,48,128]{2,1,0:T(8,128)S(1)} %get-tuple-element.63.hidden), custom_call_target="tpu_custom_call" | custom-call | flops 12000000000 | bytes 8355840 | tf_op jit(solution)/shard_map/weight_kernel/pallas_call | solution.py:548
  114.3 0.0 all-reduce.5.cloned.1.call-update
  114.3 0.0 all-reduce.7.cloned.1.call-start
  114.4 79.0 %all-reduce.5.cloned.1.call-done = (f32[768,128]{1,0:T(8,128)}, f32[768,128]{1,0:T(8,128)}) async-done(((f32[768,128]{1,0:T(8,128)}, f32[768,128]{1,0:T(8,128)}), (f32[768,128]{1,0:T(8,128)}, f32[768,128]{1,0:T(8,128)})) %all-reduce.5.cloned.1.call-update) | async-done | bytes 786448 | tf_op jit(solution)/shard_map/psum | solution.py:573
  193.4 13.6 %input_kernel.1 = bf16[16,48,512]{2,1,0:T(8,128)(2,1)} custom-call(s32[16]{0:T(128)S(1)} %bitcast.21, bf16[144,48,128]{2,1,0:T(8,128)(2,1)S(1)} %get-tuple-element.74.grad_h, bf16[9,48,128]{2,1,0:T(8,128)(2,1)S(1)} %collective-permute-done.8.from_left, bf16[9,48,128]{2,1,0:T(8,128)(2,1)S(1)} %collective-permute-done.9.from_right, ...), custom_call_target="tpu_custom_call" | custom-call | flops 8000000000 | bytes 3974720 | tf_op jit(solution)/shard_map/input_kernel/pallas_call | solution.py:548
  207.0 22.6 %all-reduce.7.cloned.1.call-done = (f32[768,128]{1,0:T(8,128)}, f32[768,128]{1,0:T(8,128)}) async-done(((f32[768,128]{1,0:T(8,128)}, f32[768,128]{1,0:T(8,128)}), (f32[768,128]{1,0:T(8,128)}, f32[768,128]{1,0:T(8,128)})) %all-reduce.7.cloned.1.call-update) | async-done | bytes 786448 | tf_op jit(solution)/shard_map/psum | solution.py:573
  229.6 1.0 copy-done.3
  230.6 1.0 copy-done.4
  231.6 1.6 finish_kernel.1
  233.2 0.7 copy.19
  (33 shorter events, 0.1 us)
Async XLA Ops:
  7.2 186.2 %all-reduce.5.cloned.1.call-start = ((), (), s32[]{:S(2)}) async-start(), calls=%async_computation | async-start | bytes 1572864 | tf_op jit(solution)/shard_map/psum | solution.py:573
  7.9 1.0 copy-start
  8.9 1.1 copy-start.1
  10.0 1.1 copy-start.2
  11.2 0.7 copy-start.5
  11.8 13.2 %copy-start.13 = (bf16[48,8,48]{2,1,0:T(8,128)(2,1)S(1)}, bf16[48,8,48]{2,1,0:T(8,128)(2,1)}, u32[]{:S(2)}) copy-start(bf16[48,8,48]{2,1,0:T(8,128)(2,1)} %param.17) | copy-start | bytes 110596
  11.8 19.4 %copy-start.7 = (bf16[48,27,48]{2,0,1:T(8,128)(2,1)S(1)}, bf16[48,27,48]{2,0,1:T(8,128)(2,1)}, u32[]{:S(2)}) copy-start(bf16[48,27,48]{2,0,1:T(8,128)(2,1)} %param.16) | copy-start | bytes 373252
  11.8 19.4 %copy-start.8 = (bf16[48,27,48]{2,0,1:T(8,128)(2,1)S(1)}, bf16[48,27,48]{2,0,1:T(8,128)(2,1)}, u32[]{:S(2)}) copy-start(bf16[48,27,48]{2,0,1:T(8,128)(2,1)} %param.18) | copy-start | bytes 373252
  11.8 19.4 %copy-start.9 = (bf16[8,48,48]{2,1,0:T(8,128)(2,1)S(1)}, bf16[8,48,48]{2,1,0:T(8,128)(2,1)}, u32[]{:S(2)}) copy-start(bf16[8,48,48]{2,1,0:T(8,128)(2,1)} %up.1) | copy-start | bytes 110596
  11.8 19.4 %copy-start.12 = (bf16[512,1024]{1,0:T(8,128)(2,1)S(1)}, bf16[512,1024]{1,0:T(8,128)(2,1)}, u32[]{:S(2)}) copy-start(bf16[512,1024]{1,0:T(8,128)(2,1)} %constant.8.clone.place) | copy-start | bytes 3145732
  15.9 9.2 %collective-permute-start = (bf16[3,48,512]{2,1,0:T(8,128)(2,1)S(1)}, bf16[3,48,512]{2,1,0:T(8,128)(2,1)S(1)}, u32[]{:S(2)}, u32[]{:S(2)}) collective-permute-start(bf16[3,48,512]{2,1,0:T(8,128)(2,1)S(1)} %get-tuple-element.49), channel_id=1, source_target_pairs={{0,1},{1,2},{2,3},{4,5},{5,6},{6,7},{8,9},{9,10},{10,11},{12,13},{... | collective-permute-start | bytes 442376 | tf_op jit(solution)/shard_map/ppermute | solution.py:569
  18.2 6.9 %collective-permute-start.1 = (bf16[3,48,512]{2,1,0:T(8,128)(2,1)S(1)}, bf16[3,48,512]{2,1,0:T(8,128)(2,1)S(1)}, u32[]{:S(2)}, u32[]{:S(2)}) collective-permute-start(bf16[3,48,512]{2,1,0:T(8,128)(2,1)S(1)} %get-tuple-element.50), channel_id=1, source_target_pairs={{1,0},{2,1},{3,2},{5,4},{6,5},{7,6},{9,8},{10,9},{11,10},{13,12},{... | collective-permute-start | bytes 442376 | tf_op jit(solution)/shard_map/ppermute | solution.py:569
  19.5 24.8 %collective-permute-start.2 = (bf16[17,48,256]{2,1,0:T(8,128)(2,1)S(1)}, bf16[17,48,256]{2,1,0:T(8,128)(2,1)S(1)}, u32[]{:S(2)}, u32[]{:S(2)}) collective-permute-start(bf16[17,48,256]{2,1,0:T(8,128)(2,1)S(1)} %get-tuple-element.56), channel_id=1, source_target_pairs={{0,4},{1,5},{2,6},{3,7},{4,8},{5,9},{6,10},{7,11},{8,12},{9,13},{1... | collective-permute-start | bytes 1253384 | tf_op jit(solution)/shard_map/ppermute | solution.py:569
  23.8 20.5 %collective-permute-start.3 = (bf16[17,48,256]{2,1,0:T(8,128)(2,1)S(1)}, bf16[17,48,256]{2,1,0:T(8,128)(2,1)S(1)}, u32[]{:S(2)}, u32[]{:S(2)}) collective-permute-start(bf16[17,48,256]{2,1,0:T(8,128)(2,1)S(1)} %get-tuple-element.57), channel_id=1, source_target_pairs={{4,0},{5,1},{6,2},{7,3},{8,4},{9,5},{10,6},{11,7},{12,8},{13,9},{1... | collective-permute-start | bytes 1253384 | tf_op jit(solution)/shard_map/ppermute | solution.py:569
  25.4 18.9 %collective-permute-start.4 = (bf16[3,48,256]{2,1,0:T(8,128)(2,1)S(1)}, bf16[3,48,256]{2,1,0:T(8,128)(2,1)S(1)}, u32[]{:S(2)}, u32[]{:S(2)}) collective-permute-start(bf16[3,48,256]{2,1,0:T(8,128)(2,1)S(1)} %get-tuple-element.58), channel_id=1, source_target_pairs={{0,4},{1,5},{2,6},{3,7},{4,8},{5,9},{6,10},{7,11},{8,12},{9,13},{1... | collective-permute-start | bytes 221192 | tf_op jit(solution)/shard_map/ppermute | solution.py:569
  29.9 14.4 %collective-permute-start.5 = (bf16[3,48,256]{2,1,0:T(8,128)(2,1)S(1)}, bf16[3,48,256]{2,1,0:T(8,128)(2,1)S(1)}, u32[]{:S(2)}, u32[]{:S(2)}) collective-permute-start(bf16[3,48,256]{2,1,0:T(8,128)(2,1)S(1)} %get-tuple-element.59), channel_id=1, source_target_pairs={{4,0},{5,1},{6,2},{7,3},{8,4},{9,5},{10,6},{11,7},{12,8},{13,9},{1... | collective-permute-start | bytes 221192 | tf_op jit(solution)/shard_map/ppermute | solution.py:569
  31.3 13.0 %copy-start.11 = (bf16[512,1024]{1,0:T(8,128)(2,1)S(1)}, bf16[512,1024]{1,0:T(8,128)(2,1)}, u32[]{:S(2)}) copy-start(bf16[512,1024]{1,0:T(8,128)(2,1)} %constant.9.clone.place) | copy-start | bytes 3145732
  44.3 26.3 %copy-start.6 = (s32[1,1,16]{2,1,0:T(1,128)S(1)}, s32[1,1,16]{2,1,0:T(1,128)}, u32[]{:S(2)}) copy-start(s32[1,1,16]{2,1,0:T(1,128)} %param.13) | copy-start | bytes 196
  44.3 26.3 %copy-start.10 = (bf16[1024,512]{1,0:T(8,128)(2,1)S(1)}, bf16[1024,512]{1,0:T(8,128)(2,1)}, u32[]{:S(2)}) copy-start(bf16[1024,512]{1,0:T(8,128)(2,1)} %constant.10.clone.place) | copy-start | bytes 3145732
  65.0 18.2 %collective-permute-start.6 = (bf16[3,48,128]{2,1,0:T(8,128)(2,1)S(1)}, bf16[3,48,128]{2,1,0:T(8,128)(2,1)S(1)}, u32[]{:S(2)}, u32[]{:S(2)}) collective-permute-start(bf16[3,48,128]{2,1,0:T(8,128)(2,1)S(1)} %get-tuple-element.71), channel_id=1, source_target_pairs={{0,4},{1,5},{2,6},{3,7},{4,8},{5,9},{6,10},{7,11},{8,12},{9,13},{1... | collective-permute-start | bytes 110600 | tf_op jit(solution)/shard_map/ppermute | solution.py:569
  69.4 13.8 %collective-permute-start.7 = (bf16[3,48,128]{2,1,0:T(8,128)(2,1)S(1)}, bf16[3,48,128]{2,1,0:T(8,128)(2,1)S(1)}, u32[]{:S(2)}, u32[]{:S(2)}) collective-permute-start(bf16[3,48,128]{2,1,0:T(8,128)(2,1)S(1)} %get-tuple-element.72), channel_id=1, source_target_pairs={{4,0},{5,1},{6,2},{7,3},{8,4},{9,5},{10,6},{11,7},{12,8},{13,9},{1... | collective-permute-start | bytes 110600 | tf_op jit(solution)/shard_map/ppermute | solution.py:569
  93.7 20.6 %collective-permute-start.8 = (bf16[9,48,128]{2,1,0:T(8,128)(2,1)S(1)}, bf16[9,48,128]{2,1,0:T(8,128)(2,1)S(1)}, u32[]{:S(2)}, u32[]{:S(2)}) collective-permute-start(bf16[9,48,128]{2,1,0:T(8,128)(2,1)S(1)} %get-tuple-element.77), channel_id=1, source_target_pairs={{0,4},{1,5},{2,6},{3,7},{4,8},{5,9},{6,10},{7,11},{8,12},{9,13},{1... | collective-permute-start | bytes 331784 | tf_op jit(solution)/shard_map/ppermute | solution.py:569
  100.2 14.1 %collective-permute-start.9 = (bf16[9,48,128]{2,1,0:T(8,128)(2,1)S(1)}, bf16[9,48,128]{2,1,0:T(8,128)(2,1)S(1)}, u32[]{:S(2)}, u32[]{:S(2)}) collective-permute-start(bf16[9,48,128]{2,1,0:T(8,128)(2,1)S(1)} %get-tuple-element.78), channel_id=1, source_target_pairs={{4,0},{5,1},{6,2},{7,3},{8,4},{9,5},{10,6},{11,7},{12,8},{13,9},{1... | collective-permute-start | bytes 331784 | tf_op jit(solution)/shard_map/ppermute | solution.py:569
  114.3 115.3 %all-reduce.7.cloned.1.call-start = ((), (), s32[]{:S(2)}) async-start(), calls=%async_computation.1 | async-start | bytes 1572864 | tf_op jit(solution)/shard_map/psum | solution.py:573
  229.6 1.0 copy-start.3
  230.6 1.0 copy-start.4
Sparse Core Ops, SparseCore 0:
  114.4 78.8 all-reduce.4
  195.9 33.7 all-reduce.6

commit v5 on v3

v5 whole, which is shorter than its diff:
```python
import functools
import math

import jax
import jax.numpy as jnp
import numpy as np
from jax import lax
from jax.experimental import pallas as pl
from jax.experimental.pallas import tpu as pltpu
from jax.sharding import PartitionSpec as P

C = 48
EDGE = 8
VOX = 512
LANES = 128
F32 = jnp.float32
BF16 = jnp.bfloat16
SLACK = 8 * 1024 * 1024
SHIFTS = (0, 1, 16, 17)


def placing_matrix():
    place = np.zeros((1024, 8 * LANES), np.float32)
    for z in range(8):
        for y in range(8):
            for x in range(8):
                place[64 * z + 8 * x + y, LANES * y + 16 * z + x + 4] = 1.0
            for x in range(4):
                place[512 + 32 * z + 8 * x + y, LANES * y + 16 * z + x] = 1.0
                place[768 + 32 * z + 8 * x + y, LANES * y + 16 * z + x + 12] = 1.0
    return place


def pair_matrix():
    place = np.zeros((1024, 8 * LANES), np.float32)
    for half in range(2):
        for z in range(8):
            for x in range(8):
                for y in range(8):
                    lane = (16 * z + 8 * half + x + 4) % LANES
                    place[512 * half + 64 * z + 8 * x + y, LANES * y + lane] = 1.0
    return place


def edge_matrix():
    pick = np.zeros((512, 512), np.float32)
    for z in range(8):
        for y in range(8):
            for x in range(8):
                pick[64 * z + 8 * x + y, 256 * (x // 4) + 32 * z + 8 * (x % 4) + y] = 1.0
    return pick


def dot(left, right, contract=(1, 0)):
    dims = (((contract[0],), (contract[1],)), ((), ()))
    return lax.dot_general(left, right, dims, preferred_element_type=F32)


def roll(value, shift):
    return pltpu.roll(value, shift % LANES, 1)


def lane_ids(rows):
    return lax.broadcasted_iota(jnp.int32, (rows, LANES), 1)


def silu_parts(value):
    sigma = 1.0 / (1.0 + jnp.exp(-value))
    return value * sigma, sigma * (1.0 + value * (1.0 - sigma))


def depth_columns(base, masks, step):
    zero = jnp.zeros_like(base)
    below = jnp.where(masks[0], zero, roll(base, step))
    above = jnp.where(masks[1], zero, roll(base, -step))
    return jnp.concatenate([below, base, above], axis=0)


def depth_masks(step, first):
    ids = (lane_ids(3 * C) - first) % LANES
    return ids < step, ids >= LANES - step


def across_columns(tile, step):
    return jnp.concatenate([roll(tile, step), tile, roll(tile, -step)], axis=0)


def pair_columns(tile, halo, step):
    ids = lane_ids(C) % 8
    left = jnp.where(ids == 4, roll(halo, step), roll(tile, step))
    right = jnp.where(ids == 4 - step, roll(halo, -step), roll(tile, -step))
    return jnp.concatenate([left, tile, right], axis=0)


def own_lanes(rows):
    across = lane_ids(rows) % 16
    return (across >= 4) & (across < 12)


def join_halves(lower, upper):
    return jnp.where(own_lanes(lower.shape[0]), lower, roll(upper, 8))


def join_halos(lower, upper):
    return jnp.where(own_lanes(lower.shape[0]), roll(upper, 8), lower)


def packed_halo(from_left, from_right, first, second, place, step):
    ids = lane_ids(C) % 16
    zero = jnp.zeros((C, LANES), BF16)
    halo = jnp.where(ids == 4 - step, roll(from_left[first], 4 - step - place), zero)
    halo = jnp.where(ids == 12 - step, roll(from_left[second], 12 - step - place), halo)
    halo = jnp.where(ids == 12, roll(from_right[first], 12 - place), halo)
    return jnp.where(ids == 4, roll(from_right[second], 20 - place), halo)


def gather_sub(parts):
    total = parts[:C]
    for index in range(1, 4):
        total = total + roll(parts[index * C : (index + 1) * C], -SHIFTS[index])
    return total


def spread_sub(anchored):
    return jnp.concatenate([anchored] + [roll(anchored, step) for step in SHIFTS[1:]], axis=0)


def anchor_mask(first):
    ids = (lane_ids(C) - first) % LANES
    return (((ids // 16) % 2 == 0) & (ids % 2 == 0)).astype(F32)


def loop(low, high, body, unroll=1):
    def step(index, carry):
        body(index)
        return carry

    lax.fori_loop(low, high, step, 0, unroll=unroll)


def prepare_kernel(
    slots, count, feats, cots, pick, own, cot, flag_rows, x_low, x_high, y_low, y_high, rows_in
):
    number = feats.shape[0]
    rows = lax.broadcasted_iota(jnp.int32, (C, VOX), 0)
    flags = jnp.zeros((C, VOX), F32)
    first = jnp.zeros((), F32)
    last = jnp.zeros((), F32)
    zero = jnp.zeros((C, VOX), BF16)
    for slot in range(number):
        live = slot < count[0]
        alive = jnp.where(live, 1.0, 0.0)
        place = slots[slot]
        block = jnp.where(live, feats[slot], zero)
        own[place] = block
        rows_in[pl.ds(pl.multiple_of(place * C, 16), C), :] = block
        cot[place] = jnp.where(live, cots[slot], zero)
        flags = jnp.where(rows == place + 1, alive, flags)
        first = first + jnp.where(place == 0, alive, 0.0)
        last = last + jnp.where(place == number - 1, alive, 0.0)
    flag_rows[...] = flags.astype(BF16)
    rows_in[number * C :, :] = flags.astype(BF16)
    first_flag = jnp.where(rows == number + 1, first, 0.0).astype(BF16)
    last_flag = jnp.where(rows == 0, last, 0.0).astype(BF16)
    packed = dot(rows_in[...], pick[...]).astype(BF16)
    packed = packed.reshape(number + 1, C, VOX)
    x_low[...] = packed[:, :, :256]
    x_high[...] = packed[:, :, 256:]
    for out, index, flag in ((y_low, 0, first_flag), (y_high, number - 1, last_flag)):
        out[0] = own[index]
        out[1] = cot[index]
        out[2] = flag


def corner_kernel(y_left, y_right, flag_rows, pick, low, high, flags):
    extra = y_left[2] + y_right[2]
    rows = jnp.concatenate([y_left[0], y_right[0], extra], axis=0)
    packed = dot(rows, pick[...]).astype(BF16).reshape(3, C, VOX)
    low[...] = packed[:, :, :256]
    high[...] = packed[:, :, 256:]
    flags[...] = flag_rows[...] + extra


def arrange_weights(fine, down, coarse, up, fine_w, fine_b, coarse_w, coarse_b, down_w, up_w):
    for source, fore, back in ((fine, fine_w, fine_b), (coarse, coarse_w, coarse_b)):
        for along in range(3):
            rows = slice(C * along, C * (along + 1))
            turned_rows = slice(C * (2 - along), C * (3 - along))
            ahead = []
            behind = []
            for depth in range(3):
                for across in range(3):
                    ahead.append(source[9 * depth + 3 * across + along])
                    behind.append(source[9 * (2 - depth) + 3 * (2 - across) + along].T)
            fore[rows, :] = jnp.concatenate(ahead, axis=1)
            back[turned_rows, :] = jnp.concatenate(behind, axis=1)
    for index in range(4):
        pair = [down[2 * index], down[2 * index + 1]]
        down_w[C * index : C * (index + 1), :] = jnp.concatenate(pair, axis=1)
    for along in range(2):
        row = jnp.concatenate([up[2 * index + along] for index in range(4)], axis=1)
        up_w[C * along : C * (along + 1), :] = row


def place_kernel(
    own, cot, y_left, y_right, flags, place, place_pair, fine, down, coarse, up,
    grid, cot_grid, grad_r, live, fine_w, fine_b, coarse_w, coarse_b, down_w, up_w,
    rows_in, rows_cot,
):
    arrange_weights(fine, down, coarse, up, fine_w, fine_b, coarse_w, coarse_b, down_w, up_w)
    number = cot.shape[0]
    last = number + 1
    rows_in[0:C, :] = y_left[0]
    for block in range(number):
        at = (block + 1) * C
        rows_in[at : at + C, :] = own[block]
    rows_in[last * C : (last + 1) * C, :] = y_right[0]
    rows_in[(last + 1) * C :, :] = flags[...]
    pairs = number // 2 + 2
    for group in range(pairs):
        at = group * C
        lower = y_left[1] if group == 0 else cot[group - 1]
        upper = y_right[1] if group == pairs - 1 else cot[group + number // 2 - 1]
        rows_cot[at : at + C, 0:512] = lower
        rows_cot[at : at + C, 512:1024] = upper
    for pair in range(4):
        lanes = slice(256 * pair, 256 * pair + 256)
        placed_cot = dot(rows_cot[...], place_pair[:, lanes])
        placed = dot(rows_in[...], place[:, lanes])
        for half in range(2):
            span = slice(LANES * half, LANES * (half + 1))
            for block in range(last + 1):
                tile = EDGE * block + 2 * pair + half
                grid[tile] = placed[block * C : (block + 1) * C, span].astype(BF16)
            for block in range(pairs):
                tile = EDGE * block + 2 * pair + half
                cot_grid[tile] = placed_cot[block * C : (block + 1) * C, span].astype(BF16)
        if pair == 0:
            live[...] = placed[(last + 1) * C :, 0:LANES]

    def rect_step(block):
        tiles = []
        for inner in range(4):
            tile = EDGE * block + 2 * inner
            tiles.append(jnp.concatenate([cot_grid[tile], cot_grid[tile + 1]], axis=0))
        parts = dot(up_w[...], jnp.concatenate(tiles, axis=1), (0, 0))
        for inner in range(4):
            grad_r[4 * block + inner] = gather_sub(parts[:, LANES * inner : LANES * (inner + 1)])

    loop(0, pairs, rect_step, 2)


def conv_sum(parts, tile):
    return parts[tile, 0:C] + parts[tile + 1, C : 2 * C] + parts[tile + 2, 2 * C :]


def conv_steps(parts, weight, load, tiles, step, first, unroll):
    masks = depth_masks(step, first)
    spare = jnp.zeros((3 * C, LANES), F32)
    parts[0] = spare
    parts[tiles + 1] = spare

    def body(index):
        tile = 4 * index
        for pair in range(2):
            at = tile + 2 * pair
            cols = [depth_columns(load(at + i), masks, step) for i in range(2)]
            out = dot(weight[...], jnp.concatenate(cols, axis=1))
            parts[at + 1] = out[:, :LANES]
            parts[at + 2] = out[:, LANES:]

    loop(0, tiles // 4, body, unroll)


def forward_kernel(
    grid_own, live_own, grad_r, x_left, x_right, c_left, c_right, place, fine_w, down_w, coarse_w,
    grid, hidden, low_cols, rects, grad_c, live, pack_low, pack_high,
    rows_in, fine_p, coarse_p, hidden_all, lowered, live_all,
):
    number = x_left.shape[0] - 1
    last = number + 1
    for block in range(number):
        at = (block + 1) * C
        rows_in[at : at + C, 0:256] = x_left[block]
        rows_in[at : at + C, 256:512] = x_right[block]
    for at, index in ((0, 0), (last * C, 1)):
        rows_in[at : at + C, 0:256] = c_left[index]
        rows_in[at : at + C, 256:512] = c_right[index]
    at = (last + 1) * C
    rows_in[at : at + C, 0:256] = x_left[number] + c_left[2]
    rows_in[at : at + C, 256:512] = x_right[number] + c_right[2]
    for pair in range(4):
        lanes = slice(256 * pair, 256 * pair + 256)
        placed = dot(rows_in[...], place[:, lanes])
        for half in range(2):
            span = slice(LANES * half, LANES * (half + 1))
            for block in range(last + 1):
                tile = EDGE * block + 2 * pair + half
                halo = placed[block * C : (block + 1) * C, span].astype(BF16)
                grid[tile] = grid_own[tile] + halo
        if pair == 0:
            live_all[...] = live_own[...] + placed[(last + 1) * C :, 0:LANES]
    live[...] = join_halves(live_all[0:16, :], live_all[8:24, :])
    tiles = grid.shape[0]
    conv_steps(fine_p, fine_w, lambda tile: across_columns(grid[tile], 1), tiles, 16, 0, 2)
    anchors = anchor_mask(0)

    def lower_step(block):
        alive = jnp.broadcast_to(live_all[pl.ds(block, 1), :], (C, LANES))
        keep = alive * anchors
        pairs = []
        for inner in range(4):
            actives = []
            for half in range(2):
                tile = EDGE * block + 2 * inner + half
                value = conv_sum(fine_p, tile) * alive
                hidden_all[tile] = value
                actives.append(silu_parts(value)[0].astype(BF16))
            pairs.append(jnp.concatenate(actives, axis=0))
        parts = dot(down_w[...], jnp.concatenate(pairs, axis=1))
        for inner in range(4):
            total = gather_sub(parts[:, LANES * inner : LANES * (inner + 1)])
            lowered[4 * block + inner] = (total * keep).astype(BF16)

    loop(0, last + 1, lower_step, 2)
    pairs = hidden.shape[0] // EDGE
    shift = last - pairs + 1

    def pair_step(block):
        for inner in range(EDGE):
            tile = EDGE * block + inner
            hidden[tile] = join_halves(hidden_all[tile], hidden_all[tile + EDGE * shift])
        for inner in range(4):
            tile = 4 * block + inner
            lower, upper = lowered[tile], lowered[tile + 4 * shift]
            low_cols[tile] = pair_columns(join_halves(lower, upper), join_halos(lower, upper), 2)

    loop(0, pairs, pair_step, 2)
    conv_steps(coarse_p, coarse_w, lambda tile: low_cols[tile], 4 * pairs, 32, 4, 2)
    pair_anchors = anchor_mask(4)

    def grad_step(block):
        alive = jnp.broadcast_to(live[pl.ds(block, 1), :], (C, LANES))
        keep = alive * pair_anchors
        for inner in range(4):
            coarse = 4 * block + inner
            smooth, slope = silu_parts(conv_sum(coarse_p, coarse))
            rects[coarse] = (smooth * pair_anchors).astype(BF16)
            grad_c[coarse] = (grad_r[coarse] * slope * keep).astype(BF16)

    loop(0, pairs, grad_step, 2)
    ids = lane_ids(C)
    zero = jnp.zeros((C, LANES), BF16)
    half = 2 * number
    for out, lane in ((pack_low, 4), (pack_high, 10)):
        for group in range(out.shape[0]):
            total = zero
            for coarse in range(max(2, 32 * group), min(2 * half + 6, 32 * group + 32)):
                upper = coarse >= half + 4
                tile = grad_c[coarse - half] if upper else grad_c[coarse]
                at = lane + 8 if upper else lane
                picked = jnp.where(ids % 32 == at, tile, zero)
                total = total + roll(picked, coarse % 32 - at)
            out[group] = total


def to_blocks(slots, rows_out, place_back, flat, out):
    flat[...] = dot(rows_out[...], place_back[...]).astype(BF16)
    number = out.shape[0]
    for slot in range(number):
        place = slots[slot]
        upper = place >= number // 2
        start = pl.multiple_of(jnp.where(upper, place - number // 2, place) * C, 16)
        rows = flat[pl.ds(start, C), :]
        out[slot] = jnp.where(upper, rows[:, 512:], rows[:, :512])


def stacks(own, tiles):
    parts = [jnp.concatenate([own[t + 1], own[t], own[t - 1]], axis=0) for t in tiles]
    return jnp.concatenate(parts, axis=1)


def flatten_weights(total, out, at):
    turned = total[...].T.astype(BF16)
    for group in range(4):
        out[at + 3 * C * group : at + 3 * C * (group + 1), :] = turned[
            :, LANES * group : LANES * (group + 1)
        ]


def output_kernel(slots, hidden, rects, live, place_back, up_w, out, rows_out, flat):
    pairs = hidden.shape[0] // EDGE

    def block_step(block):
        alive = jnp.broadcast_to(live[pl.ds(block, 1), :], (C, LANES))
        start = pl.multiple_of((block - 1) * C, 16)
        spreads = [spread_sub(rects[4 * block + inner]) for inner in range(4)]
        upward = dot(up_w[...], jnp.concatenate(spreads, axis=1))
        for inner in range(4):
            for half in range(2):
                part = upward[half * C : (half + 1) * C, LANES * inner : LANES * (inner + 1)]
                value = hidden[EDGE * block + 2 * inner + half] + part
                at = LANES * (2 * inner + half)
                rows_out[pl.ds(start, C), at : at + LANES] = (value * alive).astype(BF16)

    loop(1, pairs - 1, block_step, 2)
    to_blocks(slots, rows_out, place_back, flat, out)


def side_kernel(rects, cot_grid, low_cols, grad_c, flat, grad_own, up_g, coarse_g):
    tiles = low_cols.shape[0]
    up_g[...] = jnp.zeros_like(up_g)
    coarse_g[...] = jnp.zeros_like(coarse_g)

    def up_step(block):
        spreads = []
        pairs = []
        for inner in range(4):
            coarse = 4 * block + inner
            spreads.append(spread_sub(rects[coarse]))
            pairs.append(
                jnp.concatenate([cot_grid[2 * coarse], cot_grid[2 * coarse + 1]], axis=0)
            )
        up_g[:, 0 : 2 * C] += dot(
            jnp.concatenate(spreads, axis=1), jnp.concatenate(pairs, axis=1), (1, 1)
        )

    loop(1, tiles // 4 - 1, up_step, 2)
    zero = jnp.zeros((C, LANES), BF16)
    for coarse in range(1, 4):
        grad_own[coarse] = zero
        grad_own[tiles - 1 - coarse] = zero

    def copy_step(coarse):
        grad_own[coarse] = grad_c[coarse]

    loop(4, tiles - 4, copy_step, 8)
    masks = depth_masks(32, 4)

    def weight_step(index):
        at = [2 + 4 * index + inner for inner in range(4)]
        rights = [depth_columns(low_cols[tile], masks, 32) for tile in at]
        coarse_g[0 : 9 * C, :] += dot(
            jnp.concatenate(rights, axis=1), stacks(grad_own, at), (1, 1)
        )

    loop(0, (tiles - 4) // 4, weight_step, 3)
    flatten_weights(coarse_g, flat, 0)
    flat[12 * C :, :] = up_g[...].astype(BF16)


def backward_kernel(
    grad_c, from_left, from_right, hidden, cot_grid, live, coarse_w, down_w,
    grad_h, grad_d, pack_low, pack_high, coarse_p, grad_x,
):
    tiles = grad_c.shape[0]
    half = tiles - 8
    for coarse in range(tiles):
        first, second = coarse // 32, (coarse + half) // 32
        halo = packed_halo(from_left, from_right, first, second, coarse % 32, 2)
        grad_x[coarse] = pair_columns(grad_c[coarse], halo, 2)
    conv_steps(coarse_p, coarse_w, lambda tile: grad_x[tile], tiles, 32, 4, 2)
    anchors = anchor_mask(4)

    def step(block):
        alive = jnp.broadcast_to(live[pl.ds(block, 1), :], (C, LANES))
        keep = alive * anchors
        spreads = []
        for inner in range(4):
            coarse = 4 * block + inner
            down = (conv_sum(coarse_p, coarse) * keep).astype(BF16)
            grad_d[coarse] = down
            spreads.append(spread_sub(down))
        acts = dot(down_w[...], jnp.concatenate(spreads, axis=1), (0, 0))
        for inner in range(4):
            for side in range(2):
                tile = EDGE * block + 2 * inner + side
                slope = silu_parts(hidden[tile])[1]
                part = acts[side * C : (side + 1) * C, LANES * inner : LANES * (inner + 1)]
                grad = cot_grid[tile].astype(F32) + part * slope
                grad_h[tile] = (grad * alive).astype(BF16)

    loop(0, tiles // 4, step, 2)
    fine = 2 * tiles
    shift = fine - 16
    ids = lane_ids(C) % 16
    zero = jnp.zeros((C, LANES), BF16)
    for out, lane in ((pack_low, 4), (pack_high, 11)):
        for group in range(out.shape[0]):
            total = zero
            for tile in range(16 * group, 16 * group + 16):
                upper = tile >= shift + 8
                source = grad_h[tile - shift] if upper else grad_h[tile]
                at = lane + 8 if upper else lane
                picked = jnp.where(ids == at % 16, source, zero)
                total = total + roll(picked, tile % 16 - at)
            out[group] = total


def weight_kernel(grid, grad_h, grad_d, hidden, early, joined, grad_own, fine_g, down_g):
    tiles = grad_h.shape[0]
    shift = tiles - 16
    fine_g[...] = jnp.zeros_like(fine_g)
    down_g[...] = jnp.zeros_like(down_g)
    zero = jnp.zeros((C, LANES), BF16)
    for tile in range(3, 8):
        grad_own[tile] = zero
        grad_own[tiles - 1 - tile] = zero

    def copy_step(tile):
        grad_own[tile] = grad_h[tile]

    loop(8, tiles - 8, copy_step, 8)
    masks = depth_masks(16, 4)

    def fine_step(index):
        at = [4 + 8 * index + inner for inner in range(8)]
        rights = []
        for tile in at:
            lower, upper = grid[tile], grid[tile + shift]
            base = pair_columns(join_halves(lower, upper), join_halos(lower, upper), 1)
            rights.append(depth_columns(base, masks, 16))
        fine_g[0 : 9 * C, :] += dot(
            jnp.concatenate(rights, axis=1), stacks(grad_own, at), (1, 1)
        )

    loop(0, (tiles - 8) // 8, fine_step)

    def down_step(index):
        lefts = []
        rights = []
        for inner in range(4):
            coarse = 4 + 4 * index + inner
            lefts.append(spread_sub(grad_d[coarse]))
            actives = [silu_parts(hidden[2 * coarse + side])[0].astype(BF16) for side in range(2)]
            rights.append(jnp.concatenate(actives, axis=0))
        down_g[:, 0 : 2 * C] += dot(
            jnp.concatenate(lefts, axis=1), jnp.concatenate(rights, axis=1), (1, 1)
        )

    loop(0, (tiles // 2 - 8) // 4, down_step, 2)
    flatten_weights(fine_g, joined, 0)
    joined[12 * C : 16 * C, :] = down_g[...].astype(BF16)
    joined[16 * C :, :] = early[...]


def input_kernel(
    slots, grad_h, from_left, from_right, live, place_back, fine_w, out,
    fine_p, rows_out, flat, grad_x,
):
    tiles = grad_h.shape[0]
    shift = tiles - 16

    def fill_step(group):
        for inner in range(16):
            tile = 16 * group + inner
            second = group + shift // 16
            halo = packed_halo(from_left, from_right, group, second, inner, 1)
            grad_x[tile] = pair_columns(grad_h[tile], halo, 1)

    loop(0, tiles // 16, fill_step)
    conv_steps(fine_p, fine_w, lambda tile: grad_x[tile], tiles, 16, 4, 2)

    def block_step(block):
        alive = jnp.broadcast_to(live[pl.ds(block, 1), :], (C, LANES))
        start = pl.multiple_of((block - 1) * C, 16)
        for inner in range(EDGE):
            value = conv_sum(fine_p, EDGE * block + inner)
            rows_out[pl.ds(start, C), LANES * inner : LANES * (inner + 1)] = (
                value * alive
            ).astype(BF16)

    loop(1, tiles // EDGE - 1, block_step, 2)
    to_blocks(slots, rows_out, place_back, flat, out)


def finish_kernel(scale, total, fine, down, coarse, up):
    for out, at in ((fine, 0), (coarse, 16 * C)):
        for along in range(3):
            first = at + C * along
            rows = [total[first + 3 * C * g : first + 3 * C * g + C, :] for g in range(4)]
            row = jnp.concatenate(rows, axis=1).astype(F32) * scale
            for index in range(9):
                out[3 * index + along] = row[:, C * index : C * (index + 1)]
    for out, at, turn in ((down, 12 * C, False), (up, 28 * C, True)):
        for index in range(4):
            rows = total[at + C * index : at + C * (index + 1), :].astype(F32) * scale
            for along in range(2):
                part = rows[:, C * along : C * (along + 1)]
                out[2 * index + along] = part.T if turn else part


def call(kernel, inputs, outs, scratch=(), scalars=0, flops=0, limit=None):
    vmem = pl.BlockSpec(memory_space=pltpu.VMEM)
    smem = pl.BlockSpec(memory_space=pltpu.SMEM)
    held = SLACK
    for shape, kind in [(a.shape, a.dtype) for a in inputs[scalars:]] + list(outs) + list(scratch):
        rows, lanes = -(-shape[-2] // 16) * 16, -(-shape[-1] // LANES) * LANES
        held += math.prod(shape[:-2]) * rows * lanes * jnp.dtype(kind).itemsize
    moved = sum(math.prod(s) * jnp.dtype(d).itemsize for s, d in outs)
    moved += sum(math.prod(a.shape) * a.dtype.itemsize for a in inputs)
    return pl.pallas_call(
        kernel,
        out_shape=tuple(jax.ShapeDtypeStruct(s, d) for s, d in outs),
        in_specs=[smem] * scalars + [vmem] * (len(inputs) - scalars),
        out_specs=tuple(vmem for _ in outs),
        scratch_shapes=[pltpu.VMEM(s, d) for s, d in scratch],
        compiler_params=pltpu.CompilerParams(vmem_limit_bytes=limit or held),
        cost_estimate=pl.CostEstimate(flops=flops, bytes_accessed=moved, transcendentals=0),
        name=getattr(kernel, "func", kernel).__name__,
    )(*inputs)


def send(array, step_x, step_y):
    number_x, number_y = lax.axis_size("gx"), lax.axis_size("gy")
    pairs = []
    for i in range(number_x):
        for j in range(number_y):
            to_x, to_y = i + step_x, j + step_y
            if 0 <= to_x < number_x and 0 <= to_y < number_y:
                pairs.append((i * number_y + j, to_x * number_y + to_y))
    return lax.ppermute(array, ("gx", "gy"), pairs)


def reduce_all(joined):
    axes = ("gx", "gy")
    devices = lax.axis_size("gx") * lax.axis_size("gy")
    rows = joined.shape[0]
    share = -(-rows // devices)
    joined = jnp.pad(joined, ((0, share * devices - rows), (0, 0)))
    mine = lax.all_to_all(joined.reshape(devices, share, LANES), axes, 0, 0)
    mine = jnp.sum(mine.astype(F32), axis=0).astype(BF16)
    spread = jnp.broadcast_to(mine[None], (devices, share, LANES))
    full = lax.all_to_all(spread, axes, 0, 0)
    return full.reshape(devices * share, LANES)[:rows]


def on_device(
    features, block_slots, block_count, cotangent, fine_weight, down_weight, coarse_weight,
    up_weight,
):
    number = features.shape[2]
    slots = block_slots.reshape(number)
    count = block_count.reshape(1)
    feats = features.reshape(number, C, VOX)
    cots = cotangent.reshape(number, C, VOX)
    place_own = jnp.asarray(placing_matrix()[:512], BF16)
    place_halo = jnp.asarray(placing_matrix()[512:], BF16)
    place_pair = jnp.asarray(pair_matrix(), BF16)
    place_back = jnp.asarray(pair_matrix().T, BF16)
    pick = jnp.asarray(edge_matrix(), BF16)
    tiles = EDGE * (number + 2)
    coarse_tiles = tiles // 2
    pairs = number // 2 + 2
    groups = -(-coarse_tiles // 32)
    fine_groups = tiles // 16

    fine_3, down_3, coarse_3 = (
        weight.transpose(1, 0, 2) for weight in (fine_weight, down_weight, coarse_weight)
    )
    own, cot, flag_rows, x_low, x_high, y_low, y_high = call(
        prepare_kernel,
        (slots, count, feats, cots, pick),
        [((number, C, VOX), BF16)] * 2
        + [((C, VOX), BF16)]
        + [((number + 1, C, 256), BF16)] * 2
        + [((3, C, VOX), BF16)] * 2,
        [(((number + 1) * C, VOX), BF16)],
        scalars=2,
        limit=56 * 1024 * 1024,
    )
    x_left = send(x_high, 1, 0)
    x_right = send(x_low, -1, 0)
    y_left = send(y_high, 0, 1)
    y_right = send(y_low, 0, -1)
    corner_low, corner_high, flags = call(
        corner_kernel,
        (y_left, y_right, flag_rows, pick),
        [((3, C, 256), BF16), ((3, C, 256), BF16), ((C, VOX), BF16)],
    )
    c_left = send(corner_high, 1, 0)
    c_right = send(corner_low, -1, 0)
    (grid_own, cot_grid, grad_r, live_own, fine_fore, fine_back, coarse_fore, coarse_back, down_w,
     up_w) = call(
        place_kernel,
        (own, cot, y_left, y_right, flags, place_own, place_pair, fine_3, down_3, coarse_3,
         up_weight),
        [
            ((tiles, C, LANES), BF16),
            ((EDGE * pairs, C, LANES), BF16),
            ((4 * pairs, C, LANES), F32),
            ((C, LANES), F32),
        ]
        + [((3 * C, 9 * C), BF16)] * 4
        + [((4 * C, 2 * C), BF16), ((2 * C, 4 * C), BF16)],
        [(((number + 3) * C, VOX), BF16), ((pairs * C, 1024), BF16)],
        flops=8 * 10**9,
    )
    grid, hidden, low_cols, rects, grad_c, live, pack_low, pack_high = call(
        forward_kernel,
        (grid_own, live_own, grad_r, x_left, x_right, c_left, c_right, place_halo, fine_fore,
         down_w, coarse_fore),
        [
            ((tiles, C, LANES), BF16),
            ((EDGE * pairs, C, LANES), F32),
            ((4 * pairs, 3 * C, LANES), BF16),
            ((4 * pairs, C, LANES), BF16),
            ((4 * pairs, C, LANES), BF16),
            ((16, LANES), F32),
            ((groups, C, LANES), BF16),
            ((groups, C, LANES), BF16),
        ],
        [
            (((number + 3) * C, VOX), BF16),
            ((tiles + 2, 3 * C, LANES), F32),
            ((4 * pairs + 2, 3 * C, LANES), F32),
            ((tiles, C, LANES), F32),
            ((coarse_tiles, C, LANES), BF16),
            ((C, LANES), F32),
        ],
        flops=8 * 10**9,
    )
    grad_left = send(pack_high, 1, 0)
    grad_right = send(pack_low, -1, 0)
    (early,) = call(
        side_kernel,
        (rects, cot_grid, low_cols, grad_c),
        [((16 * C, LANES), BF16)],
        [((4 * pairs, C, LANES), BF16), ((4 * C, LANES), F32), ((VOX, 3 * C), F32)],
        flops=8 * 10**9,
    )
    grad_h, grad_d, edge_low, edge_high = call(
        backward_kernel,
        (grad_c, grad_left, grad_right, hidden, cot_grid, live, coarse_back, down_w),
        [
            ((EDGE * pairs, C, LANES), BF16),
            ((4 * pairs, C, LANES), BF16),
            ((fine_groups, C, LANES), BF16),
            ((fine_groups, C, LANES), BF16),
        ],
        [((4 * pairs + 2, 3 * C, LANES), F32), ((4 * pairs, 3 * C, LANES), BF16)],
        flops=8 * 10**9,
    )
    edge_left = send(edge_high, 1, 0)
    edge_right = send(edge_low, -1, 0)
    (joined,) = call(
        weight_kernel,
        (grid, grad_h, grad_d, hidden, early),
        [((32 * C, LANES), BF16)],
        [((EDGE * pairs, C, LANES), BF16), ((VOX, 3 * C), F32), ((4 * C, LANES), F32)],
        flops=12 * 10**9,
    )
    (output,) = call(
        output_kernel,
        (slots, hidden, rects, live, place_back, up_w),
        [((number, C, VOX), BF16)],
        [((number // 2 * C, 1024), BF16), ((number // 2 * C, 1024), BF16)],
        scalars=1,
        flops=8 * 10**9,
    )
    joined, edge_left, edge_right = lax.optimization_barrier((joined, edge_left, edge_right))
    total = reduce_all(joined)
    (input_grad,) = call(
        input_kernel,
        (slots, grad_h, edge_left, edge_right, live, place_back, fine_back),
        [((number, C, VOX), BF16)],
        [
            ((EDGE * pairs + 2, 3 * C, LANES), F32),
            ((number // 2 * C, 1024), BF16),
            ((number // 2 * C, 1024), BF16),
            ((EDGE * pairs, 3 * C, LANES), BF16),
        ],
        scalars=1,
        flops=8 * 10**9,
    )
    scale = 1.0 / math.sqrt(number * VOX * lax.axis_size("gx") * lax.axis_size("gy"))
    fine_total, down_total, coarse_total, up_total = call(
        functools.partial(finish_kernel, scale),
        (total,),
        [((27, C, C), F32), ((8, C, C), F32), ((27, C, C), F32), ((8, C, C), F32)],
    )
    shape_out = (1, 1, number, C, VOX)
    return (
        output.reshape(shape_out),
        input_grad.reshape(shape_out),
        fine_total.transpose(1, 0, 2),
        down_total.transpose(1, 0, 2),
        coarse_total.transpose(1, 0, 2),
        up_total,
    )


def solution(mesh):
    split = P("gx", "gy", None, None, None)
    return jax.shard_map(
        on_device,
        mesh=mesh,
        in_specs=(split, P("gx", "gy", None), P("gx", "gy"), split, P(), P(), P(), P()),
        out_specs=(split, split, P(), P(), P(), P()),
        check_vma=False,
    )
```

time: 146 us -> 133 us (0.911)
  Pallas kernels: 77.7 us -> 65.5 us
  local copies, waits for them, and re-layouts: 7.11 us -> 9.01 us
  blocking collectives: 21.8 us -> 20.1 us
    pallas_call x9 -> x10, Pallas kernels: 77.7 us -> 65.5 us  [call(): pl.pallas_call(kernel, out_shape=tuple((jax.ShapeDtypeStruct(s, d) for s,...]
    unnamed x30 -> x36, local copies, waits for them, and re-layouts: 6.31 us -> 8.21 us
    all_to_all x1, blocking collectives: 21.8 us -> 20.1 us  [reduce_all(): mine = lax.all_to_all(joined.reshape(devices, share, LANES), axes, 0, 0)]
    ppermute x10, starting transfers between devices: 28.4 us -> 26.8 us  [send(): return lax.ppermute(array, ('gx', 'gy'), pairs)]
  transfers between devices with their start and end apart: 11 -> 11, of which waited for: 1 -> 2; matrix products, arithmetic and copies ran while one was open for 0% -> 0% of each run, Pallas kernels for 30% -> 24%
where the time goes in v5:
time: 133 us; the launch traced here: 132 us
  Pallas kernels  65.5 us (49%)
  starting transfers between devices  29.6 us (22%)
  blocking collectives  20.1 us (15%)
  local copies, waits for them, and re-layouts  9.01 us (7%)
  waiting for transfers between devices  6.27 us (5%)
  between operations  1.74 us (1%)
    pallas_call x10, Pallas kernels, call(): pl.pallas_call(kernel, out_shape=tuple((jax.ShapeDtypeStruct(s, d) for s,...  65.5 us
    ppermute x10, starting transfers between devices, send(): return lax.ppermute(array, ('gx', 'gy'), pairs)  26.8 us
    all_to_all x1, blocking collectives, reduce_all(): mine = lax.all_to_all(joined.reshape(devices, share, LANES), axes, 0, 0)  20.1 us
    unnamed x36, local copies, waits for them, and re-layouts  8.21 us
    ppermute x10, waiting for transfers between devices, send(): return lax.ppermute(array, ('gx', 'gy'), pairs)  6.27 us
    all_to_all x1, starting transfers between devices, reduce_all(): full = lax.all_to_all(spread, axes, 0, 0)  2.82 us
  transfers between devices with their start and end apart: 11, of which 2 were waited for; matrix products, arithmetic and copies ran while one was open for 0% of the time, Pallas kernels for 24%

profile of v5, /device:TPU:0, one launch (start us, length us, event | category | flops | bytes accessed | tf_op | source)
XLA Modules:
  0.0 132.3 jit_solution(257141986202558111)
XLA Ops:
  1.4 3.2 %prepare_kernel.1 = (bf16[16,48,512]{2,1,0:T(8,128)(2,1)}, bf16[16,48,512]{2,1,0:T(8,128)(2,1)}, bf16[48,512]{1,0:T(8,128)(2,1)}, bf16[17,48,256]{2,1,0:T(8,128)...) custom-call(s32[16]{0:T(128)} %bitcast.21, s32[1]{0:T(128)} %bitcast.16.count, ...), custom_call_target="tpu_custom_call" | custom-call | bytes 4849732 | tf_op jit(solution)/shard_map/prepare_kernel/pallas_call | solution.py:602
  4.7 2.4 %collective-permute-start = (bf16[3,48,512]{2,1,0:T(8,128)(2,1)}, bf16[3,48,512]{2,1,0:T(8,128)(2,1)S(1)}, u32[]{:S(2)}, u32[]{:S(2)}) collective-permute-start(bf16[3,48,512]{2,1,0:T(8,128)(2,1)} %get-tuple-element.47), channel_id=1, source_target_pairs={{0,1},{1,2},{2,3},{4,5},{5,6},{6,7},{8,9},{9,10},{10,11},{12,13},{... | collective-permute-start | bytes 442376 | tf_op jit(solution)/shard_map/ppermute | solution.py:622
  7.0 1.3 collective-permute-start.1
  8.3 4.2 %collective-permute-start.2 = (bf16[17,48,256]{2,1,0:T(8,128)(2,1)}, bf16[17,48,256]{2,1,0:T(8,128)(2,1)S(1)}, u32[]{:S(2)}, u32[]{:S(2)}) collective-permute-start(bf16[17,48,256]{2,1,0:T(8,128)(2,1)} %get-tuple-element.54), channel_id=1, source_target_pairs={{0,4},{1,5},{2,6},{3,7},{4,8},{5,9},{6,10},{7,11},{8,12},{9,13},{1... | collective-permute-start | bytes 1253384 | tf_op jit(solution)/shard_map/ppermute | solution.py:622
  12.6 1.3 collective-permute-start.3
  14.0 0.8 copy-done.1
  14.7 0.2 corner_kernel.1
  15.0 4.5 %collective-permute-start.4 = (bf16[3,48,256]{2,1,0:T(8,128)(2,1)S(1)}, bf16[3,48,256]{2,1,0:T(8,128)(2,1)S(1)}, u32[]{:S(2)}, u32[]{:S(2)}) collective-permute-start(bf16[3,48,256]{2,1,0:T(8,128)(2,1)S(1)} %get-tuple-element.56), channel_id=1, source_target_pairs={{0,4},{1,5},{2,6},{3,7},{4,8},{5,9},{6,10},{7,11},{8,12},{9,13},{1... | collective-permute-start | bytes 221192 | tf_op jit(solution)/shard_map/ppermute | solution.py:622
  19.5 1.3 collective-permute-start.5
  20.9 1.1 copy-done.3
  22.0 1.1 copy-done.4
  23.1 1.6 %copy-done.9 = bf16[1024,1024]{1,0:T(8,128)(2,1)S(1)} copy-done((bf16[1024,1024]{1,0:T(8,128)(2,1)S(1)}, bf16[1024,1024]{1,0:T(8,128)(2,1)}, u32[]{:S(2)}) %copy-start.9) | copy-done | bytes 2097176
  24.7 1.2 copy-done.11
  26.0 4.3 %place_kernel.1 = (bf16[144,48,128]{2,1,0:T(8,128)(2,1)S(1)}, bf16[80,48,128]{2,1,0:T(8,128)(2,1)S(1)}, f32[40,48,128]{2,1,0:T(8,128)S(1)}, f32[48,128]{1,0:T(8,...) custom-call(bf16[16,48,512]{2,1,0:T(8,128)(2,1)S(1)} %copy-done.3, ...), custom_call_target="tpu_custom_call" | custom-call | flops 8000000000 | bytes 9716736 | tf_op jit(solution)/shard_map/place_kernel/pallas_call | solution.py:602
  30.3 3.1 %collective-permute-done.4.c_left = bf16[3,48,256]{2,1,0:T(8,128)(2,1)S(1)} collective-permute-done((bf16[3,48,256]{2,1,0:T(8,128)(2,1)S(1)}, bf16[3,48,256]{2,1,0:T(8,128)(2,1)S(1)}, u32[]{:S(2)}, u32[]{:S(2)}) %collective-permute-start.4) | collective-permute-done | bytes 73760 | tf_op jit(solution)/shard_map/ppermute | solution.py:622
  33.4 20.3 %forward_kernel.1 = (bf16[144,48,128]{2,1,0:T(8,128)(2,1)S(1)}, f32[80,48,128]{2,1,0:T(8,128)S(1)}, bf16[40,144,128]{2,1,0:T(8,128)(2,1)S(1)}, bf16[40,48,128]{2...) custom-call(bf16[144,48,128]{2,1,0:T(8,128)(2,1)S(1)} %get-tuple-ele, ...), custom_call_target="tpu_custom_call" | custom-call | flops 8000000000 | bytes 11369472 | tf_op jit(solution)/shard_map/forward_kernel/pallas_call | solution.py:602
  53.7 4.4 %collective-permute-start.6 = (bf16[3,48,128]{2,1,0:T(8,128)(2,1)S(1)}, bf16[3,48,128]{2,1,0:T(8,128)(2,1)S(1)}, u32[]{:S(2)}, u32[]{:S(2)}) collective-permute-start(bf16[3,48,128]{2,1,0:T(8,128)(2,1)S(1)} %get-tuple-element.66), channel_id=1, source_target_pairs={{0,4},{1,5},{2,6},{3,7},{4,8},{5,9},{6,10},{7,11},{8,12},{9,13},{1... | collective-permute-start | bytes 110600 | tf_op jit(solution)/shard_map/ppermute | solution.py:622
  58.1 1.3 collective-permute-start.7
  59.4 3.3 %side_kernel.1.early = bf16[768,128]{1,0:T(8,128)(2,1)S(1)} custom-call(bf16[40,48,128]{2,1,0:T(8,128)(2,1)S(1)} %get-tuple-element.62.rects, bf16[80,48,128]{2,1,0:T(8,128)(2,1)S(1)} %get-tuple-element.68.cot_grid, bf16[40,144,128]{2,1,0:T(8,128)(2,1)S(1)} %get-tuple-element.73.low_cols, bf16[40,48,128]{2,1,0:T(8,128)(2,1)S(1)} %get-tuple-element.65.grad_c), custom_call_target="tpu_custom_call" | custom-call | flops 8000000000 | bytes 3637248 | tf_op jit(solution)/shard_map/side_kernel/pallas_call | solution.py:602
  62.6 3.1 %collective-permute-done.7.from_right = bf16[3,48,128]{2,1,0:T(8,128)(2,1)S(1)} collective-permute-done((bf16[3,48,128]{2,1,0:T(8,128)(2,1)S(1)}, bf16[3,48,128]{2,1,0:T(8,128)(2,1)S(1)}, u32[]{:S(2)}, u32[]{:S(2)}) %collective-permute-start.7) | collective-permute-done | bytes 36896 | tf_op jit(solution)/shard_map/ppermute | solution.py:622
  65.8 8.2 %backward_kernel.1 = (bf16[80,48,128]{2,1,0:T(8,128)(2,1)S(1)}, bf16[40,48,128]{2,1,0:T(8,128)(2,1)S(1)}, bf16[9,48,128]{2,1,0:T(8,128)(2,1)S(1)}, bf16[9,48,128]{2,1,0:T(8,128)(2,1)S(1)}) custom-call(bf16[40,48,128]{2,1,0:T(8,128)(2,1)S(1)} %get-tuple-element.65.grad_c, bf16[3,48,128]{2,1,0:T(8,128)(2,1)S(1)} %collective-permute-done.6.from_left, ...), custom_call_target="tpu_custom_call" | custom-call | flops 8000000000 | bytes 5379584 | tf_op jit(solution)/shard_map/backward_kernel/pallas_call | solution.py:602
  74.0 4.8 %collective-permute-start.8 = (bf16[9,48,128]{2,1,0:T(8,128)(2,1)S(1)}, bf16[9,48,128]{2,1,0:T(8,128)(2,1)S(1)}, u32[]{:S(2)}, u32[]{:S(2)}) collective-permute-start(bf16[9,48,128]{2,1,0:T(8,128)(2,1)S(1)} %get-tuple-element.74), channel_id=1, source_target_pairs={{0,4},{1,5},{2,6},{3,7},{4,8},{5,9},{6,10},{7,11},{8,12},{9,13},{1... | collective-permute-start | bytes 331784 | tf_op jit(solution)/shard_map/ppermute | solution.py:622
  78.9 1.3 collective-permute-start.9
  80.2 7.7 %weight_kernel.1 = bf16[1536,128]{1,0:T(8,128)(2,1)S(1)} custom-call(bf16[144,48,128]{2,1,0:T(8,128)(2,1)S(1)} %get-tuple-element.71.grid, bf16[80,48,128]{2,1,0:T(8,128)(2,1)S(1)} %get-tuple-element.70.grad_h, bf16[40,48,128]{2,1,0:T(8,128)(2,1)S(1)} %get-tuple-element.72.grad_d, f32[80,48,128]{2,1,0:T(8,128)S(1)} %get-tuple-element.61.hidden, ...), custom_call_target="tpu_custom_call" | custom-call | flops 12000000000 | bytes 5799936 | tf_op jit(solution)/shard_map/weight_kernel/pallas_call | solution.py:602
  87.9 20.1 %all_to_all.10 = bf16[32,48,128]{2,1,0:T(8,128)(2,1)S(1)} all-to-all(bf16[32,48,128]{2,1,0:T(8,128)(2,1)S(1)} %bitcast.18), channel_id=1, replica_groups=mesh['gx'=8,'gy'=4] {'gx','gy'}, dimensions={0} | all-to-all | bytes 786432 | tf_op jit(solution)/shard_map/all_to_all | solution.py:631
  108.1 0.8 broadcast_in_dim.2
  108.9 2.8 %all-to-all-start.1 = ((bf16[32,48,128]{2,1,0:T(8,128)(2,1)}), bf16[32,48,128]{2,1,0:T(8,128)(2,1)S(1)}, u32[]{:S(2)}, u32[]{:S(2)}) async-start(bf16[32,48,128]{2,1,0:T(8,128)(2,1)} %broadcast_in_dim.2), calls=%async_computation.1 | async-start | bytes 786432 | tf_op jit(solution)/shard_map/all_to_all | solution.py:634
  111.7 1.5 %copy-done.13 = f32[80,48,128]{2,1,0:T(8,128)S(1)} copy-done((f32[80,48,128]{2,1,0:T(8,128)S(1)}, f32[80,48,128]{2,1,0:T(8,128)}, u32[]{:S(2)}) %copy-start.13) | copy-done | bytes 1966104
  113.3 3.7 %output_kernel.1 = bf16[16,48,512]{2,1,0:T(8,128)(2,1)} custom-call(s32[16]{0:T(128)S(1)} %bitcast.22, f32[80,48,128]{2,1,0:T(8,128)S(1)} %copy-done.13, bf16[40,48,128]{2,1,0:T(8,128)(2,1)S(1)} %get-tuple-element.62.rects, f32[16,128]{1,0:T(8,128)S(1)} %get-tuple-element.63.live, bf16[1024,1024]{1,0:T(8,128)(2,1)S(1)} %copy-done.8, ...), custom_call_target="tpu_custom_call" | custom-call | flops 8000000000 | bytes 5386304 | tf_op jit(solution)/shard_map/output_kernel/pallas_call | solution.py:602
  117.0 13.0 %input_kernel.1 = bf16[16,48,512]{2,1,0:T(8,128)(2,1)} custom-call(s32[16]{0:T(128)S(1)} %bitcast.23, bf16[80,48,128]{2,1,0:T(8,128)(2,1)S(1)} %copy-done.15, bf16[9,48,128]{2,1,0:T(8,128)(2,1)S(1)} %collective-permute-done.8.from_left, bf16[9,48,128]{2,1,0:T(8,128)(2,1)S(1)} %collective-permute-done.9.from_right, f32[16,128]{1,0:T(8,128)S(1)} %get-tuple-element.63.live, ...), custom_call_target="tpu_custom_call" | custom-call | flops 8000000000 | bytes 4220480 | tf_op jit(solution)/shard_map/input_kernel/pallas_call | solution.py:602
  130.0 1.6 %finish_kernel.1 = (f32[27,48,48]{2,1,0:T(8,128)}, f32[8,48,48]{2,1,0:T(8,128)S(1)}, f32[27,48,48]{2,1,0:T(8,128)}, f32[8,48,48]{2,1,0:T(8,128)}) custom-call(bf16[1536,128]{1,0:T(8,128)(2,1)S(1)} %bitcast.17), custom_call_target="tpu_custom_call" | custom-call | bytes 1038336 | tf_op jit(solution)/shard_map/finish_kernel/pallas_call | solution.py:602
  131.5 0.7 copy.20
  (39 shorter events, 0.2 us)
Async XLA Ops:
  0.6 13.3 %copy-start = (bf16[512,512]{1,0:T(8,128)(2,1)S(1)}, bf16[512,512]{1,0:T(8,128)(2,1)}, u32[]{:S(2)}) copy-start(bf16[512,512]{1,0:T(8,128)(2,1)} %constant.18.clone.pick) | copy-start | bytes 1572868
  0.6 13.2 %copy-start.16 = (bf16[48,8,48]{2,1,0:T(8,128)(2,1)S(1)}, bf16[48,8,48]{2,1,0:T(8,128)(2,1)}, u32[]{:S(2)}) copy-start(bf16[48,8,48]{2,1,0:T(8,128)(2,1)} %param.18) | copy-start | bytes 110596
  0.7 20.2 %copy-start.7 = (bf16[8,48,48]{2,1,0:T(8,128)(2,1)S(1)}, bf16[8,48,48]{2,1,0:T(8,128)(2,1)}, u32[]{:S(2)}) copy-start(bf16[8,48,48]{2,1,0:T(8,128)(2,1)} %up.1) | copy-start | bytes 110596
  0.7 20.2 %copy-start.6 = (bf16[48,27,48]{2,0,1:T(8,128)(2,1)S(1)}, bf16[48,27,48]{2,0,1:T(8,128)(2,1)}, u32[]{:S(2)}) copy-start(bf16[48,27,48]{2,0,1:T(8,128)(2,1)} %param.19) | copy-start | bytes 373252
  0.7 20.2 %copy-start.5 = (bf16[48,27,48]{2,0,1:T(8,128)(2,1)S(1)}, bf16[48,27,48]{2,0,1:T(8,128)(2,1)}, u32[]{:S(2)}) copy-start(bf16[48,27,48]{2,0,1:T(8,128)(2,1)} %param.17) | copy-start | bytes 373252
  4.7 9.3 %collective-permute-start = (bf16[3,48,512]{2,1,0:T(8,128)(2,1)}, bf16[3,48,512]{2,1,0:T(8,128)(2,1)S(1)}, u32[]{:S(2)}, u32[]{:S(2)}) collective-permute-start(bf16[3,48,512]{2,1,0:T(8,128)(2,1)} %get-tuple-element.47), channel_id=1, source_target_pairs={{0,1},{1,2},{2,3},{4,5},{5,6},{6,7},{8,9},{9,10},{10,11},{12,13},{... | collective-permute-start | bytes 442376 | tf_op jit(solution)/shard_map/ppermute | solution.py:622
  7.0 6.9 %collective-permute-start.1 = (bf16[3,48,512]{2,1,0:T(8,128)(2,1)}, bf16[3,48,512]{2,1,0:T(8,128)(2,1)S(1)}, u32[]{:S(2)}, u32[]{:S(2)}) collective-permute-start(bf16[3,48,512]{2,1,0:T(8,128)(2,1)} %get-tuple-element.48), channel_id=1, source_target_pairs={{1,0},{2,1},{3,2},{5,4},{6,5},{7,6},{9,8},{10,9},{11,10},{13,12},{... | collective-permute-start | bytes 442376 | tf_op jit(solution)/shard_map/ppermute | solution.py:622
  8.3 25.1 %collective-permute-start.2 = (bf16[17,48,256]{2,1,0:T(8,128)(2,1)}, bf16[17,48,256]{2,1,0:T(8,128)(2,1)S(1)}, u32[]{:S(2)}, u32[]{:S(2)}) collective-permute-start(bf16[17,48,256]{2,1,0:T(8,128)(2,1)} %get-tuple-element.54), channel_id=1, source_target_pairs={{0,4},{1,5},{2,6},{3,7},{4,8},{5,9},{6,10},{7,11},{8,12},{9,13},{1... | collective-permute-start | bytes 1253384 | tf_op jit(solution)/shard_map/ppermute | solution.py:622
  12.6 20.8 %collective-permute-start.3 = (bf16[17,48,256]{2,1,0:T(8,128)(2,1)}, bf16[17,48,256]{2,1,0:T(8,128)(2,1)S(1)}, u32[]{:S(2)}, u32[]{:S(2)}) collective-permute-start(bf16[17,48,256]{2,1,0:T(8,128)(2,1)} %get-tuple-element.55), channel_id=1, source_target_pairs={{4,0},{5,1},{6,2},{7,3},{8,4},{9,5},{10,6},{11,7},{12,8},{13,9},{1... | collective-permute-start | bytes 1253384 | tf_op jit(solution)/shard_map/ppermute | solution.py:622
  13.9 0.8 copy-start.1
  15.0 18.4 %collective-permute-start.4 = (bf16[3,48,256]{2,1,0:T(8,128)(2,1)S(1)}, bf16[3,48,256]{2,1,0:T(8,128)(2,1)S(1)}, u32[]{:S(2)}, u32[]{:S(2)}) collective-permute-start(bf16[3,48,256]{2,1,0:T(8,128)(2,1)S(1)} %get-tuple-element.56), channel_id=1, source_target_pairs={{0,4},{1,5},{2,6},{3,7},{4,8},{5,9},{6,10},{7,11},{8,12},{9,13},{1... | collective-permute-start | bytes 221192 | tf_op jit(solution)/shard_map/ppermute | solution.py:622
  19.5 13.8 %collective-permute-start.5 = (bf16[3,48,256]{2,1,0:T(8,128)(2,1)S(1)}, bf16[3,48,256]{2,1,0:T(8,128)(2,1)S(1)}, u32[]{:S(2)}, u32[]{:S(2)}) collective-permute-start(bf16[3,48,256]{2,1,0:T(8,128)(2,1)S(1)} %get-tuple-element.57), channel_id=1, source_target_pairs={{4,0},{5,1},{6,2},{7,3},{8,4},{9,5},{10,6},{11,7},{12,8},{13,9},{1... | collective-permute-start | bytes 221192 | tf_op jit(solution)/shard_map/ppermute | solution.py:622
  20.9 1.1 copy-start.3
  22.0 1.1 copy-start.4
  23.1 1.6 %copy-start.9 = (bf16[1024,1024]{1,0:T(8,128)(2,1)S(1)}, bf16[1024,1024]{1,0:T(8,128)(2,1)}, u32[]{:S(2)}) copy-start(bf16[1024,1024]{1,0:T(8,128)(2,1)} %constant.16.clone.place_pair) | copy-start | bytes 6291460
  24.7 1.2 copy-start.11
  26.0 7.4 %copy-start.10 = (bf16[512,1024]{1,0:T(8,128)(2,1)S(1)}, bf16[512,1024]{1,0:T(8,128)(2,1)}, u32[]{:S(2)}) copy-start(bf16[512,1024]{1,0:T(8,128)(2,1)} %constant.15.clone.place) | copy-start | bytes 3145732
  53.7 26.5 %copy-start.12 = (f32[80,48,128]{2,1,0:T(8,128)}, f32[80,48,128]{2,1,0:T(8,128)S(1)}, u32[]{:S(2)}) copy-start(f32[80,48,128]{2,1,0:T(8,128)S(1)} %get-tuple-element.61.hidden) | copy-start | bytes 5898244
  53.7 9.0 %collective-permute-start.6 = (bf16[3,48,128]{2,1,0:T(8,128)(2,1)S(1)}, bf16[3,48,128]{2,1,0:T(8,128)(2,1)S(1)}, u32[]{:S(2)}, u32[]{:S(2)}) collective-permute-start(bf16[3,48,128]{2,1,0:T(8,128)(2,1)S(1)} %get-tuple-element.66), channel_id=1, source_target_pairs={{0,4},{1,5},{2,6},{3,7},{4,8},{5,9},{6,10},{7,11},{8,12},{9,13},{1... | collective-permute-start | bytes 110600 | tf_op jit(solution)/shard_map/ppermute | solution.py:622
  58.1 7.7 %collective-permute-start.7 = (bf16[3,48,128]{2,1,0:T(8,128)(2,1)S(1)}, bf16[3,48,128]{2,1,0:T(8,128)(2,1)S(1)}, u32[]{:S(2)}, u32[]{:S(2)}) collective-permute-start(bf16[3,48,128]{2,1,0:T(8,128)(2,1)S(1)} %get-tuple-element.67), channel_id=1, source_target_pairs={{4,0},{5,1},{6,2},{7,3},{8,4},{9,5},{10,6},{11,7},{12,8},{13,9},{1... | collective-permute-start | bytes 110600 | tf_op jit(solution)/shard_map/ppermute | solution.py:622
  74.0 13.8 %copy-start.14 = (bf16[80,48,128]{2,1,0:T(8,128)(2,1)}, bf16[80,48,128]{2,1,0:T(8,128)(2,1)S(1)}, u32[]{:S(2)}) copy-start(bf16[80,48,128]{2,1,0:T(8,128)(2,1)S(1)} %get-tuple-element.70.grad_h) | copy-start | bytes 2949124
  74.0 13.9 %collective-permute-start.8 = (bf16[9,48,128]{2,1,0:T(8,128)(2,1)S(1)}, bf16[9,48,128]{2,1,0:T(8,128)(2,1)S(1)}, u32[]{:S(2)}, u32[]{:S(2)}) collective-permute-start(bf16[9,48,128]{2,1,0:T(8,128)(2,1)S(1)} %get-tuple-element.74), channel_id=1, source_target_pairs={{0,4},{1,5},{2,6},{3,7},{4,8},{5,9},{6,10},{7,11},{8,12},{9,13},{1... | collective-permute-start | bytes 331784 | tf_op jit(solution)/shard_map/ppermute | solution.py:622
  78.9 9.0 %collective-permute-start.9 = (bf16[9,48,128]{2,1,0:T(8,128)(2,1)S(1)}, bf16[9,48,128]{2,1,0:T(8,128)(2,1)S(1)}, u32[]{:S(2)}, u32[]{:S(2)}) collective-permute-start(bf16[9,48,128]{2,1,0:T(8,128)(2,1)S(1)} %get-tuple-element.75), channel_id=1, source_target_pairs={{4,0},{5,1},{6,2},{7,3},{8,4},{9,5},{10,6},{11,7},{12,8},{13,9},{1... | collective-permute-start | bytes 331784 | tf_op jit(solution)/shard_map/ppermute | solution.py:622
  87.9 23.8 %copy-start.2 = (s32[1,1,16]{2,1,0:T(1,128)S(1)}, s32[1,1,16]{2,1,0:T(1,128)}, u32[]{:S(2)}) copy-start(s32[1,1,16]{2,1,0:T(1,128)} %param.14) | copy-start | bytes 196
  87.9 23.8 %copy-start.8 = (bf16[1024,1024]{1,0:T(8,128)(2,1)S(1)}, bf16[1024,1024]{1,0:T(8,128)(2,1)}, u32[]{:S(2)}) copy-start(bf16[1024,1024]{1,0:T(8,128)(2,1)} %constant.17.clone.place_back) | copy-start | bytes 6291460
  108.9 21.1 %all-to-all-start.1 = ((bf16[32,48,128]{2,1,0:T(8,128)(2,1)}), bf16[32,48,128]{2,1,0:T(8,128)(2,1)S(1)}, u32[]{:S(2)}, u32[]{:S(2)}) async-start(bf16[32,48,128]{2,1,0:T(8,128)(2,1)} %broadcast_in_dim.2), calls=%async_computation.1 | async-start | bytes 786432 | tf_op jit(solution)/shard_map/all_to_all | solution.py:634
  111.7 1.5 %copy-start.13 = (f32[80,48,128]{2,1,0:T(8,128)S(1)}, f32[80,48,128]{2,1,0:T(8,128)}, u32[]{:S(2)}) copy-start(f32[80,48,128]{2,1,0:T(8,128)} %copy-done.12) | copy-start | bytes 5898244
  113.3 3.7 %copy-start.15 = (bf16[80,48,128]{2,1,0:T(8,128)(2,1)S(1)}, bf16[80,48,128]{2,1,0:T(8,128)(2,1)}, u32[]{:S(2)}) copy-start(bf16[80,48,128]{2,1,0:T(8,128)(2,1)} %copy-done.14) | copy-start | bytes 2949124

commit v6 on v5

--- a/solution.py
+++ b/solution.py
@@ -69,60 +69,140 @@
     return value * sigma, sigma * (1.0 + value * (1.0 - sigma))
 
 
-def depth_columns(base, masks, step):
-    zero = jnp.zeros_like(base)
-    below = jnp.where(masks[0], zero, roll(base, step))
-    above = jnp.where(masks[1], zero, roll(base, -step))
-    return jnp.concatenate([below, base, above], axis=0)
-
-
-def depth_masks(step, first):
-    ids = (lane_ids(3 * C) - first) % LANES
-    return ids < step, ids >= LANES - step
+def lane_matrix(rows, sources):
+    ids = lax.broadcasted_iota(jnp.int32, (rows, LANES), 0)
+    lanes = lax.broadcasted_iota(jnp.int32, (rows, LANES), 1)
+    blocks = [jnp.where(ids == source(lanes), 1.0, 0.0).astype(BF16) for source in sources]
+    return jnp.concatenate(blocks, axis=1) if len(blocks) > 1 else blocks[0]
+
+
+def move(rows, matrix):
+    return dot(rows, matrix).astype(BF16)
+
+
+def is_own(lane):
+    return (lane % 16 >= 4) & (lane % 16 < 12)
+
+
+def depth_matrix(step, first):
+    def below(lane):
+        return jnp.where((lane - first) % LANES >= step, (lane - step) % LANES, -1)
+
+    def above(lane):
+        return jnp.where((lane - first) % LANES < LANES - step, (lane + step) % LANES, -1)
+
+    return lane_matrix(LANES, [below, above])
+
+
+def gather_matrix():
+    return lane_matrix(LANES, [lambda lane, s=s: (lane + s) % LANES for s in SHIFTS[1:]])
+
+
+def spread_matrix():
+    return lane_matrix(LANES, [lambda lane, s=s: (lane - s) % LANES for s in SHIFTS[1:]])
+
+
+def pair_matrix_across(step):
+    def joined(lane):
+        return jnp.where(is_own(lane), lane, LANES + (lane - 8) % LANES)
+
+    def halo(lane):
+        return jnp.where(is_own(lane), LANES + (lane - 8) % LANES, lane)
+
+    def left(lane):
+        at = (lane - step) % LANES
+        return jnp.where(lane % 8 == 4, halo(at), joined(at))
+
+    def right(lane):
+        at = (lane + step) % LANES
+        return jnp.where(lane % 8 == 4 - step, halo(at), joined(at))
+
+    return lane_matrix(2 * LANES, [left, joined, right])
+
+
+def inner_matrix(step):
+    def left(lane):
+        return jnp.where(lane % 8 == 4, -1, (lane - step) % LANES)
+
+    def right(lane):
+        return jnp.where(lane % 8 == 4 - step, -1, (lane + step) % LANES)
+
+    return lane_matrix(LANES, [left, right])
+
+
+def pack_matrix(step):
+    def low(lane):
+        place = (lane - 4) % 8
+        return LANES * place + (lane - place) % LANES
+
+    def high(lane):
+        place = (lane - 4) % 8
+        return LANES * place + (lane - place + 8 - step) % LANES
+
+    return lane_matrix(8 * LANES, [low, high])
+
+
+def unpack_matrix(step, right):
+    def source(place):
+        def from_left(lane):
+            return jnp.where(lane % 8 == 4, (lane + place) % LANES, -1)
+
+        def from_right(lane):
+            return jnp.where(lane % 8 == 4 - step, (lane - 8 + step + place) % LANES, -1)
+
+        return from_right if right else from_left
+
+    return lane_matrix(LANES, [source(place) for place in range(8)])
+
+
+def lane_block(array, index):
+    return array[:, LANES * index : LANES * (index + 1)]
+
+
+def depth_stack(bases, matrix):
+    moved = move(jnp.concatenate(bases, axis=0), matrix)
+    out = []
+    for index, base in enumerate(bases):
+        rows = moved[3 * C * index : 3 * C * (index + 1)]
+        out.append(jnp.concatenate([lane_block(rows, 0), base, lane_block(rows, 1)], axis=0))
+    return out
+
+
+def sub_stack(tiles, matrix):
+    moved = move(jnp.concatenate(tiles, axis=0), matrix)
+    size = tiles[0].shape[0]
+    out = []
+    for index, tile in enumerate(tiles):
+        rows = moved[size * index : size * (index + 1)]
+        out.append(jnp.concatenate([tile] + [lane_block(rows, i) for i in range(3)], axis=0))
+    return out
+
+
+def pair_stack(lowers, uppers, matrix):
+    rows = jnp.concatenate(
+        [jnp.concatenate([a, b], axis=1) for a, b in zip(lowers, uppers)], axis=0
+    )
+    moved = move(rows, matrix)
+    out = []
+    for index in range(len(lowers)):
+        part = moved[C * index : C * (index + 1)]
+        out.append(jnp.concatenate([lane_block(part, i) for i in range(3)], axis=0))
+    return out
+
+
+def halo_stack(tiles, left_halos, right_halos, matrix):
+    inner = dot(jnp.concatenate(tiles, axis=0), matrix)
+    out = []
+    for index, tile in enumerate(tiles):
+        part = inner[C * index : C * (index + 1)]
+        left = (lane_block(part, 0) + lane_block(left_halos, index)).astype(BF16)
+        right = (lane_block(part, 1) + lane_block(right_halos, index)).astype(BF16)
+        out.append(jnp.concatenate([left, tile, right], axis=0))
+    return out
 
 
 def across_columns(tile, step):
     return jnp.concatenate([roll(tile, step), tile, roll(tile, -step)], axis=0)
-
-
-def pair_columns(tile, halo, step):
-    ids = lane_ids(C) % 8
-    left = jnp.where(ids == 4, roll(halo, step), roll(tile, step))
-    right = jnp.where(ids == 4 - step, roll(halo, -step), roll(tile, -step))
-    return jnp.concatenate([left, tile, right], axis=0)
-
-
-def own_lanes(rows):
-    across = lane_ids(rows) % 16
-    return (across >= 4) & (across < 12)
-
-
-def join_halves(lower, upper):
-    return jnp.where(own_lanes(lower.shape[0]), lower, roll(upper, 8))
-
-
-def join_halos(lower, upper):
-    return jnp.where(own_lanes(lower.shape[0]), roll(upper, 8), lower)
-
-
-def packed_halo(from_left, from_right, first, second, place, step):
-    ids = lane_ids(C) % 16
-    zero = jnp.zeros((C, LANES), BF16)
-    halo = jnp.where(ids == 4 - step, roll(from_left[first], 4 - step - place), zero)
-    halo = jnp.where(ids == 12 - step, roll(from_left[second], 12 - step - place), halo)
-    halo = jnp.where(ids == 12, roll(from_right[first], 12 - place), halo)
-    return jnp.where(ids == 4, roll(from_right[second], 20 - place), halo)
-
-
-def gather_sub(parts):
-    total = parts[:C]
-    for index in range(1, 4):
-        total = total + roll(parts[index * C : (index + 1) * C], -SHIFTS[index])
-    return total
-
-
-def spread_sub(anchored):
-    return jnp.concatenate([anchored] + [roll(anchored, step) for step in SHIFTS[1:]], axis=0)
 
 
 def anchor_mask(first):
@@ -181,7 +261,9 @@
     flags[...] = flag_rows[...] + extra
 
 
-def arrange_weights(fine, down, coarse, up, fine_w, fine_b, coarse_w, coarse_b, down_w, up_w):
+def arrange_weights(
+    fine, down, coarse, up, fine_w, fine_b, coarse_w, coarse_b, down_w, down_t, up_w, up_t
+):
     for source, fore, back in ((fine, fine_w, fine_b), (coarse, coarse_w, coarse_b)):
         for along in range(3):
             rows = slice(C * along, C * (along + 1))
@@ -194,20 +276,23 @@
                     behind.append(source[9 * (2 - depth) + 3 * (2 - across) + along].T)
             fore[rows, :] = jnp.concatenate(ahead, axis=1)
             back[turned_rows, :] = jnp.concatenate(behind, axis=1)
-    for index in range(4):
-        pair = [down[2 * index], down[2 * index + 1]]
-        down_w[C * index : C * (index + 1), :] = jnp.concatenate(pair, axis=1)
+    down_w[...] = jnp.concatenate([down[index] for index in range(8)], axis=1)
+    up_t[...] = jnp.concatenate([up[index].T for index in range(8)], axis=1)
     for along in range(2):
-        row = jnp.concatenate([up[2 * index + along] for index in range(4)], axis=1)
-        up_w[C * along : C * (along + 1), :] = row
+        rows = slice(C * along, C * (along + 1))
+        turned = [down[2 * index + along].T for index in range(4)]
+        down_t[rows, :] = jnp.concatenate(turned, axis=1)
+        up_w[rows, :] = jnp.concatenate([up[2 * index + along] for index in range(4)], axis=1)
 
 
 def place_kernel(
     own, cot, y_left, y_right, flags, place, place_pair, fine, down, coarse, up,
-    grid, cot_grid, grad_r, live, fine_w, fine_b, coarse_w, coarse_b, down_w, up_w,
+    grid, cot_grid, grad_r, live, fine_w, fine_b, coarse_w, coarse_b, down_w, down_t, up_w, up_t,
     rows_in, rows_cot,
 ):
-    arrange_weights(fine, down, coarse, up, fine_w, fine_b, coarse_w, coarse_b, down_w, up_w)
+    arrange_weights(
+        fine, down, coarse, up, fine_w, fine_b, coarse_w, coarse_b, down_w, down_t, up_w, up_t
+    )
     number = cot.shape[0]
     last = number + 1
     rows_in[0:C, :] = y_left[0]
@@ -238,14 +323,16 @@
         if pair == 0:
             live[...] = placed[(last + 1) * C :, 0:LANES]
 
+    gather = gather_matrix()
+
     def rect_step(block):
         tiles = []
         for inner in range(4):
             tile = EDGE * block + 2 * inner
             tiles.append(jnp.concatenate([cot_grid[tile], cot_grid[tile + 1]], axis=0))
-        parts = dot(up_w[...], jnp.concatenate(tiles, axis=1), (0, 0))
+        parts = dot(up_t[...], jnp.concatenate(sub_stack(tiles, gather), axis=1))
         for inner in range(4):
-            grad_r[4 * block + inner] = gather_sub(parts[:, LANES * inner : LANES * (inner + 1)])
+            grad_r[4 * block + inner] = lane_block(parts, inner)
 
     loop(0, pairs, rect_step, 2)
 
@@ -255,19 +342,18 @@
 
 
 def conv_steps(parts, weight, load, tiles, step, first, unroll):
-    masks = depth_masks(step, first)
+    matrix = depth_matrix(step, first)
     spare = jnp.zeros((3 * C, LANES), F32)
     parts[0] = spare
     parts[tiles + 1] = spare
 
     def body(index):
         tile = 4 * index
+        cols = depth_stack([load(tile + i) for i in range(4)], matrix)
         for pair in range(2):
-            at = tile + 2 * pair
-            cols = [depth_columns(load(at + i), masks, step) for i in range(2)]
-            out = dot(weight[...], jnp.concatenate(cols, axis=1))
-            parts[at + 1] = out[:, :LANES]
-            parts[at + 2] = out[:, LANES:]
+            out = dot(weight[...], jnp.concatenate(cols[2 * pair : 2 * pair + 2], axis=1))
+            parts[tile + 2 * pair + 1] = lane_block(out, 0)
+            parts[tile + 2 * pair + 2] = lane_block(out, 1)
 
     loop(0, tiles // 4, body, unroll)
 
@@ -300,10 +386,12 @@
                 grid[tile] = grid_own[tile] + halo
         if pair == 0:
             live_all[...] = live_own[...] + placed[(last + 1) * C :, 0:LANES]
-    live[...] = join_halves(live_all[0:16, :], live_all[8:24, :])
+    own = is_own(lane_ids(16))
+    live[...] = jnp.where(own, live_all[0:16, :], roll(live_all[8:24, :], 8))
     tiles = grid.shape[0]
     conv_steps(fine_p, fine_w, lambda tile: across_columns(grid[tile], 1), tiles, 16, 0, 2)
     anchors = anchor_mask(0)
+    gather = gather_matrix()
 
     def lower_step(block):
         alive = jnp.broadcast_to(live_all[pl.ds(block, 1), :], (C, LANES))
@@ -317,23 +405,32 @@
                 hidden_all[tile] = value
                 actives.append(silu_parts(value)[0].astype(BF16))
             pairs.append(jnp.concatenate(actives, axis=0))
-        parts = dot(down_w[...], jnp.concatenate(pairs, axis=1))
+        parts = dot(down_w[...], jnp.concatenate(sub_stack(pairs, gather), axis=1))
         for inner in range(4):
-            total = gather_sub(parts[:, LANES * inner : LANES * (inner + 1)])
-            lowered[4 * block + inner] = (total * keep).astype(BF16)
+            lowered[4 * block + inner] = (lane_block(parts, inner) * keep).astype(BF16)
 
     loop(0, last + 1, lower_step, 2)
     pairs = hidden.shape[0] // EDGE
     shift = last - pairs + 1
 
+    own_lanes = is_own(lane_ids(C))
+    turn = lane_matrix(LANES, [lambda lane: (lane - 8) % LANES])
+    across = pair_matrix_across(2)
+
     def pair_step(block):
+        first = EDGE * (block + shift)
+        upper = jnp.concatenate([hidden_all[first + inner] for inner in range(EDGE)], axis=0)
+        high = upper.astype(BF16)
+        low = (upper - high.astype(F32)).astype(BF16)
+        turned = dot(high, turn) + dot(low, turn)
         for inner in range(EDGE):
             tile = EDGE * block + inner
-            hidden[tile] = join_halves(hidden_all[tile], hidden_all[tile + EDGE * shift])
-        for inner in range(4):
-            tile = 4 * block + inner
-            lower, upper = lowered[tile], lowered[tile + 4 * shift]
-            low_cols[tile] = pair_columns(join_halves(lower, upper), join_halos(lower, upper), 2)
+            part = turned[C * inner : C * (inner + 1)]
+            hidden[tile] = jnp.where(own_lanes, hidden_all[tile], part)
+        lowers = [lowered[4 * block + inner] for inner in range(4)]
+        uppers = [lowered[4 * (block + shift) + inner] for inner in range(4)]
+        for inner, cols in enumerate(pair_stack(lowers, uppers, across)):
+            low_cols[4 * block + inner] = cols
 
     loop(0, pairs, pair_step, 2)
     conv_steps(coarse_p, coarse_w, lambda tile: low_cols[tile], 4 * pairs, 32, 4, 2)
@@ -349,19 +446,34 @@
             grad_c[coarse] = (grad_r[coarse] * slope * keep).astype(BF16)
 
     loop(0, pairs, grad_step, 2)
-    ids = lane_ids(C)
-    zero = jnp.zeros((C, LANES), BF16)
-    half = 2 * number
-    for out, lane in ((pack_low, 4), (pack_high, 10)):
-        for group in range(out.shape[0]):
-            total = zero
-            for coarse in range(max(2, 32 * group), min(2 * half + 6, 32 * group + 32)):
-                upper = coarse >= half + 4
-                tile = grad_c[coarse - half] if upper else grad_c[coarse]
-                at = lane + 8 if upper else lane
-                picked = jnp.where(ids % 32 == at, tile, zero)
-                total = total + roll(picked, coarse % 32 - at)
-            out[group] = total
+    pack_columns(grad_c, pack_low, pack_high, 2)
+
+
+def pack_columns(tiles, low, high, step):
+    groups = low.shape[0]
+    rows = [
+        jnp.concatenate([tiles[8 * group + inner] for inner in range(8)], axis=1)
+        for group in range(groups)
+    ]
+    packed = move(jnp.concatenate(rows, axis=0), pack_matrix(step))
+    for group in range(groups):
+        part = packed[C * group : C * (group + 1)]
+        low[group] = lane_block(part, 0)
+        high[group] = lane_block(part, 1)
+
+
+def fill_columns(tiles, from_left, from_right, out, step):
+    matrix = inner_matrix(step)
+    left_matrix, right_matrix = unpack_matrix(step, False), unpack_matrix(step, True)
+
+    def body(group):
+        left = dot(from_left[group], left_matrix)
+        right = dot(from_right[group], right_matrix)
+        at = [8 * group + inner for inner in range(8)]
+        for tile, cols in zip(at, halo_stack([tiles[i] for i in at], left, right, matrix)):
+            out[tile] = cols
+
+    loop(0, from_left.shape[0], body)
 
 
 def to_blocks(slots, rows_out, place_back, flat, out):
@@ -390,11 +502,12 @@
 
 def output_kernel(slots, hidden, rects, live, place_back, up_w, out, rows_out, flat):
     pairs = hidden.shape[0] // EDGE
+    spread = spread_matrix()
 
     def block_step(block):
         alive = jnp.broadcast_to(live[pl.ds(block, 1), :], (C, LANES))
         start = pl.multiple_of((block - 1) * C, 16)
-        spreads = [spread_sub(rects[4 * block + inner]) for inner in range(4)]
+        spreads = sub_stack([rects[4 * block + inner] for inner in range(4)], spread)
         upward = dot(up_w[...], jnp.concatenate(spreads, axis=1))
         for inner in range(4):
             for half in range(2):
@@ -412,15 +525,12 @@
     up_g[...] = jnp.zeros_like(up_g)
     coarse_g[...] = jnp.zeros_like(coarse_g)
 
+    spread = spread_matrix()
+
     def up_step(block):
-        spreads = []
-        pairs = []
-        for inner in range(4):
-            coarse = 4 * block + inner
-            spreads.append(spread_sub(rects[coarse]))
-            pairs.append(
-                jnp.concatenate([cot_grid[2 * coarse], cot_grid[2 * coarse + 1]], axis=0)
-            )
+        at = [4 * block + inner for inner in range(4)]
+        spreads = sub_stack([rects[tile] for tile in at], spread)
+        pairs = [jnp.concatenate([cot_grid[2 * i], cot_grid[2 * i + 1]], axis=0) for i in at]
         up_g[:, 0 : 2 * C] += dot(
             jnp.concatenate(spreads, axis=1), jnp.concatenate(pairs, axis=1), (1, 1)
         )
@@ -435,11 +545,11 @@
         grad_own[coarse] = grad_c[coarse]
 
     loop(4, tiles - 4, copy_step, 8)
-    masks = depth_masks(32, 4)
+    matrix = depth_matrix(32, 4)
 
     def weight_step(index):
         at = [2 + 4 * index + inner for inner in range(4)]
-        rights = [depth_columns(low_cols[tile], masks, 32) for tile in at]
+        rights = depth_stack([low_cols[tile] for tile in at], matrix)
         coarse_g[0 : 9 * C, :] += dot(
             jnp.concatenate(rights, axis=1), stacks(grad_own, at), (1, 1)
         )
@@ -450,28 +560,25 @@
 
 
 def backward_kernel(
-    grad_c, from_left, from_right, hidden, cot_grid, live, coarse_w, down_w,
+    grad_c, from_left, from_right, hidden, cot_grid, live, coarse_w, down_t,
     grad_h, grad_d, pack_low, pack_high, coarse_p, grad_x,
 ):
     tiles = grad_c.shape[0]
-    half = tiles - 8
-    for coarse in range(tiles):
-        first, second = coarse // 32, (coarse + half) // 32
-        halo = packed_halo(from_left, from_right, first, second, coarse % 32, 2)
-        grad_x[coarse] = pair_columns(grad_c[coarse], halo, 2)
+    fill_columns(grad_c, from_left, from_right, grad_x, 2)
     conv_steps(coarse_p, coarse_w, lambda tile: grad_x[tile], tiles, 32, 4, 2)
     anchors = anchor_mask(4)
+    spread = spread_matrix()
 
     def step(block):
         alive = jnp.broadcast_to(live[pl.ds(block, 1), :], (C, LANES))
         keep = alive * anchors
-        spreads = []
+        downs = []
         for inner in range(4):
             coarse = 4 * block + inner
             down = (conv_sum(coarse_p, coarse) * keep).astype(BF16)
             grad_d[coarse] = down
-            spreads.append(spread_sub(down))
-        acts = dot(down_w[...], jnp.concatenate(spreads, axis=1), (0, 0))
+            downs.append(down)
+        acts = dot(down_t[...], jnp.concatenate(sub_stack(downs, spread), axis=1))
         for inner in range(4):
             for side in range(2):
                 tile = EDGE * block + 2 * inner + side
@@ -481,20 +588,7 @@
                 grad_h[tile] = (grad * alive).astype(BF16)
 
     loop(0, tiles // 4, step, 2)
-    fine = 2 * tiles
-    shift = fine - 16
-    ids = lane_ids(C) % 16
-    zero = jnp.zeros((C, LANES), BF16)
-    for out, lane in ((pack_low, 4), (pack_high, 11)):
-        for group in range(out.shape[0]):
-            total = zero
-            for tile in range(16 * group, 16 * group + 16):
-                upper = tile >= shift + 8
-                source = grad_h[tile - shift] if upper else grad_h[tile]
-                at = lane + 8 if upper else lane
-                picked = jnp.where(ids == at % 16, source, zero)
-                total = total + roll(picked, tile % 16 - at)
-            out[group] = total
+    pack_columns(grad_h, pack_low, pack_high, 1)
 
 
 def weight_kernel(grid, grad_h, grad_d, hidden, early, joined, grad_own, fine_g, down_g):
@@ -511,15 +605,14 @@
         grad_own[tile] = grad_h[tile]
 
     loop(8, tiles - 8, copy_step, 8)
-    masks = depth_masks(16, 4)
+    matrix = depth_matrix(16, 4)
+    across = pair_matrix_across(1)
+    spread = spread_matrix()
 
     def fine_step(index):
         at = [4 + 8 * index + inner for inner in range(8)]
-        rights = []
-        for tile in at:
-            lower, upper = grid[tile], grid[tile + shift]
-            base = pair_columns(join_halves(lower, upper), join_halos(lower, upper), 1)
-            rights.append(depth_columns(base, masks, 16))
+        bases = pair_stack([grid[i] for i in at], [grid[i + shift] for i in at], across)
+        rights = depth_stack(bases, matrix)
         fine_g[0 : 9 * C, :] += dot(
             jnp.concatenate(rights, axis=1), stacks(grad_own, at), (1, 1)
         )
@@ -527,11 +620,10 @@
     loop(0, (tiles - 8) // 8, fine_step)
 
     def down_step(index):
-        lefts = []
+        at = [4 + 4 * index + inner for inner in range(4)]
+        lefts = sub_stack([grad_d[i] for i in at], spread)
         rights = []
-        for inner in range(4):
-            coarse = 4 + 4 * index + inner
-            lefts.append(spread_sub(grad_d[coarse]))
+        for coarse in at:
             actives = [silu_parts(hidden[2 * coarse + side])[0].astype(BF16) for side in range(2)]
             rights.append(jnp.concatenate(actives, axis=0))
         down_g[:, 0 : 2 * C] += dot(
@@ -549,16 +641,7 @@
     fine_p, rows_out, flat, grad_x,
 ):
     tiles = grad_h.shape[0]
-    shift = tiles - 16
-
-    def fill_step(group):
-        for inner in range(16):
-            tile = 16 * group + inner
-            second = group + shift // 16
-            halo = packed_halo(from_left, from_right, group, second, inner, 1)
-            grad_x[tile] = pair_columns(grad_h[tile], halo, 1)
-
-    loop(0, tiles // 16, fill_step)
+    fill_columns(grad_h, from_left, from_right, grad_x, 1)
     conv_steps(fine_p, fine_w, lambda tile: grad_x[tile], tiles, 16, 4, 2)
 
     def block_step(block):
@@ -652,8 +735,8 @@
     tiles = EDGE * (number + 2)
     coarse_tiles = tiles // 2
     pairs = number // 2 + 2
-    groups = -(-coarse_tiles // 32)
-    fine_groups = tiles // 16
+    groups = pairs // 2
+    fine_groups = pairs
 
     fine_3, down_3, coarse_3 = (
         weight.transpose(1, 0, 2) for weight in (fine_weight, down_weight, coarse_weight)
@@ -681,7 +764,7 @@
     c_left = send(corner_high, 1, 0)
     c_right = send(corner_low, -1, 0)
     (grid_own, cot_grid, grad_r, live_own, fine_fore, fine_back, coarse_fore, coarse_back, down_w,
-     up_w) = call(
+     down_t, up_w, up_t) = call(
         place_kernel,
         (own, cot, y_left, y_right, flags, place_own, place_pair, fine_3, down_3, coarse_3,
          up_weight),
@@ -692,7 +775,9 @@
             ((C, LANES), F32),
         ]
         + [((3 * C, 9 * C), BF16)] * 4
-        + [((4 * C, 2 * C), BF16), ((2 * C, 4 * C), BF16)],
+        + [((C, 8 * C), BF16)]
+        + [((2 * C, 4 * C), BF16)] * 2
+        + [((C, 8 * C), BF16)],
         [(((number + 3) * C, VOX), BF16), ((pairs * C, 1024), BF16)],
         flops=8 * 10**9,
     )
@@ -731,7 +816,7 @@
     )
     grad_h, grad_d, edge_low, edge_high = call(
         backward_kernel,
-        (grad_c, grad_left, grad_right, hidden, cot_grid, live, coarse_back, down_w),
+        (grad_c, grad_left, grad_right, hidden, cot_grid, live, coarse_back, down_t),
         [
             ((EDGE * pairs, C, LANES), BF16),
             ((4 * pairs, C, LANES), BF16),

time: 133 us -> 142 us (1.068)
  Pallas kernels: 65.5 us -> 75.8 us
  waiting for transfers between devices: 6.27 us -> 4.08 us
    pallas_call x10, Pallas kernels: 65.5 us -> 75.8 us  [call(): pl.pallas_call(kernel, out_shape=tuple((jax.ShapeDtypeStruct(s, d) for s,...]
    ppermute x10, waiting for transfers between devices: 6.27 us -> 4.08 us  [send(): return lax.ppermute(array, ('gx', 'gy'), pairs)]
  transfers between devices with their start and end apart: 11 -> 11, of which waited for: 2 -> 2; matrix products, arithmetic and copies ran while one was open for 0% -> 0% of each run, Pallas kernels for 24% -> 26%
where the time goes in v6:
time: 142 us
  Pallas kernels  75.8 us (53%)
  starting transfers between devices  29.7 us (21%)
  blocking collectives  21.4 us (15%)
  local copies, waits for them, and re-layouts  9.01 us (6%)
  waiting for transfers between devices  4.08 us (3%)
  between operations  1.74 us (1%)
    pallas_call x10, Pallas kernels, call(): pl.pallas_call(kernel, out_shape=tuple((jax.ShapeDtypeStruct(s, d) for s,...  75.8 us
    ppermute x10, starting transfers between devices, send(): return lax.ppermute(array, ('gx', 'gy'), pairs)  26.8 us
    all_to_all x1, blocking collectives, reduce_all(): mine = lax.all_to_all(joined.reshape(devices, share, LANES), axes, 0, 0)  21.4 us
    unnamed x36, local copies, waits for them, and re-layouts  8.21 us
    ppermute x10, waiting for transfers between devices, send(): return lax.ppermute(array, ('gx', 'gy'), pairs)  4.08 us
  transfers between devices with their start and end apart: 11, of which 2 were waited for; matrix products, arithmetic and copies ran while one was open for 0% of the time, Pallas kernels for 26%

profile of v6, /device:TPU:0, one launch (start us, length us, event | category | flops | bytes accessed | tf_op | source)
XLA Modules:
  0.0 141.8 jit_solution(1156190534606373465)
XLA Ops:
  1.4 3.2 %prepare_kernel.1 = (bf16[16,48,512]{2,1,0:T(8,128)(2,1)}, bf16[16,48,512]{2,1,0:T(8,128)(2,1)}, bf16[48,512]{1,0:T(8,128)(2,1)}, bf16[17,48,256]{2,1,0:T(8,128)...) custom-call(s32[16]{0:T(128)} %bitcast.21, s32[1]{0:T(128)} %bitcast.16.count, ...), custom_call_target="tpu_custom_call" | custom-call | bytes 4849732 | tf_op jit(solution)/shard_map/prepare_kernel/pallas_call | solution.py:685
  4.7 2.4 %collective-permute-start = (bf16[3,48,512]{2,1,0:T(8,128)(2,1)}, bf16[3,48,512]{2,1,0:T(8,128)(2,1)S(1)}, u32[]{:S(2)}, u32[]{:S(2)}) collective-permute-start(bf16[3,48,512]{2,1,0:T(8,128)(2,1)} %get-tuple-element.48), channel_id=1, source_target_pairs={{0,1},{1,2},{2,3},{4,5},{5,6},{6,7},{8,9},{9,10},{10,11},{12,13},{... | collective-permute-start | bytes 442376 | tf_op jit(solution)/shard_map/ppermute | solution.py:705
  7.0 1.3 collective-permute-start.1
  8.3 4.2 %collective-permute-start.2 = (bf16[17,48,256]{2,1,0:T(8,128)(2,1)}, bf16[17,48,256]{2,1,0:T(8,128)(2,1)S(1)}, u32[]{:S(2)}, u32[]{:S(2)}) collective-permute-start(bf16[17,48,256]{2,1,0:T(8,128)(2,1)} %get-tuple-element.55), channel_id=1, source_target_pairs={{0,4},{1,5},{2,6},{3,7},{4,8},{5,9},{6,10},{7,11},{8,12},{9,13},{1... | collective-permute-start | bytes 1253384 | tf_op jit(solution)/shard_map/ppermute | solution.py:705
  12.6 1.3 collective-permute-start.3
  14.0 0.8 copy-done.1
  14.7 0.2 corner_kernel.1
  15.0 4.5 %collective-permute-start.4 = (bf16[3,48,256]{2,1,0:T(8,128)(2,1)S(1)}, bf16[3,48,256]{2,1,0:T(8,128)(2,1)S(1)}, u32[]{:S(2)}, u32[]{:S(2)}) collective-permute-start(bf16[3,48,256]{2,1,0:T(8,128)(2,1)S(1)} %get-tuple-element.57), channel_id=1, source_target_pairs={{0,4},{1,5},{2,6},{3,7},{4,8},{5,9},{6,10},{7,11},{8,12},{9,13},{1... | collective-permute-start | bytes 221192 | tf_op jit(solution)/shard_map/ppermute | solution.py:705
  19.5 1.3 collective-permute-start.5
  20.9 1.1 copy-done.3
  22.0 1.1 copy-done.4
  23.1 1.6 %copy-done.9 = bf16[1024,1024]{1,0:T(8,128)(2,1)S(1)} copy-done((bf16[1024,1024]{1,0:T(8,128)(2,1)S(1)}, bf16[1024,1024]{1,0:T(8,128)(2,1)}, u32[]{:S(2)}) %copy-start.9) | copy-done | bytes 2097176
  24.7 1.2 copy-done.11
  26.0 5.3 %place_kernel.1 = (bf16[144,48,128]{2,1,0:T(8,128)(2,1)S(1)}, bf16[80,48,128]{2,1,0:T(8,128)(2,1)S(1)}, f32[40,48,128]{2,1,0:T(8,128)S(1)}, f32[48,128]{1,0:T(8,...) custom-call(bf16[16,48,512]{2,1,0:T(8,128)(2,1)S(1)} %copy-done.3, ...), custom_call_target="tpu_custom_call" | custom-call | flops 8000000000 | bytes 9790464 | tf_op jit(solution)/shard_map/place_kernel/pallas_call | solution.py:685
  31.3 2.1 %collective-permute-done.4.c_left = bf16[3,48,256]{2,1,0:T(8,128)(2,1)S(1)} collective-permute-done((bf16[3,48,256]{2,1,0:T(8,128)(2,1)S(1)}, bf16[3,48,256]{2,1,0:T(8,128)(2,1)S(1)}, u32[]{:S(2)}, u32[]{:S(2)}) %collective-permute-start.4) | collective-permute-done | bytes 73760 | tf_op jit(solution)/shard_map/ppermute | solution.py:705
  33.4 25.5 %forward_kernel.1 = (bf16[144,48,128]{2,1,0:T(8,128)(2,1)S(1)}, f32[80,48,128]{2,1,0:T(8,128)S(1)}, bf16[40,144,128]{2,1,0:T(8,128)(2,1)S(1)}, bf16[40,48,128]{2...) custom-call(bf16[144,48,128]{2,1,0:T(8,128)(2,1)S(1)} %get-tuple-ele, ...), custom_call_target="tpu_custom_call" | custom-call | flops 8000000000 | bytes 11418624 | tf_op jit(solution)/shard_map/forward_kernel/pallas_call | solution.py:685
  58.9 4.4 %collective-permute-start.6 = (bf16[5,48,128]{2,1,0:T(8,128)(2,1)S(1)}, bf16[5,48,128]{2,1,0:T(8,128)(2,1)S(1)}, u32[]{:S(2)}, u32[]{:S(2)}) collective-permute-start(bf16[5,48,128]{2,1,0:T(8,128)(2,1)S(1)} %get-tuple-element.67), channel_id=1, source_target_pairs={{0,4},{1,5},{2,6},{3,7},{4,8},{5,9},{6,10},{7,11},{8,12},{9,13},{1... | collective-permute-start | bytes 184328 | tf_op jit(solution)/shard_map/ppermute | solution.py:705
  63.3 1.3 collective-permute-start.7
  64.6 4.7 %side_kernel.1.early = bf16[768,128]{1,0:T(8,128)(2,1)S(1)} custom-call(bf16[40,48,128]{2,1,0:T(8,128)(2,1)S(1)} %get-tuple-element.63.rects, bf16[80,48,128]{2,1,0:T(8,128)(2,1)S(1)} %get-tuple-element.69.cot_grid, bf16[40,144,128]{2,1,0:T(8,128)(2,1)S(1)} %get-tuple-element.75.low_cols, bf16[40,48,128]{2,1,0:T(8,128)(2,1)S(1)} %get-tuple-element.66.grad_c), custom_call_target="tpu_custom_call" | custom-call | flops 8000000000 | bytes 3637248 | tf_op jit(solution)/shard_map/side_kernel/pallas_call | solution.py:685
  69.3 1.9 %collective-permute-done.7.from_right = bf16[5,48,128]{2,1,0:T(8,128)(2,1)S(1)} collective-permute-done((bf16[5,48,128]{2,1,0:T(8,128)(2,1)S(1)}, bf16[5,48,128]{2,1,0:T(8,128)(2,1)S(1)}, u32[]{:S(2)}, u32[]{:S(2)}) %collective-permute-start.7) | collective-permute-done | bytes 61472 | tf_op jit(solution)/shard_map/ppermute | solution.py:705
  71.3 8.1 %backward_kernel.1 = (bf16[80,48,128]{2,1,0:T(8,128)(2,1)S(1)}, bf16[40,48,128]{2,1,0:T(8,128)(2,1)S(1)}, bf16[10,48,128]{2,1,0:T(8,128)(2,1)S(1)}, bf16[10,48,128]{2,1,0:T(8,128)(2,1)S(1)}) custom-call(bf16[40,48,128]{2,1,0:T(8,128)(2,1)S(1)} %get-tuple-element.66.grad_c, bf16[5,48,128]{2,1,0:T(8,128)(2,1)S(1)} %collective-permute-done.6.from_left, ...), custom_call_target="tpu_custom_call" | custom-call | flops 8000000000 | bytes 5453312 | tf_op jit(solution)/shard_map/backward_kernel/pallas_call | solution.py:685
  79.4 4.8 %collective-permute-start.8 = (bf16[10,48,128]{2,1,0:T(8,128)(2,1)S(1)}, bf16[10,48,128]{2,1,0:T(8,128)(2,1)S(1)}, u32[]{:S(2)}, u32[]{:S(2)}) collective-permute-start(bf16[10,48,128]{2,1,0:T(8,128)(2,1)S(1)} %get-tuple-element.76), channel_id=1, source_target_pairs={{0,4},{1,5},{2,6},{3,7},{4,8},{5,9},{6,10},{7,11},{8,12},{9,13},{1... | collective-permute-start | bytes 368648 | tf_op jit(solution)/shard_map/ppermute | solution.py:705
  84.2 1.3 collective-permute-start.9
  85.5 10.2 %weight_kernel.1 = bf16[1536,128]{1,0:T(8,128)(2,1)S(1)} custom-call(bf16[144,48,128]{2,1,0:T(8,128)(2,1)S(1)} %get-tuple-element.73.grid, bf16[80,48,128]{2,1,0:T(8,128)(2,1)S(1)} %get-tuple-element.72.grad_h, bf16[40,48,128]{2,1,0:T(8,128)(2,1)S(1)} %get-tuple-element.74.grad_d, f32[80,48,128]{2,1,0:T(8,128)S(1)} %get-tuple-element.62.hidden, ...), custom_call_target="tpu_custom_call" | custom-call | flops 12000000000 | bytes 5799936 | tf_op jit(solution)/shard_map/weight_kernel/pallas_call | solution.py:685
  95.8 21.4 %all_to_all.10 = bf16[32,48,128]{2,1,0:T(8,128)(2,1)S(1)} all-to-all(bf16[32,48,128]{2,1,0:T(8,128)(2,1)S(1)} %bitcast.18), channel_id=1, replica_groups=mesh['gx'=8,'gy'=4] {'gx','gy'}, dimensions={0} | all-to-all | bytes 786432 | tf_op jit(solution)/shard_map/all_to_all | solution.py:714
  117.2 0.8 broadcast_in_dim.2
  118.0 2.8 %all-to-all-start.1 = ((bf16[32,48,128]{2,1,0:T(8,128)(2,1)}), bf16[32,48,128]{2,1,0:T(8,128)(2,1)S(1)}, u32[]{:S(2)}, u32[]{:S(2)}) async-start(bf16[32,48,128]{2,1,0:T(8,128)(2,1)} %broadcast_in_dim.2), calls=%async_computation.1 | async-start | bytes 786432 | tf_op jit(solution)/shard_map/all_to_all | solution.py:717
  120.9 1.5 %copy-done.13 = f32[80,48,128]{2,1,0:T(8,128)S(1)} copy-done((f32[80,48,128]{2,1,0:T(8,128)S(1)}, f32[80,48,128]{2,1,0:T(8,128)}, u32[]{:S(2)}) %copy-start.13) | copy-done | bytes 1966104
  122.4 4.7 %output_kernel.1 = bf16[16,48,512]{2,1,0:T(8,128)(2,1)} custom-call(s32[16]{0:T(128)S(1)} %bitcast.22, f32[80,48,128]{2,1,0:T(8,128)S(1)} %copy-done.13, bf16[40,48,128]{2,1,0:T(8,128)(2,1)S(1)} %get-tuple-element.63.rects, f32[16,128]{1,0:T(8,128)S(1)} %get-tuple-element.64.live, bf16[1024,1024]{1,0:T(8,128)(2,1)S(1)} %copy-done.8, ...), custom_call_target="tpu_custom_call" | custom-call | flops 8000000000 | bytes 5386304 | tf_op jit(solution)/shard_map/output_kernel/pallas_call | solution.py:685
  127.1 12.3 %input_kernel.1 = bf16[16,48,512]{2,1,0:T(8,128)(2,1)} custom-call(s32[16]{0:T(128)S(1)} %bitcast.23, bf16[80,48,128]{2,1,0:T(8,128)(2,1)S(1)} %copy-done.15, bf16[10,48,128]{2,1,0:T(8,128)(2,1)S(1)} %collective-permute-done.8.from_left, bf16[10,48,128]{2,1,0:T(8,128)(2,1)S(1)} %collective-permute-done.9.from_right, f32[16,128]{1,0:T(8,128)S(1)} %get-tuple-element.64.live, ...), custom_call_target="tpu_custom_call" | custom-call | flops 8000000000 | bytes 4245056 | tf_op jit(solution)/shard_map/input_kernel/pallas_call | solution.py:685
  139.4 1.6 %finish_kernel.1 = (f32[27,48,48]{2,1,0:T(8,128)}, f32[8,48,48]{2,1,0:T(8,128)S(1)}, f32[27,48,48]{2,1,0:T(8,128)}, f32[8,48,48]{2,1,0:T(8,128)}) custom-call(bf16[1536,128]{1,0:T(8,128)(2,1)S(1)} %bitcast.17), custom_call_target="tpu_custom_call" | custom-call | bytes 1038336 | tf_op jit(solution)/shard_map/finish_kernel/pallas_call | solution.py:685
  141.0 0.7 copy.20
  (39 shorter events, 0.2 us)
Async XLA Ops:
  0.6 13.3 %copy-start = (bf16[512,512]{1,0:T(8,128)(2,1)S(1)}, bf16[512,512]{1,0:T(8,128)(2,1)}, u32[]{:S(2)}) copy-start(bf16[512,512]{1,0:T(8,128)(2,1)} %constant.18.clone.pick) | copy-start | bytes 1572868
  0.6 13.2 %copy-start.16 = (bf16[48,8,48]{2,1,0:T(8,128)(2,1)S(1)}, bf16[48,8,48]{2,1,0:T(8,128)(2,1)}, u32[]{:S(2)}) copy-start(bf16[48,8,48]{2,1,0:T(8,128)(2,1)} %param.18) | copy-start | bytes 110596
  0.7 20.2 %copy-start.7 = (bf16[8,48,48]{2,1,0:T(8,128)(2,1)S(1)}, bf16[8,48,48]{2,1,0:T(8,128)(2,1)}, u32[]{:S(2)}) copy-start(bf16[8,48,48]{2,1,0:T(8,128)(2,1)} %up.1) | copy-start | bytes 110596
  0.7 20.2 %copy-start.6 = (bf16[48,27,48]{2,0,1:T(8,128)(2,1)S(1)}, bf16[48,27,48]{2,0,1:T(8,128)(2,1)}, u32[]{:S(2)}) copy-start(bf16[48,27,48]{2,0,1:T(8,128)(2,1)} %param.19) | copy-start | bytes 373252
  0.7 20.2 %copy-start.5 = (bf16[48,27,48]{2,0,1:T(8,128)(2,1)S(1)}, bf16[48,27,48]{2,0,1:T(8,128)(2,1)}, u32[]{:S(2)}) copy-start(bf16[48,27,48]{2,0,1:T(8,128)(2,1)} %param.17) | copy-start | bytes 373252
  4.7 9.3 %collective-permute-start = (bf16[3,48,512]{2,1,0:T(8,128)(2,1)}, bf16[3,48,512]{2,1,0:T(8,128)(2,1)S(1)}, u32[]{:S(2)}, u32[]{:S(2)}) collective-permute-start(bf16[3,48,512]{2,1,0:T(8,128)(2,1)} %get-tuple-element.48), channel_id=1, source_target_pairs={{0,1},{1,2},{2,3},{4,5},{5,6},{6,7},{8,9},{9,10},{10,11},{12,13},{... | collective-permute-start | bytes 442376 | tf_op jit(solution)/shard_map/ppermute | solution.py:705
  7.0 6.9 %collective-permute-start.1 = (bf16[3,48,512]{2,1,0:T(8,128)(2,1)}, bf16[3,48,512]{2,1,0:T(8,128)(2,1)S(1)}, u32[]{:S(2)}, u32[]{:S(2)}) collective-permute-start(bf16[3,48,512]{2,1,0:T(8,128)(2,1)} %get-tuple-element.49), channel_id=1, source_target_pairs={{1,0},{2,1},{3,2},{5,4},{6,5},{7,6},{9,8},{10,9},{11,10},{13,12},{... | collective-permute-start | bytes 442376 | tf_op jit(solution)/shard_map/ppermute | solution.py:705
  8.3 25.1 %collective-permute-start.2 = (bf16[17,48,256]{2,1,0:T(8,128)(2,1)}, bf16[17,48,256]{2,1,0:T(8,128)(2,1)S(1)}, u32[]{:S(2)}, u32[]{:S(2)}) collective-permute-start(bf16[17,48,256]{2,1,0:T(8,128)(2,1)} %get-tuple-element.55), channel_id=1, source_target_pairs={{0,4},{1,5},{2,6},{3,7},{4,8},{5,9},{6,10},{7,11},{8,12},{9,13},{1... | collective-permute-start | bytes 1253384 | tf_op jit(solution)/shard_map/ppermute | solution.py:705
  12.6 20.8 %collective-permute-start.3 = (bf16[17,48,256]{2,1,0:T(8,128)(2,1)}, bf16[17,48,256]{2,1,0:T(8,128)(2,1)S(1)}, u32[]{:S(2)}, u32[]{:S(2)}) collective-permute-start(bf16[17,48,256]{2,1,0:T(8,128)(2,1)} %get-tuple-element.56), channel_id=1, source_target_pairs={{4,0},{5,1},{6,2},{7,3},{8,4},{9,5},{10,6},{11,7},{12,8},{13,9},{1... | collective-permute-start | bytes 1253384 | tf_op jit(solution)/shard_map/ppermute | solution.py:705
  13.9 0.8 copy-start.1
  15.0 18.4 %collective-permute-start.4 = (bf16[3,48,256]{2,1,0:T(8,128)(2,1)S(1)}, bf16[3,48,256]{2,1,0:T(8,128)(2,1)S(1)}, u32[]{:S(2)}, u32[]{:S(2)}) collective-permute-start(bf16[3,48,256]{2,1,0:T(8,128)(2,1)S(1)} %get-tuple-element.57), channel_id=1, source_target_pairs={{0,4},{1,5},{2,6},{3,7},{4,8},{5,9},{6,10},{7,11},{8,12},{9,13},{1... | collective-permute-start | bytes 221192 | tf_op jit(solution)/shard_map/ppermute | solution.py:705
  19.5 13.8 %collective-permute-start.5 = (bf16[3,48,256]{2,1,0:T(8,128)(2,1)S(1)}, bf16[3,48,256]{2,1,0:T(8,128)(2,1)S(1)}, u32[]{:S(2)}, u32[]{:S(2)}) collective-permute-start(bf16[3,48,256]{2,1,0:T(8,128)(2,1)S(1)} %get-tuple-element.58), channel_id=1, source_target_pairs={{4,0},{5,1},{6,2},{7,3},{8,4},{9,5},{10,6},{11,7},{12,8},{13,9},{1... | collective-permute-start | bytes 221192 | tf_op jit(solution)/shard_map/ppermute | solution.py:705
  20.9 1.1 copy-start.3
  22.0 1.1 copy-start.4
  23.1 1.6 %copy-start.9 = (bf16[1024,1024]{1,0:T(8,128)(2,1)S(1)}, bf16[1024,1024]{1,0:T(8,128)(2,1)}, u32[]{:S(2)}) copy-start(bf16[1024,1024]{1,0:T(8,128)(2,1)} %constant.16.clone.place_pair) | copy-start | bytes 6291460
  24.7 1.2 copy-start.11
  26.0 7.4 %copy-start.10 = (bf16[512,1024]{1,0:T(8,128)(2,1)S(1)}, bf16[512,1024]{1,0:T(8,128)(2,1)}, u32[]{:S(2)}) copy-start(bf16[512,1024]{1,0:T(8,128)(2,1)} %constant.15.clone.place) | copy-start | bytes 3145732
  58.9 26.6 %copy-start.12 = (f32[80,48,128]{2,1,0:T(8,128)}, f32[80,48,128]{2,1,0:T(8,128)S(1)}, u32[]{:S(2)}) copy-start(f32[80,48,128]{2,1,0:T(8,128)S(1)} %get-tuple-element.62.hidden) | copy-start | bytes 5898244
  58.9 10.4 %collective-permute-start.6 = (bf16[5,48,128]{2,1,0:T(8,128)(2,1)S(1)}, bf16[5,48,128]{2,1,0:T(8,128)(2,1)S(1)}, u32[]{:S(2)}, u32[]{:S(2)}) collective-permute-start(bf16[5,48,128]{2,1,0:T(8,128)(2,1)S(1)} %get-tuple-element.67), channel_id=1, source_target_pairs={{0,4},{1,5},{2,6},{3,7},{4,8},{5,9},{6,10},{7,11},{8,12},{9,13},{1... | collective-permute-start | bytes 184328 | tf_op jit(solution)/shard_map/ppermute | solution.py:705
  63.3 8.0 %collective-permute-start.7 = (bf16[5,48,128]{2,1,0:T(8,128)(2,1)S(1)}, bf16[5,48,128]{2,1,0:T(8,128)(2,1)S(1)}, u32[]{:S(2)}, u32[]{:S(2)}) collective-permute-start(bf16[5,48,128]{2,1,0:T(8,128)(2,1)S(1)} %get-tuple-element.68), channel_id=1, source_target_pairs={{4,0},{5,1},{6,2},{7,3},{8,4},{9,5},{10,6},{11,7},{12,8},{13,9},{1... | collective-permute-start | bytes 184328 | tf_op jit(solution)/shard_map/ppermute | solution.py:705
  79.3 16.4 %copy-start.14 = (bf16[80,48,128]{2,1,0:T(8,128)(2,1)}, bf16[80,48,128]{2,1,0:T(8,128)(2,1)S(1)}, u32[]{:S(2)}) copy-start(bf16[80,48,128]{2,1,0:T(8,128)(2,1)S(1)} %get-tuple-element.72.grad_h) | copy-start | bytes 2949124
  79.4 16.4 %collective-permute-start.8 = (bf16[10,48,128]{2,1,0:T(8,128)(2,1)S(1)}, bf16[10,48,128]{2,1,0:T(8,128)(2,1)S(1)}, u32[]{:S(2)}, u32[]{:S(2)}) collective-permute-start(bf16[10,48,128]{2,1,0:T(8,128)(2,1)S(1)} %get-tuple-element.76), channel_id=1, source_target_pairs={{0,4},{1,5},{2,6},{3,7},{4,8},{5,9},{6,10},{7,11},{8,12},{9,13},{1... | collective-permute-start | bytes 368648 | tf_op jit(solution)/shard_map/ppermute | solution.py:705
  84.2 11.6 %collective-permute-start.9 = (bf16[10,48,128]{2,1,0:T(8,128)(2,1)S(1)}, bf16[10,48,128]{2,1,0:T(8,128)(2,1)S(1)}, u32[]{:S(2)}, u32[]{:S(2)}) collective-permute-start(bf16[10,48,128]{2,1,0:T(8,128)(2,1)S(1)} %get-tuple-element.77), channel_id=1, source_target_pairs={{4,0},{5,1},{6,2},{7,3},{8,4},{9,5},{10,6},{11,7},{12,8},{13,9},{1... | collective-permute-start | bytes 368648 | tf_op jit(solution)/shard_map/ppermute | solution.py:705
  95.8 25.1 %copy-start.2 = (s32[1,1,16]{2,1,0:T(1,128)S(1)}, s32[1,1,16]{2,1,0:T(1,128)}, u32[]{:S(2)}) copy-start(s32[1,1,16]{2,1,0:T(1,128)} %param.14) | copy-start | bytes 196
  95.8 25.1 %copy-start.8 = (bf16[1024,1024]{1,0:T(8,128)(2,1)S(1)}, bf16[1024,1024]{1,0:T(8,128)(2,1)}, u32[]{:S(2)}) copy-start(bf16[1024,1024]{1,0:T(8,128)(2,1)} %constant.17.clone.place_back) | copy-start | bytes 6291460
  118.0 21.4 %all-to-all-start.1 = ((bf16[32,48,128]{2,1,0:T(8,128)(2,1)}), bf16[32,48,128]{2,1,0:T(8,128)(2,1)S(1)}, u32[]{:S(2)}, u32[]{:S(2)}) async-start(bf16[32,48,128]{2,1,0:T(8,128)(2,1)} %broadcast_in_dim.2), calls=%async_computation.1 | async-start | bytes 786432 | tf_op jit(solution)/shard_map/all_to_all | solution.py:717
  120.9 1.5 %copy-start.13 = (f32[80,48,128]{2,1,0:T(8,128)S(1)}, f32[80,48,128]{2,1,0:T(8,128)}, u32[]{:S(2)}) copy-start(f32[80,48,128]{2,1,0:T(8,128)} %copy-done.12) | copy-start | bytes 5898244
  122.4 4.7 %copy-start.15 = (bf16[80,48,128]{2,1,0:T(8,128)(2,1)S(1)}, bf16[80,48,128]{2,1,0:T(8,128)(2,1)}, u32[]{:S(2)}) copy-start(bf16[80,48,128]{2,1,0:T(8,128)(2,1)} %copy-done.14) | copy-start | bytes 2949124

commit v7 on v5

--- a/solution.py
+++ b/solution.py
@@ -3,7 +3,6 @@
 
 import jax
 import jax.numpy as jnp
-import numpy as np
 from jax import lax
 from jax.experimental import pallas as pl
 from jax.experimental.pallas import tpu as pltpu
@@ -19,36 +18,39 @@
 SHIFTS = (0, 1, 16, 17)
 
 
-def placing_matrix():
-    place = np.zeros((1024, 8 * LANES), np.float32)
-    for z in range(8):
-        for y in range(8):
-            for x in range(8):
-                place[64 * z + 8 * x + y, LANES * y + 16 * z + x + 4] = 1.0
-            for x in range(4):
-                place[512 + 32 * z + 8 * x + y, LANES * y + 16 * z + x] = 1.0
-                place[768 + 32 * z + 8 * x + y, LANES * y + 16 * z + x + 12] = 1.0
-    return place
-
-
-def pair_matrix():
-    place = np.zeros((1024, 8 * LANES), np.float32)
-    for half in range(2):
-        for z in range(8):
-            for x in range(8):
-                for y in range(8):
-                    lane = (16 * z + 8 * half + x + 4) % LANES
-                    place[512 * half + 64 * z + 8 * x + y, LANES * y + lane] = 1.0
-    return place
-
-
-def edge_matrix():
-    pick = np.zeros((512, 512), np.float32)
-    for z in range(8):
-        for y in range(8):
-            for x in range(8):
-                pick[64 * z + 8 * x + y, 256 * (x // 4) + 32 * z + 8 * (x % 4) + y] = 1.0
-    return pick
+def marks(rows, columns, row_key, column_key):
+    across = column_key(lax.broadcasted_iota(jnp.int32, (1, columns), 1))
+    down = row_key(lax.broadcasted_iota(jnp.int32, (rows, 1), 0))
+    return jnp.where(down == across, 1.0, 0.0).astype(BF16)
+
+
+def plain(index):
+    return index
+
+
+def own_source(column):
+    lane, y = column % LANES, column // LANES
+    x = lane % 16 - 4
+    return jnp.where((x >= 0) & (x < 8), 64 * (lane // 16) + 8 * x + y, -1)
+
+
+def halo_source(column):
+    lane, y = column % LANES, column // LANES
+    x = lane % 16
+    at = 24 * (lane // 16) + y
+    left = jnp.where((x >= 1) & (x < 4), at + 8 * (x - 1), -1)
+    return jnp.where((x >= 12) & (x < 15), at + 8 * (x - 12) + 256, left)
+
+
+def pair_source(column):
+    lane, y = (column - 4) % LANES, column // LANES
+    return 512 * (lane % 16 // 8) + 64 * (lane // 16) + 8 * (lane % 8) + y
+
+
+def edge_source(column):
+    at, side = column % 256, column // 256
+    x = at % 24 // 8 + 5 * side
+    return jnp.where(at < 192, 64 * (at // 24) + 8 * x + at % 8, -1)
 
 
 def dot(left, right, contract=(1, 0)):
@@ -138,12 +140,31 @@
     lax.fori_loop(low, high, step, 0, unroll=unroll)
 
 
+def join_rows(first, second):
+    low = lane_ids(C) < 64
+    lead = roll(second[:, :LANES], 64)
+    parts = [
+        first[:, :LANES],
+        jnp.where(low, first[:, LANES:], lead),
+        jnp.where(low, lead, roll(second[:, LANES:], 64)),
+    ]
+    return jnp.concatenate(parts, axis=1)
+
+
+def split_rows(joined):
+    low = lane_ids(C) < 64
+    middle = roll(joined[:, LANES : 2 * LANES], 64)
+    last = roll(joined[:, 2 * LANES :], 64)
+    second = jnp.concatenate([jnp.where(low, middle, last), last], axis=1)
+    return joined[:, : 2 * LANES], second
+
+
 def prepare_kernel(
-    slots, count, feats, cots, pick, own, cot, flag_rows, x_low, x_high, y_low, y_high, rows_in
+    slots, count, feats, cots, own, cot, flag_rows, x_low, x_high, y_low, y_high, rows_in
 ):
     number = feats.shape[0]
-    rows = lax.broadcasted_iota(jnp.int32, (C, VOX), 0)
-    flags = jnp.zeros((C, VOX), F32)
+    rows = lax.broadcasted_iota(jnp.int32, (16, LANES), 0)
+    flags = jnp.zeros((16, LANES), F32)
     first = jnp.zeros((), F32)
     last = jnp.zeros((), F32)
     zero = jnp.zeros((C, VOX), BF16)
@@ -155,30 +176,34 @@
         own[place] = block
         rows_in[pl.ds(pl.multiple_of(place * C, 16), C), :] = block
         cot[place] = jnp.where(live, cots[slot], zero)
-        flags = jnp.where(rows == place + 1, alive, flags)
+        flags = jnp.where(rows == place, alive, flags)
         first = first + jnp.where(place == 0, alive, 0.0)
         last = last + jnp.where(place == number - 1, alive, 0.0)
-    flag_rows[...] = flags.astype(BF16)
-    rows_in[number * C :, :] = flags.astype(BF16)
-    first_flag = jnp.where(rows == number + 1, first, 0.0).astype(BF16)
-    last_flag = jnp.where(rows == 0, last, 0.0).astype(BF16)
-    packed = dot(rows_in[...], pick[...]).astype(BF16)
-    packed = packed.reshape(number + 1, C, VOX)
-    x_low[...] = packed[:, :, :256]
-    x_high[...] = packed[:, :, 256:]
-    for out, index, flag in ((y_low, 0, first_flag), (y_high, number - 1, last_flag)):
-        out[0] = own[index]
-        out[1] = cot[index]
-        out[2] = flag
-
-
-def corner_kernel(y_left, y_right, flag_rows, pick, low, high, flags):
-    extra = y_left[2] + y_right[2]
-    rows = jnp.concatenate([y_left[0], y_right[0], extra], axis=0)
-    packed = dot(rows, pick[...]).astype(BF16).reshape(3, C, VOX)
-    low[...] = packed[:, :, :256]
-    high[...] = packed[:, :, 256:]
-    flags[...] = flag_rows[...] + extra
+    flag_rows[...] = flags
+    packed = dot(rows_in[...], marks(VOX, 512, plain, edge_source)).astype(BF16)
+    spare = jnp.zeros((16, 2 * LANES), BF16)
+    for out, at in ((x_low, 0), (x_high, 256)):
+        for pair in range(number // 2):
+            edges = [packed[C * i : C * (i + 1), at : at + 256] for i in (2 * pair, 2 * pair + 1)]
+            out[C * pair : C * (pair + 1), :] = join_rows(*edges)
+        out[C * number // 2 :, :LANES] = flags.astype(BF16)
+        out[C * number // 2 :, LANES:] = spare
+    for out, index, flag in ((y_low, 0, first), (y_high, number - 1, last)):
+        out[0:C, :] = own[index]
+        out[C : 2 * C, :] = cot[index]
+        out[2 * C :, :] = (jnp.zeros((16, VOX), F32) + flag).astype(BF16)
+
+
+def corner_kernel(y_left, y_right, low, high):
+    rows = jnp.concatenate([y_left[0:C, :], y_right[0:C, :]], axis=0)
+    packed = dot(rows, marks(VOX, 512, plain, edge_source)).astype(BF16)
+    ids = lax.broadcasted_iota(jnp.int32, (16, LANES), 0)
+    flags = jnp.where(ids == 0, y_left[2 * C :, :LANES], y_right[2 * C :, :LANES])
+    spare = jnp.zeros((16, 2 * LANES), BF16)
+    for out, at in ((low, 0), (high, 256)):
+        out[0:C, :] = join_rows(packed[:C, at : at + 256], packed[C:, at : at + 256])
+        out[C:, :LANES] = flags
+        out[C:, LANES:] = spare
 
 
 def arrange_weights(fine, down, coarse, up, fine_w, fine_b, coarse_w, coarse_b, down_w, up_w):
@@ -203,30 +228,32 @@
 
 
 def place_kernel(
-    own, cot, y_left, y_right, flags, place, place_pair, fine, down, coarse, up,
-    grid, cot_grid, grad_r, live, fine_w, fine_b, coarse_w, coarse_b, down_w, up_w,
+    own, cot, y_left, y_right, c_low, fine, down, coarse, up,
+    grid, cot_grid, grad_r, fine_w, fine_b, coarse_w, coarse_b, down_w, up_w,
     rows_in, rows_cot,
 ):
     arrange_weights(fine, down, coarse, up, fine_w, fine_b, coarse_w, coarse_b, down_w, up_w)
     number = cot.shape[0]
     last = number + 1
-    rows_in[0:C, :] = y_left[0]
+    rows_in[0:C, :] = y_left[0:C, :]
     for block in range(number):
         at = (block + 1) * C
         rows_in[at : at + C, :] = own[block]
-    rows_in[last * C : (last + 1) * C, :] = y_right[0]
-    rows_in[(last + 1) * C :, :] = flags[...]
+    rows_in[last * C : (last + 1) * C, :] = y_right[0:C, :]
     pairs = number // 2 + 2
     for group in range(pairs):
         at = group * C
-        lower = y_left[1] if group == 0 else cot[group - 1]
-        upper = y_right[1] if group == pairs - 1 else cot[group + number // 2 - 1]
+        lower = y_left[C : 2 * C, :] if group == 0 else cot[group - 1]
+        upper = y_right[C : 2 * C, :] if group == pairs - 1 else cot[group + number // 2 - 1]
         rows_cot[at : at + C, 0:512] = lower
         rows_cot[at : at + C, 512:1024] = upper
     for pair in range(4):
-        lanes = slice(256 * pair, 256 * pair + 256)
-        placed_cot = dot(rows_cot[...], place_pair[:, lanes])
-        placed = dot(rows_in[...], place[:, lanes])
+        placed_cot = dot(
+            rows_cot[...], marks(1024, 256, plain, lambda j, at=256 * pair: pair_source(j + at))
+        )
+        placed = dot(
+            rows_in[...], marks(VOX, 256, plain, lambda j, at=256 * pair: own_source(j + at))
+        )
         for half in range(2):
             span = slice(LANES * half, LANES * (half + 1))
             for block in range(last + 1):
@@ -235,8 +262,6 @@
             for block in range(pairs):
                 tile = EDGE * block + 2 * pair + half
                 cot_grid[tile] = placed_cot[block * C : (block + 1) * C, span].astype(BF16)
-        if pair == 0:
-            live[...] = placed[(last + 1) * C :, 0:LANES]
 
     def rect_step(block):
         tiles = []
@@ -262,44 +287,53 @@
 
     def body(index):
         tile = 4 * index
-        for pair in range(2):
-            at = tile + 2 * pair
-            cols = [depth_columns(load(at + i), masks, step) for i in range(2)]
-            out = dot(weight[...], jnp.concatenate(cols, axis=1))
-            parts[at + 1] = out[:, :LANES]
-            parts[at + 2] = out[:, LANES:]
+        cols = [depth_columns(load(tile + i), masks, step) for i in range(4)]
+        out = dot(weight[...], jnp.concatenate(cols, axis=1))
+        for i in range(4):
+            parts[tile + i + 1] = out[:, LANES * i : LANES * (i + 1)]
 
     loop(0, tiles // 4, body, unroll)
 
 
 def forward_kernel(
-    grid_own, live_own, grad_r, x_left, x_right, c_left, c_right, place, fine_w, down_w, coarse_w,
+    grid_own, flags, y_left, y_right, grad_r, x_left, x_right, c_left, c_right, fine_w, down_w,
+    coarse_w,
     grid, hidden, low_cols, rects, grad_c, live, pack_low, pack_high,
     rows_in, fine_p, coarse_p, hidden_all, lowered, live_all,
 ):
-    number = x_left.shape[0] - 1
+    number = 2 * (x_left.shape[0] - 16) // C
     last = number + 1
-    for block in range(number):
-        at = (block + 1) * C
-        rows_in[at : at + C, 0:256] = x_left[block]
-        rows_in[at : at + C, 256:512] = x_right[block]
-    for at, index in ((0, 0), (last * C, 1)):
-        rows_in[at : at + C, 0:256] = c_left[index]
-        rows_in[at : at + C, 256:512] = c_right[index]
-    at = (last + 1) * C
-    rows_in[at : at + C, 0:256] = x_left[number] + c_left[2]
-    rows_in[at : at + C, 256:512] = x_right[number] + c_right[2]
+    for at, left, right in ((0, x_left, x_right), (None, c_left, c_right)):
+        for pair in range((left.shape[0] - 16) // C):
+            rows = slice(C * pair, C * (pair + 1))
+            lefts, rights = split_rows(left[rows, :]), split_rows(right[rows, :])
+            for inner in range(2):
+                block = last * inner if at is None else 2 * pair + inner + 1
+                rows_in[block * C : (block + 1) * C, 0:256] = lefts[inner]
+                rows_in[block * C : (block + 1) * C, 256:512] = rights[inner]
+    across = lane_ids(16) % 16
+    for start, middle, left, right in (
+        (1, flags[...], x_left[number // 2 * C :, :LANES], x_right[number // 2 * C :, :LANES]),
+        (0, y_left[2 * C :, :LANES], c_left[C:, :LANES], c_right[C:, :LANES]),
+        (last, y_right[2 * C :, :LANES], c_left[C:, :LANES], c_right[C:, :LANES]),
+    ):
+        rows = jnp.where(across < 4, left.astype(F32), middle.astype(F32))
+        rows = jnp.where(across >= 12, right.astype(F32), rows)
+        if start == 1:
+            live_all[1 : number + 1, :] = rows
+        else:
+            at = 0 if start == 0 else 1
+            live_all[start : start + 1, :] = rows[at : at + 1, :]
     for pair in range(4):
-        lanes = slice(256 * pair, 256 * pair + 256)
-        placed = dot(rows_in[...], place[:, lanes])
+        placed = dot(
+            rows_in[...], marks(512, 256, plain, lambda j, at=256 * pair: halo_source(j + at))
+        )
         for half in range(2):
             span = slice(LANES * half, LANES * (half + 1))
             for block in range(last + 1):
                 tile = EDGE * block + 2 * pair + half
                 halo = placed[block * C : (block + 1) * C, span].astype(BF16)
                 grid[tile] = grid_own[tile] + halo
-        if pair == 0:
-            live_all[...] = live_own[...] + placed[(last + 1) * C :, 0:LANES]
     live[...] = join_halves(live_all[0:16, :], live_all[8:24, :])
     tiles = grid.shape[0]
     conv_steps(fine_p, fine_w, lambda tile: across_columns(grid[tile], 1), tiles, 16, 0, 2)
@@ -364,8 +398,8 @@
             out[group] = total
 
 
-def to_blocks(slots, rows_out, place_back, flat, out):
-    flat[...] = dot(rows_out[...], place_back[...]).astype(BF16)
+def to_blocks(slots, rows_out, flat, out):
+    flat[...] = dot(rows_out[...], marks(1024, 1024, pair_source, plain)).astype(BF16)
     number = out.shape[0]
     for slot in range(number):
         place = slots[slot]
@@ -388,7 +422,7 @@
         ]
 
 
-def output_kernel(slots, hidden, rects, live, place_back, up_w, out, rows_out, flat):
+def output_kernel(slots, hidden, rects, live, up_w, out, rows_out, flat):
     pairs = hidden.shape[0] // EDGE
 
     def block_step(block):
@@ -404,7 +438,7 @@
                 rows_out[pl.ds(start, C), at : at + LANES] = (value * alive).astype(BF16)
 
     loop(1, pairs - 1, block_step, 2)
-    to_blocks(slots, rows_out, place_back, flat, out)
+    to_blocks(slots, rows_out, flat, out)
 
 
 def side_kernel(rects, cot_grid, low_cols, grad_c, flat, grad_own, up_g, coarse_g):
@@ -545,7 +579,7 @@
 
 
 def input_kernel(
-    slots, grad_h, from_left, from_right, live, place_back, fine_w, out,
+    slots, grad_h, from_left, from_right, live, fine_w, out,
     fine_p, rows_out, flat, grad_x,
 ):
     tiles = grad_h.shape[0]
@@ -571,7 +605,7 @@
             ).astype(BF16)
 
     loop(1, tiles // EDGE - 1, block_step, 2)
-    to_blocks(slots, rows_out, place_back, flat, out)
+    to_blocks(slots, rows_out, flat, out)
 
 
 def finish_kernel(scale, total, fine, down, coarse, up):
@@ -622,17 +656,21 @@
     return lax.ppermute(array, ("gx", "gy"), pairs)
 
 
-def reduce_all(joined):
-    axes = ("gx", "gy")
+def reduce_share(joined):
     devices = lax.axis_size("gx") * lax.axis_size("gy")
     rows = joined.shape[0]
     share = -(-rows // devices)
     joined = jnp.pad(joined, ((0, share * devices - rows), (0, 0)))
-    mine = lax.all_to_all(joined.reshape(devices, share, LANES), axes, 0, 0)
-    mine = jnp.sum(mine.astype(F32), axis=0).astype(BF16)
-    spread = jnp.broadcast_to(mine[None], (devices, share, LANES))
-    full = lax.all_to_all(spread, axes, 0, 0)
-    return full.reshape(devices * share, LANES)[:rows]
+    mine = lax.all_to_all(joined.reshape(devices, share, LANES), ("gx", "gy"), 0, 0)
+    return jnp.sum(mine.astype(F32), axis=0).astype(BF16)
+
+
+def spread_share(share):
+    devices = lax.axis_size("gx") * lax.axis_size("gy")
+    rows = share.shape[0]
+    copies = jnp.broadcast_to(share[None], (devices, rows, LANES))
+    full = lax.all_to_all(copies, ("gx", "gy"), 0, 0)
+    return full.reshape(devices * rows, LANES)
 
 
 def on_device(
@@ -644,11 +682,6 @@
     count = block_count.reshape(1)
     feats = features.reshape(number, C, VOX)
     cots = cotangent.reshape(number, C, VOX)
-    place_own = jnp.asarray(placing_matrix()[:512], BF16)
-    place_halo = jnp.asarray(placing_matrix()[512:], BF16)
-    place_pair = jnp.asarray(pair_matrix(), BF16)
-    place_back = jnp.asarray(pair_matrix().T, BF16)
-    pick = jnp.asarray(edge_matrix(), BF16)
     tiles = EDGE * (number + 2)
     coarse_tiles = tiles // 2
     pairs = number // 2 + 2
@@ -660,12 +693,12 @@
     )
     own, cot, flag_rows, x_low, x_high, y_low, y_high = call(
         prepare_kernel,
-        (slots, count, feats, cots, pick),
+        (slots, count, feats, cots),
         [((number, C, VOX), BF16)] * 2
-        + [((C, VOX), BF16)]
-        + [((number + 1, C, 256), BF16)] * 2
-        + [((3, C, VOX), BF16)] * 2,
-        [(((number + 1) * C, VOX), BF16)],
+        + [((16, LANES), F32)]
+        + [((number // 2 * C + 16, 384), BF16)] * 2
+        + [((2 * C + 16, VOX), BF16)] * 2,
+        [((number * C, VOX), BF16)],
         scalars=2,
         limit=56 * 1024 * 1024,
     )
@@ -673,33 +706,31 @@
     x_right = send(x_low, -1, 0)
     y_left = send(y_high, 0, 1)
     y_right = send(y_low, 0, -1)
-    corner_low, corner_high, flags = call(
+    corner_low, corner_high = call(
         corner_kernel,
-        (y_left, y_right, flag_rows, pick),
-        [((3, C, 256), BF16), ((3, C, 256), BF16), ((C, VOX), BF16)],
+        (y_left, y_right),
+        [((C + 16, 384), BF16), ((C + 16, 384), BF16)],
     )
     c_left = send(corner_high, 1, 0)
     c_right = send(corner_low, -1, 0)
-    (grid_own, cot_grid, grad_r, live_own, fine_fore, fine_back, coarse_fore, coarse_back, down_w,
+    (grid_own, cot_grid, grad_r, fine_fore, fine_back, coarse_fore, coarse_back, down_w,
      up_w) = call(
         place_kernel,
-        (own, cot, y_left, y_right, flags, place_own, place_pair, fine_3, down_3, coarse_3,
-         up_weight),
+        (own, cot, y_left, y_right, corner_low, fine_3, down_3, coarse_3, up_weight),
         [
             ((tiles, C, LANES), BF16),
             ((EDGE * pairs, C, LANES), BF16),
             ((4 * pairs, C, LANES), F32),
-            ((C, LANES), F32),
         ]
         + [((3 * C, 9 * C), BF16)] * 4
         + [((4 * C, 2 * C), BF16), ((2 * C, 4 * C), BF16)],
-        [(((number + 3) * C, VOX), BF16), ((pairs * C, 1024), BF16)],
+        [(((number + 2) * C, VOX), BF16), ((pairs * C, 1024), BF16)],
         flops=8 * 10**9,
     )
     grid, hidden, low_cols, rects, grad_c, live, pack_low, pack_high = call(
         forward_kernel,
-        (grid_own, live_own, grad_r, x_left, x_right, c_left, c_right, place_halo, fine_fore,
-         down_w, coarse_fore),
+        (grid_own, flag_rows, y_left, y_right, grad_r, x_left, x_right, c_left, c_right,
+         fine_fore, down_w, coarse_fore),
         [
             ((tiles, C, LANES), BF16),
             ((EDGE * pairs, C, LANES), F32),
@@ -711,7 +742,7 @@
             ((groups, C, LANES), BF16),
         ],
         [
-            (((number + 3) * C, VOX), BF16),
+            (((number + 2) * C, VOX), BF16),
             ((tiles + 2, 3 * C, LANES), F32),
             ((4 * pairs + 2, 3 * C, LANES), F32),
             ((tiles, C, LANES), F32),
@@ -750,19 +781,21 @@
         [((EDGE * pairs, C, LANES), BF16), ((VOX, 3 * C), F32), ((4 * C, LANES), F32)],
         flops=12 * 10**9,
     )
+    joined, edge_left, edge_right, slots = lax.optimization_barrier(
+        (joined, edge_left, edge_right, slots)
+    )
+    share = reduce_share(joined)
     (output,) = call(
         output_kernel,
-        (slots, hidden, rects, live, place_back, up_w),
+        (slots, hidden, rects, live, up_w),
         [((number, C, VOX), BF16)],
         [((number // 2 * C, 1024), BF16), ((number // 2 * C, 1024), BF16)],
         scalars=1,
         flops=8 * 10**9,
     )
-    joined, edge_left, edge_right = lax.optimization_barrier((joined, edge_left, edge_right))
-    total = reduce_all(joined)
     (input_grad,) = call(
         input_kernel,
-        (slots, grad_h, edge_left, edge_right, live, place_back, fine_back),
+        (slots, grad_h, edge_left, edge_right, live, fine_back),
         [((number, C, VOX), BF16)],
         [
             ((EDGE * pairs + 2, 3 * C, LANES), F32),
@@ -773,6 +806,8 @@
         scalars=1,
         flops=8 * 10**9,
     )
+    share, output, input_grad = lax.optimization_barrier((share, output, input_grad))
+    total = spread_share(share)
     scale = 1.0 / math.sqrt(number * VOX * lax.axis_size("gx") * lax.axis_size("gy"))
     fine_total, down_total, coarse_total, up_total = call(
         functools.partial(finish_kernel, scale),

time: 133 us -> 134 us (level)
  starting transfers between devices: 29.6 us -> 36.3 us
  local copies, waits for them, and re-layouts: 9.01 us -> 5.02 us
  waiting for transfers between devices: 6.27 us -> 2.93 us
  Pallas kernels: 65.5 us -> 67.4 us
  blocking collectives: 20.1 us -> 18.6 us
    all_to_all x1, starting transfers between devices: 2.82 us -> 9.21 us  [reduce_share(): lax.all_to_all(joined.reshape(devices, share, LANES), ('gx', 'gy'), 0, 0)]
    ppermute x10, waiting for transfers between devices: 6.27 us -> 2.93 us  [send(): return lax.ppermute(array, ('gx', 'gy'), pairs)]
    unnamed x36 -> x20, local copies, waits for them, and re-layouts: 8.21 us -> 4.96 us
    pallas_call x10, Pallas kernels: 65.5 us -> 67.4 us  [call(): pl.pallas_call(kernel, out_shape=tuple((jax.ShapeDtypeStruct(s, d) for s,...]
    all_to_all x1, blocking collectives: 20.1 us -> 18.6 us  [spread_share(): full = lax.all_to_all(copies, ('gx', 'gy'), 0, 0)]
  transfers between devices with their start and end apart: 11 -> 11, of which waited for: 2 -> 1; matrix products, arithmetic and copies ran while one was open for 0% -> 1% of each run, Pallas kernels for 24% -> 26%
where the time goes in v7:
time: 134 us; the launch traced here: 133 us
  Pallas kernels  67.4 us (50%)
  starting transfers between devices  36.3 us (27%)
  blocking collectives  18.6 us (14%)
  local copies, waits for them, and re-layouts  5.02 us (4%)
  waiting for transfers between devices  2.93 us (2%)
  between operations  1.64 us (1%)
    pallas_call x10, Pallas kernels, call(): pl.pallas_call(kernel, out_shape=tuple((jax.ShapeDtypeStruct(s, d) for s,...  67.4 us
    ppermute x10, starting transfers between devices, send(): return lax.ppermute(array, ('gx', 'gy'), pairs)  27.1 us
    all_to_all x1, blocking collectives, spread_share(): full = lax.all_to_all(copies, ('gx', 'gy'), 0, 0)  18.6 us
    all_to_all x1, starting transfers between devices, reduce_share(): lax.all_to_all(joined.reshape(devices, share, LANES), ('gx', 'gy'), 0, 0)  9.21 us
    unnamed x20, local copies, waits for them, and re-layouts  4.96 us
    ppermute x10, waiting for transfers between devices, send(): return lax.ppermute(array, ('gx', 'gy'), pairs)  2.93 us
  transfers between devices with their start and end apart: 11, of which 1 were waited for; matrix products, arithmetic and copies ran while one was open for 1% of the time, Pallas kernels for 26%

profile of v7, /device:TPU:0, one launch (start us, length us, event | category | flops | bytes accessed | tf_op | source)
XLA Modules:
  0.0 132.9 jit_solution(4294198883928056788)
XLA Ops:
  1.4 3.0 %prepare_kernel.1 = (bf16[16,48,512]{2,1,0:T(8,128)(2,1)}, bf16[16,48,512]{2,1,0:T(8,128)(2,1)}, f32[16,128]{1,0:T(8,128)}, bf16[400,384]{1,0:T(8,128)(2,1)}, bf...) custom-call(s32[16]{0:T(128)} %bitcast.20, s32[1]{0:T(128)} %bitcast.16.count, ...), custom_call_target="tpu_custom_call" | custom-call | bytes 3997764 | tf_op jit(solution)/shard_map/prepare_kernel/pallas_call | solution.py:636
  4.4 2.4 %collective-permute-start = (bf16[112,512]{1,0:T(8,128)(2,1)}, bf16[112,512]{1,0:T(8,128)(2,1)S(1)}, u32[]{:S(2)}, u32[]{:S(2)}) collective-permute-start(bf16[112,512]{1,0:T(8,128)(2,1)} %get-tuple-element.49), channel_id=1, source_target_pairs={{0,1},{1,2},{2,3},{4,5},{5,6},{6,7},{8,9},{9,10},{10,11},{12,13},{... | collective-permute-start | bytes 344072 | tf_op jit(solution)/shard_map/ppermute | solution.py:656
  6.8 1.3 collective-permute-start.1
  8.1 4.2 %collective-permute-start.2 = (bf16[400,384]{1,0:T(8,128)(2,1)}, bf16[400,384]{1,0:T(8,128)(2,1)S(1)}, u32[]{:S(2)}, u32[]{:S(2)}) collective-permute-start(bf16[400,384]{1,0:T(8,128)(2,1)} %get-tuple-element.55), channel_id=1, source_target_pairs={{0,4},{1,5},{2,6},{3,7},{4,8},{5,9},{6,10},{7,11},{8,12},{9,13},{1... | collective-permute-start | bytes 921608 | tf_op jit(solution)/shard_map/ppermute | solution.py:656
  12.3 1.3 collective-permute-start.3
  13.6 0.9 copy.17
  14.5 0.3 corner_kernel.1
  14.9 4.5 %collective-permute-start.4 = (bf16[64,384]{1,0:T(8,128)(2,1)S(1)}, bf16[64,384]{1,0:T(8,128)(2,1)S(1)}, u32[]{:S(2)}, u32[]{:S(2)}) collective-permute-start(bf16[64,384]{1,0:T(8,128)(2,1)S(1)} %get-tuple-element.57), channel_id=1, source_target_pairs={{0,4},{1,5},{2,6},{3,7},{4,8},{5,9},{6,10},{7,11},{8,12},{9,13},{1... | collective-permute-start | bytes 147464 | tf_op jit(solution)/shard_map/ppermute | solution.py:656
  19.4 1.3 collective-permute-start.5
  20.8 1.1 copy-done.1
  21.9 1.1 copy-done.2
  23.0 4.3 %place_kernel.1 = (bf16[144,48,128]{2,1,0:T(8,128)(2,1)S(1)}, bf16[80,48,128]{2,1,0:T(8,128)(2,1)S(1)}, f32[40,48,128]{2,1,0:T(8,128)S(1)}, bf16[144,432]{1,0:T(...) custom-call(bf16[16,48,512]{2,1,0:T(8,128)(2,1)S(1)} %copy-done.1, ...), custom_call_target="tpu_custom_call" | custom-call | flops 8000000000 | bytes 6480896 | tf_op jit(solution)/shard_map/place_kernel/pallas_call | solution.py:636
  27.3 20.2 %forward_kernel.1 = (bf16[144,48,128]{2,1,0:T(8,128)(2,1)S(1)}, f32[80,48,128]{2,1,0:T(8,128)S(1)}, bf16[40,144,128]{2,1,0:T(8,128)(2,1)S(1)}, bf16[40,48,128]{2...) custom-call(bf16[144,48,128]{2,1,0:T(8,128)(2,1)S(1)} %get-tuple-ele, ...), custom_call_target="tpu_custom_call" | custom-call | flops 8000000000 | bytes 10263552 | tf_op jit(solution)/shard_map/forward_kernel/pallas_call | solution.py:636
  47.6 0.0 copy-start.7
  47.6 5.0 %collective-permute-start.6 = (bf16[3,48,128]{2,1,0:T(8,128)(2,1)S(1)}, bf16[3,48,128]{2,1,0:T(8,128)(2,1)S(1)}, u32[]{:S(2)}, u32[]{:S(2)}) collective-permute-start(bf16[3,48,128]{2,1,0:T(8,128)(2,1)S(1)} %get-tuple-element.63), channel_id=1, source_target_pairs={{0,4},{1,5},{2,6},{3,7},{4,8},{5,9},{6,10},{7,11},{8,12},{9,13},{1... | collective-permute-start | bytes 110600 | tf_op jit(solution)/shard_map/ppermute | solution.py:656
  52.6 1.3 collective-permute-start.7
  53.9 3.2 %side_kernel.1.early = bf16[768,128]{1,0:T(8,128)(2,1)S(1)} custom-call(bf16[40,48,128]{2,1,0:T(8,128)(2,1)S(1)} %get-tuple-element.71.rects, bf16[80,48,128]{2,1,0:T(8,128)(2,1)S(1)} %get-tuple-element.66.cot_grid, bf16[40,144,128]{2,1,0:T(8,128)(2,1)S(1)} %get-tuple-element.72.low_cols, bf16[40,48,128]{2,1,0:T(8,128)(2,1)S(1)} %get-tuple-element.62.grad_c), custom_call_target="tpu_custom_call" | custom-call | flops 8000000000 | bytes 3637248 | tf_op jit(solution)/shard_map/side_kernel/pallas_call | solution.py:636
  57.2 2.9 %collective-permute-done.7.from_right = bf16[3,48,128]{2,1,0:T(8,128)(2,1)S(1)} collective-permute-done((bf16[3,48,128]{2,1,0:T(8,128)(2,1)S(1)}, bf16[3,48,128]{2,1,0:T(8,128)(2,1)S(1)}, u32[]{:S(2)}, u32[]{:S(2)}) %collective-permute-start.7) | collective-permute-done | bytes 36896 | tf_op jit(solution)/shard_map/ppermute | solution.py:656
  60.1 8.2 %backward_kernel.1 = (bf16[80,48,128]{2,1,0:T(8,128)(2,1)S(1)}, bf16[40,48,128]{2,1,0:T(8,128)(2,1)S(1)}, bf16[9,48,128]{2,1,0:T(8,128)(2,1)S(1)}, bf16[9,48,128]{2,1,0:T(8,128)(2,1)S(1)}) custom-call(bf16[40,48,128]{2,1,0:T(8,128)(2,1)S(1)} %get-tuple-element.62.grad_c, bf16[3,48,128]{2,1,0:T(8,128)(2,1)S(1)} %collective-permute-done.6.from_left, ...), custom_call_target="tpu_custom_call" | custom-call | flops 8000000000 | bytes 5379584 | tf_op jit(solution)/shard_map/backward_kernel/pallas_call | solution.py:636
  68.3 4.5 %collective-permute-start.8 = (bf16[9,48,128]{2,1,0:T(8,128)(2,1)S(1)}, bf16[9,48,128]{2,1,0:T(8,128)(2,1)S(1)}, u32[]{:S(2)}, u32[]{:S(2)}) collective-permute-start(bf16[9,48,128]{2,1,0:T(8,128)(2,1)S(1)} %get-tuple-element.73), channel_id=1, source_target_pairs={{0,4},{1,5},{2,6},{3,7},{4,8},{5,9},{6,10},{7,11},{8,12},{9,13},{1... | collective-permute-start | bytes 331784 | tf_op jit(solution)/shard_map/ppermute | solution.py:656
  72.8 1.3 collective-permute-start.9
  74.1 0.0 copy-start
  74.1 8.4 %weight_kernel.1 = bf16[1536,128]{1,0:T(8,128)(2,1)} custom-call(bf16[144,48,128]{2,1,0:T(8,128)(2,1)S(1)} %get-tuple-element.61.grid, bf16[80,48,128]{2,1,0:T(8,128)(2,1)S(1)} %get-tuple-element.69.grad_h, bf16[40,48,128]{2,1,0:T(8,128)(2,1)S(1)} %get-tuple-element.70.grad_d, f32[80,48,128]{2,1,0:T(8,128)S(1)} %get-tuple-element.65.hidden, ...), custom_call_target="tpu_custom_call" | custom-call | flops 12000000000 | bytes 5799936 | tf_op jit(solution)/shard_map/weight_kernel/pallas_call | solution.py:636
  82.5 9.2 %all-to-all-start = ((bf16[32,48,128]{2,1,0:T(8,128)(2,1)}), bf16[32,48,128]{2,1,0:T(8,128)(2,1)}, u32[]{:S(2)}, u32[]{:S(2)}) async-start(bf16[32,48,128]{2,1,0:T(8,128)(2,1)} %bitcast.7), calls=%async_computation | async-start | bytes 786432 | tf_op jit(solution)/shard_map/all_to_all | solution.py:664
  91.8 1.0 copy-done.8
  92.8 4.4 %output_kernel.1 = bf16[16,48,512]{2,1,0:T(8,128)(2,1)} custom-call(s32[16]{0:T(128)S(1)} %bitcast.21, f32[80,48,128]{2,1,0:T(8,128)S(1)} %get-tuple-element.65.hidden, bf16[40,48,128]{2,1,0:T(8,128)(2,1)S(1)} %copy-done.8, f32[16,128]{1,0:T(8,128)S(1)} %get-tuple-element.67.live, bf16[96,192]{1,0:T(8,128)(2,1)S(1)} %get-tuple-element.77.up_w), custom_call_target="tpu_custom_call" | custom-call | flops 8000000000 | bytes 3289152 | tf_op jit(solution)/shard_map/output_kernel/pallas_call | solution.py:636
  97.2 13.7 %input_kernel.1 = bf16[16,48,512]{2,1,0:T(8,128)(2,1)} custom-call(s32[16]{0:T(128)S(1)} %bitcast.22, bf16[80,48,128]{2,1,0:T(8,128)(2,1)S(1)} %get-tuple-element.69.grad_h, bf16[9,48,128]{2,1,0:T(8,128)(2,1)S(1)} %collective-permute-done.8.from_left, bf16[9,48,128]{2,1,0:T(8,128)(2,1)S(1)} %collective-permute-done.9.from_right, ...), custom_call_target="tpu_custom_call" | custom-call | flops 8000000000 | bytes 2123328 | tf_op jit(solution)/shard_map/input_kernel/pallas_call | solution.py:636
  110.9 1.1 reduce_sum.12
  112.0 0.1 broadcast_in_dim.2
  112.0 18.6 %all_to_all.10 = bf16[32,48,128]{2,1,0:T(8,128)(2,1)S(1)} all-to-all(bf16[32,48,128]{2,1,0:T(8,128)(2,1)S(1)} %broadcast_in_dim.2), channel_id=1, replica_groups=mesh['gx'=8,'gy'=4] {'gx','gy'}, dimensions={0} | all-to-all | bytes 786432 | tf_op jit(solution)/shard_map/all_to_all | solution.py:672
  130.6 1.6 %finish_kernel.1 = (f32[27,48,48]{2,1,0:T(8,128)}, f32[8,48,48]{2,1,0:T(8,128)S(1)}, f32[27,48,48]{2,1,0:T(8,128)}, f32[8,48,48]{2,1,0:T(8,128)}) custom-call(bf16[1536,128]{1,0:T(8,128)(2,1)S(1)} %bitcast.17), custom_call_target="tpu_custom_call" | custom-call | bytes 1038336 | tf_op jit(solution)/shard_map/finish_kernel/pallas_call | solution.py:636
  132.2 0.7 copy.15
  (23 shorter events, 0.1 us)
Async XLA Ops:
  0.6 20.1 %copy-start.5 = (bf16[8,48,48]{2,1,0:T(8,128)(2,1)S(1)}, bf16[8,48,48]{2,1,0:T(8,128)(2,1)}, u32[]{:S(2)}) copy-start(bf16[8,48,48]{2,1,0:T(8,128)(2,1)} %up.1) | copy-start | bytes 110596
  0.6 20.1 %copy-start.4 = (bf16[48,27,48]{2,0,1:T(8,128)(2,1)S(1)}, bf16[48,27,48]{2,0,1:T(8,128)(2,1)}, u32[]{:S(2)}) copy-start(bf16[48,27,48]{2,0,1:T(8,128)(2,1)} %param.14) | copy-start | bytes 373252
  0.7 20.1 %copy-start.3 = (bf16[48,27,48]{2,0,1:T(8,128)(2,1)S(1)}, bf16[48,27,48]{2,0,1:T(8,128)(2,1)}, u32[]{:S(2)}) copy-start(bf16[48,27,48]{2,0,1:T(8,128)(2,1)} %param.12) | copy-start | bytes 373252
  4.4 10.1 %collective-permute-start = (bf16[112,512]{1,0:T(8,128)(2,1)}, bf16[112,512]{1,0:T(8,128)(2,1)S(1)}, u32[]{:S(2)}, u32[]{:S(2)}) collective-permute-start(bf16[112,512]{1,0:T(8,128)(2,1)} %get-tuple-element.49), channel_id=1, source_target_pairs={{0,1},{1,2},{2,3},{4,5},{5,6},{6,7},{8,9},{9,10},{10,11},{12,13},{... | collective-permute-start | bytes 344072 | tf_op jit(solution)/shard_map/ppermute | solution.py:656
  6.8 7.8 %collective-permute-start.1 = (bf16[112,512]{1,0:T(8,128)(2,1)}, bf16[112,512]{1,0:T(8,128)(2,1)S(1)}, u32[]{:S(2)}, u32[]{:S(2)}) collective-permute-start(bf16[112,512]{1,0:T(8,128)(2,1)} %get-tuple-element.50), channel_id=1, source_target_pairs={{1,0},{2,1},{3,2},{5,4},{6,5},{7,6},{9,8},{10,9},{11,10},{13,12},{... | collective-permute-start | bytes 344072 | tf_op jit(solution)/shard_map/ppermute | solution.py:656
  8.1 19.3 %collective-permute-start.2 = (bf16[400,384]{1,0:T(8,128)(2,1)}, bf16[400,384]{1,0:T(8,128)(2,1)S(1)}, u32[]{:S(2)}, u32[]{:S(2)}) collective-permute-start(bf16[400,384]{1,0:T(8,128)(2,1)} %get-tuple-element.55), channel_id=1, source_target_pairs={{0,4},{1,5},{2,6},{3,7},{4,8},{5,9},{6,10},{7,11},{8,12},{9,13},{1... | collective-permute-start | bytes 921608 | tf_op jit(solution)/shard_map/ppermute | solution.py:656
  12.3 15.0 %collective-permute-start.3 = (bf16[400,384]{1,0:T(8,128)(2,1)}, bf16[400,384]{1,0:T(8,128)(2,1)S(1)}, u32[]{:S(2)}, u32[]{:S(2)}) collective-permute-start(bf16[400,384]{1,0:T(8,128)(2,1)} %get-tuple-element.56), channel_id=1, source_target_pairs={{4,0},{5,1},{6,2},{7,3},{8,4},{9,5},{10,6},{11,7},{12,8},{13,9},{1... | collective-permute-start | bytes 921608 | tf_op jit(solution)/shard_map/ppermute | solution.py:656
  14.9 12.4 %collective-permute-start.4 = (bf16[64,384]{1,0:T(8,128)(2,1)S(1)}, bf16[64,384]{1,0:T(8,128)(2,1)S(1)}, u32[]{:S(2)}, u32[]{:S(2)}) collective-permute-start(bf16[64,384]{1,0:T(8,128)(2,1)S(1)} %get-tuple-element.57), channel_id=1, source_target_pairs={{0,4},{1,5},{2,6},{3,7},{4,8},{5,9},{6,10},{7,11},{8,12},{9,13},{1... | collective-permute-start | bytes 147464 | tf_op jit(solution)/shard_map/ppermute | solution.py:656
  19.4 7.9 %collective-permute-start.5 = (bf16[64,384]{1,0:T(8,128)(2,1)S(1)}, bf16[64,384]{1,0:T(8,128)(2,1)S(1)}, u32[]{:S(2)}, u32[]{:S(2)}) collective-permute-start(bf16[64,384]{1,0:T(8,128)(2,1)S(1)} %get-tuple-element.51.c_low), channel_id=1, source_target_pairs={{4,0},{5,1},{6,2},{7,3},{8,4},{9,5},{10,6},{11,7},{12,8},{13,9},{1... | collective-permute-start | bytes 147464 | tf_op jit(solution)/shard_map/ppermute | solution.py:656
  20.7 1.1 copy-start.1
  21.9 1.1 copy-start.2
  23.0 4.3 %copy-start.6 = (f32[16,128]{1,0:T(8,128)S(1)}, f32[16,128]{1,0:T(8,128)}, u32[]{:S(2)}) copy-start(f32[16,128]{1,0:T(8,128)} %get-tuple-element.53.flags) | copy-start | bytes 24580
  47.6 9.5 %copy-start.7 = (bf16[40,48,128]{2,1,0:T(8,128)(2,1)}, bf16[40,48,128]{2,1,0:T(8,128)(2,1)S(1)}, u32[]{:S(2)}) copy-start(bf16[40,48,128]{2,1,0:T(8,128)(2,1)S(1)} %get-tuple-element.71.rects) | copy-start | bytes 1474564
  47.6 9.5 %collective-permute-start.6 = (bf16[3,48,128]{2,1,0:T(8,128)(2,1)S(1)}, bf16[3,48,128]{2,1,0:T(8,128)(2,1)S(1)}, u32[]{:S(2)}, u32[]{:S(2)}) collective-permute-start(bf16[3,48,128]{2,1,0:T(8,128)(2,1)S(1)} %get-tuple-element.63), channel_id=1, source_target_pairs={{0,4},{1,5},{2,6},{3,7},{4,8},{5,9},{6,10},{7,11},{8,12},{9,13},{1... | collective-permute-start | bytes 110600 | tf_op jit(solution)/shard_map/ppermute | solution.py:656
  52.6 7.5 %collective-permute-start.7 = (bf16[3,48,128]{2,1,0:T(8,128)(2,1)S(1)}, bf16[3,48,128]{2,1,0:T(8,128)(2,1)S(1)}, u32[]{:S(2)}, u32[]{:S(2)}) collective-permute-start(bf16[3,48,128]{2,1,0:T(8,128)(2,1)S(1)} %get-tuple-element.64), channel_id=1, source_target_pairs={{4,0},{5,1},{6,2},{7,3},{8,4},{9,5},{10,6},{11,7},{12,8},{13,9},{1... | collective-permute-start | bytes 110600 | tf_op jit(solution)/shard_map/ppermute | solution.py:656
  68.3 14.2 %collective-permute-start.8 = (bf16[9,48,128]{2,1,0:T(8,128)(2,1)S(1)}, bf16[9,48,128]{2,1,0:T(8,128)(2,1)S(1)}, u32[]{:S(2)}, u32[]{:S(2)}) collective-permute-start(bf16[9,48,128]{2,1,0:T(8,128)(2,1)S(1)} %get-tuple-element.73), channel_id=1, source_target_pairs={{0,4},{1,5},{2,6},{3,7},{4,8},{5,9},{6,10},{7,11},{8,12},{9,13},{1... | collective-permute-start | bytes 331784 | tf_op jit(solution)/shard_map/ppermute | solution.py:656
  72.8 9.7 %collective-permute-start.9 = (bf16[9,48,128]{2,1,0:T(8,128)(2,1)S(1)}, bf16[9,48,128]{2,1,0:T(8,128)(2,1)S(1)}, u32[]{:S(2)}, u32[]{:S(2)}) collective-permute-start(bf16[9,48,128]{2,1,0:T(8,128)(2,1)S(1)} %get-tuple-element.74), channel_id=1, source_target_pairs={{4,0},{5,1},{6,2},{7,3},{8,4},{9,5},{10,6},{11,7},{12,8},{13,9},{1... | collective-permute-start | bytes 331784 | tf_op jit(solution)/shard_map/ppermute | solution.py:656
  74.1 17.6 %copy-start = (s32[1,1,16]{2,1,0:T(1,128)S(1)}, s32[1,1,16]{2,1,0:T(1,128)}, u32[]{:S(2)}) copy-start(s32[1,1,16]{2,1,0:T(1,128)} %param.9) | copy-start | bytes 196
  82.5 28.4 %all-to-all-start = ((bf16[32,48,128]{2,1,0:T(8,128)(2,1)}), bf16[32,48,128]{2,1,0:T(8,128)(2,1)}, u32[]{:S(2)}, u32[]{:S(2)}) async-start(bf16[32,48,128]{2,1,0:T(8,128)(2,1)} %bitcast.7), calls=%async_computation | async-start | bytes 786432 | tf_op jit(solution)/shard_map/all_to_all | solution.py:664
  91.8 1.0 copy-start.8

commit v8 on v7

--- a/solution.py
+++ b/solution.py
@@ -159,26 +159,21 @@
     return joined[:, : 2 * LANES], second
 
 
-def prepare_kernel(
-    slots, count, feats, cots, own, cot, flag_rows, x_low, x_high, y_low, y_high, rows_in
-):
+def prepare_kernel(slots, count, feats, cots, flag_rows, x_low, x_high, y_low, y_high, rows_in):
     number = feats.shape[0]
     rows = lax.broadcasted_iota(jnp.int32, (16, LANES), 0)
     flags = jnp.zeros((16, LANES), F32)
-    first = jnp.zeros((), F32)
-    last = jnp.zeros((), F32)
     zero = jnp.zeros((C, VOX), BF16)
+    first = jnp.zeros((), jnp.int32)
+    last = jnp.zeros((), jnp.int32)
     for slot in range(number):
         live = slot < count[0]
-        alive = jnp.where(live, 1.0, 0.0)
         place = slots[slot]
         block = jnp.where(live, feats[slot], zero)
-        own[place] = block
         rows_in[pl.ds(pl.multiple_of(place * C, 16), C), :] = block
-        cot[place] = jnp.where(live, cots[slot], zero)
-        flags = jnp.where(rows == place, alive, flags)
-        first = first + jnp.where(place == 0, alive, 0.0)
-        last = last + jnp.where(place == number - 1, alive, 0.0)
+        flags = jnp.where(rows == place, jnp.where(live, 1.0, 0.0), flags)
+        first = jnp.where(place == 0, slot, first)
+        last = jnp.where(place == number - 1, slot, last)
     flag_rows[...] = flags
     packed = dot(rows_in[...], marks(VOX, 512, plain, edge_source)).astype(BF16)
     spare = jnp.zeros((16, 2 * LANES), BF16)
@@ -188,10 +183,11 @@
             out[C * pair : C * (pair + 1), :] = join_rows(*edges)
         out[C * number // 2 :, :LANES] = flags.astype(BF16)
         out[C * number // 2 :, LANES:] = spare
-    for out, index, flag in ((y_low, 0, first), (y_high, number - 1, last)):
-        out[0:C, :] = own[index]
-        out[C : 2 * C, :] = cot[index]
-        out[2 * C :, :] = (jnp.zeros((16, VOX), F32) + flag).astype(BF16)
+    for out, index, slot in ((y_low, 0, first), (y_high, number - 1, last)):
+        live = slot < count[0]
+        out[0:C, :] = rows_in[C * index : C * (index + 1), :]
+        out[C : 2 * C, :] = jnp.where(live, cots[slot], zero)
+        out[2 * C :, :] = (jnp.zeros((16, VOX), F32) + jnp.where(live, 1.0, 0.0)).astype(BF16)
 
 
 def corner_kernel(y_left, y_right, low, high):
@@ -228,18 +224,22 @@
 
 
 def place_kernel(
-    own, cot, y_left, y_right, c_low, fine, down, coarse, up,
+    slots, count, feats, cots, y_left, y_right, c_low, fine, down, coarse, up,
     grid, cot_grid, grad_r, fine_w, fine_b, coarse_w, coarse_b, down_w, up_w,
-    rows_in, rows_cot,
+    rows_in, rows_cot, cot,
 ):
     arrange_weights(fine, down, coarse, up, fine_w, fine_b, coarse_w, coarse_b, down_w, up_w)
-    number = cot.shape[0]
+    number = feats.shape[0]
     last = number + 1
+    zero = jnp.zeros((C, VOX), BF16)
     rows_in[0:C, :] = y_left[0:C, :]
-    for block in range(number):
-        at = (block + 1) * C
-        rows_in[at : at + C, :] = own[block]
     rows_in[last * C : (last + 1) * C, :] = y_right[0:C, :]
+    for slot in range(number):
+        live = slot < count[0]
+        place = slots[slot]
+        start = pl.multiple_of((place + 1) * C, 16)
+        rows_in[pl.ds(start, C), :] = jnp.where(live, feats[slot], zero)
+        cot[place] = jnp.where(live, cots[slot], zero)
     pairs = number // 2 + 2
     for group in range(pairs):
         at = group * C
@@ -299,7 +299,7 @@
     grid_own, flags, y_left, y_right, grad_r, x_left, x_right, c_left, c_right, fine_w, down_w,
     coarse_w,
     grid, hidden, low_cols, rects, grad_c, live, pack_low, pack_high,
-    rows_in, fine_p, coarse_p, hidden_all, lowered, live_all,
+    rows_in, fine_p, coarse_p, hidden_all, lowered, live_all, ring,
 ):
     number = 2 * (x_left.shape[0] - 16) // C
     last = number + 1
@@ -336,10 +336,13 @@
                 grid[tile] = grid_own[tile] + halo
     live[...] = join_halves(live_all[0:16, :], live_all[8:24, :])
     tiles = grid.shape[0]
-    conv_steps(fine_p, fine_w, lambda tile: across_columns(grid[tile], 1), tiles, 16, 0, 2)
     anchors = anchor_mask(0)
-
-    def lower_step(block):
+    masks = depth_masks(16, 0)
+    blocks = last + 1
+    ring[1] = jnp.zeros(ring.shape[1:], BF16)
+
+    def fine_step(index):
+        block = jnp.maximum(index - 3, 0)
         alive = jnp.broadcast_to(live_all[pl.ds(block, 1), :], (C, LANES))
         keep = alive * anchors
         pairs = []
@@ -347,7 +350,7 @@
             actives = []
             for half in range(2):
                 tile = EDGE * block + 2 * inner + half
-                value = conv_sum(fine_p, tile) * alive
+                value = conv_sum(fine_p, tile + EDGE - 1) * alive
                 hidden_all[tile] = value
                 actives.append(silu_parts(value)[0].astype(BF16))
             pairs.append(jnp.concatenate(actives, axis=0))
@@ -355,8 +358,17 @@
         for inner in range(4):
             total = gather_sub(parts[:, LANES * inner : LANES * (inner + 1)])
             lowered[4 * block + inner] = (total * keep).astype(BF16)
-
-    loop(0, last + 1, lower_step, 2)
+        ready = lax.rem(index + 1, 2)
+        for quad in range(2):
+            out = dot(fine_w[...], ring[ready, quad])
+            for i in range(4):
+                fine_p[EDGE * index + 4 * quad + i] = out[:, LANES * i : LANES * (i + 1)]
+        first = EDGE * jnp.minimum(index, blocks - 1)
+        for inner in range(EDGE):
+            cols = depth_columns(across_columns(grid[first + inner], 1), masks, 16)
+            ring[lax.rem(index, 2), inner // 4, :, LANES * (inner % 4) : LANES * (inner % 4 + 1)] = cols
+
+    loop(0, blocks + 3, fine_step)
     pairs = hidden.shape[0] // EDGE
     shift = last - pairs + 1
 
@@ -531,7 +543,7 @@
             out[group] = total
 
 
-def weight_kernel(grid, grad_h, grad_d, hidden, early, joined, grad_own, fine_g, down_g):
+def weight_kernel(grid, grad_h, grad_d, hidden, early, joined, grad_own, fine_g, down_g, ring):
     tiles = grad_h.shape[0]
     shift = tiles - 16
     fine_g[...] = jnp.zeros_like(fine_g)
@@ -547,18 +559,21 @@
     loop(8, tiles - 8, copy_step, 8)
     masks = depth_masks(16, 4)
 
+    steps = (tiles - 8) // 8
+    ring[1] = jnp.zeros(ring.shape[1:], BF16)
+
     def fine_step(index):
-        at = [4 + 8 * index + inner for inner in range(8)]
-        rights = []
-        for tile in at:
-            lower, upper = grid[tile], grid[tile + shift]
+        at = [4 + 8 * jnp.maximum(index - 1, 0) + inner for inner in range(8)]
+        fine_g[0 : 9 * C, :] += dot(ring[lax.rem(index + 1, 2)], stacks(grad_own, at), (1, 1))
+        first = 4 + 8 * jnp.minimum(index, steps - 1)
+        for inner in range(8):
+            lower, upper = grid[first + inner], grid[first + inner + shift]
             base = pair_columns(join_halves(lower, upper), join_halos(lower, upper), 1)
-            rights.append(depth_columns(base, masks, 16))
-        fine_g[0 : 9 * C, :] += dot(
-            jnp.concatenate(rights, axis=1), stacks(grad_own, at), (1, 1)
-        )
-
-    loop(0, (tiles - 8) // 8, fine_step)
+            ring[lax.rem(index, 2), :, LANES * inner : LANES * (inner + 1)] = depth_columns(
+                base, masks, 16
+            )
+
+    loop(0, steps + 1, fine_step)
 
     def down_step(index):
         lefts = []
@@ -691,11 +706,10 @@
     fine_3, down_3, coarse_3 = (
         weight.transpose(1, 0, 2) for weight in (fine_weight, down_weight, coarse_weight)
     )
-    own, cot, flag_rows, x_low, x_high, y_low, y_high = call(
+    flag_rows, x_low, x_high, y_low, y_high = call(
         prepare_kernel,
         (slots, count, feats, cots),
-        [((number, C, VOX), BF16)] * 2
-        + [((16, LANES), F32)]
+        [((16, LANES), F32)]
         + [((number // 2 * C + 16, 384), BF16)] * 2
         + [((2 * C + 16, VOX), BF16)] * 2,
         [((number * C, VOX), BF16)],
@@ -716,7 +730,8 @@
     (grid_own, cot_grid, grad_r, fine_fore, fine_back, coarse_fore, coarse_back, down_w,
      up_w) = call(
         place_kernel,
-        (own, cot, y_left, y_right, corner_low, fine_3, down_3, coarse_3, up_weight),
+        (slots, count, feats, cots, y_left, y_right, corner_low, fine_3, down_3, coarse_3,
+         up_weight),
         [
             ((tiles, C, LANES), BF16),
             ((EDGE * pairs, C, LANES), BF16),
@@ -724,7 +739,12 @@
         ]
         + [((3 * C, 9 * C), BF16)] * 4
         + [((4 * C, 2 * C), BF16), ((2 * C, 4 * C), BF16)],
-        [(((number + 2) * C, VOX), BF16), ((pairs * C, 1024), BF16)],
+        [
+            (((number + 2) * C, VOX), BF16),
+            ((pairs * C, 1024), BF16),
+            ((number, C, VOX), BF16),
+        ],
+        scalars=2,
         flops=8 * 10**9,
     )
     grid, hidden, low_cols, rects, grad_c, live, pack_low, pack_high = call(
@@ -743,11 +763,12 @@
         ],
         [
             (((number + 2) * C, VOX), BF16),
-            ((tiles + 2, 3 * C, LANES), F32),
+            ((tiles + 3 * EDGE, 3 * C, LANES), F32),
             ((4 * pairs + 2, 3 * C, LANES), F32),
             ((tiles, C, LANES), F32),
             ((coarse_tiles, C, LANES), BF16),
             ((C, LANES), F32),
+            ((2, 2, 9 * C, 4 * LANES), BF16),
         ],
         flops=8 * 10**9,
     )
@@ -778,7 +799,12 @@
         weight_kernel,
         (grid, grad_h, grad_d, hidden, early),
         [((32 * C, LANES), BF16)],
-        [((EDGE * pairs, C, LANES), BF16), ((VOX, 3 * C), F32), ((4 * C, LANES), F32)],
+        [
+            ((EDGE * pairs, C, LANES), BF16),
+            ((VOX, 3 * C), F32),
+            ((4 * C, LANES), F32),
+            ((2, 9 * C, 8 * LANES), BF16),
+        ],
         flops=12 * 10**9,
     )
     joined, edge_left, edge_right, slots = lax.optimization_barrier(
@@ -793,6 +819,7 @@
         scalars=1,
         flops=8 * 10**9,
     )
+    share, output, slots = lax.optimization_barrier((share, output, slots))
     (input_grad,) = call(
         input_kernel,
         (slots, grad_h, edge_left, edge_right, live, fine_back),
@@ -806,7 +833,6 @@
         scalars=1,
         flops=8 * 10**9,
     )
-    share, output, input_grad = lax.optimization_barrier((share, output, input_grad))
     total = spread_share(share)
     scale = 1.0 / math.sqrt(number * VOX * lax.axis_size("gx") * lax.axis_size("gy"))
     fine_total, down_total, coarse_total, up_total = call(

time: 134 us -> 129 us (0.963)
  blocking collectives: 18.6 us -> 0 us
  waiting for transfers between devices: 2.93 us -> 12.3 us
  Pallas kernels: 67.4 us -> 71.3 us
  starting transfers between devices: 36.3 us -> 38.1 us
    all_to_all x1 -> x0, blocking collectives: 18.6 us -> none  [spread_share(): full = lax.all_to_all(copies, ('gx', 'gy'), 0, 0)]
    all_to_all x1, waiting for transfers between devices: 0.01 us -> 8.57 us  [reduce_share(): lax.all_to_all(joined.reshape(devices, share, LANES), ('gx', 'gy'), 0, 0)]
    pallas_call x10, Pallas kernels: 67.4 us -> 71.3 us  [call(): pl.pallas_call(kernel, out_shape=tuple((jax.ShapeDtypeStruct(s, d) for s,...]
    all_to_all x0 -> x1, starting transfers between devices: none -> 2.64 us  [spread_share(): full = lax.all_to_all(copies, ('gx', 'gy'), 0, 0)]
  transfers between devices with their start and end apart: 11 -> 12, of which waited for: 1 -> 3; matrix products, arithmetic and copies ran while one was open for 1% -> 1% of each run, Pallas kernels for 26% -> 29%
where the time goes in v8:
time: 129 us; the launch traced here: 128 us
  Pallas kernels  71.3 us (55%)
  starting transfers between devices  38.1 us (30%)
  waiting for transfers between devices  12.3 us (10%)
  local copies, waits for them, and re-layouts  4.64 us (4%)
  between operations  1.7 us (1%)
    pallas_call x10, Pallas kernels, call(): pl.pallas_call(kernel, out_shape=tuple((jax.ShapeDtypeStruct(s, d) for s,...  71.3 us
    ppermute x10, starting transfers between devices, send(): return lax.ppermute(array, ('gx', 'gy'), pairs)  26.9 us
    all_to_all x1, waiting for transfers between devices, reduce_share(): lax.all_to_all(joined.reshape(devices, share, LANES), ('gx', 'gy'), 0, 0)  8.57 us
    all_to_all x1, starting transfers between devices, reduce_share(): lax.all_to_all(joined.reshape(devices, share, LANES), ('gx', 'gy'), 0, 0)  8.53 us
    unnamed x20, local copies, waits for them, and re-layouts  3.84 us
    ppermute x10, waiting for transfers between devices, send(): return lax.ppermute(array, ('gx', 'gy'), pairs)  3.7 us
    all_to_all x1, starting transfers between devices, spread_share(): full = lax.all_to_all(copies, ('gx', 'gy'), 0, 0)  2.64 us
  transfers between devices with their start and end apart: 12, of which 3 were waited for; matrix products, arithmetic and copies ran while one was open for 1% of the time, Pallas kernels for 29%

profile of v8, /device:TPU:0, one launch (start us, length us, event | category | flops | bytes accessed | tf_op | source)
XLA Modules:
  0.0 128.0 jit_solution(17697624017794203052)
XLA Ops:
  1.5 2.9 %prepare_kernel.1 = (f32[16,128]{1,0:T(8,128)}, bf16[400,384]{1,0:T(8,128)(2,1)}, bf16[400,384]{1,0:T(8,128)(2,1)}, bf16[112,512]{1,0:T(8,128)(2,1)}, bf16[112,512]{1,0:T(8,128)(2,1)}) custom-call(s32[16]{0:T(128)} %bitcast.25, s32[1]{0:T(128)} %bitcast.16.count, bf16[16,48,512]{2,1,0:T(8,128)(2,1)} %bitcast.19, bf16[16,48,512]{2,1,0:T(8,128)(2,1)} %bitcast.21), custom_call_target="tpu_custom_call" | custom-call | bytes 2424900 | tf_op jit(solution)/shard_map/prepare_kernel/pallas_call | solution.py:651
  4.4 2.4 %collective-permute-start = (bf16[112,512]{1,0:T(8,128)(2,1)}, bf16[112,512]{1,0:T(8,128)(2,1)S(1)}, u32[]{:S(2)}, u32[]{:S(2)}) collective-permute-start(bf16[112,512]{1,0:T(8,128)(2,1)} %get-tuple-element.45), channel_id=1, source_target_pairs={{0,1},{1,2},{2,3},{4,5},{5,6},{6,7},{8,9},{9,10},{10,11},{12,13},{... | collective-permute-start | bytes 344072 | tf_op jit(solution)/shard_map/ppermute | solution.py:671
  6.8 1.3 %collective-permute-start.1 = (bf16[112,512]{1,0:T(8,128)(2,1)}, bf16[112,512]{1,0:T(8,128)(2,1)S(1)}, u32[]{:S(2)}, u32[]{:S(2)}) collective-permute-start(bf16[112,512]{1,0:T(8,128)(2,1)} %get-tuple-element.46), channel_id=1, source_target_pairs={{1,0},{2,1},{3,2},{5,4},{6,5},{7,6},{9,8},{10,9},{11,10},{13,12},{... | collective-permute-start | bytes 344072 | tf_op jit(solution)/shard_map/ppermute | solution.py:671
  8.1 4.2 %collective-permute-start.2 = (bf16[400,384]{1,0:T(8,128)(2,1)}, bf16[400,384]{1,0:T(8,128)(2,1)S(1)}, u32[]{:S(2)}, u32[]{:S(2)}) collective-permute-start(bf16[400,384]{1,0:T(8,128)(2,1)} %get-tuple-element.51), channel_id=1, source_target_pairs={{0,4},{1,5},{2,6},{3,7},{4,8},{5,9},{6,10},{7,11},{8,12},{9,13},{1... | collective-permute-start | bytes 921608 | tf_op jit(solution)/shard_map/ppermute | solution.py:671
  12.3 1.3 %collective-permute-start.3 = (bf16[400,384]{1,0:T(8,128)(2,1)}, bf16[400,384]{1,0:T(8,128)(2,1)S(1)}, u32[]{:S(2)}, u32[]{:S(2)}) collective-permute-start(bf16[400,384]{1,0:T(8,128)(2,1)} %get-tuple-element.52), channel_id=1, source_target_pairs={{4,0},{5,1},{6,2},{7,3},{8,4},{9,5},{10,6},{11,7},{12,8},{13,9},{1... | collective-permute-start | bytes 921608 | tf_op jit(solution)/shard_map/ppermute | solution.py:671
  13.6 0.9 copy.17
  14.5 0.3 corner_kernel.1
  14.9 4.5 %collective-permute-start.4 = (bf16[64,384]{1,0:T(8,128)(2,1)S(1)}, bf16[64,384]{1,0:T(8,128)(2,1)S(1)}, u32[]{:S(2)}, u32[]{:S(2)}) collective-permute-start(bf16[64,384]{1,0:T(8,128)(2,1)S(1)} %get-tuple-element.53), channel_id=1, source_target_pairs={{0,4},{1,5},{2,6},{3,7},{4,8},{5,9},{6,10},{7,11},{8,12},{9,13},{1... | collective-permute-start | bytes 147464 | tf_op jit(solution)/shard_map/ppermute | solution.py:671
  19.4 1.3 %collective-permute-start.5 = (bf16[64,384]{1,0:T(8,128)(2,1)S(1)}, bf16[64,384]{1,0:T(8,128)(2,1)S(1)}, u32[]{:S(2)}, u32[]{:S(2)}) collective-permute-start(bf16[64,384]{1,0:T(8,128)(2,1)S(1)} %get-tuple-element.47.c_low), channel_id=1, source_target_pairs={{4,0},{5,1},{6,2},{7,3},{8,4},{9,5},{10,6},{11,7},{12,8},{13,9},{1... | collective-permute-start | bytes 147464 | tf_op jit(solution)/shard_map/ppermute | solution.py:671
  20.8 0.0 copy-start.4
  20.8 1.0 copy-done.4
  21.7 4.9 %place_kernel.1 = (bf16[144,48,128]{2,1,0:T(8,128)(2,1)S(1)}, bf16[80,48,128]{2,1,0:T(8,128)(2,1)S(1)}, f32[40,48,128]{2,1,0:T(8,128)S(1)}, bf16[144,432]{1,0:T(...) custom-call(s32[16]{0:T(128)S(1)} %bitcast.26, ...), custom_call_target="tpu_custom_call" | custom-call | flops 8000000000 | bytes 6480964 | tf_op jit(solution)/shard_map/place_kernel/pallas_call | solution.py:651
  26.7 0.5 collective-permute-done.4.c_left
  27.2 21.6 %forward_kernel.1 = (bf16[144,48,128]{2,1,0:T(8,128)(2,1)S(1)}, f32[80,48,128]{2,1,0:T(8,128)S(1)}, bf16[40,144,128]{2,1,0:T(8,128)(2,1)S(1)}, bf16[40,48,128]{2...) custom-call(bf16[144,48,128]{2,1,0:T(8,128)(2,1)S(1)} %get-tuple-ele, ...), custom_call_target="tpu_custom_call" | custom-call | flops 8000000000 | bytes 10263552 | tf_op jit(solution)/shard_map/forward_kernel/pallas_call | solution.py:651
  48.8 4.5 %collective-permute-start.6 = (bf16[3,48,128]{2,1,0:T(8,128)(2,1)S(1)}, bf16[3,48,128]{2,1,0:T(8,128)(2,1)S(1)}, u32[]{:S(2)}, u32[]{:S(2)}) collective-permute-start(bf16[3,48,128]{2,1,0:T(8,128)(2,1)S(1)} %get-tuple-element.59), channel_id=1, source_target_pairs={{0,4},{1,5},{2,6},{3,7},{4,8},{5,9},{6,10},{7,11},{8,12},{9,13},{1... | collective-permute-start | bytes 110600 | tf_op jit(solution)/shard_map/ppermute | solution.py:671
  53.2 1.3 %collective-permute-start.7 = (bf16[3,48,128]{2,1,0:T(8,128)(2,1)S(1)}, bf16[3,48,128]{2,1,0:T(8,128)(2,1)S(1)}, u32[]{:S(2)}, u32[]{:S(2)}) collective-permute-start(bf16[3,48,128]{2,1,0:T(8,128)(2,1)S(1)} %get-tuple-element.60), channel_id=1, source_target_pairs={{4,0},{5,1},{6,2},{7,3},{8,4},{9,5},{10,6},{11,7},{12,8},{13,9},{1... | collective-permute-start | bytes 110600 | tf_op jit(solution)/shard_map/ppermute | solution.py:671
  54.5 3.3 %side_kernel.1.early = bf16[768,128]{1,0:T(8,128)(2,1)S(1)} custom-call(bf16[40,48,128]{2,1,0:T(8,128)(2,1)S(1)} %get-tuple-element.67.rects, bf16[80,48,128]{2,1,0:T(8,128)(2,1)S(1)} %get-tuple-element.62.cot_grid, bf16[40,144,128]{2,1,0:T(8,128)(2,1)S(1)} %get-tuple-element.68.low_cols, bf16[40,48,128]{2,1,0:T(8,128)(2,1)S(1)} %get-tuple-element.58.grad_c), custom_call_target="tpu_custom_call" | custom-call | flops 8000000000 | bytes 3637248 | tf_op jit(solution)/shard_map/side_kernel/pallas_call | solution.py:651
  57.8 3.2 %collective-permute-done.7.from_right = bf16[3,48,128]{2,1,0:T(8,128)(2,1)S(1)} collective-permute-done((bf16[3,48,128]{2,1,0:T(8,128)(2,1)S(1)}, bf16[3,48,128]{2,1,0:T(8,128)(2,1)S(1)}, u32[]{:S(2)}, u32[]{:S(2)}) %collective-permute-start.7) | collective-permute-done | bytes 36896 | tf_op jit(solution)/shard_map/ppermute | solution.py:671
  61.0 8.2 %backward_kernel.1 = (bf16[80,48,128]{2,1,0:T(8,128)(2,1)S(1)}, bf16[40,48,128]{2,1,0:T(8,128)(2,1)S(1)}, bf16[9,48,128]{2,1,0:T(8,128)(2,1)S(1)}, bf16[9,48,128]{2,1,0:T(8,128)(2,1)S(1)}) custom-call(bf16[40,48,128]{2,1,0:T(8,128)(2,1)S(1)} %get-tuple-element.58.grad_c, bf16[3,48,128]{2,1,0:T(8,128)(2,1)S(1)} %collective-permute-done.6.from_left, ...), custom_call_target="tpu_custom_call" | custom-call | flops 8000000000 | bytes 5379584 | tf_op jit(solution)/shard_map/backward_kernel/pallas_call | solution.py:651
  69.2 4.8 %collective-permute-start.8 = (bf16[9,48,128]{2,1,0:T(8,128)(2,1)S(1)}, bf16[9,48,128]{2,1,0:T(8,128)(2,1)S(1)}, u32[]{:S(2)}, u32[]{:S(2)}) collective-permute-start(bf16[9,48,128]{2,1,0:T(8,128)(2,1)S(1)} %get-tuple-element.69), channel_id=1, source_target_pairs={{0,4},{1,5},{2,6},{3,7},{4,8},{5,9},{6,10},{7,11},{8,12},{9,13},{1... | collective-permute-start | bytes 331784 | tf_op jit(solution)/shard_map/ppermute | solution.py:671
  74.1 1.3 %collective-permute-start.9 = (bf16[9,48,128]{2,1,0:T(8,128)(2,1)S(1)}, bf16[9,48,128]{2,1,0:T(8,128)(2,1)S(1)}, u32[]{:S(2)}, u32[]{:S(2)}) collective-permute-start(bf16[9,48,128]{2,1,0:T(8,128)(2,1)S(1)} %get-tuple-element.70), channel_id=1, source_target_pairs={{4,0},{5,1},{6,2},{7,3},{8,4},{9,5},{10,6},{11,7},{12,8},{13,9},{1... | collective-permute-start | bytes 331784 | tf_op jit(solution)/shard_map/ppermute | solution.py:671
  75.4 10.4 %weight_kernel.1 = bf16[1536,128]{1,0:T(8,128)(2,1)} custom-call(bf16[144,48,128]{2,1,0:T(8,128)(2,1)S(1)} %get-tuple-element.57.grid, bf16[80,48,128]{2,1,0:T(8,128)(2,1)S(1)} %get-tuple-element.65.grad_h, bf16[40,48,128]{2,1,0:T(8,128)(2,1)S(1)} %get-tuple-element.66.grad_d, f32[80,48,128]{2,1,0:T(8,128)S(1)} %get-tuple-element.61.hidden, ...), custom_call_target="tpu_custom_call" | custom-call | flops 12000000000 | bytes 5799936 | tf_op jit(solution)/shard_map/weight_kernel/pallas_call | solution.py:651
  85.8 8.5 %all-to-all-start = ((bf16[32,48,128]{2,1,0:T(8,128)(2,1)}), bf16[32,48,128]{2,1,0:T(8,128)(2,1)S(1)}, u32[]{:S(2)}, u32[]{:S(2)}) async-start(bf16[32,48,128]{2,1,0:T(8,128)(2,1)} %bitcast.7), calls=%async_computation | async-start | bytes 786432 | tf_op jit(solution)/shard_map/all_to_all | solution.py:679
  94.3 4.4 %output_kernel.1 = bf16[16,48,512]{2,1,0:T(8,128)(2,1)} custom-call(s32[16]{0:T(128)S(1)} %bitcast.27, f32[80,48,128]{2,1,0:T(8,128)S(1)} %get-tuple-element.61.hidden, bf16[40,48,128]{2,1,0:T(8,128)(2,1)S(1)} %get-tuple-element.67.rects, f32[16,128]{1,0:T(8,128)S(1)} %get-tuple-element.63.live, bf16[96,192]{1,0:T(8,128)(2,1)S(1)} %get-tuple-element.73.up_w), custom_call_target="tpu_custom_call" | custom-call | flops 8000000000 | bytes 3289152 | tf_op jit(solution)/shard_map/output_kernel/pallas_call | solution.py:651
  98.7 8.6 %all-to-all-done = bf16[32,48,128]{2,1,0:T(8,128)(2,1)S(1)} async-done(((bf16[32,48,128]{2,1,0:T(8,128)(2,1)}), bf16[32,48,128]{2,1,0:T(8,128)(2,1)S(1)}, u32[]{:S(2)}, u32[]{:S(2)}) %all-to-all-start) | async-done | bytes 393248 | tf_op jit(solution)/shard_map/all_to_all | solution.py:679
  107.3 0.1 reduce_sum.12
  107.4 0.8 broadcast_in_dim.2
  108.2 2.6 %all-to-all-start.1 = ((bf16[32,48,128]{2,1,0:T(8,128)(2,1)}), bf16[32,48,128]{2,1,0:T(8,128)(2,1)S(1)}, u32[]{:S(2)}, u32[]{:S(2)}) async-start(bf16[32,48,128]{2,1,0:T(8,128)(2,1)} %broadcast_in_dim.2), calls=%async_computation.1 | async-start | bytes 786432 | tf_op jit(solution)/shard_map/all_to_all | solution.py:687
  110.8 1.2 copy-done.8
  112.0 13.7 %input_kernel.1 = bf16[16,48,512]{2,1,0:T(8,128)(2,1)} custom-call(s32[16]{0:T(128)S(1)} %bitcast.28, bf16[80,48,128]{2,1,0:T(8,128)(2,1)S(1)} %copy-done.8, bf16[9,48,128]{2,1,0:T(8,128)(2,1)S(1)} %collective-permute-done.8.from_left, bf16[9,48,128]{2,1,0:T(8,128)(2,1)S(1)} %collective-permute-done.9.from_right, f32[16,128]{1,0:T(8,128)S(1)} %get-tuple-element.63.live, ...), custom_call_target="tpu_custom_call" | custom-call | flops 8000000000 | bytes 2123328 | tf_op jit(solution)/shard_map/input_kernel/pallas_call | solution.py:651
  125.7 1.6 %finish_kernel.1 = (f32[27,48,48]{2,1,0:T(8,128)}, f32[8,48,48]{2,1,0:T(8,128)S(1)}, f32[27,48,48]{2,1,0:T(8,128)}, f32[8,48,48]{2,1,0:T(8,128)}) custom-call(bf16[1536,128]{1,0:T(8,128)(2,1)S(1)} %bitcast.18), custom_call_target="tpu_custom_call" | custom-call | bytes 1038336 | tf_op jit(solution)/shard_map/finish_kernel/pallas_call | solution.py:651
  127.3 0.7 copy.15
  (24 shorter events, 0.1 us)
Async XLA Ops:
  0.6 20.1 %copy-start.1 = (bf16[1,1,16,48,512]{4,3,2,1,0:T(8,128)(2,1)S(1)}, bf16[1,1,16,48,512]{4,3,2,1,0:T(8,128)(2,1)}, u32[]{:S(2)}) copy-start(bf16[1,1,16,48,512]{4,3,2,1,0:T(8,128)(2,1)} %param.11) | copy-start | bytes 2359300
  0.6 20.1 %copy-start.2 = (s32[1,1,16]{2,1,0:T(1,128)S(1)}, s32[1,1,16]{2,1,0:T(1,128)}, u32[]{:S(2)}) copy-start(s32[1,1,16]{2,1,0:T(1,128)} %param.9) | copy-start | bytes 196
  0.7 20.1 %copy-start = (bf16[1,1,16,48,512]{4,3,2,1,0:T(8,128)(2,1)S(1)}, bf16[1,1,16,48,512]{4,3,2,1,0:T(8,128)(2,1)}, u32[]{:S(2)}) copy-start(bf16[1,1,16,48,512]{4,3,2,1,0:T(8,128)(2,1)} %param.8) | copy-start | bytes 2359300
  0.7 20.1 %copy-start.5 = (bf16[8,48,48]{2,1,0:T(8,128)(2,1)S(1)}, bf16[8,48,48]{2,1,0:T(8,128)(2,1)}, u32[]{:S(2)}) copy-start(bf16[8,48,48]{2,1,0:T(8,128)(2,1)} %up.1) | copy-start | bytes 110596
  0.7 20.1 %copy-start.3 = (bf16[48,27,48]{2,0,1:T(8,128)(2,1)S(1)}, bf16[48,27,48]{2,0,1:T(8,128)(2,1)}, u32[]{:S(2)}) copy-start(bf16[48,27,48]{2,0,1:T(8,128)(2,1)} %param.12) | copy-start | bytes 373252
  4.4 10.1 %collective-permute-start = (bf16[112,512]{1,0:T(8,128)(2,1)}, bf16[112,512]{1,0:T(8,128)(2,1)S(1)}, u32[]{:S(2)}, u32[]{:S(2)}) collective-permute-start(bf16[112,512]{1,0:T(8,128)(2,1)} %get-tuple-element.45), channel_id=1, source_target_pairs={{0,1},{1,2},{2,3},{4,5},{5,6},{6,7},{8,9},{9,10},{10,11},{12,13},{... | collective-permute-start | bytes 344072 | tf_op jit(solution)/shard_map/ppermute | solution.py:671
  6.8 7.8 %collective-permute-start.1 = (bf16[112,512]{1,0:T(8,128)(2,1)}, bf16[112,512]{1,0:T(8,128)(2,1)S(1)}, u32[]{:S(2)}, u32[]{:S(2)}) collective-permute-start(bf16[112,512]{1,0:T(8,128)(2,1)} %get-tuple-element.46), channel_id=1, source_target_pairs={{1,0},{2,1},{3,2},{5,4},{6,5},{7,6},{9,8},{10,9},{11,10},{13,12},{... | collective-permute-start | bytes 344072 | tf_op jit(solution)/shard_map/ppermute | solution.py:671
  8.1 19.1 %collective-permute-start.2 = (bf16[400,384]{1,0:T(8,128)(2,1)}, bf16[400,384]{1,0:T(8,128)(2,1)S(1)}, u32[]{:S(2)}, u32[]{:S(2)}) collective-permute-start(bf16[400,384]{1,0:T(8,128)(2,1)} %get-tuple-element.51), channel_id=1, source_target_pairs={{0,4},{1,5},{2,6},{3,7},{4,8},{5,9},{6,10},{7,11},{8,12},{9,13},{1... | collective-permute-start | bytes 921608 | tf_op jit(solution)/shard_map/ppermute | solution.py:671
  12.3 14.9 %collective-permute-start.3 = (bf16[400,384]{1,0:T(8,128)(2,1)}, bf16[400,384]{1,0:T(8,128)(2,1)S(1)}, u32[]{:S(2)}, u32[]{:S(2)}) collective-permute-start(bf16[400,384]{1,0:T(8,128)(2,1)} %get-tuple-element.52), channel_id=1, source_target_pairs={{4,0},{5,1},{6,2},{7,3},{8,4},{9,5},{10,6},{11,7},{12,8},{13,9},{1... | collective-permute-start | bytes 921608 | tf_op jit(solution)/shard_map/ppermute | solution.py:671
  14.9 12.3 %collective-permute-start.4 = (bf16[64,384]{1,0:T(8,128)(2,1)S(1)}, bf16[64,384]{1,0:T(8,128)(2,1)S(1)}, u32[]{:S(2)}, u32[]{:S(2)}) collective-permute-start(bf16[64,384]{1,0:T(8,128)(2,1)S(1)} %get-tuple-element.53), channel_id=1, source_target_pairs={{0,4},{1,5},{2,6},{3,7},{4,8},{5,9},{6,10},{7,11},{8,12},{9,13},{1... | collective-permute-start | bytes 147464 | tf_op jit(solution)/shard_map/ppermute | solution.py:671
  19.4 7.8 %collective-permute-start.5 = (bf16[64,384]{1,0:T(8,128)(2,1)S(1)}, bf16[64,384]{1,0:T(8,128)(2,1)S(1)}, u32[]{:S(2)}, u32[]{:S(2)}) collective-permute-start(bf16[64,384]{1,0:T(8,128)(2,1)S(1)} %get-tuple-element.47.c_low), channel_id=1, source_target_pairs={{4,0},{5,1},{6,2},{7,3},{8,4},{9,5},{10,6},{11,7},{12,8},{13,9},{1... | collective-permute-start | bytes 147464 | tf_op jit(solution)/shard_map/ppermute | solution.py:671
  20.8 1.0 copy-start.4
  21.7 5.4 %copy-start.6 = (f32[16,128]{1,0:T(8,128)S(1)}, f32[16,128]{1,0:T(8,128)}, u32[]{:S(2)}) copy-start(f32[16,128]{1,0:T(8,128)} %get-tuple-element.49.flags) | copy-start | bytes 24580
  48.8 9.0 %collective-permute-start.6 = (bf16[3,48,128]{2,1,0:T(8,128)(2,1)S(1)}, bf16[3,48,128]{2,1,0:T(8,128)(2,1)S(1)}, u32[]{:S(2)}, u32[]{:S(2)}) collective-permute-start(bf16[3,48,128]{2,1,0:T(8,128)(2,1)S(1)} %get-tuple-element.59), channel_id=1, source_target_pairs={{0,4},{1,5},{2,6},{3,7},{4,8},{5,9},{6,10},{7,11},{8,12},{9,13},{1... | collective-permute-start | bytes 110600 | tf_op jit(solution)/shard_map/ppermute | solution.py:671
  53.2 7.8 %collective-permute-start.7 = (bf16[3,48,128]{2,1,0:T(8,128)(2,1)S(1)}, bf16[3,48,128]{2,1,0:T(8,128)(2,1)S(1)}, u32[]{:S(2)}, u32[]{:S(2)}) collective-permute-start(bf16[3,48,128]{2,1,0:T(8,128)(2,1)S(1)} %get-tuple-element.60), channel_id=1, source_target_pairs={{4,0},{5,1},{6,2},{7,3},{8,4},{9,5},{10,6},{11,7},{12,8},{13,9},{1... | collective-permute-start | bytes 110600 | tf_op jit(solution)/shard_map/ppermute | solution.py:671
  69.2 16.5 %copy-start.7 = (bf16[80,48,128]{2,1,0:T(8,128)(2,1)}, bf16[80,48,128]{2,1,0:T(8,128)(2,1)S(1)}, u32[]{:S(2)}) copy-start(bf16[80,48,128]{2,1,0:T(8,128)(2,1)S(1)} %get-tuple-element.65.grad_h) | copy-start | bytes 2949124
  69.2 16.5 %collective-permute-start.8 = (bf16[9,48,128]{2,1,0:T(8,128)(2,1)S(1)}, bf16[9,48,128]{2,1,0:T(8,128)(2,1)S(1)}, u32[]{:S(2)}, u32[]{:S(2)}) collective-permute-start(bf16[9,48,128]{2,1,0:T(8,128)(2,1)S(1)} %get-tuple-element.69), channel_id=1, source_target_pairs={{0,4},{1,5},{2,6},{3,7},{4,8},{5,9},{6,10},{7,11},{8,12},{9,13},{1... | collective-permute-start | bytes 331784 | tf_op jit(solution)/shard_map/ppermute | solution.py:671
  74.1 11.7 %collective-permute-start.9 = (bf16[9,48,128]{2,1,0:T(8,128)(2,1)S(1)}, bf16[9,48,128]{2,1,0:T(8,128)(2,1)S(1)}, u32[]{:S(2)}, u32[]{:S(2)}) collective-permute-start(bf16[9,48,128]{2,1,0:T(8,128)(2,1)S(1)} %get-tuple-element.70), channel_id=1, source_target_pairs={{4,0},{5,1},{6,2},{7,3},{8,4},{9,5},{10,6},{11,7},{12,8},{13,9},{1... | collective-permute-start | bytes 331784 | tf_op jit(solution)/shard_map/ppermute | solution.py:671
  85.8 21.5 %all-to-all-start = ((bf16[32,48,128]{2,1,0:T(8,128)(2,1)}), bf16[32,48,128]{2,1,0:T(8,128)(2,1)S(1)}, u32[]{:S(2)}, u32[]{:S(2)}) async-start(bf16[32,48,128]{2,1,0:T(8,128)(2,1)} %bitcast.7), calls=%async_computation | async-start | bytes 786432 | tf_op jit(solution)/shard_map/all_to_all | solution.py:679
  108.2 17.5 %all-to-all-start.1 = ((bf16[32,48,128]{2,1,0:T(8,128)(2,1)}), bf16[32,48,128]{2,1,0:T(8,128)(2,1)S(1)}, u32[]{:S(2)}, u32[]{:S(2)}) async-start(bf16[32,48,128]{2,1,0:T(8,128)(2,1)} %broadcast_in_dim.2), calls=%async_computation.1 | async-start | bytes 786432 | tf_op jit(solution)/shard_map/all_to_all | solution.py:687
  110.8 1.2 copy-start.8

commit v9 on v8

--- a/solution.py
+++ b/solution.py
@@ -72,26 +72,75 @@
 
 
 def depth_columns(base, masks, step):
-    zero = jnp.zeros_like(base)
-    below = jnp.where(masks[0], zero, roll(base, step))
-    above = jnp.where(masks[1], zero, roll(base, -step))
+    below = roll(base, step) * masks[0]
+    above = roll(base, -step) * masks[1]
     return jnp.concatenate([below, base, above], axis=0)
 
 
 def depth_masks(step, first):
     ids = (lane_ids(3 * C) - first) % LANES
-    return ids < step, ids >= LANES - step
+    return (ids >= step).astype(BF16), (ids < LANES - step).astype(BF16)
 
 
 def across_columns(tile, step):
     return jnp.concatenate([roll(tile, step), tile, roll(tile, -step)], axis=0)
 
 
-def pair_columns(tile, halo, step):
+def edge_masks(step):
     ids = lane_ids(C) % 8
-    left = jnp.where(ids == 4, roll(halo, step), roll(tile, step))
-    right = jnp.where(ids == 4 - step, roll(halo, -step), roll(tile, -step))
+    first, last = (ids == 4).astype(BF16), (ids == 4 - step).astype(BF16)
+    return first, (ids != 4).astype(BF16), last, (ids != 4 - step).astype(BF16)
+
+
+def pair_columns(tile, halo, masks, step):
+    left = roll(halo, step) * masks[0] + roll(tile, step) * masks[1]
+    right = roll(halo, -step) * masks[2] + roll(tile, -step) * masks[3]
     return jnp.concatenate([left, tile, right], axis=0)
+
+
+def fill_columns(tiles, from_left, from_right, out, step):
+    masks = edge_masks(step)
+
+    def body(group):
+        packed_left, packed_right = from_left[group], from_right[group]
+        for place in range(8):
+            tile = tiles[8 * group + place]
+            left = roll(packed_left, -place) * masks[0] + roll(tile, step) * masks[1]
+            right = roll(packed_right, 8 - step - place) * masks[2]
+            right = right + roll(tile, -step) * masks[3]
+            out[8 * group + place] = jnp.concatenate([left, tile, right], axis=0)
+
+    loop(0, from_left.shape[0], body)
+
+
+def pack_columns(tiles, low, high, step):
+    masks = edge_masks(step)
+
+    def body(group):
+        lows, highs = [], []
+        for place in range(8):
+            tile = tiles[8 * group + place]
+            lows.append(roll(tile * masks[0], place))
+            highs.append(roll(tile * masks[2], place - 8 + step))
+        for out, parts in ((low, lows), (high, highs)):
+            while len(parts) > 1:
+                parts = [a + b for a, b in zip(parts[::2], parts[1::2])]
+            out[group] = parts[0]
+
+    loop(0, low.shape[0], body)
+
+
+def own_masks():
+    own = own_lanes(C)
+    return own.astype(BF16), jnp.logical_not(own).astype(BF16)
+
+
+def pair_tiles(lower, upper, masks):
+    turned = roll(upper, 8)
+    return (
+        lower * masks[0] + turned * masks[1],
+        lower * masks[1] + turned * masks[0],
+    )
 
 
 def own_lanes(rows):
@@ -101,19 +150,6 @@
 
 def join_halves(lower, upper):
     return jnp.where(own_lanes(lower.shape[0]), lower, roll(upper, 8))
-
-
-def join_halos(lower, upper):
-    return jnp.where(own_lanes(lower.shape[0]), roll(upper, 8), lower)
-
-
-def packed_halo(from_left, from_right, first, second, place, step):
-    ids = lane_ids(C) % 16
-    zero = jnp.zeros((C, LANES), BF16)
-    halo = jnp.where(ids == 4 - step, roll(from_left[first], 4 - step - place), zero)
-    halo = jnp.where(ids == 12 - step, roll(from_left[second], 12 - step - place), halo)
-    halo = jnp.where(ids == 12, roll(from_right[first], 12 - place), halo)
-    return jnp.where(ids == 4, roll(from_right[second], 20 - place), halo)
 
 
 def gather_sub(parts):
@@ -216,7 +252,7 @@
             fore[rows, :] = jnp.concatenate(ahead, axis=1)
             back[turned_rows, :] = jnp.concatenate(behind, axis=1)
     for index in range(4):
-        pair = [down[2 * index], down[2 * index + 1]]
+        pair = [down[:, 2 * index, :], down[:, 2 * index + 1, :]]
         down_w[C * index : C * (index + 1), :] = jnp.concatenate(pair, axis=1)
     for along in range(2):
         row = jnp.concatenate([up[2 * index + along] for index in range(4)], axis=1)
@@ -299,7 +335,7 @@
     grid_own, flags, y_left, y_right, grad_r, x_left, x_right, c_left, c_right, fine_w, down_w,
     coarse_w,
     grid, hidden, low_cols, rects, grad_c, live, pack_low, pack_high,
-    rows_in, fine_p, coarse_p, hidden_all, lowered, live_all, ring,
+    rows_in, fine_p, coarse_p, hidden_all, lowered, live_all,
 ):
     number = 2 * (x_left.shape[0] - 16) // C
     last = number + 1
@@ -336,13 +372,10 @@
                 grid[tile] = grid_own[tile] + halo
     live[...] = join_halves(live_all[0:16, :], live_all[8:24, :])
     tiles = grid.shape[0]
+    conv_steps(fine_p, fine_w, lambda tile: across_columns(grid[tile], 1), tiles, 16, 0, 2)
     anchors = anchor_mask(0)
-    masks = depth_masks(16, 0)
-    blocks = last + 1
-    ring[1] = jnp.zeros(ring.shape[1:], BF16)
-
-    def fine_step(index):
-        block = jnp.maximum(index - 3, 0)
+
+    def lower_step(block):
         alive = jnp.broadcast_to(live_all[pl.ds(block, 1), :], (C, LANES))
         keep = alive * anchors
         pairs = []
@@ -350,7 +383,7 @@
             actives = []
             for half in range(2):
                 tile = EDGE * block + 2 * inner + half
-                value = conv_sum(fine_p, tile + EDGE - 1) * alive
+                value = conv_sum(fine_p, tile) * alive
                 hidden_all[tile] = value
                 actives.append(silu_parts(value)[0].astype(BF16))
             pairs.append(jnp.concatenate(actives, axis=0))
@@ -358,19 +391,12 @@
         for inner in range(4):
             total = gather_sub(parts[:, LANES * inner : LANES * (inner + 1)])
             lowered[4 * block + inner] = (total * keep).astype(BF16)
-        ready = lax.rem(index + 1, 2)
-        for quad in range(2):
-            out = dot(fine_w[...], ring[ready, quad])
-            for i in range(4):
-                fine_p[EDGE * index + 4 * quad + i] = out[:, LANES * i : LANES * (i + 1)]
-        first = EDGE * jnp.minimum(index, blocks - 1)
-        for inner in range(EDGE):
-            cols = depth_columns(across_columns(grid[first + inner], 1), masks, 16)
-            ring[lax.rem(index, 2), inner // 4, :, LANES * (inner % 4) : LANES * (inner % 4 + 1)] = cols
-
-    loop(0, blocks + 3, fine_step)
+
+    loop(0, last + 1, lower_step, 2)
     pairs = hidden.shape[0] // EDGE
     shift = last - pairs + 1
+    edges = edge_masks(2)
+    halves = own_masks()
 
     def pair_step(block):
         for inner in range(EDGE):
@@ -379,7 +405,7 @@
         for inner in range(4):
             tile = 4 * block + inner
             lower, upper = lowered[tile], lowered[tile + 4 * shift]
-            low_cols[tile] = pair_columns(join_halves(lower, upper), join_halos(lower, upper), 2)
+            low_cols[tile] = pair_columns(*pair_tiles(lower, upper, halves), edges, 2)
 
     loop(0, pairs, pair_step, 2)
     conv_steps(coarse_p, coarse_w, lambda tile: low_cols[tile], 4 * pairs, 32, 4, 2)
@@ -395,19 +421,7 @@
             grad_c[coarse] = (grad_r[coarse] * slope * keep).astype(BF16)
 
     loop(0, pairs, grad_step, 2)
-    ids = lane_ids(C)
-    zero = jnp.zeros((C, LANES), BF16)
-    half = 2 * number
-    for out, lane in ((pack_low, 4), (pack_high, 10)):
-        for group in range(out.shape[0]):
-            total = zero
-            for coarse in range(max(2, 32 * group), min(2 * half + 6, 32 * group + 32)):
-                upper = coarse >= half + 4
-                tile = grad_c[coarse - half] if upper else grad_c[coarse]
-                at = lane + 8 if upper else lane
-                picked = jnp.where(ids % 32 == at, tile, zero)
-                total = total + roll(picked, coarse % 32 - at)
-            out[group] = total
+    pack_columns(grad_c, pack_low, pack_high, 2)
 
 
 def to_blocks(slots, rows_out, flat, out):
@@ -500,11 +514,7 @@
     grad_h, grad_d, pack_low, pack_high, coarse_p, grad_x,
 ):
     tiles = grad_c.shape[0]
-    half = tiles - 8
-    for coarse in range(tiles):
-        first, second = coarse // 32, (coarse + half) // 32
-        halo = packed_halo(from_left, from_right, first, second, coarse % 32, 2)
-        grad_x[coarse] = pair_columns(grad_c[coarse], halo, 2)
+    fill_columns(grad_c, from_left, from_right, grad_x, 2)
     conv_steps(coarse_p, coarse_w, lambda tile: grad_x[tile], tiles, 32, 4, 2)
     anchors = anchor_mask(4)
 
@@ -527,23 +537,10 @@
                 grad_h[tile] = (grad * alive).astype(BF16)
 
     loop(0, tiles // 4, step, 2)
-    fine = 2 * tiles
-    shift = fine - 16
-    ids = lane_ids(C) % 16
-    zero = jnp.zeros((C, LANES), BF16)
-    for out, lane in ((pack_low, 4), (pack_high, 11)):
-        for group in range(out.shape[0]):
-            total = zero
-            for tile in range(16 * group, 16 * group + 16):
-                upper = tile >= shift + 8
-                source = grad_h[tile - shift] if upper else grad_h[tile]
-                at = lane + 8 if upper else lane
-                picked = jnp.where(ids == at % 16, source, zero)
-                total = total + roll(picked, tile % 16 - at)
-            out[group] = total
-
-
-def weight_kernel(grid, grad_h, grad_d, hidden, early, joined, grad_own, fine_g, down_g, ring):
+    pack_columns(grad_h, pack_low, pack_high, 1)
+
+
+def weight_kernel(grid, grad_h, grad_d, hidden, early, joined, grad_own, fine_g, down_g):
     tiles = grad_h.shape[0]
     shift = tiles - 16
     fine_g[...] = jnp.zeros_like(fine_g)
@@ -558,22 +555,21 @@
 
     loop(8, tiles - 8, copy_step, 8)
     masks = depth_masks(16, 4)
-
-    steps = (tiles - 8) // 8
-    ring[1] = jnp.zeros(ring.shape[1:], BF16)
+    edges = edge_masks(1)
+    halves = own_masks()
 
     def fine_step(index):
-        at = [4 + 8 * jnp.maximum(index - 1, 0) + inner for inner in range(8)]
-        fine_g[0 : 9 * C, :] += dot(ring[lax.rem(index + 1, 2)], stacks(grad_own, at), (1, 1))
-        first = 4 + 8 * jnp.minimum(index, steps - 1)
-        for inner in range(8):
-            lower, upper = grid[first + inner], grid[first + inner + shift]
-            base = pair_columns(join_halves(lower, upper), join_halos(lower, upper), 1)
-            ring[lax.rem(index, 2), :, LANES * inner : LANES * (inner + 1)] = depth_columns(
-                base, masks, 16
-            )
-
-    loop(0, steps + 1, fine_step)
+        at = [4 + 8 * index + inner for inner in range(8)]
+        rights = []
+        for tile in at:
+            lower, upper = grid[tile], grid[tile + shift]
+            base = pair_columns(*pair_tiles(lower, upper, halves), edges, 1)
+            rights.append(depth_columns(base, masks, 16))
+        fine_g[0 : 9 * C, :] += dot(
+            jnp.concatenate(rights, axis=1), stacks(grad_own, at), (1, 1)
+        )
+
+    loop(0, (tiles - 8) // 8, fine_step)
 
     def down_step(index):
         lefts = []
@@ -598,16 +594,7 @@
     fine_p, rows_out, flat, grad_x,
 ):
     tiles = grad_h.shape[0]
-    shift = tiles - 16
-
-    def fill_step(group):
-        for inner in range(16):
-            tile = 16 * group + inner
-            second = group + shift // 16
-            halo = packed_halo(from_left, from_right, group, second, inner, 1)
-            grad_x[tile] = pair_columns(grad_h[tile], halo, 1)
-
-    loop(0, tiles // 16, fill_step)
+    fill_columns(grad_h, from_left, from_right, grad_x, 1)
     conv_steps(fine_p, fine_w, lambda tile: grad_x[tile], tiles, 16, 4, 2)
 
     def block_step(block):
@@ -700,12 +687,10 @@
     tiles = EDGE * (number + 2)
     coarse_tiles = tiles // 2
     pairs = number // 2 + 2
-    groups = -(-coarse_tiles // 32)
-    fine_groups = tiles // 16
-
-    fine_3, down_3, coarse_3 = (
-        weight.transpose(1, 0, 2) for weight in (fine_weight, down_weight, coarse_weight)
-    )
+    groups = pairs // 2
+    fine_groups = pairs
+
+    fine_3, coarse_3 = (weight.transpose(1, 0, 2) for weight in (fine_weight, coarse_weight))
     flag_rows, x_low, x_high, y_low, y_high = call(
         prepare_kernel,
         (slots, count, feats, cots),
@@ -730,7 +715,7 @@
     (grid_own, cot_grid, grad_r, fine_fore, fine_back, coarse_fore, coarse_back, down_w,
      up_w) = call(
         place_kernel,
-        (slots, count, feats, cots, y_left, y_right, corner_low, fine_3, down_3, coarse_3,
+        (slots, count, feats, cots, y_left, y_right, corner_low, fine_3, down_weight, coarse_3,
          up_weight),
         [
             ((tiles, C, LANES), BF16),
@@ -763,12 +748,11 @@
         ],
         [
             (((number + 2) * C, VOX), BF16),
-            ((tiles + 3 * EDGE, 3 * C, LANES), F32),
+            ((tiles + 2, 3 * C, LANES), F32),
             ((4 * pairs + 2, 3 * C, LANES), F32),
             ((tiles, C, LANES), F32),
             ((coarse_tiles, C, LANES), BF16),
             ((C, LANES), F32),
-            ((2, 2, 9 * C, 4 * LANES), BF16),
         ],
         flops=8 * 10**9,
     )
@@ -799,12 +783,7 @@
         weight_kernel,
         (grid, grad_h, grad_d, hidden, early),
         [((32 * C, LANES), BF16)],
-        [
-            ((EDGE * pairs, C, LANES), BF16),
-            ((VOX, 3 * C), F32),
-            ((4 * C, LANES), F32),
-            ((2, 9 * C, 8 * LANES), BF16),
-        ],
+        [((EDGE * pairs, C, LANES), BF16), ((VOX, 3 * C), F32), ((4 * C, LANES), F32)],
         flops=12 * 10**9,
     )
     joined, edge_left, edge_right, slots = lax.optimization_barrier(

time: 129 us -> 122 us (0.946)
  Pallas kernels: 71.3 us -> 61.7 us
  waiting for transfers between devices: 12.3 us -> 15.5 us
    pallas_call x10, Pallas kernels: 71.3 us -> 61.7 us  [call(): pl.pallas_call(kernel, out_shape=tuple((jax.ShapeDtypeStruct(s, d) for s,...]
    all_to_all x1, waiting for transfers between devices: 0.01 us -> 2.74 us  [spread_share(): full = lax.all_to_all(copies, ('gx', 'gy'), 0, 0)]
    unnamed x20 -> x21, local copies, waits for them, and re-layouts: 3.84 us -> 3.9 us
  transfers between devices with their start and end apart: 12 -> 12, of which waited for: 3 -> 4; matrix products, arithmetic and copies ran while one was open for 1% -> 0% of each run, Pallas kernels for 29% -> 25%
where the time goes in v9:
time: 122 us; the launch traced here: 121 us
  Pallas kernels  61.7 us (51%)
  starting transfers between devices  37.6 us (31%)
  waiting for transfers between devices  15.5 us (13%)
  local copies, waits for them, and re-layouts  4.7 us (4%)
  between operations  1.68 us (1%)
    pallas_call x10, Pallas kernels, call(): pl.pallas_call(kernel, out_shape=tuple((jax.ShapeDtypeStruct(s, d) for s,...  61.7 us
    ppermute x10, starting transfers between devices, send(): return lax.ppermute(array, ('gx', 'gy'), pairs)  26.8 us
    all_to_all x1, waiting for transfers between devices, reduce_share(): lax.all_to_all(joined.reshape(devices, share, LANES), ('gx', 'gy'), 0, 0)  8.75 us
    all_to_all x1, starting transfers between devices, reduce_share(): lax.all_to_all(joined.reshape(devices, share, LANES), ('gx', 'gy'), 0, 0)  8.18 us
    ppermute x10, waiting for transfers between devices, send(): return lax.ppermute(array, ('gx', 'gy'), pairs)  4.01 us
    unnamed x21, local copies, waits for them, and re-layouts  3.9 us
    all_to_all x1, waiting for transfers between devices, spread_share(): full = lax.all_to_all(copies, ('gx', 'gy'), 0, 0)  2.74 us
    all_to_all x1, starting transfers between devices, spread_share(): full = lax.all_to_all(copies, ('gx', 'gy'), 0, 0)  2.64 us
  transfers between devices with their start and end apart: 12, of which 4 were waited for; matrix products, arithmetic and copies ran while one was open for 0% of the time, Pallas kernels for 25%

profile of v9, /device:TPU:0, one launch (start us, length us, event | category | flops | bytes accessed | tf_op | source)
XLA Modules:
  0.0 121.2 jit_solution(5427377686989547758)
XLA Ops:
  1.5 2.9 %prepare_kernel.1 = (f32[16,128]{1,0:T(8,128)}, bf16[400,384]{1,0:T(8,128)(2,1)}, bf16[400,384]{1,0:T(8,128)(2,1)}, bf16[112,512]{1,0:T(8,128)(2,1)}, bf16[112,512]{1,0:T(8,128)(2,1)}) custom-call(s32[16]{0:T(128)} %bitcast.21, s32[1]{0:T(128)} %bitcast.13.count, bf16[16,48,512]{2,1,0:T(8,128)(2,1)} %bitcast.16, bf16[16,48,512]{2,1,0:T(8,128)(2,1)} %bitcast.18), custom_call_target="tpu_custom_call" | custom-call | bytes 2424900 | tf_op jit(solution)/shard_map/prepare_kernel/pallas_call | solution.py:638
  4.4 2.4 %collective-permute-start = (bf16[112,512]{1,0:T(8,128)(2,1)}, bf16[112,512]{1,0:T(8,128)(2,1)S(1)}, u32[]{:S(2)}, u32[]{:S(2)}) collective-permute-start(bf16[112,512]{1,0:T(8,128)(2,1)} %get-tuple-element.45), channel_id=1, source_target_pairs={{0,1},{1,2},{2,3},{4,5},{5,6},{6,7},{8,9},{9,10},{10,11},{12,13},{... | collective-permute-start | bytes 344072 | tf_op jit(solution)/shard_map/ppermute | solution.py:658
  6.7 1.3 %collective-permute-start.1 = (bf16[112,512]{1,0:T(8,128)(2,1)}, bf16[112,512]{1,0:T(8,128)(2,1)S(1)}, u32[]{:S(2)}, u32[]{:S(2)}) collective-permute-start(bf16[112,512]{1,0:T(8,128)(2,1)} %get-tuple-element.46), channel_id=1, source_target_pairs={{1,0},{2,1},{3,2},{5,4},{6,5},{7,6},{9,8},{10,9},{11,10},{13,12},{... | collective-permute-start | bytes 344072 | tf_op jit(solution)/shard_map/ppermute | solution.py:658
  8.0 4.2 %collective-permute-start.2 = (bf16[400,384]{1,0:T(8,128)(2,1)}, bf16[400,384]{1,0:T(8,128)(2,1)S(1)}, u32[]{:S(2)}, u32[]{:S(2)}) collective-permute-start(bf16[400,384]{1,0:T(8,128)(2,1)} %get-tuple-element.51), channel_id=1, source_target_pairs={{0,4},{1,5},{2,6},{3,7},{4,8},{5,9},{6,10},{7,11},{8,12},{9,13},{1... | collective-permute-start | bytes 921608 | tf_op jit(solution)/shard_map/ppermute | solution.py:658
  12.3 1.3 %collective-permute-start.3 = (bf16[400,384]{1,0:T(8,128)(2,1)}, bf16[400,384]{1,0:T(8,128)(2,1)S(1)}, u32[]{:S(2)}, u32[]{:S(2)}) collective-permute-start(bf16[400,384]{1,0:T(8,128)(2,1)} %get-tuple-element.52), channel_id=1, source_target_pairs={{4,0},{5,1},{6,2},{7,3},{8,4},{9,5},{10,6},{11,7},{12,8},{13,9},{1... | collective-permute-start | bytes 921608 | tf_op jit(solution)/shard_map/ppermute | solution.py:658
  13.6 0.3 corner_kernel.1
  13.9 4.5 %collective-permute-start.4 = (bf16[64,384]{1,0:T(8,128)(2,1)S(1)}, bf16[64,384]{1,0:T(8,128)(2,1)S(1)}, u32[]{:S(2)}, u32[]{:S(2)}) collective-permute-start(bf16[64,384]{1,0:T(8,128)(2,1)S(1)} %get-tuple-element.53), channel_id=1, source_target_pairs={{0,4},{1,5},{2,6},{3,7},{4,8},{5,9},{6,10},{7,11},{8,12},{9,13},{1... | collective-permute-start | bytes 147464 | tf_op jit(solution)/shard_map/ppermute | solution.py:658
  18.5 1.3 %collective-permute-start.5 = (bf16[64,384]{1,0:T(8,128)(2,1)S(1)}, bf16[64,384]{1,0:T(8,128)(2,1)S(1)}, u32[]{:S(2)}, u32[]{:S(2)}) collective-permute-start(bf16[64,384]{1,0:T(8,128)(2,1)S(1)} %get-tuple-element.47.c_low), channel_id=1, source_target_pairs={{4,0},{5,1},{6,2},{7,3},{8,4},{9,5},{10,6},{11,7},{12,8},{13,9},{1... | collective-permute-start | bytes 147464 | tf_op jit(solution)/shard_map/ppermute | solution.py:658
  19.8 1.0 copy-done.3
  20.8 1.0 copy-done.4
  21.8 5.0 %place_kernel.1 = (bf16[144,48,128]{2,1,0:T(8,128)(2,1)S(1)}, bf16[80,48,128]{2,1,0:T(8,128)(2,1)S(1)}, f32[40,48,128]{2,1,0:T(8,128)S(1)}, bf16[144,432]{1,0:T(...) custom-call(s32[16]{0:T(128)S(1)} %bitcast.22, ...), custom_call_target="tpu_custom_call" | custom-call | flops 8000000000 | bytes 6480964 | tf_op jit(solution)/shard_map/place_kernel/pallas_call | solution.py:638
  26.8 0.5 collective-permute-done.4.c_left
  27.3 20.5 %forward_kernel.1 = (bf16[144,48,128]{2,1,0:T(8,128)(2,1)S(1)}, f32[80,48,128]{2,1,0:T(8,128)S(1)}, bf16[40,144,128]{2,1,0:T(8,128)(2,1)S(1)}, bf16[40,48,128]{2...) custom-call(bf16[144,48,128]{2,1,0:T(8,128)(2,1)S(1)} %get-tuple-ele, ...), custom_call_target="tpu_custom_call" | custom-call | flops 8000000000 | bytes 10312704 | tf_op jit(solution)/shard_map/forward_kernel/pallas_call | solution.py:638
  47.8 4.5 %collective-permute-start.6 = (bf16[5,48,128]{2,1,0:T(8,128)(2,1)S(1)}, bf16[5,48,128]{2,1,0:T(8,128)(2,1)S(1)}, u32[]{:S(2)}, u32[]{:S(2)}) collective-permute-start(bf16[5,48,128]{2,1,0:T(8,128)(2,1)S(1)} %get-tuple-element.59), channel_id=1, source_target_pairs={{0,4},{1,5},{2,6},{3,7},{4,8},{5,9},{6,10},{7,11},{8,12},{9,13},{1... | collective-permute-start | bytes 184328 | tf_op jit(solution)/shard_map/ppermute | solution.py:658
  52.3 1.3 %collective-permute-start.7 = (bf16[5,48,128]{2,1,0:T(8,128)(2,1)S(1)}, bf16[5,48,128]{2,1,0:T(8,128)(2,1)S(1)}, u32[]{:S(2)}, u32[]{:S(2)}) collective-permute-start(bf16[5,48,128]{2,1,0:T(8,128)(2,1)S(1)} %get-tuple-element.60), channel_id=1, source_target_pairs={{4,0},{5,1},{6,2},{7,3},{8,4},{9,5},{10,6},{11,7},{12,8},{13,9},{1... | collective-permute-start | bytes 184328 | tf_op jit(solution)/shard_map/ppermute | solution.py:658
  53.6 3.3 %side_kernel.1.early = bf16[768,128]{1,0:T(8,128)(2,1)S(1)} custom-call(bf16[40,48,128]{2,1,0:T(8,128)(2,1)S(1)} %get-tuple-element.67.rects, bf16[80,48,128]{2,1,0:T(8,128)(2,1)S(1)} %get-tuple-element.62.cot_grid, bf16[40,144,128]{2,1,0:T(8,128)(2,1)S(1)} %get-tuple-element.68.low_cols, bf16[40,48,128]{2,1,0:T(8,128)(2,1)S(1)} %get-tuple-element.58.grad_c), custom_call_target="tpu_custom_call" | custom-call | flops 8000000000 | bytes 3637248 | tf_op jit(solution)/shard_map/side_kernel/pallas_call | solution.py:638
  56.8 3.4 %collective-permute-done.7.from_right = bf16[5,48,128]{2,1,0:T(8,128)(2,1)S(1)} collective-permute-done((bf16[5,48,128]{2,1,0:T(8,128)(2,1)S(1)}, bf16[5,48,128]{2,1,0:T(8,128)(2,1)S(1)}, u32[]{:S(2)}, u32[]{:S(2)}) %collective-permute-start.7) | collective-permute-done | bytes 61472 | tf_op jit(solution)/shard_map/ppermute | solution.py:658
  60.3 5.9 %backward_kernel.1 = (bf16[80,48,128]{2,1,0:T(8,128)(2,1)S(1)}, bf16[40,48,128]{2,1,0:T(8,128)(2,1)S(1)}, bf16[10,48,128]{2,1,0:T(8,128)(2,1)S(1)}, bf16[10,48,128]{2,1,0:T(8,128)(2,1)S(1)}) custom-call(bf16[40,48,128]{2,1,0:T(8,128)(2,1)S(1)} %get-tuple-element.58.grad_c, bf16[5,48,128]{2,1,0:T(8,128)(2,1)S(1)} %collective-permute-done.6.from_left, ...), custom_call_target="tpu_custom_call" | custom-call | flops 8000000000 | bytes 5453312 | tf_op jit(solution)/shard_map/backward_kernel/pallas_call | solution.py:638
  66.2 4.7 %collective-permute-start.8 = (bf16[10,48,128]{2,1,0:T(8,128)(2,1)S(1)}, bf16[10,48,128]{2,1,0:T(8,128)(2,1)S(1)}, u32[]{:S(2)}, u32[]{:S(2)}) collective-permute-start(bf16[10,48,128]{2,1,0:T(8,128)(2,1)S(1)} %get-tuple-element.69), channel_id=1, source_target_pairs={{0,4},{1,5},{2,6},{3,7},{4,8},{5,9},{6,10},{7,11},{8,12},{9,13},{1... | collective-permute-start | bytes 368648 | tf_op jit(solution)/shard_map/ppermute | solution.py:658
  70.9 1.3 %collective-permute-start.9 = (bf16[10,48,128]{2,1,0:T(8,128)(2,1)S(1)}, bf16[10,48,128]{2,1,0:T(8,128)(2,1)S(1)}, u32[]{:S(2)}, u32[]{:S(2)}) collective-permute-start(bf16[10,48,128]{2,1,0:T(8,128)(2,1)S(1)} %get-tuple-element.70), channel_id=1, source_target_pairs={{4,0},{5,1},{6,2},{7,3},{8,4},{9,5},{10,6},{11,7},{12,8},{13,9},{1... | collective-permute-start | bytes 368648 | tf_op jit(solution)/shard_map/ppermute | solution.py:658
  72.2 8.6 %weight_kernel.1 = bf16[1536,128]{1,0:T(8,128)(2,1)} custom-call(bf16[144,48,128]{2,1,0:T(8,128)(2,1)S(1)} %get-tuple-element.57.grid, bf16[80,48,128]{2,1,0:T(8,128)(2,1)S(1)} %get-tuple-element.65.grad_h, bf16[40,48,128]{2,1,0:T(8,128)(2,1)S(1)} %get-tuple-element.66.grad_d, f32[80,48,128]{2,1,0:T(8,128)S(1)} %get-tuple-element.61.hidden, ...), custom_call_target="tpu_custom_call" | custom-call | flops 12000000000 | bytes 5799936 | tf_op jit(solution)/shard_map/weight_kernel/pallas_call | solution.py:638
  80.8 8.2 %all-to-all-start = ((bf16[32,48,128]{2,1,0:T(8,128)(2,1)}), bf16[32,48,128]{2,1,0:T(8,128)(2,1)S(1)}, u32[]{:S(2)}, u32[]{:S(2)}) async-start(bf16[32,48,128]{2,1,0:T(8,128)(2,1)} %bitcast.6), calls=%async_computation | async-start | bytes 786432 | tf_op jit(solution)/shard_map/all_to_all | solution.py:666
  89.0 4.4 %output_kernel.1 = bf16[16,48,512]{2,1,0:T(8,128)(2,1)} custom-call(s32[16]{0:T(128)S(1)} %bitcast.23, f32[80,48,128]{2,1,0:T(8,128)S(1)} %get-tuple-element.61.hidden, bf16[40,48,128]{2,1,0:T(8,128)(2,1)S(1)} %get-tuple-element.67.rects, f32[16,128]{1,0:T(8,128)S(1)} %get-tuple-element.63.live, bf16[96,192]{1,0:T(8,128)(2,1)S(1)} %get-tuple-element.73.up_w), custom_call_target="tpu_custom_call" | custom-call | flops 8000000000 | bytes 3289152 | tf_op jit(solution)/shard_map/output_kernel/pallas_call | solution.py:638
  93.5 8.7 %all-to-all-done = bf16[32,48,128]{2,1,0:T(8,128)(2,1)S(1)} async-done(((bf16[32,48,128]{2,1,0:T(8,128)(2,1)}), bf16[32,48,128]{2,1,0:T(8,128)(2,1)S(1)}, u32[]{:S(2)}, u32[]{:S(2)}) %all-to-all-start) | async-done | bytes 393248 | tf_op jit(solution)/shard_map/all_to_all | solution.py:666
  102.2 0.1 reduce_sum.12
  102.3 0.8 broadcast_in_dim.2
  103.1 2.6 %all-to-all-start.1 = ((bf16[32,48,128]{2,1,0:T(8,128)(2,1)}), bf16[32,48,128]{2,1,0:T(8,128)(2,1)S(1)}, u32[]{:S(2)}, u32[]{:S(2)}) async-start(bf16[32,48,128]{2,1,0:T(8,128)(2,1)} %broadcast_in_dim.2), calls=%async_computation.1 | async-start | bytes 786432 | tf_op jit(solution)/shard_map/all_to_all | solution.py:674
  105.7 1.2 copy-done.9
  106.9 9.2 %input_kernel.1 = bf16[16,48,512]{2,1,0:T(8,128)(2,1)} custom-call(s32[16]{0:T(128)S(1)} %bitcast.24, bf16[80,48,128]{2,1,0:T(8,128)(2,1)S(1)} %copy-done.9, bf16[10,48,128]{2,1,0:T(8,128)(2,1)S(1)} %collective-permute-done.8.from_left, bf16[10,48,128]{2,1,0:T(8,128)(2,1)S(1)} %collective-permute-done.9.from_right, f32[16,128]{1,0:T(8,128)S(1)} %get-tuple-element.63.live, ...), custom_call_target="tpu_custom_call" | custom-call | flops 8000000000 | bytes 2147904 | tf_op jit(solution)/shard_map/input_kernel/pallas_call | solution.py:638
  116.2 2.7 %all-to-all-done.1 = bf16[32,48,128]{2,1,0:T(8,128)(2,1)S(1)} async-done(((bf16[32,48,128]{2,1,0:T(8,128)(2,1)}), bf16[32,48,128]{2,1,0:T(8,128)(2,1)S(1)}, u32[]{:S(2)}, u32[]{:S(2)}) %all-to-all-start.1) | async-done | bytes 393248 | tf_op jit(solution)/shard_map/all_to_all | solution.py:674
  118.9 1.6 %finish_kernel.1 = (f32[27,48,48]{2,1,0:T(8,128)}, f32[8,48,48]{2,1,0:T(8,128)S(1)}, f32[27,48,48]{2,1,0:T(8,128)}, f32[8,48,48]{2,1,0:T(8,128)}) custom-call(bf16[1536,128]{1,0:T(8,128)(2,1)S(1)} %bitcast.15), custom_call_target="tpu_custom_call" | custom-call | bytes 1038336 | tf_op jit(solution)/shard_map/finish_kernel/pallas_call | solution.py:638
  120.5 0.7 copy.14
  (25 shorter events, 0.1 us)
Async XLA Ops:
  0.6 19.2 %copy-start.1 = (bf16[1,1,16,48,512]{4,3,2,1,0:T(8,128)(2,1)S(1)}, bf16[1,1,16,48,512]{4,3,2,1,0:T(8,128)(2,1)}, u32[]{:S(2)}) copy-start(bf16[1,1,16,48,512]{4,3,2,1,0:T(8,128)(2,1)} %param.11) | copy-start | bytes 2359300
  0.6 19.2 %copy-start.2 = (s32[1,1,16]{2,1,0:T(1,128)S(1)}, s32[1,1,16]{2,1,0:T(1,128)}, u32[]{:S(2)}) copy-start(s32[1,1,16]{2,1,0:T(1,128)} %param.9) | copy-start | bytes 196
  0.7 19.2 %copy-start = (bf16[1,1,16,48,512]{4,3,2,1,0:T(8,128)(2,1)S(1)}, bf16[1,1,16,48,512]{4,3,2,1,0:T(8,128)(2,1)}, u32[]{:S(2)}) copy-start(bf16[1,1,16,48,512]{4,3,2,1,0:T(8,128)(2,1)} %param.8) | copy-start | bytes 2359300
  0.7 19.2 %copy-start.6 = (bf16[8,48,48]{2,1,0:T(8,128)(2,1)S(1)}, bf16[8,48,48]{2,1,0:T(8,128)(2,1)}, u32[]{:S(2)}) copy-start(bf16[8,48,48]{2,1,0:T(8,128)(2,1)} %up.1) | copy-start | bytes 110596
  0.7 19.2 %copy-start.5 = (bf16[48,8,48]{2,1,0:T(8,128)(2,1)S(1)}, bf16[48,8,48]{2,1,0:T(8,128)(2,1)}, u32[]{:S(2)}) copy-start(bf16[48,8,48]{2,1,0:T(8,128)(2,1)} %down.1) | copy-start | bytes 110596
  4.4 9.2 %collective-permute-start = (bf16[112,512]{1,0:T(8,128)(2,1)}, bf16[112,512]{1,0:T(8,128)(2,1)S(1)}, u32[]{:S(2)}, u32[]{:S(2)}) collective-permute-start(bf16[112,512]{1,0:T(8,128)(2,1)} %get-tuple-element.45), channel_id=1, source_target_pairs={{0,1},{1,2},{2,3},{4,5},{5,6},{6,7},{8,9},{9,10},{10,11},{12,13},{... | collective-permute-start | bytes 344072 | tf_op jit(solution)/shard_map/ppermute | solution.py:658
  6.7 6.9 %collective-permute-start.1 = (bf16[112,512]{1,0:T(8,128)(2,1)}, bf16[112,512]{1,0:T(8,128)(2,1)S(1)}, u32[]{:S(2)}, u32[]{:S(2)}) collective-permute-start(bf16[112,512]{1,0:T(8,128)(2,1)} %get-tuple-element.46), channel_id=1, source_target_pairs={{1,0},{2,1},{3,2},{5,4},{6,5},{7,6},{9,8},{10,9},{11,10},{13,12},{... | collective-permute-start | bytes 344072 | tf_op jit(solution)/shard_map/ppermute | solution.py:658
  8.0 19.3 %collective-permute-start.2 = (bf16[400,384]{1,0:T(8,128)(2,1)}, bf16[400,384]{1,0:T(8,128)(2,1)S(1)}, u32[]{:S(2)}, u32[]{:S(2)}) collective-permute-start(bf16[400,384]{1,0:T(8,128)(2,1)} %get-tuple-element.51), channel_id=1, source_target_pairs={{0,4},{1,5},{2,6},{3,7},{4,8},{5,9},{6,10},{7,11},{8,12},{9,13},{1... | collective-permute-start | bytes 921608 | tf_op jit(solution)/shard_map/ppermute | solution.py:658
  12.3 15.0 %collective-permute-start.3 = (bf16[400,384]{1,0:T(8,128)(2,1)}, bf16[400,384]{1,0:T(8,128)(2,1)S(1)}, u32[]{:S(2)}, u32[]{:S(2)}) collective-permute-start(bf16[400,384]{1,0:T(8,128)(2,1)} %get-tuple-element.52), channel_id=1, source_target_pairs={{4,0},{5,1},{6,2},{7,3},{8,4},{9,5},{10,6},{11,7},{12,8},{13,9},{1... | collective-permute-start | bytes 921608 | tf_op jit(solution)/shard_map/ppermute | solution.py:658
  13.9 13.4 %collective-permute-start.4 = (bf16[64,384]{1,0:T(8,128)(2,1)S(1)}, bf16[64,384]{1,0:T(8,128)(2,1)S(1)}, u32[]{:S(2)}, u32[]{:S(2)}) collective-permute-start(bf16[64,384]{1,0:T(8,128)(2,1)S(1)} %get-tuple-element.53), channel_id=1, source_target_pairs={{0,4},{1,5},{2,6},{3,7},{4,8},{5,9},{6,10},{7,11},{8,12},{9,13},{1... | collective-permute-start | bytes 147464 | tf_op jit(solution)/shard_map/ppermute | solution.py:658
  18.5 8.8 %collective-permute-start.5 = (bf16[64,384]{1,0:T(8,128)(2,1)S(1)}, bf16[64,384]{1,0:T(8,128)(2,1)S(1)}, u32[]{:S(2)}, u32[]{:S(2)}) collective-permute-start(bf16[64,384]{1,0:T(8,128)(2,1)S(1)} %get-tuple-element.47.c_low), channel_id=1, source_target_pairs={{4,0},{5,1},{6,2},{7,3},{8,4},{9,5},{10,6},{11,7},{12,8},{13,9},{1... | collective-permute-start | bytes 147464 | tf_op jit(solution)/shard_map/ppermute | solution.py:658
  19.8 1.0 copy-start.3
  20.8 1.0 copy-start.4
  21.8 5.5 %copy-start.7 = (f32[16,128]{1,0:T(8,128)S(1)}, f32[16,128]{1,0:T(8,128)}, u32[]{:S(2)}) copy-start(f32[16,128]{1,0:T(8,128)} %get-tuple-element.49.flags) | copy-start | bytes 24580
  47.8 9.0 %collective-permute-start.6 = (bf16[5,48,128]{2,1,0:T(8,128)(2,1)S(1)}, bf16[5,48,128]{2,1,0:T(8,128)(2,1)S(1)}, u32[]{:S(2)}, u32[]{:S(2)}) collective-permute-start(bf16[5,48,128]{2,1,0:T(8,128)(2,1)S(1)} %get-tuple-element.59), channel_id=1, source_target_pairs={{0,4},{1,5},{2,6},{3,7},{4,8},{5,9},{6,10},{7,11},{8,12},{9,13},{1... | collective-permute-start | bytes 184328 | tf_op jit(solution)/shard_map/ppermute | solution.py:658
  52.3 8.0 %collective-permute-start.7 = (bf16[5,48,128]{2,1,0:T(8,128)(2,1)S(1)}, bf16[5,48,128]{2,1,0:T(8,128)(2,1)S(1)}, u32[]{:S(2)}, u32[]{:S(2)}) collective-permute-start(bf16[5,48,128]{2,1,0:T(8,128)(2,1)S(1)} %get-tuple-element.60), channel_id=1, source_target_pairs={{4,0},{5,1},{6,2},{7,3},{8,4},{9,5},{10,6},{11,7},{12,8},{13,9},{1... | collective-permute-start | bytes 184328 | tf_op jit(solution)/shard_map/ppermute | solution.py:658
  66.2 14.6 %copy-start.8 = (bf16[80,48,128]{2,1,0:T(8,128)(2,1)}, bf16[80,48,128]{2,1,0:T(8,128)(2,1)S(1)}, u32[]{:S(2)}) copy-start(bf16[80,48,128]{2,1,0:T(8,128)(2,1)S(1)} %get-tuple-element.65.grad_h) | copy-start | bytes 2949124
  66.2 14.6 %collective-permute-start.8 = (bf16[10,48,128]{2,1,0:T(8,128)(2,1)S(1)}, bf16[10,48,128]{2,1,0:T(8,128)(2,1)S(1)}, u32[]{:S(2)}, u32[]{:S(2)}) collective-permute-start(bf16[10,48,128]{2,1,0:T(8,128)(2,1)S(1)} %get-tuple-element.69), channel_id=1, source_target_pairs={{0,4},{1,5},{2,6},{3,7},{4,8},{5,9},{6,10},{7,11},{8,12},{9,13},{1... | collective-permute-start | bytes 368648 | tf_op jit(solution)/shard_map/ppermute | solution.py:658
  70.9 9.9 %collective-permute-start.9 = (bf16[10,48,128]{2,1,0:T(8,128)(2,1)S(1)}, bf16[10,48,128]{2,1,0:T(8,128)(2,1)S(1)}, u32[]{:S(2)}, u32[]{:S(2)}) collective-permute-start(bf16[10,48,128]{2,1,0:T(8,128)(2,1)S(1)} %get-tuple-element.70), channel_id=1, source_target_pairs={{4,0},{5,1},{6,2},{7,3},{8,4},{9,5},{10,6},{11,7},{12,8},{13,9},{1... | collective-permute-start | bytes 368648 | tf_op jit(solution)/shard_map/ppermute | solution.py:658
  80.8 21.4 %all-to-all-start = ((bf16[32,48,128]{2,1,0:T(8,128)(2,1)}), bf16[32,48,128]{2,1,0:T(8,128)(2,1)S(1)}, u32[]{:S(2)}, u32[]{:S(2)}) async-start(bf16[32,48,128]{2,1,0:T(8,128)(2,1)} %bitcast.6), calls=%async_computation | async-start | bytes 786432 | tf_op jit(solution)/shard_map/all_to_all | solution.py:666
  103.1 15.8 %all-to-all-start.1 = ((bf16[32,48,128]{2,1,0:T(8,128)(2,1)}), bf16[32,48,128]{2,1,0:T(8,128)(2,1)S(1)}, u32[]{:S(2)}, u32[]{:S(2)}) async-start(bf16[32,48,128]{2,1,0:T(8,128)(2,1)} %broadcast_in_dim.2), calls=%async_computation.1 | async-start | bytes 786432 | tf_op jit(solution)/shard_map/all_to_all | solution.py:674
  105.7 1.2 copy-start.9

commit v10 on v9

--- a/solution.py
+++ b/solution.py
@@ -315,27 +315,39 @@
     return parts[tile, 0:C] + parts[tile + 1, C : 2 * C] + parts[tile + 2, 2 * C :]
 
 
-def conv_steps(parts, weight, load, tiles, step, first, unroll):
+def conv_steps(parts, weight, load, tiles, step, first, even, odd):
     masks = depth_masks(step, first)
     spare = jnp.zeros((3 * C, LANES), F32)
     parts[0] = spare
     parts[tiles + 1] = spare
 
-    def body(index):
-        tile = 4 * index
-        cols = [depth_columns(load(tile + i), masks, step) for i in range(4)]
-        out = dot(weight[...], jnp.concatenate(cols, axis=1))
+    def fill(buffer, tile):
+        for i in range(4):
+            cols = depth_columns(load(tile + i), masks, step)
+            buffer[:, LANES * i : LANES * (i + 1)] = cols
+
+    def multiply(buffer, tile):
+        out = dot(weight[...], buffer[...])
         for i in range(4):
             parts[tile + i + 1] = out[:, LANES * i : LANES * (i + 1)]
 
-    loop(0, tiles // 4, body, unroll)
+    fill(even, 0)
+
+    def body(index):
+        tile = 8 * index
+        fill(odd, tile + 4)
+        multiply(even, tile)
+        fill(even, jnp.minimum(tile + 8, tiles - 4))
+        multiply(odd, tile + 4)
+
+    loop(0, tiles // 8, body)
 
 
 def forward_kernel(
     grid_own, flags, y_left, y_right, grad_r, x_left, x_right, c_left, c_right, fine_w, down_w,
     coarse_w,
     grid, hidden, low_cols, rects, grad_c, live, pack_low, pack_high,
-    rows_in, fine_p, coarse_p, hidden_all, lowered, live_all,
+    rows_in, fine_p, coarse_p, hidden_all, lowered, live_all, even, odd,
 ):
     number = 2 * (x_left.shape[0] - 16) // C
     last = number + 1
@@ -372,7 +384,7 @@
                 grid[tile] = grid_own[tile] + halo
     live[...] = join_halves(live_all[0:16, :], live_all[8:24, :])
     tiles = grid.shape[0]
-    conv_steps(fine_p, fine_w, lambda tile: across_columns(grid[tile], 1), tiles, 16, 0, 2)
+    conv_steps(fine_p, fine_w, lambda tile: across_columns(grid[tile], 1), tiles, 16, 0, even, odd)
     anchors = anchor_mask(0)
 
     def lower_step(block):
@@ -408,7 +420,7 @@
             low_cols[tile] = pair_columns(*pair_tiles(lower, upper, halves), edges, 2)
 
     loop(0, pairs, pair_step, 2)
-    conv_steps(coarse_p, coarse_w, lambda tile: low_cols[tile], 4 * pairs, 32, 4, 2)
+    conv_steps(coarse_p, coarse_w, lambda tile: low_cols[tile], 4 * pairs, 32, 4, even, odd)
     pair_anchors = anchor_mask(4)
 
     def grad_step(block):
@@ -511,11 +523,11 @@
 
 def backward_kernel(
     grad_c, from_left, from_right, hidden, cot_grid, live, coarse_w, down_w,
-    grad_h, grad_d, pack_low, pack_high, coarse_p, grad_x,
+    grad_h, grad_d, pack_low, pack_high, coarse_p, grad_x, even, odd,
 ):
     tiles = grad_c.shape[0]
     fill_columns(grad_c, from_left, from_right, grad_x, 2)
-    conv_steps(coarse_p, coarse_w, lambda tile: grad_x[tile], tiles, 32, 4, 2)
+    conv_steps(coarse_p, coarse_w, lambda tile: grad_x[tile], tiles, 32, 4, even, odd)
     anchors = anchor_mask(4)
 
     def step(block):
@@ -540,7 +552,7 @@
     pack_columns(grad_h, pack_low, pack_high, 1)
 
 
-def weight_kernel(grid, grad_h, grad_d, hidden, early, joined, grad_own, fine_g, down_g):
+def weight_kernel(grid, grad_h, grad_d, hidden, early, joined, grad_own, fine_g, down_g, even, odd):
     tiles = grad_h.shape[0]
     shift = tiles - 16
     fine_g[...] = jnp.zeros_like(fine_g)
@@ -558,18 +570,30 @@
     edges = edge_masks(1)
     halves = own_masks()
 
-    def fine_step(index):
-        at = [4 + 8 * index + inner for inner in range(8)]
-        rights = []
-        for tile in at:
+    groups = (tiles - 8) // 8
+
+    def fill(buffer, group):
+        for inner in range(8):
+            tile = 4 + 8 * group + inner
             lower, upper = grid[tile], grid[tile + shift]
             base = pair_columns(*pair_tiles(lower, upper, halves), edges, 1)
-            rights.append(depth_columns(base, masks, 16))
-        fine_g[0 : 9 * C, :] += dot(
-            jnp.concatenate(rights, axis=1), stacks(grad_own, at), (1, 1)
-        )
-
-    loop(0, (tiles - 8) // 8, fine_step)
+            buffer[:, LANES * inner : LANES * (inner + 1)] = depth_columns(base, masks, 16)
+
+    def multiply(buffer, group):
+        at = [4 + 8 * group + inner for inner in range(8)]
+        fine_g[0 : 9 * C, :] += dot(buffer[...], stacks(grad_own, at), (1, 1))
+
+    fill(even, 0)
+
+    def fine_step(index):
+        fill(odd, 2 * index + 1)
+        multiply(even, 2 * index)
+        fill(even, jnp.minimum(2 * index + 2, groups - 1))
+        multiply(odd, 2 * index + 1)
+
+    loop(0, groups // 2, fine_step)
+    if groups % 2:
+        multiply(even, groups - 1)
 
     def down_step(index):
         lefts = []
@@ -591,11 +615,11 @@
 
 def input_kernel(
     slots, grad_h, from_left, from_right, live, fine_w, out,
-    fine_p, rows_out, flat, grad_x,
+    fine_p, rows_out, flat, grad_x, even, odd,
 ):
     tiles = grad_h.shape[0]
     fill_columns(grad_h, from_left, from_right, grad_x, 1)
-    conv_steps(fine_p, fine_w, lambda tile: grad_x[tile], tiles, 16, 4, 2)
+    conv_steps(fine_p, fine_w, lambda tile: grad_x[tile], tiles, 16, 4, even, odd)
 
     def block_step(block):
         alive = jnp.broadcast_to(live[pl.ds(block, 1), :], (C, LANES))
@@ -623,7 +647,10 @@
             rows = total[at + C * index : at + C * (index + 1), :].astype(F32) * scale
             for along in range(2):
                 part = rows[:, C * along : C * (along + 1)]
-                out[2 * index + along] = part.T if turn else part
+                if turn:
+                    out[2 * index + along] = part.T
+                else:
+                    out[:, 2 * index + along, :] = part
 
 
 def call(kernel, inputs, outs, scratch=(), scalars=0, flops=0, limit=None):
@@ -753,7 +780,8 @@
             ((tiles, C, LANES), F32),
             ((coarse_tiles, C, LANES), BF16),
             ((C, LANES), F32),
-        ],
+        ]
+        + [((9 * C, 4 * LANES), BF16)] * 2,
         flops=8 * 10**9,
     )
     grad_left = send(pack_high, 1, 0)
@@ -774,7 +802,8 @@
             ((fine_groups, C, LANES), BF16),
             ((fine_groups, C, LANES), BF16),
         ],
-        [((4 * pairs + 2, 3 * C, LANES), F32), ((4 * pairs, 3 * C, LANES), BF16)],
+        [((4 * pairs + 2, 3 * C, LANES), F32), ((4 * pairs, 3 * C, LANES), BF16)]
+        + [((9 * C, 4 * LANES), BF16)] * 2,
         flops=8 * 10**9,
     )
     edge_left = send(edge_high, 1, 0)
@@ -783,7 +812,8 @@
         weight_kernel,
         (grid, grad_h, grad_d, hidden, early),
         [((32 * C, LANES), BF16)],
-        [((EDGE * pairs, C, LANES), BF16), ((VOX, 3 * C), F32), ((4 * C, LANES), F32)],
+        [((EDGE * pairs, C, LANES), BF16), ((VOX, 3 * C), F32), ((4 * C, LANES), F32)]
+        + [((9 * C, 8 * LANES), BF16)] * 2,
         flops=12 * 10**9,
     )
     joined, edge_left, edge_right, slots = lax.optimization_barrier(
@@ -808,7 +838,8 @@
             ((number // 2 * C, 1024), BF16),
             ((number // 2 * C, 1024), BF16),
             ((EDGE * pairs, 3 * C, LANES), BF16),
-        ],
+        ]
+        + [((9 * C, 4 * LANES), BF16)] * 2,
         scalars=1,
         flops=8 * 10**9,
     )
@@ -817,14 +848,14 @@
     fine_total, down_total, coarse_total, up_total = call(
         functools.partial(finish_kernel, scale),
         (total,),
-        [((27, C, C), F32), ((8, C, C), F32), ((27, C, C), F32), ((8, C, C), F32)],
+        [((27, C, C), F32), ((C, 8, C), F32), ((27, C, C), F32), ((8, C, C), F32)],
     )
     shape_out = (1, 1, number, C, VOX)
     return (
         output.reshape(shape_out),
         input_grad.reshape(shape_out),
         fine_total.transpose(1, 0, 2),
-        down_total.transpose(1, 0, 2),
+        down_total,
         coarse_total.transpose(1, 0, 2),
         up_total,
     )

time: 122 us -> 124 us (1.016)
  Pallas kernels: 61.7 us -> 64.1 us
    pallas_call x10, Pallas kernels: 61.7 us -> 64.1 us  [call(): pl.pallas_call(kernel, out_shape=tuple((jax.ShapeDtypeStruct(s, d) for s,...]
    unnamed x21 -> x20, local copies, waits for them, and re-layouts: 3.9 us -> 3.17 us
  transfers between devices with their start and end apart: 12 -> 12, of which waited for: 4 -> 4; matrix products, arithmetic and copies ran while one was open for 0% -> 0% of each run, Pallas kernels for 25% -> 27%
where the time goes in v10:
time: 124 us; the launch traced here: 123 us
  Pallas kernels  64.1 us (52%)
  starting transfers between devices  37.8 us (30%)
  waiting for transfers between devices  15.6 us (13%)
  local copies, waits for them, and re-layouts  3.97 us (3%)
  between operations  1.68 us (1%)
    pallas_call x10, Pallas kernels, call(): pl.pallas_call(kernel, out_shape=tuple((jax.ShapeDtypeStruct(s, d) for s,...  64.1 us
    ppermute x10, starting transfers between devices, send(): return lax.ppermute(array, ('gx', 'gy'), pairs)  26.8 us
    all_to_all x1, waiting for transfers between devices, reduce_share(): lax.all_to_all(joined.reshape(devices, share, LANES), ('gx', 'gy'), 0, 0)  8.57 us
    all_to_all x1, starting transfers between devices, reduce_share(): lax.all_to_all(joined.reshape(devices, share, LANES), ('gx', 'gy'), 0, 0)  8.38 us
    ppermute x10, waiting for transfers between devices, send(): return lax.ppermute(array, ('gx', 'gy'), pairs)  4.01 us
    unnamed x20, local copies, waits for them, and re-layouts  3.17 us
    all_to_all x1, waiting for transfers between devices, spread_share(): full = lax.all_to_all(copies, ('gx', 'gy'), 0, 0)  2.99 us
    all_to_all x1, starting transfers between devices, spread_share(): full = lax.all_to_all(copies, ('gx', 'gy'), 0, 0)  2.64 us
  transfers between devices with their start and end apart: 12, of which 4 were waited for; matrix products, arithmetic and copies ran while one was open for 0% of the time, Pallas kernels for 27%

profile of v10, /device:TPU:0, one launch (start us, length us, event | category | flops | bytes accessed | tf_op | source)
XLA Modules:
  0.0 123.2 jit_solution(18150445259523408883)
XLA Ops:
  1.5 2.9 %prepare_kernel.1 = (f32[16,128]{1,0:T(8,128)}, bf16[400,384]{1,0:T(8,128)(2,1)}, bf16[400,384]{1,0:T(8,128)(2,1)}, bf16[112,512]{1,0:T(8,128)(2,1)}, bf16[112,512]{1,0:T(8,128)(2,1)}) custom-call(s32[16]{0:T(128)} %bitcast.19, s32[1]{0:T(128)} %bitcast.12.count, bf16[16,48,512]{2,1,0:T(8,128)(2,1)} %bitcast.15, bf16[16,48,512]{2,1,0:T(8,128)(2,1)} %bitcast.17), custom_call_target="tpu_custom_call" | custom-call | bytes 2424900 | tf_op jit(solution)/shard_map/prepare_kernel/pallas_call | solution.py:665
  4.4 2.3 %collective-permute-start = (bf16[112,512]{1,0:T(8,128)(2,1)}, bf16[112,512]{1,0:T(8,128)(2,1)S(1)}, u32[]{:S(2)}, u32[]{:S(2)}) collective-permute-start(bf16[112,512]{1,0:T(8,128)(2,1)} %get-tuple-element.45), channel_id=1, source_target_pairs={{0,1},{1,2},{2,3},{4,5},{5,6},{6,7},{8,9},{9,10},{10,11},{12,13},{... | collective-permute-start | bytes 344072 | tf_op jit(solution)/shard_map/ppermute | solution.py:685
  6.7 1.3 %collective-permute-start.1 = (bf16[112,512]{1,0:T(8,128)(2,1)}, bf16[112,512]{1,0:T(8,128)(2,1)S(1)}, u32[]{:S(2)}, u32[]{:S(2)}) collective-permute-start(bf16[112,512]{1,0:T(8,128)(2,1)} %get-tuple-element.46), channel_id=1, source_target_pairs={{1,0},{2,1},{3,2},{5,4},{6,5},{7,6},{9,8},{10,9},{11,10},{13,12},{... | collective-permute-start | bytes 344072 | tf_op jit(solution)/shard_map/ppermute | solution.py:685
  8.0 4.2 %collective-permute-start.2 = (bf16[400,384]{1,0:T(8,128)(2,1)}, bf16[400,384]{1,0:T(8,128)(2,1)S(1)}, u32[]{:S(2)}, u32[]{:S(2)}) collective-permute-start(bf16[400,384]{1,0:T(8,128)(2,1)} %get-tuple-element.51), channel_id=1, source_target_pairs={{0,4},{1,5},{2,6},{3,7},{4,8},{5,9},{6,10},{7,11},{8,12},{9,13},{1... | collective-permute-start | bytes 921608 | tf_op jit(solution)/shard_map/ppermute | solution.py:685
  12.3 1.3 %collective-permute-start.3 = (bf16[400,384]{1,0:T(8,128)(2,1)}, bf16[400,384]{1,0:T(8,128)(2,1)S(1)}, u32[]{:S(2)}, u32[]{:S(2)}) collective-permute-start(bf16[400,384]{1,0:T(8,128)(2,1)} %get-tuple-element.52), channel_id=1, source_target_pairs={{4,0},{5,1},{6,2},{7,3},{8,4},{9,5},{10,6},{11,7},{12,8},{13,9},{1... | collective-permute-start | bytes 921608 | tf_op jit(solution)/shard_map/ppermute | solution.py:685
  13.6 0.3 corner_kernel.1
  13.9 4.5 %collective-permute-start.4 = (bf16[64,384]{1,0:T(8,128)(2,1)S(1)}, bf16[64,384]{1,0:T(8,128)(2,1)S(1)}, u32[]{:S(2)}, u32[]{:S(2)}) collective-permute-start(bf16[64,384]{1,0:T(8,128)(2,1)S(1)} %get-tuple-element.53), channel_id=1, source_target_pairs={{0,4},{1,5},{2,6},{3,7},{4,8},{5,9},{6,10},{7,11},{8,12},{9,13},{1... | collective-permute-start | bytes 147464 | tf_op jit(solution)/shard_map/ppermute | solution.py:685
  18.5 1.3 %collective-permute-start.5 = (bf16[64,384]{1,0:T(8,128)(2,1)S(1)}, bf16[64,384]{1,0:T(8,128)(2,1)S(1)}, u32[]{:S(2)}, u32[]{:S(2)}) collective-permute-start(bf16[64,384]{1,0:T(8,128)(2,1)S(1)} %get-tuple-element.47.c_low), channel_id=1, source_target_pairs={{4,0},{5,1},{6,2},{7,3},{8,4},{9,5},{10,6},{11,7},{12,8},{13,9},{1... | collective-permute-start | bytes 147464 | tf_op jit(solution)/shard_map/ppermute | solution.py:685
  19.8 0.0 copy-start.3
  19.8 1.0 copy-done.3
  20.8 1.0 copy-done.4
  21.8 5.0 %place_kernel.1 = (bf16[144,48,128]{2,1,0:T(8,128)(2,1)S(1)}, bf16[80,48,128]{2,1,0:T(8,128)(2,1)S(1)}, f32[40,48,128]{2,1,0:T(8,128)S(1)}, bf16[144,432]{1,0:T(...) custom-call(s32[16]{0:T(128)S(1)} %bitcast.20, ...), custom_call_target="tpu_custom_call" | custom-call | flops 8000000000 | bytes 6480964 | tf_op jit(solution)/shard_map/place_kernel/pallas_call | solution.py:665
  26.8 0.5 collective-permute-done.4.c_left
  27.3 19.9 %forward_kernel.1 = (bf16[144,48,128]{2,1,0:T(8,128)(2,1)S(1)}, f32[80,48,128]{2,1,0:T(8,128)S(1)}, bf16[40,144,128]{2,1,0:T(8,128)(2,1)S(1)}, bf16[40,48,128]{2...) custom-call(bf16[144,48,128]{2,1,0:T(8,128)(2,1)S(1)} %get-tuple-ele, ...), custom_call_target="tpu_custom_call" | custom-call | flops 8000000000 | bytes 10312704 | tf_op jit(solution)/shard_map/forward_kernel/pallas_call | solution.py:665
  47.2 4.5 %collective-permute-start.6 = (bf16[5,48,128]{2,1,0:T(8,128)(2,1)S(1)}, bf16[5,48,128]{2,1,0:T(8,128)(2,1)S(1)}, u32[]{:S(2)}, u32[]{:S(2)}) collective-permute-start(bf16[5,48,128]{2,1,0:T(8,128)(2,1)S(1)} %get-tuple-element.59), channel_id=1, source_target_pairs={{0,4},{1,5},{2,6},{3,7},{4,8},{5,9},{6,10},{7,11},{8,12},{9,13},{1... | collective-permute-start | bytes 184328 | tf_op jit(solution)/shard_map/ppermute | solution.py:685
  51.7 1.3 %collective-permute-start.7 = (bf16[5,48,128]{2,1,0:T(8,128)(2,1)S(1)}, bf16[5,48,128]{2,1,0:T(8,128)(2,1)S(1)}, u32[]{:S(2)}, u32[]{:S(2)}) collective-permute-start(bf16[5,48,128]{2,1,0:T(8,128)(2,1)S(1)} %get-tuple-element.60), channel_id=1, source_target_pairs={{4,0},{5,1},{6,2},{7,3},{8,4},{9,5},{10,6},{11,7},{12,8},{13,9},{1... | collective-permute-start | bytes 184328 | tf_op jit(solution)/shard_map/ppermute | solution.py:685
  53.0 3.3 %side_kernel.1.early = bf16[768,128]{1,0:T(8,128)(2,1)S(1)} custom-call(bf16[40,48,128]{2,1,0:T(8,128)(2,1)S(1)} %get-tuple-element.67.rects, bf16[80,48,128]{2,1,0:T(8,128)(2,1)S(1)} %get-tuple-element.62.cot_grid, bf16[40,144,128]{2,1,0:T(8,128)(2,1)S(1)} %get-tuple-element.68.low_cols, bf16[40,48,128]{2,1,0:T(8,128)(2,1)S(1)} %get-tuple-element.58.grad_c), custom_call_target="tpu_custom_call" | custom-call | flops 8000000000 | bytes 3637248 | tf_op jit(solution)/shard_map/side_kernel/pallas_call | solution.py:665
  56.3 3.4 %collective-permute-done.7.from_right = bf16[5,48,128]{2,1,0:T(8,128)(2,1)S(1)} collective-permute-done((bf16[5,48,128]{2,1,0:T(8,128)(2,1)S(1)}, bf16[5,48,128]{2,1,0:T(8,128)(2,1)S(1)}, u32[]{:S(2)}, u32[]{:S(2)}) %collective-permute-start.7) | collective-permute-done | bytes 61472 | tf_op jit(solution)/shard_map/ppermute | solution.py:685
  59.7 5.9 %backward_kernel.1 = (bf16[80,48,128]{2,1,0:T(8,128)(2,1)S(1)}, bf16[40,48,128]{2,1,0:T(8,128)(2,1)S(1)}, bf16[10,48,128]{2,1,0:T(8,128)(2,1)S(1)}, bf16[10,48,128]{2,1,0:T(8,128)(2,1)S(1)}) custom-call(bf16[40,48,128]{2,1,0:T(8,128)(2,1)S(1)} %get-tuple-element.58.grad_c, bf16[5,48,128]{2,1,0:T(8,128)(2,1)S(1)} %collective-permute-done.6.from_left, ...), custom_call_target="tpu_custom_call" | custom-call | flops 8000000000 | bytes 5453312 | tf_op jit(solution)/shard_map/backward_kernel/pallas_call | solution.py:665
  65.6 4.7 %collective-permute-start.8 = (bf16[10,48,128]{2,1,0:T(8,128)(2,1)S(1)}, bf16[10,48,128]{2,1,0:T(8,128)(2,1)S(1)}, u32[]{:S(2)}, u32[]{:S(2)}) collective-permute-start(bf16[10,48,128]{2,1,0:T(8,128)(2,1)S(1)} %get-tuple-element.69), channel_id=1, source_target_pairs={{0,4},{1,5},{2,6},{3,7},{4,8},{5,9},{6,10},{7,11},{8,12},{9,13},{1... | collective-permute-start | bytes 368648 | tf_op jit(solution)/shard_map/ppermute | solution.py:685
  70.3 1.3 %collective-permute-start.9 = (bf16[10,48,128]{2,1,0:T(8,128)(2,1)S(1)}, bf16[10,48,128]{2,1,0:T(8,128)(2,1)S(1)}, u32[]{:S(2)}, u32[]{:S(2)}) collective-permute-start(bf16[10,48,128]{2,1,0:T(8,128)(2,1)S(1)} %get-tuple-element.70), channel_id=1, source_target_pairs={{4,0},{5,1},{6,2},{7,3},{8,4},{9,5},{10,6},{11,7},{12,8},{13,9},{1... | collective-permute-start | bytes 368648 | tf_op jit(solution)/shard_map/ppermute | solution.py:685
  71.6 11.7 %weight_kernel.1 = bf16[1536,128]{1,0:T(8,128)(2,1)} custom-call(bf16[144,48,128]{2,1,0:T(8,128)(2,1)S(1)} %get-tuple-element.57.grid, bf16[80,48,128]{2,1,0:T(8,128)(2,1)S(1)} %get-tuple-element.65.grad_h, bf16[40,48,128]{2,1,0:T(8,128)(2,1)S(1)} %get-tuple-element.66.grad_d, f32[80,48,128]{2,1,0:T(8,128)S(1)} %get-tuple-element.61.hidden, ...), custom_call_target="tpu_custom_call" | custom-call | flops 12000000000 | bytes 5799936 | tf_op jit(solution)/shard_map/weight_kernel/pallas_call | solution.py:665
  83.3 8.4 %all-to-all-start = ((bf16[32,48,128]{2,1,0:T(8,128)(2,1)}), bf16[32,48,128]{2,1,0:T(8,128)(2,1)S(1)}, u32[]{:S(2)}, u32[]{:S(2)}) async-start(bf16[32,48,128]{2,1,0:T(8,128)(2,1)} %bitcast.6), calls=%async_computation | async-start | bytes 786432 | tf_op jit(solution)/shard_map/all_to_all | solution.py:693
  91.7 4.4 %output_kernel.1 = bf16[16,48,512]{2,1,0:T(8,128)(2,1)} custom-call(s32[16]{0:T(128)S(1)} %bitcast.21, f32[80,48,128]{2,1,0:T(8,128)S(1)} %get-tuple-element.61.hidden, bf16[40,48,128]{2,1,0:T(8,128)(2,1)S(1)} %get-tuple-element.67.rects, f32[16,128]{1,0:T(8,128)S(1)} %get-tuple-element.63.live, bf16[96,192]{1,0:T(8,128)(2,1)S(1)} %get-tuple-element.73.up_w), custom_call_target="tpu_custom_call" | custom-call | flops 8000000000 | bytes 3289152 | tf_op jit(solution)/shard_map/output_kernel/pallas_call | solution.py:665
  96.1 8.6 %all-to-all-done = bf16[32,48,128]{2,1,0:T(8,128)(2,1)S(1)} async-done(((bf16[32,48,128]{2,1,0:T(8,128)(2,1)}), bf16[32,48,128]{2,1,0:T(8,128)(2,1)S(1)}, u32[]{:S(2)}, u32[]{:S(2)}) %all-to-all-start) | async-done | bytes 393248 | tf_op jit(solution)/shard_map/all_to_all | solution.py:693
  104.7 0.1 reduce_sum.12
  104.8 0.8 broadcast_in_dim.2
  105.6 2.6 %all-to-all-start.1 = ((bf16[32,48,128]{2,1,0:T(8,128)(2,1)}), bf16[32,48,128]{2,1,0:T(8,128)(2,1)S(1)}, u32[]{:S(2)}, u32[]{:S(2)}) async-start(bf16[32,48,128]{2,1,0:T(8,128)(2,1)} %broadcast_in_dim.2), calls=%async_computation.1 | async-start | bytes 786432 | tf_op jit(solution)/shard_map/all_to_all | solution.py:701
  108.2 1.2 copy-done.9
  109.4 9.0 %input_kernel.1 = bf16[16,48,512]{2,1,0:T(8,128)(2,1)} custom-call(s32[16]{0:T(128)S(1)} %bitcast.22, bf16[80,48,128]{2,1,0:T(8,128)(2,1)S(1)} %copy-done.9, bf16[10,48,128]{2,1,0:T(8,128)(2,1)S(1)} %collective-permute-done.8.from_left, bf16[10,48,128]{2,1,0:T(8,128)(2,1)S(1)} %collective-permute-done.9.from_right, f32[16,128]{1,0:T(8,128)S(1)} %get-tuple-element.63.live, ...), custom_call_target="tpu_custom_call" | custom-call | flops 8000000000 | bytes 2147904 | tf_op jit(solution)/shard_map/input_kernel/pallas_call | solution.py:665
  118.4 3.0 %all-to-all-done.1 = bf16[32,48,128]{2,1,0:T(8,128)(2,1)S(1)} async-done(((bf16[32,48,128]{2,1,0:T(8,128)(2,1)}), bf16[32,48,128]{2,1,0:T(8,128)(2,1)S(1)}, u32[]{:S(2)}, u32[]{:S(2)}) %all-to-all-start.1) | async-done | bytes 393248 | tf_op jit(solution)/shard_map/all_to_all | solution.py:701
  121.4 1.8 %finish_kernel.1 = (f32[27,48,48]{2,1,0:T(8,128)}, f32[48,8,48]{2,1,0:T(8,128)}, f32[27,48,48]{2,1,0:T(8,128)}, f32[8,48,48]{2,1,0:T(8,128)}) custom-call(bf16[1536,128]{1,0:T(8,128)(2,1)S(1)} %bitcast.14), custom_call_target="tpu_custom_call" | custom-call | bytes 1038336 | tf_op jit(solution)/shard_map/finish_kernel/pallas_call | solution.py:665
  (24 shorter events, 0.1 us)
Async XLA Ops:
  0.6 19.2 %copy-start.1 = (bf16[1,1,16,48,512]{4,3,2,1,0:T(8,128)(2,1)S(1)}, bf16[1,1,16,48,512]{4,3,2,1,0:T(8,128)(2,1)}, u32[]{:S(2)}) copy-start(bf16[1,1,16,48,512]{4,3,2,1,0:T(8,128)(2,1)} %param.11) | copy-start | bytes 2359300
  0.6 19.2 %copy-start.2 = (s32[1,1,16]{2,1,0:T(1,128)S(1)}, s32[1,1,16]{2,1,0:T(1,128)}, u32[]{:S(2)}) copy-start(s32[1,1,16]{2,1,0:T(1,128)} %param.9) | copy-start | bytes 196
  0.7 19.2 %copy-start = (bf16[1,1,16,48,512]{4,3,2,1,0:T(8,128)(2,1)S(1)}, bf16[1,1,16,48,512]{4,3,2,1,0:T(8,128)(2,1)}, u32[]{:S(2)}) copy-start(bf16[1,1,16,48,512]{4,3,2,1,0:T(8,128)(2,1)} %param.8) | copy-start | bytes 2359300
  0.7 19.2 %copy-start.6 = (bf16[8,48,48]{2,1,0:T(8,128)(2,1)S(1)}, bf16[8,48,48]{2,1,0:T(8,128)(2,1)}, u32[]{:S(2)}) copy-start(bf16[8,48,48]{2,1,0:T(8,128)(2,1)} %up.1) | copy-start | bytes 110596
  0.7 19.2 %copy-start.5 = (bf16[48,8,48]{2,1,0:T(8,128)(2,1)S(1)}, bf16[48,8,48]{2,1,0:T(8,128)(2,1)}, u32[]{:S(2)}) copy-start(bf16[48,8,48]{2,1,0:T(8,128)(2,1)} %down.1) | copy-start | bytes 110596
  4.4 9.2 %collective-permute-start = (bf16[112,512]{1,0:T(8,128)(2,1)}, bf16[112,512]{1,0:T(8,128)(2,1)S(1)}, u32[]{:S(2)}, u32[]{:S(2)}) collective-permute-start(bf16[112,512]{1,0:T(8,128)(2,1)} %get-tuple-element.45), channel_id=1, source_target_pairs={{0,1},{1,2},{2,3},{4,5},{5,6},{6,7},{8,9},{9,10},{10,11},{12,13},{... | collective-permute-start | bytes 344072 | tf_op jit(solution)/shard_map/ppermute | solution.py:685
  6.7 6.9 %collective-permute-start.1 = (bf16[112,512]{1,0:T(8,128)(2,1)}, bf16[112,512]{1,0:T(8,128)(2,1)S(1)}, u32[]{:S(2)}, u32[]{:S(2)}) collective-permute-start(bf16[112,512]{1,0:T(8,128)(2,1)} %get-tuple-element.46), channel_id=1, source_target_pairs={{1,0},{2,1},{3,2},{5,4},{6,5},{7,6},{9,8},{10,9},{11,10},{13,12},{... | collective-permute-start | bytes 344072 | tf_op jit(solution)/shard_map/ppermute | solution.py:685
  8.0 19.3 %collective-permute-start.2 = (bf16[400,384]{1,0:T(8,128)(2,1)}, bf16[400,384]{1,0:T(8,128)(2,1)S(1)}, u32[]{:S(2)}, u32[]{:S(2)}) collective-permute-start(bf16[400,384]{1,0:T(8,128)(2,1)} %get-tuple-element.51), channel_id=1, source_target_pairs={{0,4},{1,5},{2,6},{3,7},{4,8},{5,9},{6,10},{7,11},{8,12},{9,13},{1... | collective-permute-start | bytes 921608 | tf_op jit(solution)/shard_map/ppermute | solution.py:685
  12.3 15.0 %collective-permute-start.3 = (bf16[400,384]{1,0:T(8,128)(2,1)}, bf16[400,384]{1,0:T(8,128)(2,1)S(1)}, u32[]{:S(2)}, u32[]{:S(2)}) collective-permute-start(bf16[400,384]{1,0:T(8,128)(2,1)} %get-tuple-element.52), channel_id=1, source_target_pairs={{4,0},{5,1},{6,2},{7,3},{8,4},{9,5},{10,6},{11,7},{12,8},{13,9},{1... | collective-permute-start | bytes 921608 | tf_op jit(solution)/shard_map/ppermute | solution.py:685
  13.9 13.4 %collective-permute-start.4 = (bf16[64,384]{1,0:T(8,128)(2,1)S(1)}, bf16[64,384]{1,0:T(8,128)(2,1)S(1)}, u32[]{:S(2)}, u32[]{:S(2)}) collective-permute-start(bf16[64,384]{1,0:T(8,128)(2,1)S(1)} %get-tuple-element.53), channel_id=1, source_target_pairs={{0,4},{1,5},{2,6},{3,7},{4,8},{5,9},{6,10},{7,11},{8,12},{9,13},{1... | collective-permute-start | bytes 147464 | tf_op jit(solution)/shard_map/ppermute | solution.py:685
  18.5 8.8 %collective-permute-start.5 = (bf16[64,384]{1,0:T(8,128)(2,1)S(1)}, bf16[64,384]{1,0:T(8,128)(2,1)S(1)}, u32[]{:S(2)}, u32[]{:S(2)}) collective-permute-start(bf16[64,384]{1,0:T(8,128)(2,1)S(1)} %get-tuple-element.47.c_low), channel_id=1, source_target_pairs={{4,0},{5,1},{6,2},{7,3},{8,4},{9,5},{10,6},{11,7},{12,8},{13,9},{1... | collective-permute-start | bytes 147464 | tf_op jit(solution)/shard_map/ppermute | solution.py:685
  19.8 1.0 copy-start.3
  20.8 1.0 copy-start.4
  21.8 5.5 %copy-start.7 = (f32[16,128]{1,0:T(8,128)S(1)}, f32[16,128]{1,0:T(8,128)}, u32[]{:S(2)}) copy-start(f32[16,128]{1,0:T(8,128)} %get-tuple-element.49.flags) | copy-start | bytes 24580
  47.2 9.0 %collective-permute-start.6 = (bf16[5,48,128]{2,1,0:T(8,128)(2,1)S(1)}, bf16[5,48,128]{2,1,0:T(8,128)(2,1)S(1)}, u32[]{:S(2)}, u32[]{:S(2)}) collective-permute-start(bf16[5,48,128]{2,1,0:T(8,128)(2,1)S(1)} %get-tuple-element.59), channel_id=1, source_target_pairs={{0,4},{1,5},{2,6},{3,7},{4,8},{5,9},{6,10},{7,11},{8,12},{9,13},{1... | collective-permute-start | bytes 184328 | tf_op jit(solution)/shard_map/ppermute | solution.py:685
  51.7 8.0 %collective-permute-start.7 = (bf16[5,48,128]{2,1,0:T(8,128)(2,1)S(1)}, bf16[5,48,128]{2,1,0:T(8,128)(2,1)S(1)}, u32[]{:S(2)}, u32[]{:S(2)}) collective-permute-start(bf16[5,48,128]{2,1,0:T(8,128)(2,1)S(1)} %get-tuple-element.60), channel_id=1, source_target_pairs={{4,0},{5,1},{6,2},{7,3},{8,4},{9,5},{10,6},{11,7},{12,8},{13,9},{1... | collective-permute-start | bytes 184328 | tf_op jit(solution)/shard_map/ppermute | solution.py:685
  65.6 17.7 %copy-start.8 = (bf16[80,48,128]{2,1,0:T(8,128)(2,1)}, bf16[80,48,128]{2,1,0:T(8,128)(2,1)S(1)}, u32[]{:S(2)}) copy-start(bf16[80,48,128]{2,1,0:T(8,128)(2,1)S(1)} %get-tuple-element.65.grad_h) | copy-start | bytes 2949124
  65.6 17.7 %collective-permute-start.8 = (bf16[10,48,128]{2,1,0:T(8,128)(2,1)S(1)}, bf16[10,48,128]{2,1,0:T(8,128)(2,1)S(1)}, u32[]{:S(2)}, u32[]{:S(2)}) collective-permute-start(bf16[10,48,128]{2,1,0:T(8,128)(2,1)S(1)} %get-tuple-element.69), channel_id=1, source_target_pairs={{0,4},{1,5},{2,6},{3,7},{4,8},{5,9},{6,10},{7,11},{8,12},{9,13},{1... | collective-permute-start | bytes 368648 | tf_op jit(solution)/shard_map/ppermute | solution.py:685
  70.3 13.0 %collective-permute-start.9 = (bf16[10,48,128]{2,1,0:T(8,128)(2,1)S(1)}, bf16[10,48,128]{2,1,0:T(8,128)(2,1)S(1)}, u32[]{:S(2)}, u32[]{:S(2)}) collective-permute-start(bf16[10,48,128]{2,1,0:T(8,128)(2,1)S(1)} %get-tuple-element.70), channel_id=1, source_target_pairs={{4,0},{5,1},{6,2},{7,3},{8,4},{9,5},{10,6},{11,7},{12,8},{13,9},{1... | collective-permute-start | bytes 368648 | tf_op jit(solution)/shard_map/ppermute | solution.py:685
  83.3 21.4 %all-to-all-start = ((bf16[32,48,128]{2,1,0:T(8,128)(2,1)}), bf16[32,48,128]{2,1,0:T(8,128)(2,1)S(1)}, u32[]{:S(2)}, u32[]{:S(2)}) async-start(bf16[32,48,128]{2,1,0:T(8,128)(2,1)} %bitcast.6), calls=%async_computation | async-start | bytes 786432 | tf_op jit(solution)/shard_map/all_to_all | solution.py:693
  105.6 15.8 %all-to-all-start.1 = ((bf16[32,48,128]{2,1,0:T(8,128)(2,1)}), bf16[32,48,128]{2,1,0:T(8,128)(2,1)S(1)}, u32[]{:S(2)}, u32[]{:S(2)}) async-start(bf16[32,48,128]{2,1,0:T(8,128)(2,1)} %broadcast_in_dim.2), calls=%async_computation.1 | async-start | bytes 786432 | tf_op jit(solution)/shard_map/all_to_all | solution.py:701
  108.2 1.2 copy-start.9

commit v11 on v10

--- a/solution.py
+++ b/solution.py
@@ -153,10 +153,10 @@
 
 
 def gather_sub(parts):
-    total = parts[:C]
-    for index in range(1, 4):
-        total = total + roll(parts[index * C : (index + 1) * C], -SHIFTS[index])
-    return total
+    even = lane_ids(C) % 2 == 0
+    above = jnp.where(even, parts[2 * C : 3 * C], parts[3 * C :])
+    total = jnp.where(even, parts[:C], parts[C : 2 * C]) + roll(above, -16)
+    return total + roll(total, -1)
 
 
 def spread_sub(anchored):
@@ -311,36 +311,38 @@
     loop(0, pairs, rect_step, 2)
 
 
-def conv_sum(parts, tile):
-    return parts[tile, 0:C] + parts[tile + 1, C : 2 * C] + parts[tile + 2, 2 * C :]
-
-
-def conv_steps(parts, weight, load, tiles, step, first, even, odd):
+def conv_steps(sums, weight, load, tiles, step, first, even, odd):
     masks = depth_masks(step, first)
-    spare = jnp.zeros((3 * C, LANES), F32)
-    parts[0] = spare
-    parts[tiles + 1] = spare
 
     def fill(buffer, tile):
         for i in range(4):
             cols = depth_columns(load(tile + i), masks, step)
             buffer[:, LANES * i : LANES * (i + 1)] = cols
 
-    def multiply(buffer, tile):
+    def multiply(buffer, tile, carry):
         out = dot(weight[...], buffer[...])
-        for i in range(4):
-            parts[tile + i + 1] = out[:, LANES * i : LANES * (i + 1)]
+
+        def part(along, i):
+            return out[C * along : C * (along + 1), LANES * i : LANES * (i + 1)]
+
+        sums[tile] += part(2, 0)
+        sums[tile + 1] = carry + part(1, 0) + part(2, 1)
+        sums[tile + 2] = part(0, 0) + part(1, 1) + part(2, 2)
+        sums[tile + 3] = part(0, 1) + part(1, 2) + part(2, 3)
+        sums[tile + 4] = part(0, 2) + part(1, 3)
+        return part(0, 3)
 
     fill(even, 0)
-
-    def body(index):
+    sums[0] = jnp.zeros((C, LANES), F32)
+
+    def body(index, carry):
         tile = 8 * index
         fill(odd, tile + 4)
-        multiply(even, tile)
+        carry = multiply(even, tile, carry)
         fill(even, jnp.minimum(tile + 8, tiles - 4))
-        multiply(odd, tile + 4)
-
-    loop(0, tiles // 8, body)
+        return multiply(odd, tile + 4, carry)
+
+    lax.fori_loop(0, tiles // 8, body, jnp.zeros((C, LANES), F32))
 
 
 def forward_kernel(
@@ -395,7 +397,7 @@
             actives = []
             for half in range(2):
                 tile = EDGE * block + 2 * inner + half
-                value = conv_sum(fine_p, tile) * alive
+                value = fine_p[tile + 1] * alive
                 hidden_all[tile] = value
                 actives.append(silu_parts(value)[0].astype(BF16))
             pairs.append(jnp.concatenate(actives, axis=0))
@@ -428,7 +430,7 @@
         keep = alive * pair_anchors
         for inner in range(4):
             coarse = 4 * block + inner
-            smooth, slope = silu_parts(conv_sum(coarse_p, coarse))
+            smooth, slope = silu_parts(coarse_p[coarse + 1])
             rects[coarse] = (smooth * pair_anchors).astype(BF16)
             grad_c[coarse] = (grad_r[coarse] * slope * keep).astype(BF16)
 
@@ -536,7 +538,7 @@
         spreads = []
         for inner in range(4):
             coarse = 4 * block + inner
-            down = (conv_sum(coarse_p, coarse) * keep).astype(BF16)
+            down = (coarse_p[coarse + 1] * keep).astype(BF16)
             grad_d[coarse] = down
             spreads.append(spread_sub(down))
         acts = dot(down_w[...], jnp.concatenate(spreads, axis=1), (0, 0))
@@ -552,7 +554,7 @@
     pack_columns(grad_h, pack_low, pack_high, 1)
 
 
-def weight_kernel(grid, grad_h, grad_d, hidden, early, joined, grad_own, fine_g, down_g, even, odd):
+def weight_kernel(grid, grad_h, grad_d, hidden, early, joined, grad_own, fine_g, down_g):
     tiles = grad_h.shape[0]
     shift = tiles - 16
     fine_g[...] = jnp.zeros_like(fine_g)
@@ -570,30 +572,18 @@
     edges = edge_masks(1)
     halves = own_masks()
 
-    groups = (tiles - 8) // 8
-
-    def fill(buffer, group):
-        for inner in range(8):
-            tile = 4 + 8 * group + inner
+    def fine_step(index):
+        at = [4 + 8 * index + inner for inner in range(8)]
+        rights = []
+        for tile in at:
             lower, upper = grid[tile], grid[tile + shift]
             base = pair_columns(*pair_tiles(lower, upper, halves), edges, 1)
-            buffer[:, LANES * inner : LANES * (inner + 1)] = depth_columns(base, masks, 16)
-
-    def multiply(buffer, group):
-        at = [4 + 8 * group + inner for inner in range(8)]
-        fine_g[0 : 9 * C, :] += dot(buffer[...], stacks(grad_own, at), (1, 1))
-
-    fill(even, 0)
-
-    def fine_step(index):
-        fill(odd, 2 * index + 1)
-        multiply(even, 2 * index)
-        fill(even, jnp.minimum(2 * index + 2, groups - 1))
-        multiply(odd, 2 * index + 1)
-
-    loop(0, groups // 2, fine_step)
-    if groups % 2:
-        multiply(even, groups - 1)
+            rights.append(depth_columns(base, masks, 16))
+        fine_g[0 : 9 * C, :] += dot(
+            jnp.concatenate(rights, axis=1), stacks(grad_own, at), (1, 1)
+        )
+
+    loop(0, (tiles - 8) // 8, fine_step)
 
     def down_step(index):
         lefts = []
@@ -625,7 +615,7 @@
         alive = jnp.broadcast_to(live[pl.ds(block, 1), :], (C, LANES))
         start = pl.multiple_of((block - 1) * C, 16)
         for inner in range(EDGE):
-            value = conv_sum(fine_p, EDGE * block + inner)
+            value = fine_p[EDGE * block + inner + 1]
             rows_out[pl.ds(start, C), LANES * inner : LANES * (inner + 1)] = (
                 value * alive
             ).astype(BF16)
@@ -775,8 +765,8 @@
         ],
         [
             (((number + 2) * C, VOX), BF16),
-            ((tiles + 2, 3 * C, LANES), F32),
-            ((4 * pairs + 2, 3 * C, LANES), F32),
+            ((tiles + 1, C, LANES), F32),
+            ((4 * pairs + 1, C, LANES), F32),
             ((tiles, C, LANES), F32),
             ((coarse_tiles, C, LANES), BF16),
             ((C, LANES), F32),
@@ -802,7 +792,7 @@
             ((fine_groups, C, LANES), BF16),
             ((fine_groups, C, LANES), BF16),
         ],
-        [((4 * pairs + 2, 3 * C, LANES), F32), ((4 * pairs, 3 * C, LANES), BF16)]
+        [((4 * pairs + 1, C, LANES), F32), ((4 * pairs, 3 * C, LANES), BF16)]
         + [((9 * C, 4 * LANES), BF16)] * 2,
         flops=8 * 10**9,
     )
@@ -812,8 +802,7 @@
         weight_kernel,
         (grid, grad_h, grad_d, hidden, early),
         [((32 * C, LANES), BF16)],
-        [((EDGE * pairs, C, LANES), BF16), ((VOX, 3 * C), F32), ((4 * C, LANES), F32)]
-        + [((9 * C, 8 * LANES), BF16)] * 2,
+        [((EDGE * pairs, C, LANES), BF16), ((VOX, 3 * C), F32), ((4 * C, LANES), F32)],
         flops=12 * 10**9,
     )
     joined, edge_left, edge_right, slots = lax.optimization_barrier(
@@ -834,7 +823,7 @@
         (slots, grad_h, edge_left, edge_right, live, fine_back),
         [((number, C, VOX), BF16)],
         [
-            ((EDGE * pairs + 2, 3 * C, LANES), F32),
+            ((EDGE * pairs + 1, C, LANES), F32),
             ((number // 2 * C, 1024), BF16),
             ((number // 2 * C, 1024), BF16),
             ((EDGE * pairs, 3 * C, LANES), BF16),

time: 124 us -> 121 us (0.976)
  Pallas kernels: 64.1 us -> 60.9 us
    pallas_call x10, Pallas kernels: 64.1 us -> 60.9 us  [call(): pl.pallas_call(kernel, out_shape=tuple((jax.ShapeDtypeStruct(s, d) for s,...]
  transfers between devices with their start and end apart: 12 -> 12, of which waited for: 4 -> 4; matrix products, arithmetic and copies ran while one was open for 0% -> 0% of each run, Pallas kernels for 27% -> 25%
where the time goes in v11:
time: 121 us; the launch traced here: 120 us
  Pallas kernels  60.9 us (50%)
  starting transfers between devices  37.8 us (31%)
  waiting for transfers between devices  15.6 us (13%)
  local copies, waits for them, and re-layouts  3.97 us (3%)
  between operations  1.68 us (1%)
    pallas_call x10, Pallas kernels, call(): pl.pallas_call(kernel, out_shape=tuple((jax.ShapeDtypeStruct(s, d) for s,...  60.9 us
    ppermute x10, starting transfers between devices, send(): return lax.ppermute(array, ('gx', 'gy'), pairs)  26.8 us
    all_to_all x1, waiting for transfers between devices, reduce_share(): lax.all_to_all(joined.reshape(devices, share, LANES), ('gx', 'gy'), 0, 0)  8.75 us
    all_to_all x1, starting transfers between devices, reduce_share(): lax.all_to_all(joined.reshape(devices, share, LANES), ('gx', 'gy'), 0, 0)  8.27 us
    ppermute x10, waiting for transfers between devices, send(): return lax.ppermute(array, ('gx', 'gy'), pairs)  3.94 us
    unnamed x20, local copies, waits for them, and re-layouts  3.17 us
    all_to_all x1, waiting for transfers between devices, spread_share(): full = lax.all_to_all(copies, ('gx', 'gy'), 0, 0)  2.88 us
    all_to_all x1, starting transfers between devices, spread_share(): full = lax.all_to_all(copies, ('gx', 'gy'), 0, 0)  2.82 us
  transfers between devices with their start and end apart: 12, of which 4 were waited for; matrix products, arithmetic and copies ran while one was open for 0% of the time, Pallas kernels for 25%

profile of v11, /device:TPU:0, one launch (start us, length us, event | category | flops | bytes accessed | tf_op | source)
XLA Modules:
  0.0 120.0 jit_solution(1486889378395067297)
XLA Ops:
  1.5 2.9 %prepare_kernel.1 = (f32[16,128]{1,0:T(8,128)}, bf16[400,384]{1,0:T(8,128)(2,1)}, bf16[400,384]{1,0:T(8,128)(2,1)}, bf16[112,512]{1,0:T(8,128)(2,1)}, bf16[112,512]{1,0:T(8,128)(2,1)}) custom-call(s32[16]{0:T(128)} %bitcast.19, s32[1]{0:T(128)} %bitcast.12.count, bf16[16,48,512]{2,1,0:T(8,128)(2,1)} %bitcast.15, bf16[16,48,512]{2,1,0:T(8,128)(2,1)} %bitcast.17), custom_call_target="tpu_custom_call" | custom-call | bytes 2424900 | tf_op jit(solution)/shard_map/prepare_kernel/pallas_call | solution.py:655
  4.4 2.3 %collective-permute-start = (bf16[112,512]{1,0:T(8,128)(2,1)}, bf16[112,512]{1,0:T(8,128)(2,1)S(1)}, u32[]{:S(2)}, u32[]{:S(2)}) collective-permute-start(bf16[112,512]{1,0:T(8,128)(2,1)} %get-tuple-element.45), channel_id=1, source_target_pairs={{0,1},{1,2},{2,3},{4,5},{5,6},{6,7},{8,9},{9,10},{10,11},{12,13},{... | collective-permute-start | bytes 344072 | tf_op jit(solution)/shard_map/ppermute | solution.py:675
  6.7 1.3 %collective-permute-start.1 = (bf16[112,512]{1,0:T(8,128)(2,1)}, bf16[112,512]{1,0:T(8,128)(2,1)S(1)}, u32[]{:S(2)}, u32[]{:S(2)}) collective-permute-start(bf16[112,512]{1,0:T(8,128)(2,1)} %get-tuple-element.46), channel_id=1, source_target_pairs={{1,0},{2,1},{3,2},{5,4},{6,5},{7,6},{9,8},{10,9},{11,10},{13,12},{... | collective-permute-start | bytes 344072 | tf_op jit(solution)/shard_map/ppermute | solution.py:675
  8.0 4.2 %collective-permute-start.2 = (bf16[400,384]{1,0:T(8,128)(2,1)}, bf16[400,384]{1,0:T(8,128)(2,1)S(1)}, u32[]{:S(2)}, u32[]{:S(2)}) collective-permute-start(bf16[400,384]{1,0:T(8,128)(2,1)} %get-tuple-element.51), channel_id=1, source_target_pairs={{0,4},{1,5},{2,6},{3,7},{4,8},{5,9},{6,10},{7,11},{8,12},{9,13},{1... | collective-permute-start | bytes 921608 | tf_op jit(solution)/shard_map/ppermute | solution.py:675
  12.3 1.3 %collective-permute-start.3 = (bf16[400,384]{1,0:T(8,128)(2,1)}, bf16[400,384]{1,0:T(8,128)(2,1)S(1)}, u32[]{:S(2)}, u32[]{:S(2)}) collective-permute-start(bf16[400,384]{1,0:T(8,128)(2,1)} %get-tuple-element.52), channel_id=1, source_target_pairs={{4,0},{5,1},{6,2},{7,3},{8,4},{9,5},{10,6},{11,7},{12,8},{13,9},{1... | collective-permute-start | bytes 921608 | tf_op jit(solution)/shard_map/ppermute | solution.py:675
  13.6 0.3 corner_kernel.1
  13.9 4.5 %collective-permute-start.4 = (bf16[64,384]{1,0:T(8,128)(2,1)S(1)}, bf16[64,384]{1,0:T(8,128)(2,1)S(1)}, u32[]{:S(2)}, u32[]{:S(2)}) collective-permute-start(bf16[64,384]{1,0:T(8,128)(2,1)S(1)} %get-tuple-element.53), channel_id=1, source_target_pairs={{0,4},{1,5},{2,6},{3,7},{4,8},{5,9},{6,10},{7,11},{8,12},{9,13},{1... | collective-permute-start | bytes 147464 | tf_op jit(solution)/shard_map/ppermute | solution.py:675
  18.5 1.3 %collective-permute-start.5 = (bf16[64,384]{1,0:T(8,128)(2,1)S(1)}, bf16[64,384]{1,0:T(8,128)(2,1)S(1)}, u32[]{:S(2)}, u32[]{:S(2)}) collective-permute-start(bf16[64,384]{1,0:T(8,128)(2,1)S(1)} %get-tuple-element.47.c_low), channel_id=1, source_target_pairs={{4,0},{5,1},{6,2},{7,3},{8,4},{9,5},{10,6},{11,7},{12,8},{13,9},{1... | collective-permute-start | bytes 147464 | tf_op jit(solution)/shard_map/ppermute | solution.py:675
  19.8 0.0 copy-start.3
  19.8 1.0 copy-done.3
  20.8 1.0 copy-done.4
  21.8 5.0 %place_kernel.1 = (bf16[144,48,128]{2,1,0:T(8,128)(2,1)S(1)}, bf16[80,48,128]{2,1,0:T(8,128)(2,1)S(1)}, f32[40,48,128]{2,1,0:T(8,128)S(1)}, bf16[144,432]{1,0:T(...) custom-call(s32[16]{0:T(128)S(1)} %bitcast.20, ...), custom_call_target="tpu_custom_call" | custom-call | flops 8000000000 | bytes 6480964 | tf_op jit(solution)/shard_map/place_kernel/pallas_call | solution.py:655
  26.8 0.5 collective-permute-done.4.c_left
  27.3 19.8 %forward_kernel.1 = (bf16[144,48,128]{2,1,0:T(8,128)(2,1)S(1)}, f32[80,48,128]{2,1,0:T(8,128)S(1)}, bf16[40,144,128]{2,1,0:T(8,128)(2,1)S(1)}, bf16[40,48,128]{2...) custom-call(bf16[144,48,128]{2,1,0:T(8,128)(2,1)S(1)} %get-tuple-ele, ...), custom_call_target="tpu_custom_call" | custom-call | flops 8000000000 | bytes 10312704 | tf_op jit(solution)/shard_map/forward_kernel/pallas_call | solution.py:655
  47.1 4.5 %collective-permute-start.6 = (bf16[5,48,128]{2,1,0:T(8,128)(2,1)S(1)}, bf16[5,48,128]{2,1,0:T(8,128)(2,1)S(1)}, u32[]{:S(2)}, u32[]{:S(2)}) collective-permute-start(bf16[5,48,128]{2,1,0:T(8,128)(2,1)S(1)} %get-tuple-element.59), channel_id=1, source_target_pairs={{0,4},{1,5},{2,6},{3,7},{4,8},{5,9},{6,10},{7,11},{8,12},{9,13},{1... | collective-permute-start | bytes 184328 | tf_op jit(solution)/shard_map/ppermute | solution.py:675
  51.6 1.3 %collective-permute-start.7 = (bf16[5,48,128]{2,1,0:T(8,128)(2,1)S(1)}, bf16[5,48,128]{2,1,0:T(8,128)(2,1)S(1)}, u32[]{:S(2)}, u32[]{:S(2)}) collective-permute-start(bf16[5,48,128]{2,1,0:T(8,128)(2,1)S(1)} %get-tuple-element.60), channel_id=1, source_target_pairs={{4,0},{5,1},{6,2},{7,3},{8,4},{9,5},{10,6},{11,7},{12,8},{13,9},{1... | collective-permute-start | bytes 184328 | tf_op jit(solution)/shard_map/ppermute | solution.py:675
  52.9 3.3 %side_kernel.1.early = bf16[768,128]{1,0:T(8,128)(2,1)S(1)} custom-call(bf16[40,48,128]{2,1,0:T(8,128)(2,1)S(1)} %get-tuple-element.67.rects, bf16[80,48,128]{2,1,0:T(8,128)(2,1)S(1)} %get-tuple-element.62.cot_grid, bf16[40,144,128]{2,1,0:T(8,128)(2,1)S(1)} %get-tuple-element.68.low_cols, bf16[40,48,128]{2,1,0:T(8,128)(2,1)S(1)} %get-tuple-element.58.grad_c), custom_call_target="tpu_custom_call" | custom-call | flops 8000000000 | bytes 3637248 | tf_op jit(solution)/shard_map/side_kernel/pallas_call | solution.py:655
  56.2 3.4 %collective-permute-done.7.from_right = bf16[5,48,128]{2,1,0:T(8,128)(2,1)S(1)} collective-permute-done((bf16[5,48,128]{2,1,0:T(8,128)(2,1)S(1)}, bf16[5,48,128]{2,1,0:T(8,128)(2,1)S(1)}, u32[]{:S(2)}, u32[]{:S(2)}) %collective-permute-start.7) | collective-permute-done | bytes 61472 | tf_op jit(solution)/shard_map/ppermute | solution.py:675
  59.6 5.9 %backward_kernel.1 = (bf16[80,48,128]{2,1,0:T(8,128)(2,1)S(1)}, bf16[40,48,128]{2,1,0:T(8,128)(2,1)S(1)}, bf16[10,48,128]{2,1,0:T(8,128)(2,1)S(1)}, bf16[10,48,128]{2,1,0:T(8,128)(2,1)S(1)}) custom-call(bf16[40,48,128]{2,1,0:T(8,128)(2,1)S(1)} %get-tuple-element.58.grad_c, bf16[5,48,128]{2,1,0:T(8,128)(2,1)S(1)} %collective-permute-done.6.from_left, ...), custom_call_target="tpu_custom_call" | custom-call | flops 8000000000 | bytes 5453312 | tf_op jit(solution)/shard_map/backward_kernel/pallas_call | solution.py:655
  65.6 4.6 %collective-permute-start.8 = (bf16[10,48,128]{2,1,0:T(8,128)(2,1)S(1)}, bf16[10,48,128]{2,1,0:T(8,128)(2,1)S(1)}, u32[]{:S(2)}, u32[]{:S(2)}) collective-permute-start(bf16[10,48,128]{2,1,0:T(8,128)(2,1)S(1)} %get-tuple-element.69), channel_id=1, source_target_pairs={{0,4},{1,5},{2,6},{3,7},{4,8},{5,9},{6,10},{7,11},{8,12},{9,13},{1... | collective-permute-start | bytes 368648 | tf_op jit(solution)/shard_map/ppermute | solution.py:675
  70.2 1.3 %collective-permute-start.9 = (bf16[10,48,128]{2,1,0:T(8,128)(2,1)S(1)}, bf16[10,48,128]{2,1,0:T(8,128)(2,1)S(1)}, u32[]{:S(2)}, u32[]{:S(2)}) collective-permute-start(bf16[10,48,128]{2,1,0:T(8,128)(2,1)S(1)} %get-tuple-element.70), channel_id=1, source_target_pairs={{4,0},{5,1},{6,2},{7,3},{8,4},{9,5},{10,6},{11,7},{12,8},{13,9},{1... | collective-permute-start | bytes 368648 | tf_op jit(solution)/shard_map/ppermute | solution.py:675
  71.5 8.6 %weight_kernel.1 = bf16[1536,128]{1,0:T(8,128)(2,1)} custom-call(bf16[144,48,128]{2,1,0:T(8,128)(2,1)S(1)} %get-tuple-element.57.grid, bf16[80,48,128]{2,1,0:T(8,128)(2,1)S(1)} %get-tuple-element.65.grad_h, bf16[40,48,128]{2,1,0:T(8,128)(2,1)S(1)} %get-tuple-element.66.grad_d, f32[80,48,128]{2,1,0:T(8,128)S(1)} %get-tuple-element.61.hidden, ...), custom_call_target="tpu_custom_call" | custom-call | flops 12000000000 | bytes 5799936 | tf_op jit(solution)/shard_map/weight_kernel/pallas_call | solution.py:655
  80.1 8.3 %all-to-all-start = ((bf16[32,48,128]{2,1,0:T(8,128)(2,1)}), bf16[32,48,128]{2,1,0:T(8,128)(2,1)S(1)}, u32[]{:S(2)}, u32[]{:S(2)}) async-start(bf16[32,48,128]{2,1,0:T(8,128)(2,1)} %bitcast.6), calls=%async_computation | async-start | bytes 786432 | tf_op jit(solution)/shard_map/all_to_all | solution.py:683
  88.4 4.4 %output_kernel.1 = bf16[16,48,512]{2,1,0:T(8,128)(2,1)} custom-call(s32[16]{0:T(128)S(1)} %bitcast.21, f32[80,48,128]{2,1,0:T(8,128)S(1)} %get-tuple-element.61.hidden, bf16[40,48,128]{2,1,0:T(8,128)(2,1)S(1)} %get-tuple-element.67.rects, f32[16,128]{1,0:T(8,128)S(1)} %get-tuple-element.63.live, bf16[96,192]{1,0:T(8,128)(2,1)S(1)} %get-tuple-element.73.up_w), custom_call_target="tpu_custom_call" | custom-call | flops 8000000000 | bytes 3289152 | tf_op jit(solution)/shard_map/output_kernel/pallas_call | solution.py:655
  92.8 8.7 %all-to-all-done = bf16[32,48,128]{2,1,0:T(8,128)(2,1)S(1)} async-done(((bf16[32,48,128]{2,1,0:T(8,128)(2,1)}), bf16[32,48,128]{2,1,0:T(8,128)(2,1)S(1)}, u32[]{:S(2)}, u32[]{:S(2)}) %all-to-all-start) | async-done | bytes 393248 | tf_op jit(solution)/shard_map/all_to_all | solution.py:683
  101.6 0.1 reduce_sum.12
  101.6 0.8 broadcast_in_dim.2
  102.4 2.8 %all-to-all-start.1 = ((bf16[32,48,128]{2,1,0:T(8,128)(2,1)}), bf16[32,48,128]{2,1,0:T(8,128)(2,1)S(1)}, u32[]{:S(2)}, u32[]{:S(2)}) async-start(bf16[32,48,128]{2,1,0:T(8,128)(2,1)} %broadcast_in_dim.2), calls=%async_computation.1 | async-start | bytes 786432 | tf_op jit(solution)/shard_map/all_to_all | solution.py:691
  105.3 1.2 copy-done.9
  106.5 8.9 %input_kernel.1 = bf16[16,48,512]{2,1,0:T(8,128)(2,1)} custom-call(s32[16]{0:T(128)S(1)} %bitcast.22, bf16[80,48,128]{2,1,0:T(8,128)(2,1)S(1)} %copy-done.9, bf16[10,48,128]{2,1,0:T(8,128)(2,1)S(1)} %collective-permute-done.8.from_left, bf16[10,48,128]{2,1,0:T(8,128)(2,1)S(1)} %collective-permute-done.9.from_right, f32[16,128]{1,0:T(8,128)S(1)} %get-tuple-element.63.live, ...), custom_call_target="tpu_custom_call" | custom-call | flops 8000000000 | bytes 2147904 | tf_op jit(solution)/shard_map/input_kernel/pallas_call | solution.py:655
  115.4 2.9 %all-to-all-done.1 = bf16[32,48,128]{2,1,0:T(8,128)(2,1)S(1)} async-done(((bf16[32,48,128]{2,1,0:T(8,128)(2,1)}), bf16[32,48,128]{2,1,0:T(8,128)(2,1)S(1)}, u32[]{:S(2)}, u32[]{:S(2)}) %all-to-all-start.1) | async-done | bytes 393248 | tf_op jit(solution)/shard_map/all_to_all | solution.py:691
  118.2 1.8 %finish_kernel.1 = (f32[27,48,48]{2,1,0:T(8,128)}, f32[48,8,48]{2,1,0:T(8,128)}, f32[27,48,48]{2,1,0:T(8,128)}, f32[8,48,48]{2,1,0:T(8,128)}) custom-call(bf16[1536,128]{1,0:T(8,128)(2,1)S(1)} %bitcast.14), custom_call_target="tpu_custom_call" | custom-call | bytes 1038336 | tf_op jit(solution)/shard_map/finish_kernel/pallas_call | solution.py:655
  (24 shorter events, 0.1 us)
Async XLA Ops:
  0.6 19.2 %copy-start.1 = (bf16[1,1,16,48,512]{4,3,2,1,0:T(8,128)(2,1)S(1)}, bf16[1,1,16,48,512]{4,3,2,1,0:T(8,128)(2,1)}, u32[]{:S(2)}) copy-start(bf16[1,1,16,48,512]{4,3,2,1,0:T(8,128)(2,1)} %param.11) | copy-start | bytes 2359300
  0.6 19.2 %copy-start.2 = (s32[1,1,16]{2,1,0:T(1,128)S(1)}, s32[1,1,16]{2,1,0:T(1,128)}, u32[]{:S(2)}) copy-start(s32[1,1,16]{2,1,0:T(1,128)} %param.9) | copy-start | bytes 196
  0.7 19.2 %copy-start = (bf16[1,1,16,48,512]{4,3,2,1,0:T(8,128)(2,1)S(1)}, bf16[1,1,16,48,512]{4,3,2,1,0:T(8,128)(2,1)}, u32[]{:S(2)}) copy-start(bf16[1,1,16,48,512]{4,3,2,1,0:T(8,128)(2,1)} %param.8) | copy-start | bytes 2359300
  0.7 19.2 %copy-start.6 = (bf16[8,48,48]{2,1,0:T(8,128)(2,1)S(1)}, bf16[8,48,48]{2,1,0:T(8,128)(2,1)}, u32[]{:S(2)}) copy-start(bf16[8,48,48]{2,1,0:T(8,128)(2,1)} %up.1) | copy-start | bytes 110596
  0.7 19.2 %copy-start.5 = (bf16[48,8,48]{2,1,0:T(8,128)(2,1)S(1)}, bf16[48,8,48]{2,1,0:T(8,128)(2,1)}, u32[]{:S(2)}) copy-start(bf16[48,8,48]{2,1,0:T(8,128)(2,1)} %down.1) | copy-start | bytes 110596
  4.4 9.2 %collective-permute-start = (bf16[112,512]{1,0:T(8,128)(2,1)}, bf16[112,512]{1,0:T(8,128)(2,1)S(1)}, u32[]{:S(2)}, u32[]{:S(2)}) collective-permute-start(bf16[112,512]{1,0:T(8,128)(2,1)} %get-tuple-element.45), channel_id=1, source_target_pairs={{0,1},{1,2},{2,3},{4,5},{5,6},{6,7},{8,9},{9,10},{10,11},{12,13},{... | collective-permute-start | bytes 344072 | tf_op jit(solution)/shard_map/ppermute | solution.py:675
  6.7 6.9 %collective-permute-start.1 = (bf16[112,512]{1,0:T(8,128)(2,1)}, bf16[112,512]{1,0:T(8,128)(2,1)S(1)}, u32[]{:S(2)}, u32[]{:S(2)}) collective-permute-start(bf16[112,512]{1,0:T(8,128)(2,1)} %get-tuple-element.46), channel_id=1, source_target_pairs={{1,0},{2,1},{3,2},{5,4},{6,5},{7,6},{9,8},{10,9},{11,10},{13,12},{... | collective-permute-start | bytes 344072 | tf_op jit(solution)/shard_map/ppermute | solution.py:675
  8.0 19.3 %collective-permute-start.2 = (bf16[400,384]{1,0:T(8,128)(2,1)}, bf16[400,384]{1,0:T(8,128)(2,1)S(1)}, u32[]{:S(2)}, u32[]{:S(2)}) collective-permute-start(bf16[400,384]{1,0:T(8,128)(2,1)} %get-tuple-element.51), channel_id=1, source_target_pairs={{0,4},{1,5},{2,6},{3,7},{4,8},{5,9},{6,10},{7,11},{8,12},{9,13},{1... | collective-permute-start | bytes 921608 | tf_op jit(solution)/shard_map/ppermute | solution.py:675
  12.3 15.0 %collective-permute-start.3 = (bf16[400,384]{1,0:T(8,128)(2,1)}, bf16[400,384]{1,0:T(8,128)(2,1)S(1)}, u32[]{:S(2)}, u32[]{:S(2)}) collective-permute-start(bf16[400,384]{1,0:T(8,128)(2,1)} %get-tuple-element.52), channel_id=1, source_target_pairs={{4,0},{5,1},{6,2},{7,3},{8,4},{9,5},{10,6},{11,7},{12,8},{13,9},{1... | collective-permute-start | bytes 921608 | tf_op jit(solution)/shard_map/ppermute | solution.py:675
  13.9 13.4 %collective-permute-start.4 = (bf16[64,384]{1,0:T(8,128)(2,1)S(1)}, bf16[64,384]{1,0:T(8,128)(2,1)S(1)}, u32[]{:S(2)}, u32[]{:S(2)}) collective-permute-start(bf16[64,384]{1,0:T(8,128)(2,1)S(1)} %get-tuple-element.53), channel_id=1, source_target_pairs={{0,4},{1,5},{2,6},{3,7},{4,8},{5,9},{6,10},{7,11},{8,12},{9,13},{1... | collective-permute-start | bytes 147464 | tf_op jit(solution)/shard_map/ppermute | solution.py:675
  18.5 8.8 %collective-permute-start.5 = (bf16[64,384]{1,0:T(8,128)(2,1)S(1)}, bf16[64,384]{1,0:T(8,128)(2,1)S(1)}, u32[]{:S(2)}, u32[]{:S(2)}) collective-permute-start(bf16[64,384]{1,0:T(8,128)(2,1)S(1)} %get-tuple-element.47.c_low), channel_id=1, source_target_pairs={{4,0},{5,1},{6,2},{7,3},{8,4},{9,5},{10,6},{11,7},{12,8},{13,9},{1... | collective-permute-start | bytes 147464 | tf_op jit(solution)/shard_map/ppermute | solution.py:675
  19.8 1.0 copy-start.3
  20.8 1.0 copy-start.4
  21.8 5.5 %copy-start.7 = (f32[16,128]{1,0:T(8,128)S(1)}, f32[16,128]{1,0:T(8,128)}, u32[]{:S(2)}) copy-start(f32[16,128]{1,0:T(8,128)} %get-tuple-element.49.flags) | copy-start | bytes 24580
  47.1 9.1 %collective-permute-start.6 = (bf16[5,48,128]{2,1,0:T(8,128)(2,1)S(1)}, bf16[5,48,128]{2,1,0:T(8,128)(2,1)S(1)}, u32[]{:S(2)}, u32[]{:S(2)}) collective-permute-start(bf16[5,48,128]{2,1,0:T(8,128)(2,1)S(1)} %get-tuple-element.59), channel_id=1, source_target_pairs={{0,4},{1,5},{2,6},{3,7},{4,8},{5,9},{6,10},{7,11},{8,12},{9,13},{1... | collective-permute-start | bytes 184328 | tf_op jit(solution)/shard_map/ppermute | solution.py:675
  51.6 8.0 %collective-permute-start.7 = (bf16[5,48,128]{2,1,0:T(8,128)(2,1)S(1)}, bf16[5,48,128]{2,1,0:T(8,128)(2,1)S(1)}, u32[]{:S(2)}, u32[]{:S(2)}) collective-permute-start(bf16[5,48,128]{2,1,0:T(8,128)(2,1)S(1)} %get-tuple-element.60), channel_id=1, source_target_pairs={{4,0},{5,1},{6,2},{7,3},{8,4},{9,5},{10,6},{11,7},{12,8},{13,9},{1... | collective-permute-start | bytes 184328 | tf_op jit(solution)/shard_map/ppermute | solution.py:675
  65.5 14.6 %copy-start.8 = (bf16[80,48,128]{2,1,0:T(8,128)(2,1)}, bf16[80,48,128]{2,1,0:T(8,128)(2,1)S(1)}, u32[]{:S(2)}) copy-start(bf16[80,48,128]{2,1,0:T(8,128)(2,1)S(1)} %get-tuple-element.65.grad_h) | copy-start | bytes 2949124
  65.6 14.5 %collective-permute-start.8 = (bf16[10,48,128]{2,1,0:T(8,128)(2,1)S(1)}, bf16[10,48,128]{2,1,0:T(8,128)(2,1)S(1)}, u32[]{:S(2)}, u32[]{:S(2)}) collective-permute-start(bf16[10,48,128]{2,1,0:T(8,128)(2,1)S(1)} %get-tuple-element.69), channel_id=1, source_target_pairs={{0,4},{1,5},{2,6},{3,7},{4,8},{5,9},{6,10},{7,11},{8,12},{9,13},{1... | collective-permute-start | bytes 368648 | tf_op jit(solution)/shard_map/ppermute | solution.py:675
  70.2 9.9 %collective-permute-start.9 = (bf16[10,48,128]{2,1,0:T(8,128)(2,1)S(1)}, bf16[10,48,128]{2,1,0:T(8,128)(2,1)S(1)}, u32[]{:S(2)}, u32[]{:S(2)}) collective-permute-start(bf16[10,48,128]{2,1,0:T(8,128)(2,1)S(1)} %get-tuple-element.70), channel_id=1, source_target_pairs={{4,0},{5,1},{6,2},{7,3},{8,4},{9,5},{10,6},{11,7},{12,8},{13,9},{1... | collective-permute-start | bytes 368648 | tf_op jit(solution)/shard_map/ppermute | solution.py:675
  80.1 21.4 %all-to-all-start = ((bf16[32,48,128]{2,1,0:T(8,128)(2,1)}), bf16[32,48,128]{2,1,0:T(8,128)(2,1)S(1)}, u32[]{:S(2)}, u32[]{:S(2)}) async-start(bf16[32,48,128]{2,1,0:T(8,128)(2,1)} %bitcast.6), calls=%async_computation | async-start | bytes 786432 | tf_op jit(solution)/shard_map/all_to_all | solution.py:683
  102.4 15.8 %all-to-all-start.1 = ((bf16[32,48,128]{2,1,0:T(8,128)(2,1)}), bf16[32,48,128]{2,1,0:T(8,128)(2,1)S(1)}, u32[]{:S(2)}, u32[]{:S(2)}) async-start(bf16[32,48,128]{2,1,0:T(8,128)(2,1)} %broadcast_in_dim.2), calls=%async_computation.1 | async-start | bytes 786432 | tf_op jit(solution)/shard_map/all_to_all | solution.py:691
  105.3 1.2 %copy-start.9 = (bf16[80,48,128]{2,1,0:T(8,128)(2,1)S(1)}, bf16[80,48,128]{2,1,0:T(8,128)(2,1)}, u32[]{:S(2)}) copy-start(bf16[80,48,128]{2,1,0:T(8,128)(2,1)} %copy-done.8) | copy-start | bytes 2949124

commit v12 on v11

--- a/solution.py
+++ b/solution.py
@@ -796,8 +796,6 @@
         + [((9 * C, 4 * LANES), BF16)] * 2,
         flops=8 * 10**9,
     )
-    edge_left = send(edge_high, 1, 0)
-    edge_right = send(edge_low, -1, 0)
     (joined,) = call(
         weight_kernel,
         (grid, grad_h, grad_d, hidden, early),
@@ -805,9 +803,7 @@
         [((EDGE * pairs, C, LANES), BF16), ((VOX, 3 * C), F32), ((4 * C, LANES), F32)],
         flops=12 * 10**9,
     )
-    joined, edge_left, edge_right, slots = lax.optimization_barrier(
-        (joined, edge_left, edge_right, slots)
-    )
+    joined, slots = lax.optimization_barrier((joined, slots))
     share = reduce_share(joined)
     (output,) = call(
         output_kernel,
@@ -817,7 +813,12 @@
         scalars=1,
         flops=8 * 10**9,
     )
-    share, output, slots = lax.optimization_barrier((share, output, slots))
+    output, edge_low, edge_high = lax.optimization_barrier((output, edge_low, edge_high))
+    edge_left = send(edge_high, 1, 0)
+    edge_right = send(edge_low, -1, 0)
+    share, output, slots, edge_left, edge_right = lax.optimization_barrier(
+        (share, output, slots, edge_left, edge_right)
+    )
     (input_grad,) = call(
         input_kernel,
         (slots, grad_h, edge_left, edge_right, live, fine_back),

time: 121 us -> 120 us (level)
  waiting for transfers between devices: 15.6 us -> 12.6 us
  starting transfers between devices: 37.8 us -> 39.3 us
    all_to_all x1, waiting for transfers between devices: 8.75 us -> 2.79 us  [reduce_share(): lax.all_to_all(joined.reshape(devices, share, LANES), ('gx', 'gy'), 0, 0)]
    all_to_all x1, starting transfers between devices: 2.82 us -> 5.69 us  [spread_share(): full = lax.all_to_all(copies, ('gx', 'gy'), 0, 0)]
    ppermute x10, waiting for transfers between devices: 3.94 us -> 5.76 us  [send(): return lax.ppermute(array, ('gx', 'gy'), pairs)]
  transfers between devices with their start and end apart: 12 -> 12, of which waited for: 4 -> 5; matrix products, arithmetic and copies ran while one was open for 0% -> 1% of each run, Pallas kernels for 25% -> 18%
where the time goes in v12:
time: 120 us; the launch traced here: 119 us
  Pallas kernels  60.9 us (51%)
  starting transfers between devices  39.3 us (33%)
  waiting for transfers between devices  12.6 us (10%)
  local copies, waits for them, and re-layouts  3.8 us (3%)
  between operations  1.69 us (1%)
    pallas_call x10, Pallas kernels, call(): pl.pallas_call(kernel, out_shape=tuple((jax.ShapeDtypeStruct(s, d) for s,...  60.9 us
    ppermute x10, starting transfers between devices, send(): return lax.ppermute(array, ('gx', 'gy'), pairs)  25.7 us
    all_to_all x1, starting transfers between devices, reduce_share(): lax.all_to_all(joined.reshape(devices, share, LANES), ('gx', 'gy'), 0, 0)  7.89 us
    ppermute x10, waiting for transfers between devices, send(): return lax.ppermute(array, ('gx', 'gy'), pairs)  5.76 us
    all_to_all x1, starting transfers between devices, spread_share(): full = lax.all_to_all(copies, ('gx', 'gy'), 0, 0)  5.69 us
    all_to_all x1, waiting for transfers between devices, spread_share(): full = lax.all_to_all(copies, ('gx', 'gy'), 0, 0)  4.08 us
    unnamed x20, local copies, waits for them, and re-layouts  3 us
    all_to_all x1, waiting for transfers between devices, reduce_share(): lax.all_to_all(joined.reshape(devices, share, LANES), ('gx', 'gy'), 0, 0)  2.79 us
  transfers between devices with their start and end apart: 12, of which 5 were waited for; matrix products, arithmetic and copies ran while one was open for 1% of the time, Pallas kernels for 18%

profile of v12, /device:TPU:0, one launch (start us, length us, event | category | flops | bytes accessed | tf_op | source)
XLA Modules:
  0.0 119.4 jit_solution(5118048434118486410)
XLA Ops:
  1.5 2.9 %prepare_kernel.1 = (f32[16,128]{1,0:T(8,128)}, bf16[400,384]{1,0:T(8,128)(2,1)}, bf16[400,384]{1,0:T(8,128)(2,1)}, bf16[112,512]{1,0:T(8,128)(2,1)}, bf16[112,512]{1,0:T(8,128)(2,1)}) custom-call(s32[16]{0:T(128)} %bitcast.19, s32[1]{0:T(128)} %bitcast.12.count, bf16[16,48,512]{2,1,0:T(8,128)(2,1)} %bitcast.15, bf16[16,48,512]{2,1,0:T(8,128)(2,1)} %bitcast.17), custom_call_target="tpu_custom_call" | custom-call | bytes 2424900 | tf_op jit(solution)/shard_map/prepare_kernel/pallas_call | solution.py:655
  4.4 2.4 %collective-permute-start = (bf16[112,512]{1,0:T(8,128)(2,1)}, bf16[112,512]{1,0:T(8,128)(2,1)S(1)}, u32[]{:S(2)}, u32[]{:S(2)}) collective-permute-start(bf16[112,512]{1,0:T(8,128)(2,1)} %get-tuple-element.48), channel_id=1, source_target_pairs={{0,1},{1,2},{2,3},{4,5},{5,6},{6,7},{8,9},{9,10},{10,11},{12,13},{... | collective-permute-start | bytes 344072 | tf_op jit(solution)/shard_map/ppermute | solution.py:675
  6.7 1.3 %collective-permute-start.1 = (bf16[112,512]{1,0:T(8,128)(2,1)}, bf16[112,512]{1,0:T(8,128)(2,1)S(1)}, u32[]{:S(2)}, u32[]{:S(2)}) collective-permute-start(bf16[112,512]{1,0:T(8,128)(2,1)} %get-tuple-element.49), channel_id=1, source_target_pairs={{1,0},{2,1},{3,2},{5,4},{6,5},{7,6},{9,8},{10,9},{11,10},{13,12},{... | collective-permute-start | bytes 344072 | tf_op jit(solution)/shard_map/ppermute | solution.py:675
  8.0 4.2 %collective-permute-start.2 = (bf16[400,384]{1,0:T(8,128)(2,1)}, bf16[400,384]{1,0:T(8,128)(2,1)S(1)}, u32[]{:S(2)}, u32[]{:S(2)}) collective-permute-start(bf16[400,384]{1,0:T(8,128)(2,1)} %get-tuple-element.54), channel_id=1, source_target_pairs={{0,4},{1,5},{2,6},{3,7},{4,8},{5,9},{6,10},{7,11},{8,12},{9,13},{1... | collective-permute-start | bytes 921608 | tf_op jit(solution)/shard_map/ppermute | solution.py:675
  12.3 1.3 %collective-permute-start.3 = (bf16[400,384]{1,0:T(8,128)(2,1)}, bf16[400,384]{1,0:T(8,128)(2,1)S(1)}, u32[]{:S(2)}, u32[]{:S(2)}) collective-permute-start(bf16[400,384]{1,0:T(8,128)(2,1)} %get-tuple-element.55), channel_id=1, source_target_pairs={{4,0},{5,1},{6,2},{7,3},{8,4},{9,5},{10,6},{11,7},{12,8},{13,9},{1... | collective-permute-start | bytes 921608 | tf_op jit(solution)/shard_map/ppermute | solution.py:675
  13.6 0.3 corner_kernel.1
  13.9 4.5 %collective-permute-start.4 = (bf16[64,384]{1,0:T(8,128)(2,1)S(1)}, bf16[64,384]{1,0:T(8,128)(2,1)S(1)}, u32[]{:S(2)}, u32[]{:S(2)}) collective-permute-start(bf16[64,384]{1,0:T(8,128)(2,1)S(1)} %get-tuple-element.56), channel_id=1, source_target_pairs={{0,4},{1,5},{2,6},{3,7},{4,8},{5,9},{6,10},{7,11},{8,12},{9,13},{1... | collective-permute-start | bytes 147464 | tf_op jit(solution)/shard_map/ppermute | solution.py:675
  18.5 1.3 %collective-permute-start.5 = (bf16[64,384]{1,0:T(8,128)(2,1)S(1)}, bf16[64,384]{1,0:T(8,128)(2,1)S(1)}, u32[]{:S(2)}, u32[]{:S(2)}) collective-permute-start(bf16[64,384]{1,0:T(8,128)(2,1)S(1)} %get-tuple-element.50.c_low), channel_id=1, source_target_pairs={{4,0},{5,1},{6,2},{7,3},{8,4},{9,5},{10,6},{11,7},{12,8},{13,9},{1... | collective-permute-start | bytes 147464 | tf_op jit(solution)/shard_map/ppermute | solution.py:675
  19.8 1.0 copy-done.3
  20.8 1.0 copy-done.4
  21.8 5.0 %place_kernel.1 = (bf16[144,48,128]{2,1,0:T(8,128)(2,1)S(1)}, bf16[80,48,128]{2,1,0:T(8,128)(2,1)S(1)}, f32[40,48,128]{2,1,0:T(8,128)S(1)}, bf16[144,432]{1,0:T(...) custom-call(s32[16]{0:T(128)S(1)} %bitcast.20, ...), custom_call_target="tpu_custom_call" | custom-call | flops 8000000000 | bytes 6480964 | tf_op jit(solution)/shard_map/place_kernel/pallas_call | solution.py:655
  26.8 0.5 collective-permute-done.4.c_left
  27.3 19.8 %forward_kernel.1 = (bf16[144,48,128]{2,1,0:T(8,128)(2,1)S(1)}, f32[80,48,128]{2,1,0:T(8,128)S(1)}, bf16[40,144,128]{2,1,0:T(8,128)(2,1)S(1)}, bf16[40,48,128]{2...) custom-call(bf16[144,48,128]{2,1,0:T(8,128)(2,1)S(1)} %get-tuple-ele, ...), custom_call_target="tpu_custom_call" | custom-call | flops 8000000000 | bytes 10312704 | tf_op jit(solution)/shard_map/forward_kernel/pallas_call | solution.py:655
  47.1 4.5 %collective-permute-start.6 = (bf16[5,48,128]{2,1,0:T(8,128)(2,1)S(1)}, bf16[5,48,128]{2,1,0:T(8,128)(2,1)S(1)}, u32[]{:S(2)}, u32[]{:S(2)}) collective-permute-start(bf16[5,48,128]{2,1,0:T(8,128)(2,1)S(1)} %get-tuple-element.62), channel_id=1, source_target_pairs={{0,4},{1,5},{2,6},{3,7},{4,8},{5,9},{6,10},{7,11},{8,12},{9,13},{1... | collective-permute-start | bytes 184328 | tf_op jit(solution)/shard_map/ppermute | solution.py:675
  51.6 1.3 %collective-permute-start.7 = (bf16[5,48,128]{2,1,0:T(8,128)(2,1)S(1)}, bf16[5,48,128]{2,1,0:T(8,128)(2,1)S(1)}, u32[]{:S(2)}, u32[]{:S(2)}) collective-permute-start(bf16[5,48,128]{2,1,0:T(8,128)(2,1)S(1)} %get-tuple-element.63), channel_id=1, source_target_pairs={{4,0},{5,1},{6,2},{7,3},{8,4},{9,5},{10,6},{11,7},{12,8},{13,9},{1... | collective-permute-start | bytes 184328 | tf_op jit(solution)/shard_map/ppermute | solution.py:675
  52.9 3.2 %side_kernel.1.early = bf16[768,128]{1,0:T(8,128)(2,1)S(1)} custom-call(bf16[40,48,128]{2,1,0:T(8,128)(2,1)S(1)} %get-tuple-element.70.rects, bf16[80,48,128]{2,1,0:T(8,128)(2,1)S(1)} %get-tuple-element.65.cot_grid, bf16[40,144,128]{2,1,0:T(8,128)(2,1)S(1)} %get-tuple-element.71.low_cols, bf16[40,48,128]{2,1,0:T(8,128)(2,1)S(1)} %get-tuple-element.61.grad_c), custom_call_target="tpu_custom_call" | custom-call | flops 8000000000 | bytes 3637248 | tf_op jit(solution)/shard_map/side_kernel/pallas_call | solution.py:655
  56.2 3.4 %collective-permute-done.7.from_right = bf16[5,48,128]{2,1,0:T(8,128)(2,1)S(1)} collective-permute-done((bf16[5,48,128]{2,1,0:T(8,128)(2,1)S(1)}, bf16[5,48,128]{2,1,0:T(8,128)(2,1)S(1)}, u32[]{:S(2)}, u32[]{:S(2)}) %collective-permute-start.7) | collective-permute-done | bytes 61472 | tf_op jit(solution)/shard_map/ppermute | solution.py:675
  59.7 5.9 %backward_kernel.1 = (bf16[80,48,128]{2,1,0:T(8,128)(2,1)S(1)}, bf16[40,48,128]{2,1,0:T(8,128)(2,1)S(1)}, bf16[10,48,128]{2,1,0:T(8,128)(2,1)S(1)}, bf16[10,48,128]{2,1,0:T(8,128)(2,1)S(1)}) custom-call(bf16[40,48,128]{2,1,0:T(8,128)(2,1)S(1)} %get-tuple-element.61.grad_c, bf16[5,48,128]{2,1,0:T(8,128)(2,1)S(1)} %collective-permute-done.6.from_left, ...), custom_call_target="tpu_custom_call" | custom-call | flops 8000000000 | bytes 5453312 | tf_op jit(solution)/shard_map/backward_kernel/pallas_call | solution.py:655
  65.6 8.6 %weight_kernel.1 = bf16[1536,128]{1,0:T(8,128)(2,1)} custom-call(bf16[144,48,128]{2,1,0:T(8,128)(2,1)S(1)} %get-tuple-element.60.grid, bf16[80,48,128]{2,1,0:T(8,128)(2,1)S(1)} %get-tuple-element.68.grad_h, bf16[40,48,128]{2,1,0:T(8,128)(2,1)S(1)} %get-tuple-element.69.grad_d, f32[80,48,128]{2,1,0:T(8,128)S(1)} %get-tuple-element.64.hidden, ...), custom_call_target="tpu_custom_call" | custom-call | flops 12000000000 | bytes 5799936 | tf_op jit(solution)/shard_map/weight_kernel/pallas_call | solution.py:655
  74.2 7.9 %all-to-all-start = ((bf16[32,48,128]{2,1,0:T(8,128)(2,1)}), bf16[32,48,128]{2,1,0:T(8,128)(2,1)}, u32[]{:S(2)}, u32[]{:S(2)}) async-start(bf16[32,48,128]{2,1,0:T(8,128)(2,1)} %bitcast.6), calls=%async_computation | async-start | bytes 786432 | tf_op jit(solution)/shard_map/all_to_all | solution.py:683
  82.1 1.0 copy-done.9
  83.1 4.4 %output_kernel.1 = bf16[16,48,512]{2,1,0:T(8,128)(2,1)} custom-call(s32[16]{0:T(128)S(1)} %bitcast.21, f32[80,48,128]{2,1,0:T(8,128)S(1)} %get-tuple-element.64.hidden, bf16[40,48,128]{2,1,0:T(8,128)(2,1)S(1)} %copy-done.9, f32[16,128]{1,0:T(8,128)S(1)} %get-tuple-element.66.live, bf16[96,192]{1,0:T(8,128)(2,1)S(1)} %get-tuple-element.74.up_w), custom_call_target="tpu_custom_call" | custom-call | flops 8000000000 | bytes 3289152 | tf_op jit(solution)/shard_map/output_kernel/pallas_call | solution.py:655
  87.5 3.6 %collective-permute-start.8 = (bf16[10,48,128]{2,1,0:T(8,128)(2,1)S(1)}, bf16[10,48,128]{2,1,0:T(8,128)(2,1)S(1)}, u32[]{:S(2)}, u32[]{:S(2)}) collective-permute-start(bf16[10,48,128]{2,1,0:T(8,128)(2,1)S(1)} %get-tuple-element.78), channel_id=1, source_target_pairs={{0,4},{1,5},{2,6},{3,7},{4,8},{5,9},{6,10},{7,11},{8,12},{9,13},{1... | collective-permute-start | bytes 368648 | tf_op jit(solution)/shard_map/ppermute | solution.py:675
  91.1 1.3 %collective-permute-start.9 = (bf16[10,48,128]{2,1,0:T(8,128)(2,1)S(1)}, bf16[10,48,128]{2,1,0:T(8,128)(2,1)S(1)}, u32[]{:S(2)}, u32[]{:S(2)}) collective-permute-start(bf16[10,48,128]{2,1,0:T(8,128)(2,1)S(1)} %get-tuple-element.79), channel_id=1, source_target_pairs={{4,0},{5,1},{6,2},{7,3},{8,4},{9,5},{10,6},{11,7},{12,8},{13,9},{1... | collective-permute-start | bytes 368648 | tf_op jit(solution)/shard_map/ppermute | solution.py:675
  92.4 2.8 %all-to-all-done = bf16[32,48,128]{2,1,0:T(8,128)(2,1)} async-done(((bf16[32,48,128]{2,1,0:T(8,128)(2,1)}), bf16[32,48,128]{2,1,0:T(8,128)(2,1)}, u32[]{:S(2)}, u32[]{:S(2)}) %all-to-all-start) | async-done | bytes 393248 | tf_op jit(solution)/shard_map/all_to_all | solution.py:683
  95.2 1.1 reduce_sum.12
  96.3 1.8 %collective-permute-done.9.from_right = bf16[10,48,128]{2,1,0:T(8,128)(2,1)S(1)} collective-permute-done((bf16[10,48,128]{2,1,0:T(8,128)(2,1)S(1)}, bf16[10,48,128]{2,1,0:T(8,128)(2,1)S(1)}, u32[]{:S(2)}, u32[]{:S(2)}) %collective-permute-start.9) | collective-permute-done | bytes 122912 | tf_op jit(solution)/shard_map/ppermute | solution.py:675
  98.1 0.8 broadcast_in_dim.2
  98.9 5.7 %all-to-all-start.1 = ((bf16[32,48,128]{2,1,0:T(8,128)(2,1)}), bf16[32,48,128]{2,1,0:T(8,128)(2,1)S(1)}, u32[]{:S(2)}, u32[]{:S(2)}) async-start(bf16[32,48,128]{2,1,0:T(8,128)(2,1)} %broadcast_in_dim.2), calls=%async_computation.1 | async-start | bytes 786432 | tf_op jit(solution)/shard_map/all_to_all | solution.py:691
  104.6 8.9 %input_kernel.1 = bf16[16,48,512]{2,1,0:T(8,128)(2,1)} custom-call(s32[16]{0:T(128)S(1)} %bitcast.22, bf16[80,48,128]{2,1,0:T(8,128)(2,1)S(1)} %get-tuple-element.68.grad_h, bf16[10,48,128]{2,1,0:T(8,128)(2,1)S(1)} %collective-permute-done.8.from_left, bf16[10,48,128]{2,1,0:T(8,128)(2,1)S(1)} %collective-permute-done.9.from_right, ...), custom_call_target="tpu_custom_call" | custom-call | flops 8000000000 | bytes 2147904 | tf_op jit(solution)/shard_map/input_kernel/pallas_call | solution.py:655
  113.5 4.1 %all-to-all-done.1 = bf16[32,48,128]{2,1,0:T(8,128)(2,1)S(1)} async-done(((bf16[32,48,128]{2,1,0:T(8,128)(2,1)}), bf16[32,48,128]{2,1,0:T(8,128)(2,1)S(1)}, u32[]{:S(2)}, u32[]{:S(2)}) %all-to-all-start.1) | async-done | bytes 393248 | tf_op jit(solution)/shard_map/all_to_all | solution.py:691
  117.6 1.8 %finish_kernel.1 = (f32[27,48,48]{2,1,0:T(8,128)}, f32[48,8,48]{2,1,0:T(8,128)}, f32[27,48,48]{2,1,0:T(8,128)}, f32[8,48,48]{2,1,0:T(8,128)}) custom-call(bf16[1536,128]{1,0:T(8,128)(2,1)S(1)} %bitcast.14), custom_call_target="tpu_custom_call" | custom-call | bytes 1038336 | tf_op jit(solution)/shard_map/finish_kernel/pallas_call | solution.py:655
  (24 shorter events, 0.1 us)
Async XLA Ops:
  0.6 19.2 %copy-start.1 = (bf16[1,1,16,48,512]{4,3,2,1,0:T(8,128)(2,1)S(1)}, bf16[1,1,16,48,512]{4,3,2,1,0:T(8,128)(2,1)}, u32[]{:S(2)}) copy-start(bf16[1,1,16,48,512]{4,3,2,1,0:T(8,128)(2,1)} %param.11) | copy-start | bytes 2359300
  0.6 19.2 %copy-start.2 = (s32[1,1,16]{2,1,0:T(1,128)S(1)}, s32[1,1,16]{2,1,0:T(1,128)}, u32[]{:S(2)}) copy-start(s32[1,1,16]{2,1,0:T(1,128)} %param.9) | copy-start | bytes 196
  0.7 19.2 %copy-start = (bf16[1,1,16,48,512]{4,3,2,1,0:T(8,128)(2,1)S(1)}, bf16[1,1,16,48,512]{4,3,2,1,0:T(8,128)(2,1)}, u32[]{:S(2)}) copy-start(bf16[1,1,16,48,512]{4,3,2,1,0:T(8,128)(2,1)} %param.8) | copy-start | bytes 2359300
  0.7 19.2 %copy-start.6 = (bf16[8,48,48]{2,1,0:T(8,128)(2,1)S(1)}, bf16[8,48,48]{2,1,0:T(8,128)(2,1)}, u32[]{:S(2)}) copy-start(bf16[8,48,48]{2,1,0:T(8,128)(2,1)} %up.1) | copy-start | bytes 110596
  0.7 19.2 %copy-start.5 = (bf16[48,8,48]{2,1,0:T(8,128)(2,1)S(1)}, bf16[48,8,48]{2,1,0:T(8,128)(2,1)}, u32[]{:S(2)}) copy-start(bf16[48,8,48]{2,1,0:T(8,128)(2,1)} %down.1) | copy-start | bytes 110596
  4.4 9.2 %collective-permute-start = (bf16[112,512]{1,0:T(8,128)(2,1)}, bf16[112,512]{1,0:T(8,128)(2,1)S(1)}, u32[]{:S(2)}, u32[]{:S(2)}) collective-permute-start(bf16[112,512]{1,0:T(8,128)(2,1)} %get-tuple-element.48), channel_id=1, source_target_pairs={{0,1},{1,2},{2,3},{4,5},{5,6},{6,7},{8,9},{9,10},{10,11},{12,13},{... | collective-permute-start | bytes 344072 | tf_op jit(solution)/shard_map/ppermute | solution.py:675
  6.7 6.9 %collective-permute-start.1 = (bf16[112,512]{1,0:T(8,128)(2,1)}, bf16[112,512]{1,0:T(8,128)(2,1)S(1)}, u32[]{:S(2)}, u32[]{:S(2)}) collective-permute-start(bf16[112,512]{1,0:T(8,128)(2,1)} %get-tuple-element.49), channel_id=1, source_target_pairs={{1,0},{2,1},{3,2},{5,4},{6,5},{7,6},{9,8},{10,9},{11,10},{13,12},{... | collective-permute-start | bytes 344072 | tf_op jit(solution)/shard_map/ppermute | solution.py:675
  8.0 19.3 %collective-permute-start.2 = (bf16[400,384]{1,0:T(8,128)(2,1)}, bf16[400,384]{1,0:T(8,128)(2,1)S(1)}, u32[]{:S(2)}, u32[]{:S(2)}) collective-permute-start(bf16[400,384]{1,0:T(8,128)(2,1)} %get-tuple-element.54), channel_id=1, source_target_pairs={{0,4},{1,5},{2,6},{3,7},{4,8},{5,9},{6,10},{7,11},{8,12},{9,13},{1... | collective-permute-start | bytes 921608 | tf_op jit(solution)/shard_map/ppermute | solution.py:675
  12.3 15.0 %collective-permute-start.3 = (bf16[400,384]{1,0:T(8,128)(2,1)}, bf16[400,384]{1,0:T(8,128)(2,1)S(1)}, u32[]{:S(2)}, u32[]{:S(2)}) collective-permute-start(bf16[400,384]{1,0:T(8,128)(2,1)} %get-tuple-element.55), channel_id=1, source_target_pairs={{4,0},{5,1},{6,2},{7,3},{8,4},{9,5},{10,6},{11,7},{12,8},{13,9},{1... | collective-permute-start | bytes 921608 | tf_op jit(solution)/shard_map/ppermute | solution.py:675
  13.9 13.4 %collective-permute-start.4 = (bf16[64,384]{1,0:T(8,128)(2,1)S(1)}, bf16[64,384]{1,0:T(8,128)(2,1)S(1)}, u32[]{:S(2)}, u32[]{:S(2)}) collective-permute-start(bf16[64,384]{1,0:T(8,128)(2,1)S(1)} %get-tuple-element.56), channel_id=1, source_target_pairs={{0,4},{1,5},{2,6},{3,7},{4,8},{5,9},{6,10},{7,11},{8,12},{9,13},{1... | collective-permute-start | bytes 147464 | tf_op jit(solution)/shard_map/ppermute | solution.py:675
  18.5 8.8 %collective-permute-start.5 = (bf16[64,384]{1,0:T(8,128)(2,1)S(1)}, bf16[64,384]{1,0:T(8,128)(2,1)S(1)}, u32[]{:S(2)}, u32[]{:S(2)}) collective-permute-start(bf16[64,384]{1,0:T(8,128)(2,1)S(1)} %get-tuple-element.50.c_low), channel_id=1, source_target_pairs={{4,0},{5,1},{6,2},{7,3},{8,4},{9,5},{10,6},{11,7},{12,8},{13,9},{1... | collective-permute-start | bytes 147464 | tf_op jit(solution)/shard_map/ppermute | solution.py:675
  19.8 1.0 copy-start.3
  20.8 1.0 copy-start.4
  21.8 5.5 %copy-start.7 = (f32[16,128]{1,0:T(8,128)S(1)}, f32[16,128]{1,0:T(8,128)}, u32[]{:S(2)}) copy-start(f32[16,128]{1,0:T(8,128)} %get-tuple-element.52.flags) | copy-start | bytes 24580
  47.1 9.1 %copy-start.8 = (bf16[40,48,128]{2,1,0:T(8,128)(2,1)}, bf16[40,48,128]{2,1,0:T(8,128)(2,1)S(1)}, u32[]{:S(2)}) copy-start(bf16[40,48,128]{2,1,0:T(8,128)(2,1)S(1)} %get-tuple-element.70.rects) | copy-start | bytes 1474564
  47.1 9.1 %collective-permute-start.6 = (bf16[5,48,128]{2,1,0:T(8,128)(2,1)S(1)}, bf16[5,48,128]{2,1,0:T(8,128)(2,1)S(1)}, u32[]{:S(2)}, u32[]{:S(2)}) collective-permute-start(bf16[5,48,128]{2,1,0:T(8,128)(2,1)S(1)} %get-tuple-element.62), channel_id=1, source_target_pairs={{0,4},{1,5},{2,6},{3,7},{4,8},{5,9},{6,10},{7,11},{8,12},{9,13},{1... | collective-permute-start | bytes 184328 | tf_op jit(solution)/shard_map/ppermute | solution.py:675
  51.6 8.0 %collective-permute-start.7 = (bf16[5,48,128]{2,1,0:T(8,128)(2,1)S(1)}, bf16[5,48,128]{2,1,0:T(8,128)(2,1)S(1)}, u32[]{:S(2)}, u32[]{:S(2)}) collective-permute-start(bf16[5,48,128]{2,1,0:T(8,128)(2,1)S(1)} %get-tuple-element.63), channel_id=1, source_target_pairs={{4,0},{5,1},{6,2},{7,3},{8,4},{9,5},{10,6},{11,7},{12,8},{13,9},{1... | collective-permute-start | bytes 184328 | tf_op jit(solution)/shard_map/ppermute | solution.py:675
  74.2 21.1 %all-to-all-start = ((bf16[32,48,128]{2,1,0:T(8,128)(2,1)}), bf16[32,48,128]{2,1,0:T(8,128)(2,1)}, u32[]{:S(2)}, u32[]{:S(2)}) async-start(bf16[32,48,128]{2,1,0:T(8,128)(2,1)} %bitcast.6), calls=%async_computation | async-start | bytes 786432 | tf_op jit(solution)/shard_map/all_to_all | solution.py:683
  82.1 1.0 copy-start.9
  87.5 8.8 %collective-permute-start.8 = (bf16[10,48,128]{2,1,0:T(8,128)(2,1)S(1)}, bf16[10,48,128]{2,1,0:T(8,128)(2,1)S(1)}, u32[]{:S(2)}, u32[]{:S(2)}) collective-permute-start(bf16[10,48,128]{2,1,0:T(8,128)(2,1)S(1)} %get-tuple-element.78), channel_id=1, source_target_pairs={{0,4},{1,5},{2,6},{3,7},{4,8},{5,9},{6,10},{7,11},{8,12},{9,13},{1... | collective-permute-start | bytes 368648 | tf_op jit(solution)/shard_map/ppermute | solution.py:675
  91.1 7.0 %collective-permute-start.9 = (bf16[10,48,128]{2,1,0:T(8,128)(2,1)S(1)}, bf16[10,48,128]{2,1,0:T(8,128)(2,1)S(1)}, u32[]{:S(2)}, u32[]{:S(2)}) collective-permute-start(bf16[10,48,128]{2,1,0:T(8,128)(2,1)S(1)} %get-tuple-element.79), channel_id=1, source_target_pairs={{4,0},{5,1},{6,2},{7,3},{8,4},{9,5},{10,6},{11,7},{12,8},{13,9},{1... | collective-permute-start | bytes 368648 | tf_op jit(solution)/shard_map/ppermute | solution.py:675
  98.9 18.7 %all-to-all-start.1 = ((bf16[32,48,128]{2,1,0:T(8,128)(2,1)}), bf16[32,48,128]{2,1,0:T(8,128)(2,1)S(1)}, u32[]{:S(2)}, u32[]{:S(2)}) async-start(bf16[32,48,128]{2,1,0:T(8,128)(2,1)} %broadcast_in_dim.2), calls=%async_computation.1 | async-start | bytes 786432 | tf_op jit(solution)/shard_map/all_to_all | solution.py:691

commit v13 on v12

--- a/solution.py
+++ b/solution.py
@@ -525,7 +525,7 @@
 
 def backward_kernel(
     grad_c, from_left, from_right, hidden, cot_grid, live, coarse_w, down_w,
-    grad_h, grad_d, pack_low, pack_high, coarse_p, grad_x, even, odd,
+    grad_h, grad_d, coarse_p, grad_x, even, odd,
 ):
     tiles = grad_c.shape[0]
     fill_columns(grad_c, from_left, from_right, grad_x, 2)
@@ -551,7 +551,10 @@
                 grad_h[tile] = (grad * alive).astype(BF16)
 
     loop(0, tiles // 4, step, 2)
-    pack_columns(grad_h, pack_low, pack_high, 1)
+
+
+def pack_kernel(grad_h, low, high):
+    pack_columns(grad_h, low, high, 1)
 
 
 def weight_kernel(grid, grad_h, grad_d, hidden, early, joined, grad_own, fine_g, down_g):
@@ -622,6 +625,11 @@
 
     loop(1, tiles // EDGE - 1, block_step, 2)
     to_blocks(slots, rows_out, flat, out)
+
+
+def sum_kernel(parts, copies):
+    total = jnp.sum(parts[...].astype(F32), axis=0).astype(BF16)
+    copies[...] = jnp.broadcast_to(total[None], copies.shape)
 
 
 def finish_kernel(scale, total, fine, down, coarse, up):
@@ -681,15 +689,13 @@
     share = -(-rows // devices)
     joined = jnp.pad(joined, ((0, share * devices - rows), (0, 0)))
     mine = lax.all_to_all(joined.reshape(devices, share, LANES), ("gx", "gy"), 0, 0)
-    return jnp.sum(mine.astype(F32), axis=0).astype(BF16)
-
-
-def spread_share(share):
-    devices = lax.axis_size("gx") * lax.axis_size("gy")
-    rows = share.shape[0]
-    copies = jnp.broadcast_to(share[None], (devices, rows, LANES))
+    return mine
+
+
+def spread_share(parts):
+    (copies,) = call(sum_kernel, (parts,), [(parts.shape, BF16)])
     full = lax.all_to_all(copies, ("gx", "gy"), 0, 0)
-    return full.reshape(devices * rows, LANES)
+    return full.reshape(-1, LANES)
 
 
 def on_device(
@@ -783,14 +789,12 @@
         [((4 * pairs, C, LANES), BF16), ((4 * C, LANES), F32), ((VOX, 3 * C), F32)],
         flops=8 * 10**9,
     )
-    grad_h, grad_d, edge_low, edge_high = call(
+    grad_h, grad_d = call(
         backward_kernel,
         (grad_c, grad_left, grad_right, hidden, cot_grid, live, coarse_back, down_w),
         [
             ((EDGE * pairs, C, LANES), BF16),
             ((4 * pairs, C, LANES), BF16),
-            ((fine_groups, C, LANES), BF16),
-            ((fine_groups, C, LANES), BF16),
         ],
         [((4 * pairs + 1, C, LANES), F32), ((4 * pairs, 3 * C, LANES), BF16)]
         + [((9 * C, 4 * LANES), BF16)] * 2,
@@ -803,7 +807,12 @@
         [((EDGE * pairs, C, LANES), BF16), ((VOX, 3 * C), F32), ((4 * C, LANES), F32)],
         flops=12 * 10**9,
     )
-    joined, slots = lax.optimization_barrier((joined, slots))
+    joined, slots, grad_h = lax.optimization_barrier((joined, slots, grad_h))
+    edge_low, edge_high = call(
+        pack_kernel, (grad_h,), [((fine_groups, C, LANES), BF16)] * 2, flops=10**9
+    )
+    edge_left = send(edge_high, 1, 0)
+    edge_right = send(edge_low, -1, 0)
     share = reduce_share(joined)
     (output,) = call(
         output_kernel,
@@ -813,9 +822,6 @@
         scalars=1,
         flops=8 * 10**9,
     )
-    output, edge_low, edge_high = lax.optimization_barrier((output, edge_low, edge_high))
-    edge_left = send(edge_high, 1, 0)
-    edge_right = send(edge_low, -1, 0)
     share, output, slots, edge_left, edge_right = lax.optimization_barrier(
         (share, output, slots, edge_left, edge_right)
     )

time: 120 us -> 116 us (0.967)
  waiting for transfers between devices: 12.6 us -> 10.6 us
  local copies, waits for them, and re-layouts: 3.8 us -> 1.98 us
    all_to_all x1, waiting for transfers between devices: 2.79 us -> 0.33 us  [reduce_share(): lax.all_to_all(joined.reshape(devices, share, LANES), ('gx', 'gy'), 0, 0)]
    pallas_call x10 -> x12, Pallas kernels: 60.9 us -> 61.8 us  [call(): pl.pallas_call(kernel, out_shape=tuple((jax.ShapeDtypeStruct(s, d) for s,...]
  transfers between devices with their start and end apart: 12 -> 12, of which waited for: 5 -> 5; matrix products, arithmetic and copies ran while one was open for 1% -> 0% of each run, Pallas kernels for 18% -> 20%
where the time goes in v13:
time: 116 us; the launch traced here: 115 us
  Pallas kernels  61.8 us (53%)
  starting transfers between devices  39.3 us (34%)
  waiting for transfers between devices  10.6 us (9%)
  local copies, waits for them, and re-layouts  1.98 us (2%)
  between operations  1.7 us (1%)
    pallas_call x12, Pallas kernels, call(): pl.pallas_call(kernel, out_shape=tuple((jax.ShapeDtypeStruct(s, d) for s,...  61.8 us
    ppermute x10, starting transfers between devices, send(): return lax.ppermute(array, ('gx', 'gy'), pairs)  25.7 us
    all_to_all x1, starting transfers between devices, reduce_share(): lax.all_to_all(joined.reshape(devices, share, LANES), ('gx', 'gy'), 0, 0)  7.77 us
    ppermute x10, waiting for transfers between devices, send(): return lax.ppermute(array, ('gx', 'gy'), pairs)  6.16 us
    all_to_all x1, starting transfers between devices, spread_share(): full = lax.all_to_all(copies, ('gx', 'gy'), 0, 0)  5.82 us
    all_to_all x1, waiting for transfers between devices, spread_share(): full = lax.all_to_all(copies, ('gx', 'gy'), 0, 0)  4.08 us
  transfers between devices with their start and end apart: 12, of which 5 were waited for; matrix products, arithmetic and copies ran while one was open for 0% of the time, Pallas kernels for 20%

profile of v13, /device:TPU:0, one launch (start us, length us, event | category | flops | bytes accessed | tf_op | source)
XLA Modules:
  0.0 115.4 jit_solution(5587997570023558635)
XLA Ops:
  1.5 2.9 %prepare_kernel.1 = (f32[16,128]{1,0:T(8,128)}, bf16[400,384]{1,0:T(8,128)(2,1)}, bf16[400,384]{1,0:T(8,128)(2,1)}, bf16[112,512]{1,0:T(8,128)(2,1)}, bf16[112,512]{1,0:T(8,128)(2,1)}) custom-call(s32[16]{0:T(128)} %bitcast.19, s32[1]{0:T(128)} %bitcast.12.count, bf16[16,48,512]{2,1,0:T(8,128)(2,1)} %bitcast.15, bf16[16,48,512]{2,1,0:T(8,128)(2,1)} %bitcast.17), custom_call_target="tpu_custom_call" | custom-call | bytes 2424900 | tf_op jit(solution)/shard_map/prepare_kernel/pallas_call | solution.py:663
  4.4 2.3 %collective-permute-start = (bf16[112,512]{1,0:T(8,128)(2,1)}, bf16[112,512]{1,0:T(8,128)(2,1)S(1)}, u32[]{:S(2)}, u32[]{:S(2)}) collective-permute-start(bf16[112,512]{1,0:T(8,128)(2,1)} %get-tuple-element.46), channel_id=1, source_target_pairs={{0,1},{1,2},{2,3},{4,5},{5,6},{6,7},{8,9},{9,10},{10,11},{12,13},{... | collective-permute-start | bytes 344072 | tf_op jit(solution)/shard_map/ppermute | solution.py:683
  6.7 1.3 %collective-permute-start.1 = (bf16[112,512]{1,0:T(8,128)(2,1)}, bf16[112,512]{1,0:T(8,128)(2,1)S(1)}, u32[]{:S(2)}, u32[]{:S(2)}) collective-permute-start(bf16[112,512]{1,0:T(8,128)(2,1)} %get-tuple-element.47), channel_id=1, source_target_pairs={{1,0},{2,1},{3,2},{5,4},{6,5},{7,6},{9,8},{10,9},{11,10},{13,12},{... | collective-permute-start | bytes 344072 | tf_op jit(solution)/shard_map/ppermute | solution.py:683
  8.0 4.2 %collective-permute-start.2 = (bf16[400,384]{1,0:T(8,128)(2,1)}, bf16[400,384]{1,0:T(8,128)(2,1)S(1)}, u32[]{:S(2)}, u32[]{:S(2)}) collective-permute-start(bf16[400,384]{1,0:T(8,128)(2,1)} %get-tuple-element.52), channel_id=1, source_target_pairs={{0,4},{1,5},{2,6},{3,7},{4,8},{5,9},{6,10},{7,11},{8,12},{9,13},{1... | collective-permute-start | bytes 921608 | tf_op jit(solution)/shard_map/ppermute | solution.py:683
  12.3 1.3 %collective-permute-start.3 = (bf16[400,384]{1,0:T(8,128)(2,1)}, bf16[400,384]{1,0:T(8,128)(2,1)S(1)}, u32[]{:S(2)}, u32[]{:S(2)}) collective-permute-start(bf16[400,384]{1,0:T(8,128)(2,1)} %get-tuple-element.53), channel_id=1, source_target_pairs={{4,0},{5,1},{6,2},{7,3},{8,4},{9,5},{10,6},{11,7},{12,8},{13,9},{1... | collective-permute-start | bytes 921608 | tf_op jit(solution)/shard_map/ppermute | solution.py:683
  13.6 0.3 corner_kernel.1
  13.9 4.5 %collective-permute-start.4 = (bf16[64,384]{1,0:T(8,128)(2,1)S(1)}, bf16[64,384]{1,0:T(8,128)(2,1)S(1)}, u32[]{:S(2)}, u32[]{:S(2)}) collective-permute-start(bf16[64,384]{1,0:T(8,128)(2,1)S(1)} %get-tuple-element.54), channel_id=1, source_target_pairs={{0,4},{1,5},{2,6},{3,7},{4,8},{5,9},{6,10},{7,11},{8,12},{9,13},{1... | collective-permute-start | bytes 147464 | tf_op jit(solution)/shard_map/ppermute | solution.py:683
  18.5 1.3 %collective-permute-start.5 = (bf16[64,384]{1,0:T(8,128)(2,1)S(1)}, bf16[64,384]{1,0:T(8,128)(2,1)S(1)}, u32[]{:S(2)}, u32[]{:S(2)}) collective-permute-start(bf16[64,384]{1,0:T(8,128)(2,1)S(1)} %get-tuple-element.48.c_low), channel_id=1, source_target_pairs={{4,0},{5,1},{6,2},{7,3},{8,4},{9,5},{10,6},{11,7},{12,8},{13,9},{1... | collective-permute-start | bytes 147464 | tf_op jit(solution)/shard_map/ppermute | solution.py:683
  19.8 0.0 copy-start.3
  19.8 1.0 copy-done.3
  20.8 1.0 copy-done.4
  21.8 5.0 %place_kernel.1 = (bf16[144,48,128]{2,1,0:T(8,128)(2,1)S(1)}, bf16[80,48,128]{2,1,0:T(8,128)(2,1)S(1)}, f32[40,48,128]{2,1,0:T(8,128)S(1)}, bf16[144,432]{1,0:T(...) custom-call(s32[16]{0:T(128)S(1)} %bitcast.20, ...), custom_call_target="tpu_custom_call" | custom-call | flops 8000000000 | bytes 6480964 | tf_op jit(solution)/shard_map/place_kernel/pallas_call | solution.py:663
  26.8 0.5 collective-permute-done.4.c_left
  27.3 19.8 %forward_kernel.1 = (bf16[144,48,128]{2,1,0:T(8,128)(2,1)S(1)}, f32[80,48,128]{2,1,0:T(8,128)S(1)}, bf16[40,144,128]{2,1,0:T(8,128)(2,1)S(1)}, bf16[40,48,128]{2...) custom-call(bf16[144,48,128]{2,1,0:T(8,128)(2,1)S(1)} %get-tuple-ele, ...), custom_call_target="tpu_custom_call" | custom-call | flops 8000000000 | bytes 10312704 | tf_op jit(solution)/shard_map/forward_kernel/pallas_call | solution.py:663
  47.1 4.5 %collective-permute-start.6 = (bf16[5,48,128]{2,1,0:T(8,128)(2,1)S(1)}, bf16[5,48,128]{2,1,0:T(8,128)(2,1)S(1)}, u32[]{:S(2)}, u32[]{:S(2)}) collective-permute-start(bf16[5,48,128]{2,1,0:T(8,128)(2,1)S(1)} %get-tuple-element.60), channel_id=1, source_target_pairs={{0,4},{1,5},{2,6},{3,7},{4,8},{5,9},{6,10},{7,11},{8,12},{9,13},{1... | collective-permute-start | bytes 184328 | tf_op jit(solution)/shard_map/ppermute | solution.py:683
  51.6 1.3 %collective-permute-start.7 = (bf16[5,48,128]{2,1,0:T(8,128)(2,1)S(1)}, bf16[5,48,128]{2,1,0:T(8,128)(2,1)S(1)}, u32[]{:S(2)}, u32[]{:S(2)}) collective-permute-start(bf16[5,48,128]{2,1,0:T(8,128)(2,1)S(1)} %get-tuple-element.61), channel_id=1, source_target_pairs={{4,0},{5,1},{6,2},{7,3},{8,4},{9,5},{10,6},{11,7},{12,8},{13,9},{1... | collective-permute-start | bytes 184328 | tf_op jit(solution)/shard_map/ppermute | solution.py:683
  52.9 3.3 %side_kernel.1.early = bf16[768,128]{1,0:T(8,128)(2,1)S(1)} custom-call(bf16[40,48,128]{2,1,0:T(8,128)(2,1)S(1)} %get-tuple-element.68.rects, bf16[80,48,128]{2,1,0:T(8,128)(2,1)S(1)} %get-tuple-element.63.cot_grid, bf16[40,144,128]{2,1,0:T(8,128)(2,1)S(1)} %get-tuple-element.69.low_cols, bf16[40,48,128]{2,1,0:T(8,128)(2,1)S(1)} %get-tuple-element.59.grad_c), custom_call_target="tpu_custom_call" | custom-call | flops 8000000000 | bytes 3637248 | tf_op jit(solution)/shard_map/side_kernel/pallas_call | solution.py:663
  56.2 3.4 %collective-permute-done.7.from_right = bf16[5,48,128]{2,1,0:T(8,128)(2,1)S(1)} collective-permute-done((bf16[5,48,128]{2,1,0:T(8,128)(2,1)S(1)}, bf16[5,48,128]{2,1,0:T(8,128)(2,1)S(1)}, u32[]{:S(2)}, u32[]{:S(2)}) %collective-permute-start.7) | collective-permute-done | bytes 61472 | tf_op jit(solution)/shard_map/ppermute | solution.py:683
  59.6 4.7 %backward_kernel.1 = (bf16[80,48,128]{2,1,0:T(8,128)(2,1)S(1)}, bf16[40,48,128]{2,1,0:T(8,128)(2,1)S(1)}) custom-call(bf16[40,48,128]{2,1,0:T(8,128)(2,1)S(1)} %get-tuple-element.59.grad_c, bf16[5,48,128]{2,1,0:T(8,128)(2,1)S(1)} %collective-permute-done.6.from_left, bf16[5,48,128]{2,1,0:T(8,128)(2,1)S(1)} %collective-permute-done.7.from_right, ...), custom_call_target="tpu_custom_call" | custom-call | flops 8000000000 | bytes 5207552 | tf_op jit(solution)/shard_map/backward_kernel/pallas_call | solution.py:663
  64.3 8.6 %weight_kernel.1 = bf16[1536,128]{1,0:T(8,128)(2,1)} custom-call(bf16[144,48,128]{2,1,0:T(8,128)(2,1)S(1)} %get-tuple-element.58.grid, bf16[80,48,128]{2,1,0:T(8,128)(2,1)S(1)} %get-tuple-element.73.grad_h, bf16[40,48,128]{2,1,0:T(8,128)(2,1)S(1)} %get-tuple-element.67.grad_d, f32[80,48,128]{2,1,0:T(8,128)S(1)} %get-tuple-element.62.hidden, ...), custom_call_target="tpu_custom_call" | custom-call | flops 12000000000 | bytes 5799936 | tf_op jit(solution)/shard_map/weight_kernel/pallas_call | solution.py:663
  73.0 7.8 %all-to-all-start = ((bf16[32,48,128]{2,1,0:T(8,128)(2,1)}), bf16[32,48,128]{2,1,0:T(8,128)(2,1)S(1)}, u32[]{:S(2)}, u32[]{:S(2)}) async-start(bf16[32,48,128]{2,1,0:T(8,128)(2,1)} %bitcast.6), calls=%async_computation | async-start | bytes 786432 | tf_op jit(solution)/shard_map/all_to_all | solution.py:691
  80.7 1.2 %pack_kernel.1 = (bf16[10,48,128]{2,1,0:T(8,128)(2,1)S(1)}, bf16[10,48,128]{2,1,0:T(8,128)(2,1)S(1)}) custom-call(bf16[80,48,128]{2,1,0:T(8,128)(2,1)S(1)} %get-tuple-element.73.grad_h), custom_call_target="tpu_custom_call" | custom-call | flops 1000000000 | bytes 1228800 | tf_op jit(solution)/shard_map/pack_kernel/pallas_call | solution.py:663
  81.9 3.7 %collective-permute-start.8 = (bf16[10,48,128]{2,1,0:T(8,128)(2,1)S(1)}, bf16[10,48,128]{2,1,0:T(8,128)(2,1)S(1)}, u32[]{:S(2)}, u32[]{:S(2)}) collective-permute-start(bf16[10,48,128]{2,1,0:T(8,128)(2,1)S(1)} %get-tuple-element.74), channel_id=1, source_target_pairs={{0,4},{1,5},{2,6},{3,7},{4,8},{5,9},{6,10},{7,11},{8,12},{9,13},{1... | collective-permute-start | bytes 368648 | tf_op jit(solution)/shard_map/ppermute | solution.py:683
  85.6 1.3 %collective-permute-start.9 = (bf16[10,48,128]{2,1,0:T(8,128)(2,1)S(1)}, bf16[10,48,128]{2,1,0:T(8,128)(2,1)S(1)}, u32[]{:S(2)}, u32[]{:S(2)}) collective-permute-start(bf16[10,48,128]{2,1,0:T(8,128)(2,1)S(1)} %get-tuple-element.75), channel_id=1, source_target_pairs={{4,0},{5,1},{6,2},{7,3},{8,4},{9,5},{10,6},{11,7},{12,8},{13,9},{1... | collective-permute-start | bytes 368648 | tf_op jit(solution)/shard_map/ppermute | solution.py:683
  86.9 4.4 %output_kernel.1 = bf16[16,48,512]{2,1,0:T(8,128)(2,1)} custom-call(s32[16]{0:T(128)S(1)} %bitcast.21, f32[80,48,128]{2,1,0:T(8,128)S(1)} %copy-done.9, bf16[40,48,128]{2,1,0:T(8,128)(2,1)S(1)} %get-tuple-element.68.rects, f32[16,128]{1,0:T(8,128)S(1)} %get-tuple-element.64.live, bf16[96,192]{1,0:T(8,128)(2,1)S(1)} %get-tuple-element.72.up_w), custom_call_target="tpu_custom_call" | custom-call | flops 8000000000 | bytes 3289152 | tf_op jit(solution)/shard_map/output_kernel/pallas_call | solution.py:663
  91.4 2.2 %collective-permute-done.9.from_right = bf16[10,48,128]{2,1,0:T(8,128)(2,1)S(1)} collective-permute-done((bf16[10,48,128]{2,1,0:T(8,128)(2,1)S(1)}, bf16[10,48,128]{2,1,0:T(8,128)(2,1)S(1)}, u32[]{:S(2)}, u32[]{:S(2)}) %collective-permute-start.9) | collective-permute-done | bytes 122912 | tf_op jit(solution)/shard_map/ppermute | solution.py:683
  93.6 0.3 all-to-all-done.parts
  93.9 0.8 sum_kernel.1
  94.7 5.8 %all-to-all-start.1 = ((bf16[32,48,128]{2,1,0:T(8,128)(2,1)}), bf16[32,48,128]{2,1,0:T(8,128)(2,1)S(1)}, u32[]{:S(2)}, u32[]{:S(2)}) async-start(bf16[32,48,128]{2,1,0:T(8,128)(2,1)} %sum_kernel.1), calls=%async_computation.1 | async-start | bytes 786432 | tf_op jit(solution)/shard_map/all_to_all | solution.py:697
  100.6 8.9 %input_kernel.1 = bf16[16,48,512]{2,1,0:T(8,128)(2,1)} custom-call(s32[16]{0:T(128)S(1)} %bitcast.22, bf16[80,48,128]{2,1,0:T(8,128)(2,1)S(1)} %get-tuple-element.73.grad_h, bf16[10,48,128]{2,1,0:T(8,128)(2,1)S(1)} %collective-permute-done.8.from_left, bf16[10,48,128]{2,1,0:T(8,128)(2,1)S(1)} %collective-permute-done.9.from_right, ...), custom_call_target="tpu_custom_call" | custom-call | flops 8000000000 | bytes 2147904 | tf_op jit(solution)/shard_map/input_kernel/pallas_call | solution.py:663
  109.5 4.1 %all-to-all-done.1 = bf16[32,48,128]{2,1,0:T(8,128)(2,1)S(1)} async-done(((bf16[32,48,128]{2,1,0:T(8,128)(2,1)}), bf16[32,48,128]{2,1,0:T(8,128)(2,1)S(1)}, u32[]{:S(2)}, u32[]{:S(2)}) %all-to-all-start.1) | async-done | bytes 393248 | tf_op jit(solution)/shard_map/all_to_all | solution.py:697
  113.6 1.8 %finish_kernel.1 = (f32[27,48,48]{2,1,0:T(8,128)}, f32[48,8,48]{2,1,0:T(8,128)}, f32[27,48,48]{2,1,0:T(8,128)}, f32[8,48,48]{2,1,0:T(8,128)}) custom-call(bf16[1536,128]{1,0:T(8,128)(2,1)S(1)} %bitcast.14), custom_call_target="tpu_custom_call" | custom-call | bytes 1038336 | tf_op jit(solution)/shard_map/finish_kernel/pallas_call | solution.py:663
  (24 shorter events, 0.1 us)
Async XLA Ops:
  0.6 19.2 %copy-start.1 = (bf16[1,1,16,48,512]{4,3,2,1,0:T(8,128)(2,1)S(1)}, bf16[1,1,16,48,512]{4,3,2,1,0:T(8,128)(2,1)}, u32[]{:S(2)}) copy-start(bf16[1,1,16,48,512]{4,3,2,1,0:T(8,128)(2,1)} %param.11) | copy-start | bytes 2359300
  0.6 19.2 %copy-start.2 = (s32[1,1,16]{2,1,0:T(1,128)S(1)}, s32[1,1,16]{2,1,0:T(1,128)}, u32[]{:S(2)}) copy-start(s32[1,1,16]{2,1,0:T(1,128)} %param.9) | copy-start | bytes 196
  0.7 19.2 %copy-start = (bf16[1,1,16,48,512]{4,3,2,1,0:T(8,128)(2,1)S(1)}, bf16[1,1,16,48,512]{4,3,2,1,0:T(8,128)(2,1)}, u32[]{:S(2)}) copy-start(bf16[1,1,16,48,512]{4,3,2,1,0:T(8,128)(2,1)} %param.8) | copy-start | bytes 2359300
  0.7 19.2 %copy-start.6 = (bf16[8,48,48]{2,1,0:T(8,128)(2,1)S(1)}, bf16[8,48,48]{2,1,0:T(8,128)(2,1)}, u32[]{:S(2)}) copy-start(bf16[8,48,48]{2,1,0:T(8,128)(2,1)} %up.1) | copy-start | bytes 110596
  0.7 19.2 %copy-start.5 = (bf16[48,8,48]{2,1,0:T(8,128)(2,1)S(1)}, bf16[48,8,48]{2,1,0:T(8,128)(2,1)}, u32[]{:S(2)}) copy-start(bf16[48,8,48]{2,1,0:T(8,128)(2,1)} %down.1) | copy-start | bytes 110596
  4.4 9.2 %collective-permute-start = (bf16[112,512]{1,0:T(8,128)(2,1)}, bf16[112,512]{1,0:T(8,128)(2,1)S(1)}, u32[]{:S(2)}, u32[]{:S(2)}) collective-permute-start(bf16[112,512]{1,0:T(8,128)(2,1)} %get-tuple-element.46), channel_id=1, source_target_pairs={{0,1},{1,2},{2,3},{4,5},{5,6},{6,7},{8,9},{9,10},{10,11},{12,13},{... | collective-permute-start | bytes 344072 | tf_op jit(solution)/shard_map/ppermute | solution.py:683
  6.7 6.9 %collective-permute-start.1 = (bf16[112,512]{1,0:T(8,128)(2,1)}, bf16[112,512]{1,0:T(8,128)(2,1)S(1)}, u32[]{:S(2)}, u32[]{:S(2)}) collective-permute-start(bf16[112,512]{1,0:T(8,128)(2,1)} %get-tuple-element.47), channel_id=1, source_target_pairs={{1,0},{2,1},{3,2},{5,4},{6,5},{7,6},{9,8},{10,9},{11,10},{13,12},{... | collective-permute-start | bytes 344072 | tf_op jit(solution)/shard_map/ppermute | solution.py:683
  8.0 19.3 %collective-permute-start.2 = (bf16[400,384]{1,0:T(8,128)(2,1)}, bf16[400,384]{1,0:T(8,128)(2,1)S(1)}, u32[]{:S(2)}, u32[]{:S(2)}) collective-permute-start(bf16[400,384]{1,0:T(8,128)(2,1)} %get-tuple-element.52), channel_id=1, source_target_pairs={{0,4},{1,5},{2,6},{3,7},{4,8},{5,9},{6,10},{7,11},{8,12},{9,13},{1... | collective-permute-start | bytes 921608 | tf_op jit(solution)/shard_map/ppermute | solution.py:683
  12.3 15.0 %collective-permute-start.3 = (bf16[400,384]{1,0:T(8,128)(2,1)}, bf16[400,384]{1,0:T(8,128)(2,1)S(1)}, u32[]{:S(2)}, u32[]{:S(2)}) collective-permute-start(bf16[400,384]{1,0:T(8,128)(2,1)} %get-tuple-element.53), channel_id=1, source_target_pairs={{4,0},{5,1},{6,2},{7,3},{8,4},{9,5},{10,6},{11,7},{12,8},{13,9},{1... | collective-permute-start | bytes 921608 | tf_op jit(solution)/shard_map/ppermute | solution.py:683
  13.9 13.4 %collective-permute-start.4 = (bf16[64,384]{1,0:T(8,128)(2,1)S(1)}, bf16[64,384]{1,0:T(8,128)(2,1)S(1)}, u32[]{:S(2)}, u32[]{:S(2)}) collective-permute-start(bf16[64,384]{1,0:T(8,128)(2,1)S(1)} %get-tuple-element.54), channel_id=1, source_target_pairs={{0,4},{1,5},{2,6},{3,7},{4,8},{5,9},{6,10},{7,11},{8,12},{9,13},{1... | collective-permute-start | bytes 147464 | tf_op jit(solution)/shard_map/ppermute | solution.py:683
  18.5 8.8 %collective-permute-start.5 = (bf16[64,384]{1,0:T(8,128)(2,1)S(1)}, bf16[64,384]{1,0:T(8,128)(2,1)S(1)}, u32[]{:S(2)}, u32[]{:S(2)}) collective-permute-start(bf16[64,384]{1,0:T(8,128)(2,1)S(1)} %get-tuple-element.48.c_low), channel_id=1, source_target_pairs={{4,0},{5,1},{6,2},{7,3},{8,4},{9,5},{10,6},{11,7},{12,8},{13,9},{1... | collective-permute-start | bytes 147464 | tf_op jit(solution)/shard_map/ppermute | solution.py:683
  19.8 1.0 copy-start.3
  20.8 1.0 copy-start.4
  21.8 5.5 %copy-start.7 = (f32[16,128]{1,0:T(8,128)S(1)}, f32[16,128]{1,0:T(8,128)}, u32[]{:S(2)}) copy-start(f32[16,128]{1,0:T(8,128)} %get-tuple-element.50.flags) | copy-start | bytes 24580
  47.1 17.2 %copy-start.8 = (f32[80,48,128]{2,1,0:T(8,128)}, f32[80,48,128]{2,1,0:T(8,128)S(1)}, u32[]{:S(2)}) copy-start(f32[80,48,128]{2,1,0:T(8,128)S(1)} %get-tuple-element.62.hidden) | copy-start | bytes 5898244
  47.1 9.0 %collective-permute-start.6 = (bf16[5,48,128]{2,1,0:T(8,128)(2,1)S(1)}, bf16[5,48,128]{2,1,0:T(8,128)(2,1)S(1)}, u32[]{:S(2)}, u32[]{:S(2)}) collective-permute-start(bf16[5,48,128]{2,1,0:T(8,128)(2,1)S(1)} %get-tuple-element.60), channel_id=1, source_target_pairs={{0,4},{1,5},{2,6},{3,7},{4,8},{5,9},{6,10},{7,11},{8,12},{9,13},{1... | collective-permute-start | bytes 184328 | tf_op jit(solution)/shard_map/ppermute | solution.py:683
  51.6 8.0 %collective-permute-start.7 = (bf16[5,48,128]{2,1,0:T(8,128)(2,1)S(1)}, bf16[5,48,128]{2,1,0:T(8,128)(2,1)S(1)}, u32[]{:S(2)}, u32[]{:S(2)}) collective-permute-start(bf16[5,48,128]{2,1,0:T(8,128)(2,1)S(1)} %get-tuple-element.61), channel_id=1, source_target_pairs={{4,0},{5,1},{6,2},{7,3},{8,4},{9,5},{10,6},{11,7},{12,8},{13,9},{1... | collective-permute-start | bytes 184328 | tf_op jit(solution)/shard_map/ppermute | solution.py:683
  73.0 21.0 %all-to-all-start = ((bf16[32,48,128]{2,1,0:T(8,128)(2,1)}), bf16[32,48,128]{2,1,0:T(8,128)(2,1)S(1)}, u32[]{:S(2)}, u32[]{:S(2)}) async-start(bf16[32,48,128]{2,1,0:T(8,128)(2,1)} %bitcast.6), calls=%async_computation | async-start | bytes 786432 | tf_op jit(solution)/shard_map/all_to_all | solution.py:691
  80.7 6.2 %copy-start.9 = (f32[80,48,128]{2,1,0:T(8,128)S(1)}, f32[80,48,128]{2,1,0:T(8,128)}, u32[]{:S(2)}) copy-start(f32[80,48,128]{2,1,0:T(8,128)} %copy-done.8) | copy-start | bytes 5898244
  81.9 9.4 %collective-permute-start.8 = (bf16[10,48,128]{2,1,0:T(8,128)(2,1)S(1)}, bf16[10,48,128]{2,1,0:T(8,128)(2,1)S(1)}, u32[]{:S(2)}, u32[]{:S(2)}) collective-permute-start(bf16[10,48,128]{2,1,0:T(8,128)(2,1)S(1)} %get-tuple-element.74), channel_id=1, source_target_pairs={{0,4},{1,5},{2,6},{3,7},{4,8},{5,9},{6,10},{7,11},{8,12},{9,13},{1... | collective-permute-start | bytes 368648 | tf_op jit(solution)/shard_map/ppermute | solution.py:683
  85.6 8.0 %collective-permute-start.9 = (bf16[10,48,128]{2,1,0:T(8,128)(2,1)S(1)}, bf16[10,48,128]{2,1,0:T(8,128)(2,1)S(1)}, u32[]{:S(2)}, u32[]{:S(2)}) collective-permute-start(bf16[10,48,128]{2,1,0:T(8,128)(2,1)S(1)} %get-tuple-element.75), channel_id=1, source_target_pairs={{4,0},{5,1},{6,2},{7,3},{8,4},{9,5},{10,6},{11,7},{12,8},{13,9},{1... | collective-permute-start | bytes 368648 | tf_op jit(solution)/shard_map/ppermute | solution.py:683
  94.7 18.8 %all-to-all-start.1 = ((bf16[32,48,128]{2,1,0:T(8,128)(2,1)}), bf16[32,48,128]{2,1,0:T(8,128)(2,1)S(1)}, u32[]{:S(2)}, u32[]{:S(2)}) async-start(bf16[32,48,128]{2,1,0:T(8,128)(2,1)} %sum_kernel.1), calls=%async_computation.1 | async-start | bytes 786432 | tf_op jit(solution)/shard_map/all_to_all | solution.py:697

commit v14 on v13

--- a/solution.py
+++ b/solution.py
@@ -454,12 +454,36 @@
     return jnp.concatenate(parts, axis=1)
 
 
-def flatten_weights(total, out, at):
-    turned = total[...].T.astype(BF16)
-    for group in range(4):
-        out[at + 3 * C * group : at + 3 * C * (group + 1), :] = turned[
-            :, LANES * group : LANES * (group + 1)
-        ]
+def squeeze_rows(full, keep):
+    extra = full[keep:]
+    size, part = extra.shape[0], keep // 3
+    lanes = lane_ids(size)
+    pieces = []
+    for index in range(3):
+        rows = full[part * index : part * (index + 1)]
+        pieces.append(jnp.where(lanes < 96, rows[:size], roll(extra, 96 - 32 * index)))
+        if size < part:
+            pieces.append(rows[size:])
+    return jnp.concatenate(pieces, axis=0)
+
+
+def widen_rows(packed, number):
+    keep = packed.shape[0]
+    size, part = number - keep, keep // 3
+    lanes = lane_ids(size)
+    extra = jnp.zeros((size, LANES), F32)
+    for index in range(3):
+        moved = roll(packed[part * index : part * index + size], 32 * index - 96)
+        extra = jnp.where((lanes >= 32 * index) & (lanes < 32 * index + 32), moved, extra)
+    return jnp.concatenate([packed, extra], axis=0)
+
+
+def flatten_weights(total, out):
+    turned = total[...].T
+    for group in range(3):
+        part = turned[:, LANES * group : LANES * (group + 1)]
+        out[3 * C * group : 3 * C * (group + 1), :] = part.astype(BF16)
+    return turned[:, 3 * LANES :]
 
 
 def output_kernel(slots, hidden, rects, live, up_w, out, rows_out, flat):
@@ -519,8 +543,9 @@
         )
 
     loop(0, (tiles - 4) // 4, weight_step, 3)
-    flatten_weights(coarse_g, flat, 0)
-    flat[12 * C :, :] = up_g[...].astype(BF16)
+    rest = flatten_weights(coarse_g, flat)
+    flat[9 * C : 12 * C, :] = squeeze_rows(up_g[...], 3 * C).astype(BF16)
+    flat[12 * C :, :] = roll(rest, C).astype(BF16)
 
 
 def backward_kernel(
@@ -601,9 +626,12 @@
         )
 
     loop(0, (tiles // 2 - 8) // 4, down_step, 2)
-    flatten_weights(fine_g, joined, 0)
-    joined[12 * C : 16 * C, :] = down_g[...].astype(BF16)
-    joined[16 * C :, :] = early[...]
+    rest = flatten_weights(fine_g, joined) + early[12 * C :, :].astype(F32)
+    joined[9 * C : 18 * C, :] = early[0 : 9 * C, :]
+    joined[18 * C : 21 * C, :] = squeeze_rows(down_g[...], 3 * C).astype(BF16)
+    joined[21 * C : 24 * C, :] = early[9 * C : 12 * C, :]
+    squeezed = squeeze_rows(rest, 120)
+    joined[24 * C :, :] = jnp.concatenate([squeezed, squeezed[:8]], axis=0).astype(BF16)
 
 
 def input_kernel(
@@ -633,16 +661,19 @@
 
 
 def finish_kernel(scale, total, fine, down, coarse, up):
-    for out, at in ((fine, 0), (coarse, 16 * C)):
+    rest = widen_rows(total[24 * C :, :].astype(F32)[:120], 3 * C) * scale
+    for out, at, moved in ((fine, 0, rest), (coarse, 9 * C, roll(rest, -C))):
         for along in range(3):
             first = at + C * along
-            rows = [total[first + 3 * C * g : first + 3 * C * g + C, :] for g in range(4)]
+            rows = [total[first + 3 * C * g : first + 3 * C * g + C, :] for g in range(3)]
             row = jnp.concatenate(rows, axis=1).astype(F32) * scale
+            row = jnp.concatenate([row, moved[C * along : C * (along + 1)]], axis=1)
             for index in range(9):
                 out[3 * index + along] = row[:, C * index : C * (index + 1)]
-    for out, at, turn in ((down, 12 * C, False), (up, 28 * C, True)):
+    for out, at, turn in ((down, 18 * C, False), (up, 21 * C, True)):
+        full = widen_rows(total[at : at + 3 * C, :].astype(F32), 4 * C) * scale
         for index in range(4):
-            rows = total[at + C * index : at + C * (index + 1), :].astype(F32) * scale
+            rows = full[C * index : C * (index + 1)]
             for along in range(2):
                 part = rows[:, C * along : C * (along + 1)]
                 if turn:
@@ -785,7 +816,7 @@
     (early,) = call(
         side_kernel,
         (rects, cot_grid, low_cols, grad_c),
-        [((16 * C, LANES), BF16)],
+        [((15 * C, LANES), BF16)],
         [((4 * pairs, C, LANES), BF16), ((4 * C, LANES), F32), ((VOX, 3 * C), F32)],
         flops=8 * 10**9,
     )
@@ -803,7 +834,7 @@
     (joined,) = call(
         weight_kernel,
         (grid, grad_h, grad_d, hidden, early),
-        [((32 * C, LANES), BF16)],
+        [((24 * C + 128, LANES), BF16)],
         [((EDGE * pairs, C, LANES), BF16), ((VOX, 3 * C), F32), ((4 * C, LANES), F32)],
         flops=12 * 10**9,
     )

time: 116 us -> 115 us (level)
  waiting for transfers between devices: 10.6 us -> 7.64 us
    all_to_all x1, waiting for transfers between devices: 4.08 us -> 2.02 us  [spread_share(): full = lax.all_to_all(copies, ('gx', 'gy'), 0, 0)]
    unnamed x20 -> x28, local copies, waits for them, and re-layouts: 1.98 us -> 2.9 us
  transfers between devices with their start and end apart: 12 -> 12, of which waited for: 5 -> 4; matrix products, arithmetic and copies ran while one was open for 0% -> 0% of each run, Pallas kernels for 20% -> 20%
where the time goes in v14:
time: 115 us; the launch traced here: 114 us
  Pallas kernels  61.9 us (54%)
  starting transfers between devices  39.8 us (35%)
  waiting for transfers between devices  7.64 us (7%)
  local copies, waits for them, and re-layouts  2.9 us (3%)
  between operations  1.76 us (2%)
    pallas_call x12, Pallas kernels, call(): pl.pallas_call(kernel, out_shape=tuple((jax.ShapeDtypeStruct(s, d) for s,...  61.9 us
    ppermute x10, starting transfers between devices, send(): return lax.ppermute(array, ('gx', 'gy'), pairs)  25.8 us
    all_to_all x1, starting transfers between devices, reduce_share(): lax.all_to_all(joined.reshape(devices, share, LANES), ('gx', 'gy'), 0, 0)  7.8 us
    all_to_all x1, starting transfers between devices, spread_share(): full = lax.all_to_all(copies, ('gx', 'gy'), 0, 0)  6.12 us
    ppermute x10, waiting for transfers between devices, send(): return lax.ppermute(array, ('gx', 'gy'), pairs)  5.62 us
    unnamed x28, local copies, waits for them, and re-layouts  2.9 us
  transfers between devices with their start and end apart: 12, of which 4 were waited for; matrix products, arithmetic and copies ran while one was open for 0% of the time, Pallas kernels for 20%

profile of v14, /device:TPU:0, one launch (start us, length us, event | category | flops | bytes accessed | tf_op | source)
XLA Modules:
  0.0 113.9 jit_solution(5171920187287202295)
XLA Ops:
  1.5 2.9 %prepare_kernel.1 = (f32[16,128]{1,0:T(8,128)}, bf16[400,384]{1,0:T(8,128)(2,1)}, bf16[400,384]{1,0:T(8,128)(2,1)}, bf16[112,512]{1,0:T(8,128)(2,1)}, bf16[112,512]{1,0:T(8,128)(2,1)}) custom-call(s32[16]{0:T(128)} %bitcast.19, s32[1]{0:T(128)} %bitcast.12.count, bf16[16,48,512]{2,1,0:T(8,128)(2,1)} %bitcast.15, bf16[16,48,512]{2,1,0:T(8,128)(2,1)} %bitcast.17), custom_call_target="tpu_custom_call" | custom-call | bytes 2424900 | tf_op jit(solution)/shard_map/prepare_kernel/pallas_call | solution.py:694
  4.4 2.4 %collective-permute-start = (bf16[112,512]{1,0:T(8,128)(2,1)}, bf16[112,512]{1,0:T(8,128)(2,1)S(1)}, u32[]{:S(2)}, u32[]{:S(2)}) collective-permute-start(bf16[112,512]{1,0:T(8,128)(2,1)} %get-tuple-element.46), channel_id=1, source_target_pairs={{0,1},{1,2},{2,3},{4,5},{5,6},{6,7},{8,9},{9,10},{10,11},{12,13},{... | collective-permute-start | bytes 344072 | tf_op jit(solution)/shard_map/ppermute | solution.py:714
  6.7 1.3 %collective-permute-start.1 = (bf16[112,512]{1,0:T(8,128)(2,1)}, bf16[112,512]{1,0:T(8,128)(2,1)S(1)}, u32[]{:S(2)}, u32[]{:S(2)}) collective-permute-start(bf16[112,512]{1,0:T(8,128)(2,1)} %get-tuple-element.47), channel_id=1, source_target_pairs={{1,0},{2,1},{3,2},{5,4},{6,5},{7,6},{9,8},{10,9},{11,10},{13,12},{... | collective-permute-start | bytes 344072 | tf_op jit(solution)/shard_map/ppermute | solution.py:714
  8.0 4.2 %collective-permute-start.2 = (bf16[400,384]{1,0:T(8,128)(2,1)}, bf16[400,384]{1,0:T(8,128)(2,1)S(1)}, u32[]{:S(2)}, u32[]{:S(2)}) collective-permute-start(bf16[400,384]{1,0:T(8,128)(2,1)} %get-tuple-element.52), channel_id=1, source_target_pairs={{0,4},{1,5},{2,6},{3,7},{4,8},{5,9},{6,10},{7,11},{8,12},{9,13},{1... | collective-permute-start | bytes 921608 | tf_op jit(solution)/shard_map/ppermute | solution.py:714
  12.3 1.3 %collective-permute-start.3 = (bf16[400,384]{1,0:T(8,128)(2,1)}, bf16[400,384]{1,0:T(8,128)(2,1)S(1)}, u32[]{:S(2)}, u32[]{:S(2)}) collective-permute-start(bf16[400,384]{1,0:T(8,128)(2,1)} %get-tuple-element.53), channel_id=1, source_target_pairs={{4,0},{5,1},{6,2},{7,3},{8,4},{9,5},{10,6},{11,7},{12,8},{13,9},{1... | collective-permute-start | bytes 921608 | tf_op jit(solution)/shard_map/ppermute | solution.py:714
  13.6 0.3 corner_kernel.1
  13.9 4.5 %collective-permute-start.4 = (bf16[64,384]{1,0:T(8,128)(2,1)S(1)}, bf16[64,384]{1,0:T(8,128)(2,1)S(1)}, u32[]{:S(2)}, u32[]{:S(2)}) collective-permute-start(bf16[64,384]{1,0:T(8,128)(2,1)S(1)} %get-tuple-element.54), channel_id=1, source_target_pairs={{0,4},{1,5},{2,6},{3,7},{4,8},{5,9},{6,10},{7,11},{8,12},{9,13},{1... | collective-permute-start | bytes 147464 | tf_op jit(solution)/shard_map/ppermute | solution.py:714
  18.5 1.3 %collective-permute-start.5 = (bf16[64,384]{1,0:T(8,128)(2,1)S(1)}, bf16[64,384]{1,0:T(8,128)(2,1)S(1)}, u32[]{:S(2)}, u32[]{:S(2)}) collective-permute-start(bf16[64,384]{1,0:T(8,128)(2,1)S(1)} %get-tuple-element.48.c_low), channel_id=1, source_target_pairs={{4,0},{5,1},{6,2},{7,3},{8,4},{9,5},{10,6},{11,7},{12,8},{13,9},{1... | collective-permute-start | bytes 147464 | tf_op jit(solution)/shard_map/ppermute | solution.py:714
  19.8 0.0 copy-start.3
  19.8 1.0 copy-done.3
  20.8 1.0 copy-done.4
  21.8 5.0 %place_kernel.1 = (bf16[144,48,128]{2,1,0:T(8,128)(2,1)S(1)}, bf16[80,48,128]{2,1,0:T(8,128)(2,1)S(1)}, f32[40,48,128]{2,1,0:T(8,128)S(1)}, bf16[144,432]{1,0:T(...) custom-call(s32[16]{0:T(128)S(1)} %bitcast.20, ...), custom_call_target="tpu_custom_call" | custom-call | flops 8000000000 | bytes 6480964 | tf_op jit(solution)/shard_map/place_kernel/pallas_call | solution.py:694
  26.9 0.4 collective-permute-done.4.c_left
  27.3 19.8 %forward_kernel.1 = (bf16[144,48,128]{2,1,0:T(8,128)(2,1)S(1)}, f32[80,48,128]{2,1,0:T(8,128)S(1)}, bf16[40,144,128]{2,1,0:T(8,128)(2,1)S(1)}, bf16[40,48,128]{2...) custom-call(bf16[144,48,128]{2,1,0:T(8,128)(2,1)S(1)} %get-tuple-ele, ...), custom_call_target="tpu_custom_call" | custom-call | flops 8000000000 | bytes 10312704 | tf_op jit(solution)/shard_map/forward_kernel/pallas_call | solution.py:694
  47.1 4.5 %collective-permute-start.6 = (bf16[5,48,128]{2,1,0:T(8,128)(2,1)S(1)}, bf16[5,48,128]{2,1,0:T(8,128)(2,1)S(1)}, u32[]{:S(2)}, u32[]{:S(2)}) collective-permute-start(bf16[5,48,128]{2,1,0:T(8,128)(2,1)S(1)} %get-tuple-element.60), channel_id=1, source_target_pairs={{0,4},{1,5},{2,6},{3,7},{4,8},{5,9},{6,10},{7,11},{8,12},{9,13},{1... | collective-permute-start | bytes 184328 | tf_op jit(solution)/shard_map/ppermute | solution.py:714
  51.7 1.3 %collective-permute-start.7 = (bf16[5,48,128]{2,1,0:T(8,128)(2,1)S(1)}, bf16[5,48,128]{2,1,0:T(8,128)(2,1)S(1)}, u32[]{:S(2)}, u32[]{:S(2)}) collective-permute-start(bf16[5,48,128]{2,1,0:T(8,128)(2,1)S(1)} %get-tuple-element.61), channel_id=1, source_target_pairs={{4,0},{5,1},{6,2},{7,3},{8,4},{9,5},{10,6},{11,7},{12,8},{13,9},{1... | collective-permute-start | bytes 184328 | tf_op jit(solution)/shard_map/ppermute | solution.py:714
  53.0 3.3 %side_kernel.1.early = bf16[720,128]{1,0:T(8,128)(2,1)S(1)} custom-call(bf16[40,48,128]{2,1,0:T(8,128)(2,1)S(1)} %get-tuple-element.68.rects, bf16[80,48,128]{2,1,0:T(8,128)(2,1)S(1)} %get-tuple-element.63.cot_grid, bf16[40,144,128]{2,1,0:T(8,128)(2,1)S(1)} %get-tuple-element.69.low_cols, bf16[40,48,128]{2,1,0:T(8,128)(2,1)S(1)} %get-tuple-element.59.grad_c), custom_call_target="tpu_custom_call" | custom-call | flops 8000000000 | bytes 3624960 | tf_op jit(solution)/shard_map/side_kernel/pallas_call | solution.py:694
  56.3 3.4 %collective-permute-done.7.from_right = bf16[5,48,128]{2,1,0:T(8,128)(2,1)S(1)} collective-permute-done((bf16[5,48,128]{2,1,0:T(8,128)(2,1)S(1)}, bf16[5,48,128]{2,1,0:T(8,128)(2,1)S(1)}, u32[]{:S(2)}, u32[]{:S(2)}) %collective-permute-start.7) | collective-permute-done | bytes 61472 | tf_op jit(solution)/shard_map/ppermute | solution.py:714
  59.7 4.7 %backward_kernel.1 = (bf16[80,48,128]{2,1,0:T(8,128)(2,1)S(1)}, bf16[40,48,128]{2,1,0:T(8,128)(2,1)S(1)}) custom-call(bf16[40,48,128]{2,1,0:T(8,128)(2,1)S(1)} %get-tuple-element.59.grad_c, bf16[5,48,128]{2,1,0:T(8,128)(2,1)S(1)} %collective-permute-done.6.from_left, bf16[5,48,128]{2,1,0:T(8,128)(2,1)S(1)} %collective-permute-done.7.from_right, ...), custom_call_target="tpu_custom_call" | custom-call | flops 8000000000 | bytes 5207552 | tf_op jit(solution)/shard_map/backward_kernel/pallas_call | solution.py:694
  64.4 8.7 %weight_kernel.1 = bf16[1280,128]{1,0:T(8,128)(2,1)} custom-call(bf16[144,48,128]{2,1,0:T(8,128)(2,1)S(1)} %get-tuple-element.58.grid, bf16[80,48,128]{2,1,0:T(8,128)(2,1)S(1)} %get-tuple-element.73.grad_h, bf16[40,48,128]{2,1,0:T(8,128)(2,1)S(1)} %get-tuple-element.67.grad_d, f32[80,48,128]{2,1,0:T(8,128)S(1)} %get-tuple-element.62.hidden, ...), custom_call_target="tpu_custom_call" | custom-call | flops 12000000000 | bytes 5722112 | tf_op jit(solution)/shard_map/weight_kernel/pallas_call | solution.py:694
  73.1 7.8 %all-to-all-start = ((bf16[32,40,128]{2,1,0:T(8,128)(2,1)}), bf16[32,40,128]{2,1,0:T(8,128)(2,1)S(1)}, u32[]{:S(2)}, u32[]{:S(2)}) async-start(bf16[32,40,128]{2,1,0:T(8,128)(2,1)} %bitcast.6), calls=%async_computation | async-start | bytes 655360 | tf_op jit(solution)/shard_map/all_to_all | solution.py:722
  80.9 1.2 %pack_kernel.1 = (bf16[10,48,128]{2,1,0:T(8,128)(2,1)S(1)}, bf16[10,48,128]{2,1,0:T(8,128)(2,1)S(1)}) custom-call(bf16[80,48,128]{2,1,0:T(8,128)(2,1)S(1)} %get-tuple-element.73.grad_h), custom_call_target="tpu_custom_call" | custom-call | flops 1000000000 | bytes 1228800 | tf_op jit(solution)/shard_map/pack_kernel/pallas_call | solution.py:694
  82.1 3.7 %collective-permute-start.8 = (bf16[10,48,128]{2,1,0:T(8,128)(2,1)S(1)}, bf16[10,48,128]{2,1,0:T(8,128)(2,1)S(1)}, u32[]{:S(2)}, u32[]{:S(2)}) collective-permute-start(bf16[10,48,128]{2,1,0:T(8,128)(2,1)S(1)} %get-tuple-element.74), channel_id=1, source_target_pairs={{0,4},{1,5},{2,6},{3,7},{4,8},{5,9},{6,10},{7,11},{8,12},{9,13},{1... | collective-permute-start | bytes 368648 | tf_op jit(solution)/shard_map/ppermute | solution.py:714
  85.8 1.3 %collective-permute-start.9 = (bf16[10,48,128]{2,1,0:T(8,128)(2,1)S(1)}, bf16[10,48,128]{2,1,0:T(8,128)(2,1)S(1)}, u32[]{:S(2)}, u32[]{:S(2)}) collective-permute-start(bf16[10,48,128]{2,1,0:T(8,128)(2,1)S(1)} %get-tuple-element.75), channel_id=1, source_target_pairs={{4,0},{5,1},{6,2},{7,3},{8,4},{9,5},{10,6},{11,7},{12,8},{13,9},{1... | collective-permute-start | bytes 368648 | tf_op jit(solution)/shard_map/ppermute | solution.py:714
  87.1 4.4 %output_kernel.1 = bf16[16,48,512]{2,1,0:T(8,128)(2,1)} custom-call(s32[16]{0:T(128)S(1)} %bitcast.21, f32[80,48,128]{2,1,0:T(8,128)S(1)} %get-tuple-element.62.hidden, bf16[40,48,128]{2,1,0:T(8,128)(2,1)S(1)} %copy-done.9, f32[16,128]{1,0:T(8,128)S(1)} %get-tuple-element.64.live, bf16[96,192]{1,0:T(8,128)(2,1)S(1)} %copy-done.13), custom_call_target="tpu_custom_call" | custom-call | flops 8000000000 | bytes 3289152 | tf_op jit(solution)/shard_map/output_kernel/pallas_call | solution.py:694
  91.6 1.8 %collective-permute-done.9.from_right = bf16[10,48,128]{2,1,0:T(8,128)(2,1)S(1)} collective-permute-done((bf16[10,48,128]{2,1,0:T(8,128)(2,1)S(1)}, bf16[10,48,128]{2,1,0:T(8,128)(2,1)S(1)}, u32[]{:S(2)}, u32[]{:S(2)}) %collective-permute-start.9) | collective-permute-done | bytes 122912 | tf_op jit(solution)/shard_map/ppermute | solution.py:714
  93.3 0.8 sum_kernel.1
  94.1 6.1 %all-to-all-start.1 = ((bf16[32,40,128]{2,1,0:T(8,128)(2,1)}), bf16[32,40,128]{2,1,0:T(8,128)(2,1)S(1)}, u32[]{:S(2)}, u32[]{:S(2)}) async-start(bf16[32,40,128]{2,1,0:T(8,128)(2,1)} %sum_kernel.1), calls=%async_computation.1 | async-start | bytes 655360 | tf_op jit(solution)/shard_map/all_to_all | solution.py:728
  100.3 0.9 copy-done.11
  101.2 8.9 %input_kernel.1 = bf16[16,48,512]{2,1,0:T(8,128)(2,1)} custom-call(s32[16]{0:T(128)S(1)} %bitcast.22, bf16[80,48,128]{2,1,0:T(8,128)(2,1)S(1)} %get-tuple-element.73.grad_h, bf16[10,48,128]{2,1,0:T(8,128)(2,1)S(1)} %collective-permute-done.8.from_left, bf16[10,48,128]{2,1,0:T(8,128)(2,1)S(1)} %collective-permute-done.9.from_right, ...), custom_call_target="tpu_custom_call" | custom-call | flops 8000000000 | bytes 2147904 | tf_op jit(solution)/shard_map/input_kernel/pallas_call | solution.py:694
  110.1 2.0 %all-to-all-done.1 = bf16[32,40,128]{2,1,0:T(8,128)(2,1)S(1)} async-done(((bf16[32,40,128]{2,1,0:T(8,128)(2,1)}), bf16[32,40,128]{2,1,0:T(8,128)(2,1)S(1)}, u32[]{:S(2)}, u32[]{:S(2)}) %all-to-all-start.1) | async-done | bytes 327712 | tf_op jit(solution)/shard_map/all_to_all | solution.py:728
  112.1 1.9 %finish_kernel.1 = (f32[27,48,48]{2,1,0:T(8,128)}, f32[48,8,48]{2,1,0:T(8,128)}, f32[27,48,48]{2,1,0:T(8,128)}, f32[8,48,48]{2,1,0:T(8,128)}) custom-call(bf16[1280,128]{1,0:T(8,128)(2,1)S(1)} %bitcast.14), custom_call_target="tpu_custom_call" | custom-call | bytes 972800 | tf_op jit(solution)/shard_map/finish_kernel/pallas_call | solution.py:694
  (32 shorter events, 0.1 us)
Async XLA Ops:
  0.6 19.2 %copy-start.1 = (bf16[1,1,16,48,512]{4,3,2,1,0:T(8,128)(2,1)S(1)}, bf16[1,1,16,48,512]{4,3,2,1,0:T(8,128)(2,1)}, u32[]{:S(2)}) copy-start(bf16[1,1,16,48,512]{4,3,2,1,0:T(8,128)(2,1)} %param.11) | copy-start | bytes 2359300
  0.6 19.2 %copy-start.2 = (s32[1,1,16]{2,1,0:T(1,128)S(1)}, s32[1,1,16]{2,1,0:T(1,128)}, u32[]{:S(2)}) copy-start(s32[1,1,16]{2,1,0:T(1,128)} %param.9) | copy-start | bytes 196
  0.7 19.2 %copy-start = (bf16[1,1,16,48,512]{4,3,2,1,0:T(8,128)(2,1)S(1)}, bf16[1,1,16,48,512]{4,3,2,1,0:T(8,128)(2,1)}, u32[]{:S(2)}) copy-start(bf16[1,1,16,48,512]{4,3,2,1,0:T(8,128)(2,1)} %param.8) | copy-start | bytes 2359300
  0.7 19.2 %copy-start.6 = (bf16[8,48,48]{2,1,0:T(8,128)(2,1)S(1)}, bf16[8,48,48]{2,1,0:T(8,128)(2,1)}, u32[]{:S(2)}) copy-start(bf16[8,48,48]{2,1,0:T(8,128)(2,1)} %up.1) | copy-start | bytes 110596
  0.7 19.2 %copy-start.5 = (bf16[48,8,48]{2,1,0:T(8,128)(2,1)S(1)}, bf16[48,8,48]{2,1,0:T(8,128)(2,1)}, u32[]{:S(2)}) copy-start(bf16[48,8,48]{2,1,0:T(8,128)(2,1)} %down.1) | copy-start | bytes 110596
  4.4 9.2 %collective-permute-start = (bf16[112,512]{1,0:T(8,128)(2,1)}, bf16[112,512]{1,0:T(8,128)(2,1)S(1)}, u32[]{:S(2)}, u32[]{:S(2)}) collective-permute-start(bf16[112,512]{1,0:T(8,128)(2,1)} %get-tuple-element.46), channel_id=1, source_target_pairs={{0,1},{1,2},{2,3},{4,5},{5,6},{6,7},{8,9},{9,10},{10,11},{12,13},{... | collective-permute-start | bytes 344072 | tf_op jit(solution)/shard_map/ppermute | solution.py:714
  6.7 6.9 %collective-permute-start.1 = (bf16[112,512]{1,0:T(8,128)(2,1)}, bf16[112,512]{1,0:T(8,128)(2,1)S(1)}, u32[]{:S(2)}, u32[]{:S(2)}) collective-permute-start(bf16[112,512]{1,0:T(8,128)(2,1)} %get-tuple-element.47), channel_id=1, source_target_pairs={{1,0},{2,1},{3,2},{5,4},{6,5},{7,6},{9,8},{10,9},{11,10},{13,12},{... | collective-permute-start | bytes 344072 | tf_op jit(solution)/shard_map/ppermute | solution.py:714
  8.0 19.3 %collective-permute-start.2 = (bf16[400,384]{1,0:T(8,128)(2,1)}, bf16[400,384]{1,0:T(8,128)(2,1)S(1)}, u32[]{:S(2)}, u32[]{:S(2)}) collective-permute-start(bf16[400,384]{1,0:T(8,128)(2,1)} %get-tuple-element.52), channel_id=1, source_target_pairs={{0,4},{1,5},{2,6},{3,7},{4,8},{5,9},{6,10},{7,11},{8,12},{9,13},{1... | collective-permute-start | bytes 921608 | tf_op jit(solution)/shard_map/ppermute | solution.py:714
  12.3 15.0 %collective-permute-start.3 = (bf16[400,384]{1,0:T(8,128)(2,1)}, bf16[400,384]{1,0:T(8,128)(2,1)S(1)}, u32[]{:S(2)}, u32[]{:S(2)}) collective-permute-start(bf16[400,384]{1,0:T(8,128)(2,1)} %get-tuple-element.53), channel_id=1, source_target_pairs={{4,0},{5,1},{6,2},{7,3},{8,4},{9,5},{10,6},{11,7},{12,8},{13,9},{1... | collective-permute-start | bytes 921608 | tf_op jit(solution)/shard_map/ppermute | solution.py:714
  13.9 13.4 %collective-permute-start.4 = (bf16[64,384]{1,0:T(8,128)(2,1)S(1)}, bf16[64,384]{1,0:T(8,128)(2,1)S(1)}, u32[]{:S(2)}, u32[]{:S(2)}) collective-permute-start(bf16[64,384]{1,0:T(8,128)(2,1)S(1)} %get-tuple-element.54), channel_id=1, source_target_pairs={{0,4},{1,5},{2,6},{3,7},{4,8},{5,9},{6,10},{7,11},{8,12},{9,13},{1... | collective-permute-start | bytes 147464 | tf_op jit(solution)/shard_map/ppermute | solution.py:714
  18.5 8.8 %collective-permute-start.5 = (bf16[64,384]{1,0:T(8,128)(2,1)S(1)}, bf16[64,384]{1,0:T(8,128)(2,1)S(1)}, u32[]{:S(2)}, u32[]{:S(2)}) collective-permute-start(bf16[64,384]{1,0:T(8,128)(2,1)S(1)} %get-tuple-element.48.c_low), channel_id=1, source_target_pairs={{4,0},{5,1},{6,2},{7,3},{8,4},{9,5},{10,6},{11,7},{12,8},{13,9},{1... | collective-permute-start | bytes 147464 | tf_op jit(solution)/shard_map/ppermute | solution.py:714
  19.8 1.0 copy-start.3
  20.8 1.0 copy-start.4
  21.8 5.5 %copy-start.7 = (f32[16,128]{1,0:T(8,128)S(1)}, f32[16,128]{1,0:T(8,128)}, u32[]{:S(2)}) copy-start(f32[16,128]{1,0:T(8,128)} %get-tuple-element.50.flags) | copy-start | bytes 24580
  26.8 20.3 %copy-start.10 = (bf16[144,432]{1,0:T(8,128)(2,1)}, bf16[144,432]{1,0:T(8,128)(2,1)S(1)}, u32[]{:S(2)}) copy-start(bf16[144,432]{1,0:T(8,128)(2,1)S(1)} %get-tuple-element.80.fine_w) | copy-start | bytes 373252
  26.8 20.3 %copy-start.12 = (bf16[96,192]{1,0:T(8,128)(2,1)}, bf16[96,192]{1,0:T(8,128)(2,1)S(1)}, u32[]{:S(2)}) copy-start(bf16[96,192]{1,0:T(8,128)(2,1)S(1)} %get-tuple-element.72.up_w) | copy-start | bytes 110596
  47.1 9.2 %copy-start.8 = (bf16[40,48,128]{2,1,0:T(8,128)(2,1)}, bf16[40,48,128]{2,1,0:T(8,128)(2,1)S(1)}, u32[]{:S(2)}) copy-start(bf16[40,48,128]{2,1,0:T(8,128)(2,1)S(1)} %get-tuple-element.68.rects) | copy-start | bytes 1474564
  47.1 9.2 %collective-permute-start.6 = (bf16[5,48,128]{2,1,0:T(8,128)(2,1)S(1)}, bf16[5,48,128]{2,1,0:T(8,128)(2,1)S(1)}, u32[]{:S(2)}, u32[]{:S(2)}) collective-permute-start(bf16[5,48,128]{2,1,0:T(8,128)(2,1)S(1)} %get-tuple-element.60), channel_id=1, source_target_pairs={{0,4},{1,5},{2,6},{3,7},{4,8},{5,9},{6,10},{7,11},{8,12},{9,13},{1... | collective-permute-start | bytes 184328 | tf_op jit(solution)/shard_map/ppermute | solution.py:714
  51.7 8.0 %collective-permute-start.7 = (bf16[5,48,128]{2,1,0:T(8,128)(2,1)S(1)}, bf16[5,48,128]{2,1,0:T(8,128)(2,1)S(1)}, u32[]{:S(2)}, u32[]{:S(2)}) collective-permute-start(bf16[5,48,128]{2,1,0:T(8,128)(2,1)S(1)} %get-tuple-element.61), channel_id=1, source_target_pairs={{4,0},{5,1},{6,2},{7,3},{8,4},{9,5},{10,6},{11,7},{12,8},{13,9},{1... | collective-permute-start | bytes 184328 | tf_op jit(solution)/shard_map/ppermute | solution.py:714
  73.1 20.2 %all-to-all-start = ((bf16[32,40,128]{2,1,0:T(8,128)(2,1)}), bf16[32,40,128]{2,1,0:T(8,128)(2,1)S(1)}, u32[]{:S(2)}, u32[]{:S(2)}) async-start(bf16[32,40,128]{2,1,0:T(8,128)(2,1)} %bitcast.6), calls=%async_computation | async-start | bytes 655360 | tf_op jit(solution)/shard_map/all_to_all | solution.py:722
  80.9 6.2 %copy-start.9 = (bf16[40,48,128]{2,1,0:T(8,128)(2,1)S(1)}, bf16[40,48,128]{2,1,0:T(8,128)(2,1)}, u32[]{:S(2)}) copy-start(bf16[40,48,128]{2,1,0:T(8,128)(2,1)} %copy-done.8) | copy-start | bytes 1474564
  80.9 6.2 %copy-start.13 = (bf16[96,192]{1,0:T(8,128)(2,1)S(1)}, bf16[96,192]{1,0:T(8,128)(2,1)}, u32[]{:S(2)}) copy-start(bf16[96,192]{1,0:T(8,128)(2,1)} %copy-done.12) | copy-start | bytes 110596
  82.1 9.4 %collective-permute-start.8 = (bf16[10,48,128]{2,1,0:T(8,128)(2,1)S(1)}, bf16[10,48,128]{2,1,0:T(8,128)(2,1)S(1)}, u32[]{:S(2)}, u32[]{:S(2)}) collective-permute-start(bf16[10,48,128]{2,1,0:T(8,128)(2,1)S(1)} %get-tuple-element.74), channel_id=1, source_target_pairs={{0,4},{1,5},{2,6},{3,7},{4,8},{5,9},{6,10},{7,11},{8,12},{9,13},{1... | collective-permute-start | bytes 368648 | tf_op jit(solution)/shard_map/ppermute | solution.py:714
  85.8 7.5 %collective-permute-start.9 = (bf16[10,48,128]{2,1,0:T(8,128)(2,1)S(1)}, bf16[10,48,128]{2,1,0:T(8,128)(2,1)S(1)}, u32[]{:S(2)}, u32[]{:S(2)}) collective-permute-start(bf16[10,48,128]{2,1,0:T(8,128)(2,1)S(1)} %get-tuple-element.75), channel_id=1, source_target_pairs={{4,0},{5,1},{6,2},{7,3},{8,4},{9,5},{10,6},{11,7},{12,8},{13,9},{1... | collective-permute-start | bytes 368648 | tf_op jit(solution)/shard_map/ppermute | solution.py:714
  94.1 17.9 %all-to-all-start.1 = ((bf16[32,40,128]{2,1,0:T(8,128)(2,1)}), bf16[32,40,128]{2,1,0:T(8,128)(2,1)S(1)}, u32[]{:S(2)}, u32[]{:S(2)}) async-start(bf16[32,40,128]{2,1,0:T(8,128)(2,1)} %sum_kernel.1), calls=%async_computation.1 | async-start | bytes 655360 | tf_op jit(solution)/shard_map/all_to_all | solution.py:728
  100.3 0.9 copy-start.11

commit v15 on v14

--- a/solution.py
+++ b/solution.py
@@ -98,19 +98,18 @@
     return jnp.concatenate([left, tile, right], axis=0)
 
 
-def fill_columns(tiles, from_left, from_right, out, step):
+def beside_halo(tiles, from_left, from_right, step):
     masks = edge_masks(step)
 
-    def body(group):
-        packed_left, packed_right = from_left[group], from_right[group]
-        for place in range(8):
-            tile = tiles[8 * group + place]
-            left = roll(packed_left, -place) * masks[0] + roll(tile, step) * masks[1]
-            right = roll(packed_right, 8 - step - place) * masks[2]
-            right = right + roll(tile, -step) * masks[3]
-            out[8 * group + place] = jnp.concatenate([left, tile, right], axis=0)
-
-    loop(0, from_left.shape[0], body)
+    def load(index, place):
+        group = lax.div(index, 8)
+        tile = tiles[index]
+        left = roll(from_left[group], -place) * masks[0] + roll(tile, step) * masks[1]
+        right = roll(from_right[group], 8 - step - place) * masks[2]
+        right = right + roll(tile, -step) * masks[3]
+        return jnp.concatenate([left, tile, right], axis=0)
+
+    return load
 
 
 def pack_columns(tiles, low, high, step):
@@ -314,9 +313,9 @@
 def conv_steps(sums, weight, load, tiles, step, first, even, odd):
     masks = depth_masks(step, first)
 
-    def fill(buffer, tile):
+    def fill(buffer, tile, place):
         for i in range(4):
-            cols = depth_columns(load(tile + i), masks, step)
+            cols = depth_columns(load(tile + i, place + i), masks, step)
             buffer[:, LANES * i : LANES * (i + 1)] = cols
 
     def multiply(buffer, tile, carry):
@@ -332,14 +331,14 @@
         sums[tile + 4] = part(0, 2) + part(1, 3)
         return part(0, 3)
 
-    fill(even, 0)
+    fill(even, 0, 0)
     sums[0] = jnp.zeros((C, LANES), F32)
 
     def body(index, carry):
         tile = 8 * index
-        fill(odd, tile + 4)
+        fill(odd, tile + 4, 4)
         carry = multiply(even, tile, carry)
-        fill(even, jnp.minimum(tile + 8, tiles - 4))
+        fill(even, jnp.minimum(tile + 8, tiles - 4), 0)
         return multiply(odd, tile + 4, carry)
 
     lax.fori_loop(0, tiles // 8, body, jnp.zeros((C, LANES), F32))
@@ -386,7 +385,7 @@
                 grid[tile] = grid_own[tile] + halo
     live[...] = join_halves(live_all[0:16, :], live_all[8:24, :])
     tiles = grid.shape[0]
-    conv_steps(fine_p, fine_w, lambda tile: across_columns(grid[tile], 1), tiles, 16, 0, even, odd)
+    conv_steps(fine_p, fine_w, lambda tile, _: across_columns(grid[tile], 1), tiles, 16, 0, even, odd)
     anchors = anchor_mask(0)
 
     def lower_step(block):
@@ -422,7 +421,7 @@
             low_cols[tile] = pair_columns(*pair_tiles(lower, upper, halves), edges, 2)
 
     loop(0, pairs, pair_step, 2)
-    conv_steps(coarse_p, coarse_w, lambda tile: low_cols[tile], 4 * pairs, 32, 4, even, odd)
+    conv_steps(coarse_p, coarse_w, lambda tile, _: low_cols[tile], 4 * pairs, 32, 4, even, odd)
     pair_anchors = anchor_mask(4)
 
     def grad_step(block):
@@ -438,8 +437,8 @@
     pack_columns(grad_c, pack_low, pack_high, 2)
 
 
-def to_blocks(slots, rows_out, flat, out):
-    flat[...] = dot(rows_out[...], marks(1024, 1024, pair_source, plain)).astype(BF16)
+def to_blocks(slots, rows_out, back, flat, out):
+    flat[...] = dot(rows_out[...], back[...]).astype(BF16)
     number = out.shape[0]
     for slot in range(number):
         place = slots[slot]
@@ -486,7 +485,8 @@
     return turned[:, 3 * LANES :]
 
 
-def output_kernel(slots, hidden, rects, live, up_w, out, rows_out, flat):
+def output_kernel(slots, hidden, rects, live, up_w, out, back, rows_out, flat):
+    back[...] = marks(1024, 1024, pair_source, plain)
     pairs = hidden.shape[0] // EDGE
 
     def block_step(block):
@@ -502,7 +502,7 @@
                 rows_out[pl.ds(start, C), at : at + LANES] = (value * alive).astype(BF16)
 
     loop(1, pairs - 1, block_step, 2)
-    to_blocks(slots, rows_out, flat, out)
+    to_blocks(slots, rows_out, back, flat, out)
 
 
 def side_kernel(rects, cot_grid, low_cols, grad_c, flat, grad_own, up_g, coarse_g):
@@ -550,11 +550,11 @@
 
 def backward_kernel(
     grad_c, from_left, from_right, hidden, cot_grid, live, coarse_w, down_w,
-    grad_h, grad_d, coarse_p, grad_x, even, odd,
+    grad_h, grad_d, coarse_p, even, odd,
 ):
     tiles = grad_c.shape[0]
-    fill_columns(grad_c, from_left, from_right, grad_x, 2)
-    conv_steps(coarse_p, coarse_w, lambda tile: grad_x[tile], tiles, 32, 4, even, odd)
+    load = beside_halo(grad_c, from_left, from_right, 2)
+    conv_steps(coarse_p, coarse_w, load, tiles, 32, 4, even, odd)
     anchors = anchor_mask(4)
 
     def step(block):
@@ -601,7 +601,7 @@
     halves = own_masks()
 
     def fine_step(index):
-        at = [4 + 8 * index + inner for inner in range(8)]
+        at = [4 + 12 * index + inner for inner in range(12)]
         rights = []
         for tile in at:
             lower, upper = grid[tile], grid[tile + shift]
@@ -611,7 +611,7 @@
             jnp.concatenate(rights, axis=1), stacks(grad_own, at), (1, 1)
         )
 
-    loop(0, (tiles - 8) // 8, fine_step)
+    loop(0, (tiles - 8) // 12, fine_step)
 
     def down_step(index):
         lefts = []
@@ -635,12 +635,12 @@
 
 
 def input_kernel(
-    slots, grad_h, from_left, from_right, live, fine_w, out,
-    fine_p, rows_out, flat, grad_x, even, odd,
+    slots, grad_h, from_left, from_right, live, fine_w, back, out,
+    fine_p, rows_out, flat, even, odd,
 ):
     tiles = grad_h.shape[0]
-    fill_columns(grad_h, from_left, from_right, grad_x, 1)
-    conv_steps(fine_p, fine_w, lambda tile: grad_x[tile], tiles, 16, 4, even, odd)
+    load = beside_halo(grad_h, from_left, from_right, 1)
+    conv_steps(fine_p, fine_w, load, tiles, 16, 4, even, odd)
 
     def block_step(block):
         alive = jnp.broadcast_to(live[pl.ds(block, 1), :], (C, LANES))
@@ -652,7 +652,7 @@
             ).astype(BF16)
 
     loop(1, tiles // EDGE - 1, block_step, 2)
-    to_blocks(slots, rows_out, flat, out)
+    to_blocks(slots, rows_out, back, flat, out)
 
 
 def sum_kernel(parts, copies):
@@ -827,7 +827,7 @@
             ((EDGE * pairs, C, LANES), BF16),
             ((4 * pairs, C, LANES), BF16),
         ],
-        [((4 * pairs + 1, C, LANES), F32), ((4 * pairs, 3 * C, LANES), BF16)]
+        [((4 * pairs + 1, C, LANES), F32)]
         + [((9 * C, 4 * LANES), BF16)] * 2,
         flops=8 * 10**9,
     )
@@ -845,26 +845,23 @@
     edge_left = send(edge_high, 1, 0)
     edge_right = send(edge_low, -1, 0)
     share = reduce_share(joined)
-    (output,) = call(
+    output, back = call(
         output_kernel,
         (slots, hidden, rects, live, up_w),
-        [((number, C, VOX), BF16)],
+        [((number, C, VOX), BF16), ((1024, 1024), BF16)],
         [((number // 2 * C, 1024), BF16), ((number // 2 * C, 1024), BF16)],
         scalars=1,
         flops=8 * 10**9,
     )
-    share, output, slots, edge_left, edge_right = lax.optimization_barrier(
-        (share, output, slots, edge_left, edge_right)
-    )
+    share, output, slots = lax.optimization_barrier((share, output, slots))
     (input_grad,) = call(
         input_kernel,
-        (slots, grad_h, edge_left, edge_right, live, fine_back),
+        (slots, grad_h, edge_left, edge_right, live, fine_back, back),
         [((number, C, VOX), BF16)],
         [
             ((EDGE * pairs + 1, C, LANES), F32),
             ((number // 2 * C, 1024), BF16),
             ((number // 2 * C, 1024), BF16),
-            ((EDGE * pairs, 3 * C, LANES), BF16),
         ]
         + [((9 * C, 4 * LANES), BF16)] * 2,
         scalars=1,

time: 115 us -> 115 us (level)
  waiting for transfers between devices: 7.64 us -> 5.4 us
  local copies, waits for them, and re-layouts: 2.9 us -> 4.92 us
    unnamed x28 -> x24, local copies, waits for them, and re-layouts: 2.9 us -> 4.92 us
    ppermute x10, waiting for transfers between devices: 5.62 us -> 3.86 us  [send(): return lax.ppermute(array, ('gx', 'gy'), pairs)]
  transfers between devices with their start and end apart: 12 -> 12, of which waited for: 4 -> 3; matrix products, arithmetic and copies ran while one was open for 0% -> 0% of each run, Pallas kernels for 20% -> 21%
where the time goes in v15:
time: 115 us; the launch traced here: 114 us
  Pallas kernels  61.8 us (54%)
  starting transfers between devices  40.4 us (35%)
  waiting for transfers between devices  5.4 us (5%)
  local copies, waits for them, and re-layouts  4.92 us (4%)
  between operations  1.72 us (1%)
    pallas_call x12, Pallas kernels, call(): pl.pallas_call(kernel, out_shape=tuple((jax.ShapeDtypeStruct(s, d) for s,...  61.8 us
    ppermute x10, starting transfers between devices, send(): return lax.ppermute(array, ('gx', 'gy'), pairs)  25.9 us
    all_to_all x1, starting transfers between devices, reduce_share(): lax.all_to_all(joined.reshape(devices, share, LANES), ('gx', 'gy'), 0, 0)  7.79 us
    all_to_all x1, starting transfers between devices, spread_share(): full = lax.all_to_all(copies, ('gx', 'gy'), 0, 0)  6.71 us
    unnamed x24, local copies, waits for them, and re-layouts  4.92 us
    ppermute x10, waiting for transfers between devices, send(): return lax.ppermute(array, ('gx', 'gy'), pairs)  3.86 us
  transfers between devices with their start and end apart: 12, of which 3 were waited for; matrix products, arithmetic and copies ran while one was open for 0% of the time, Pallas kernels for 21%

profile of v15, /device:TPU:0, one launch (start us, length us, event | category | flops | bytes accessed | tf_op | source)
XLA Modules:
  0.0 114.3 jit_solution(2819819873041273340)
XLA Ops:
  1.5 2.9 %prepare_kernel.1 = (f32[16,128]{1,0:T(8,128)}, bf16[400,384]{1,0:T(8,128)(2,1)}, bf16[400,384]{1,0:T(8,128)(2,1)}, bf16[112,512]{1,0:T(8,128)(2,1)}, bf16[112,512]{1,0:T(8,128)(2,1)}) custom-call(s32[16]{0:T(128)} %bitcast.19, s32[1]{0:T(128)} %bitcast.12.count, bf16[16,48,512]{2,1,0:T(8,128)(2,1)} %bitcast.15, bf16[16,48,512]{2,1,0:T(8,128)(2,1)} %bitcast.17), custom_call_target="tpu_custom_call" | custom-call | bytes 2424900 | tf_op jit(solution)/shard_map/prepare_kernel/pallas_call | solution.py:694
  4.4 2.3 %collective-permute-start = (bf16[112,512]{1,0:T(8,128)(2,1)}, bf16[112,512]{1,0:T(8,128)(2,1)S(1)}, u32[]{:S(2)}, u32[]{:S(2)}) collective-permute-start(bf16[112,512]{1,0:T(8,128)(2,1)} %get-tuple-element.46), channel_id=1, source_target_pairs={{0,1},{1,2},{2,3},{4,5},{5,6},{6,7},{8,9},{9,10},{10,11},{12,13},{... | collective-permute-start | bytes 344072 | tf_op jit(solution)/shard_map/ppermute | solution.py:714
  6.7 1.3 %collective-permute-start.1 = (bf16[112,512]{1,0:T(8,128)(2,1)}, bf16[112,512]{1,0:T(8,128)(2,1)S(1)}, u32[]{:S(2)}, u32[]{:S(2)}) collective-permute-start(bf16[112,512]{1,0:T(8,128)(2,1)} %get-tuple-element.47), channel_id=1, source_target_pairs={{1,0},{2,1},{3,2},{5,4},{6,5},{7,6},{9,8},{10,9},{11,10},{13,12},{... | collective-permute-start | bytes 344072 | tf_op jit(solution)/shard_map/ppermute | solution.py:714
  8.0 4.2 %collective-permute-start.2 = (bf16[400,384]{1,0:T(8,128)(2,1)}, bf16[400,384]{1,0:T(8,128)(2,1)S(1)}, u32[]{:S(2)}, u32[]{:S(2)}) collective-permute-start(bf16[400,384]{1,0:T(8,128)(2,1)} %get-tuple-element.52), channel_id=1, source_target_pairs={{0,4},{1,5},{2,6},{3,7},{4,8},{5,9},{6,10},{7,11},{8,12},{9,13},{1... | collective-permute-start | bytes 921608 | tf_op jit(solution)/shard_map/ppermute | solution.py:714
  12.3 1.3 %collective-permute-start.3 = (bf16[400,384]{1,0:T(8,128)(2,1)}, bf16[400,384]{1,0:T(8,128)(2,1)S(1)}, u32[]{:S(2)}, u32[]{:S(2)}) collective-permute-start(bf16[400,384]{1,0:T(8,128)(2,1)} %get-tuple-element.53), channel_id=1, source_target_pairs={{4,0},{5,1},{6,2},{7,3},{8,4},{9,5},{10,6},{11,7},{12,8},{13,9},{1... | collective-permute-start | bytes 921608 | tf_op jit(solution)/shard_map/ppermute | solution.py:714
  13.6 0.3 corner_kernel.1
  13.9 4.5 %collective-permute-start.4 = (bf16[64,384]{1,0:T(8,128)(2,1)S(1)}, bf16[64,384]{1,0:T(8,128)(2,1)S(1)}, u32[]{:S(2)}, u32[]{:S(2)}) collective-permute-start(bf16[64,384]{1,0:T(8,128)(2,1)S(1)} %get-tuple-element.54), channel_id=1, source_target_pairs={{0,4},{1,5},{2,6},{3,7},{4,8},{5,9},{6,10},{7,11},{8,12},{9,13},{1... | collective-permute-start | bytes 147464 | tf_op jit(solution)/shard_map/ppermute | solution.py:714
  18.5 1.3 %collective-permute-start.5 = (bf16[64,384]{1,0:T(8,128)(2,1)S(1)}, bf16[64,384]{1,0:T(8,128)(2,1)S(1)}, u32[]{:S(2)}, u32[]{:S(2)}) collective-permute-start(bf16[64,384]{1,0:T(8,128)(2,1)S(1)} %get-tuple-element.48.c_low), channel_id=1, source_target_pairs={{4,0},{5,1},{6,2},{7,3},{8,4},{9,5},{10,6},{11,7},{12,8},{13,9},{1... | collective-permute-start | bytes 147464 | tf_op jit(solution)/shard_map/ppermute | solution.py:714
  19.8 0.0 copy-start.3
  19.8 1.0 copy-done.3
  20.8 1.0 copy-done.4
  21.8 5.0 %place_kernel.1 = (bf16[144,48,128]{2,1,0:T(8,128)(2,1)S(1)}, bf16[80,48,128]{2,1,0:T(8,128)(2,1)S(1)}, f32[40,48,128]{2,1,0:T(8,128)S(1)}, bf16[144,432]{1,0:T(...) custom-call(s32[16]{0:T(128)S(1)} %bitcast.20, ...), custom_call_target="tpu_custom_call" | custom-call | flops 8000000000 | bytes 6480964 | tf_op jit(solution)/shard_map/place_kernel/pallas_call | solution.py:694
  26.8 0.5 collective-permute-done.4.c_left
  27.3 19.8 %forward_kernel.1 = (bf16[144,48,128]{2,1,0:T(8,128)(2,1)S(1)}, f32[80,48,128]{2,1,0:T(8,128)S(1)}, bf16[40,144,128]{2,1,0:T(8,128)(2,1)S(1)}, bf16[40,48,128]{2...) custom-call(bf16[144,48,128]{2,1,0:T(8,128)(2,1)S(1)} %get-tuple-ele, ...), custom_call_target="tpu_custom_call" | custom-call | flops 8000000000 | bytes 10312704 | tf_op jit(solution)/shard_map/forward_kernel/pallas_call | solution.py:694
  47.1 4.5 %collective-permute-start.6 = (bf16[5,48,128]{2,1,0:T(8,128)(2,1)S(1)}, bf16[5,48,128]{2,1,0:T(8,128)(2,1)S(1)}, u32[]{:S(2)}, u32[]{:S(2)}) collective-permute-start(bf16[5,48,128]{2,1,0:T(8,128)(2,1)S(1)} %get-tuple-element.60), channel_id=1, source_target_pairs={{0,4},{1,5},{2,6},{3,7},{4,8},{5,9},{6,10},{7,11},{8,12},{9,13},{1... | collective-permute-start | bytes 184328 | tf_op jit(solution)/shard_map/ppermute | solution.py:714
  51.6 1.3 %collective-permute-start.7 = (bf16[5,48,128]{2,1,0:T(8,128)(2,1)S(1)}, bf16[5,48,128]{2,1,0:T(8,128)(2,1)S(1)}, u32[]{:S(2)}, u32[]{:S(2)}) collective-permute-start(bf16[5,48,128]{2,1,0:T(8,128)(2,1)S(1)} %get-tuple-element.61), channel_id=1, source_target_pairs={{4,0},{5,1},{6,2},{7,3},{8,4},{9,5},{10,6},{11,7},{12,8},{13,9},{1... | collective-permute-start | bytes 184328 | tf_op jit(solution)/shard_map/ppermute | solution.py:714
  52.9 3.3 %side_kernel.1.early = bf16[720,128]{1,0:T(8,128)(2,1)S(1)} custom-call(bf16[40,48,128]{2,1,0:T(8,128)(2,1)S(1)} %get-tuple-element.68.rects, bf16[80,48,128]{2,1,0:T(8,128)(2,1)S(1)} %get-tuple-element.63.cot_grid, bf16[40,144,128]{2,1,0:T(8,128)(2,1)S(1)} %get-tuple-element.69.low_cols, bf16[40,48,128]{2,1,0:T(8,128)(2,1)S(1)} %get-tuple-element.59.grad_c), custom_call_target="tpu_custom_call" | custom-call | flops 8000000000 | bytes 3624960 | tf_op jit(solution)/shard_map/side_kernel/pallas_call | solution.py:694
  56.2 3.4 %collective-permute-done.7.from_right = bf16[5,48,128]{2,1,0:T(8,128)(2,1)S(1)} collective-permute-done((bf16[5,48,128]{2,1,0:T(8,128)(2,1)S(1)}, bf16[5,48,128]{2,1,0:T(8,128)(2,1)S(1)}, u32[]{:S(2)}, u32[]{:S(2)}) %collective-permute-start.7) | collective-permute-done | bytes 61472 | tf_op jit(solution)/shard_map/ppermute | solution.py:714
  59.6 5.1 %backward_kernel.1 = (bf16[80,48,128]{2,1,0:T(8,128)(2,1)S(1)}, bf16[40,48,128]{2,1,0:T(8,128)(2,1)S(1)}) custom-call(bf16[40,48,128]{2,1,0:T(8,128)(2,1)S(1)} %get-tuple-element.59.grad_c, bf16[5,48,128]{2,1,0:T(8,128)(2,1)S(1)} %collective-permute-done.6.from_left, bf16[5,48,128]{2,1,0:T(8,128)(2,1)S(1)} %collective-permute-done.7.from_right, ...), custom_call_target="tpu_custom_call" | custom-call | flops 8000000000 | bytes 5207552 | tf_op jit(solution)/shard_map/backward_kernel/pallas_call | solution.py:694
  64.7 7.9 %weight_kernel.1 = bf16[1280,128]{1,0:T(8,128)(2,1)} custom-call(bf16[144,48,128]{2,1,0:T(8,128)(2,1)S(1)} %get-tuple-element.58.grid, bf16[80,48,128]{2,1,0:T(8,128)(2,1)S(1)} %get-tuple-element.76.grad_h, bf16[40,48,128]{2,1,0:T(8,128)(2,1)S(1)} %get-tuple-element.67.grad_d, f32[80,48,128]{2,1,0:T(8,128)S(1)} %get-tuple-element.62.hidden, ...), custom_call_target="tpu_custom_call" | custom-call | flops 12000000000 | bytes 5722112 | tf_op jit(solution)/shard_map/weight_kernel/pallas_call | solution.py:694
  72.6 7.8 %all-to-all-start = ((bf16[32,40,128]{2,1,0:T(8,128)(2,1)}), bf16[32,40,128]{2,1,0:T(8,128)(2,1)S(1)}, u32[]{:S(2)}, u32[]{:S(2)}) async-start(bf16[32,40,128]{2,1,0:T(8,128)(2,1)} %bitcast.6), calls=%async_computation | async-start | bytes 655360 | tf_op jit(solution)/shard_map/all_to_all | solution.py:722
  80.4 1.2 %pack_kernel.1 = (bf16[10,48,128]{2,1,0:T(8,128)(2,1)S(1)}, bf16[10,48,128]{2,1,0:T(8,128)(2,1)S(1)}) custom-call(bf16[80,48,128]{2,1,0:T(8,128)(2,1)S(1)} %get-tuple-element.76.grad_h), custom_call_target="tpu_custom_call" | custom-call | flops 1000000000 | bytes 1228800 | tf_op jit(solution)/shard_map/pack_kernel/pallas_call | solution.py:694
  81.6 3.7 %collective-permute-start.8 = (bf16[10,48,128]{2,1,0:T(8,128)(2,1)S(1)}, bf16[10,48,128]{2,1,0:T(8,128)(2,1)S(1)}, u32[]{:S(2)}, u32[]{:S(2)}) collective-permute-start(bf16[10,48,128]{2,1,0:T(8,128)(2,1)S(1)} %get-tuple-element.77), channel_id=1, source_target_pairs={{0,4},{1,5},{2,6},{3,7},{4,8},{5,9},{6,10},{7,11},{8,12},{9,13},{1... | collective-permute-start | bytes 368648 | tf_op jit(solution)/shard_map/ppermute | solution.py:714
  85.3 1.5 %collective-permute-start.9 = (bf16[10,48,128]{2,1,0:T(8,128)(2,1)S(1)}, bf16[10,48,128]{2,1,0:T(8,128)(2,1)S(1)}, u32[]{:S(2)}, u32[]{:S(2)}) collective-permute-start(bf16[10,48,128]{2,1,0:T(8,128)(2,1)S(1)} %get-tuple-element.78), channel_id=1, source_target_pairs={{4,0},{5,1},{6,2},{7,3},{8,4},{9,5},{10,6},{11,7},{12,8},{13,9},{1... | collective-permute-start | bytes 368648 | tf_op jit(solution)/shard_map/ppermute | solution.py:714
  86.8 4.8 %output_kernel.1 = (bf16[16,48,512]{2,1,0:T(8,128)(2,1)}, bf16[1024,1024]{1,0:T(8,128)(2,1)S(1)}) custom-call(s32[16]{0:T(128)S(1)} %bitcast.21, f32[80,48,128]{2,1,0:T(8,128)S(1)} %copy-done.11, bf16[40,48,128]{2,1,0:T(8,128)(2,1)S(1)} %get-tuple-element.68.rects, f32[16,128]{1,0:T(8,128)S(1)} %get-tuple-element.64.live, ...), custom_call_target="tpu_custom_call" | custom-call | flops 8000000000 | bytes 5386304 | tf_op jit(solution)/shard_map/output_kernel/pallas_call | solution.py:694
  91.6 1.4 %copy-done.8 = bf16[1024,1024]{1,0:T(8,128)(2,1)} copy-done((bf16[1024,1024]{1,0:T(8,128)(2,1)}, bf16[1024,1024]{1,0:T(8,128)(2,1)S(1)}, u32[]{:S(2)}) %copy-start.8) | copy-done | bytes 2097176
  92.9 0.8 sum_kernel.1
  93.7 6.7 %all-to-all-start.1 = ((bf16[32,40,128]{2,1,0:T(8,128)(2,1)}), bf16[32,40,128]{2,1,0:T(8,128)(2,1)S(1)}, u32[]{:S(2)}, u32[]{:S(2)}) async-start(bf16[32,40,128]{2,1,0:T(8,128)(2,1)} %sum_kernel.1), calls=%async_computation.1 | async-start | bytes 655360 | tf_op jit(solution)/shard_map/all_to_all | solution.py:728
  100.5 1.6 %copy-done.9 = bf16[1024,1024]{1,0:T(8,128)(2,1)S(1)} copy-done((bf16[1024,1024]{1,0:T(8,128)(2,1)S(1)}, bf16[1024,1024]{1,0:T(8,128)(2,1)}, u32[]{:S(2)}) %copy-start.9) | copy-done | bytes 2097176
  102.0 8.8 %input_kernel.1 = bf16[16,48,512]{2,1,0:T(8,128)(2,1)} custom-call(s32[16]{0:T(128)S(1)} %bitcast.22, bf16[80,48,128]{2,1,0:T(8,128)(2,1)S(1)} %get-tuple-element.76.grad_h, bf16[10,48,128]{2,1,0:T(8,128)(2,1)S(1)} %collective-permute-done.8.from_left, bf16[10,48,128]{2,1,0:T(8,128)(2,1)S(1)} %collective-permute-done.9.from_right, ...), custom_call_target="tpu_custom_call" | custom-call | flops 8000000000 | bytes 4245056 | tf_op jit(solution)/shard_map/input_kernel/pallas_call | solution.py:694
  110.9 1.5 %all-to-all-done.1 = bf16[32,40,128]{2,1,0:T(8,128)(2,1)S(1)} async-done(((bf16[32,40,128]{2,1,0:T(8,128)(2,1)}), bf16[32,40,128]{2,1,0:T(8,128)(2,1)S(1)}, u32[]{:S(2)}, u32[]{:S(2)}) %all-to-all-start.1) | async-done | bytes 327712 | tf_op jit(solution)/shard_map/all_to_all | solution.py:728
  112.4 1.9 %finish_kernel.1 = (f32[27,48,48]{2,1,0:T(8,128)}, f32[48,8,48]{2,1,0:T(8,128)}, f32[27,48,48]{2,1,0:T(8,128)}, f32[8,48,48]{2,1,0:T(8,128)}) custom-call(bf16[1280,128]{1,0:T(8,128)(2,1)S(1)} %bitcast.14), custom_call_target="tpu_custom_call" | custom-call | bytes 972800 | tf_op jit(solution)/shard_map/finish_kernel/pallas_call | solution.py:694
  (28 shorter events, 0.1 us)
Async XLA Ops:
  0.6 19.2 %copy-start.1 = (bf16[1,1,16,48,512]{4,3,2,1,0:T(8,128)(2,1)S(1)}, bf16[1,1,16,48,512]{4,3,2,1,0:T(8,128)(2,1)}, u32[]{:S(2)}) copy-start(bf16[1,1,16,48,512]{4,3,2,1,0:T(8,128)(2,1)} %param.11) | copy-start | bytes 2359300
  0.6 19.2 %copy-start.2 = (s32[1,1,16]{2,1,0:T(1,128)S(1)}, s32[1,1,16]{2,1,0:T(1,128)}, u32[]{:S(2)}) copy-start(s32[1,1,16]{2,1,0:T(1,128)} %param.9) | copy-start | bytes 196
  0.7 19.2 %copy-start = (bf16[1,1,16,48,512]{4,3,2,1,0:T(8,128)(2,1)S(1)}, bf16[1,1,16,48,512]{4,3,2,1,0:T(8,128)(2,1)}, u32[]{:S(2)}) copy-start(bf16[1,1,16,48,512]{4,3,2,1,0:T(8,128)(2,1)} %param.8) | copy-start | bytes 2359300
  0.7 19.2 %copy-start.6 = (bf16[8,48,48]{2,1,0:T(8,128)(2,1)S(1)}, bf16[8,48,48]{2,1,0:T(8,128)(2,1)}, u32[]{:S(2)}) copy-start(bf16[8,48,48]{2,1,0:T(8,128)(2,1)} %up.1) | copy-start | bytes 110596
  0.7 19.2 %copy-start.5 = (bf16[48,8,48]{2,1,0:T(8,128)(2,1)S(1)}, bf16[48,8,48]{2,1,0:T(8,128)(2,1)}, u32[]{:S(2)}) copy-start(bf16[48,8,48]{2,1,0:T(8,128)(2,1)} %down.1) | copy-start | bytes 110596
  4.4 9.2 %collective-permute-start = (bf16[112,512]{1,0:T(8,128)(2,1)}, bf16[112,512]{1,0:T(8,128)(2,1)S(1)}, u32[]{:S(2)}, u32[]{:S(2)}) collective-permute-start(bf16[112,512]{1,0:T(8,128)(2,1)} %get-tuple-element.46), channel_id=1, source_target_pairs={{0,1},{1,2},{2,3},{4,5},{5,6},{6,7},{8,9},{9,10},{10,11},{12,13},{... | collective-permute-start | bytes 344072 | tf_op jit(solution)/shard_map/ppermute | solution.py:714
  6.7 6.9 %collective-permute-start.1 = (bf16[112,512]{1,0:T(8,128)(2,1)}, bf16[112,512]{1,0:T(8,128)(2,1)S(1)}, u32[]{:S(2)}, u32[]{:S(2)}) collective-permute-start(bf16[112,512]{1,0:T(8,128)(2,1)} %get-tuple-element.47), channel_id=1, source_target_pairs={{1,0},{2,1},{3,2},{5,4},{6,5},{7,6},{9,8},{10,9},{11,10},{13,12},{... | collective-permute-start | bytes 344072 | tf_op jit(solution)/shard_map/ppermute | solution.py:714
  8.0 19.3 %collective-permute-start.2 = (bf16[400,384]{1,0:T(8,128)(2,1)}, bf16[400,384]{1,0:T(8,128)(2,1)S(1)}, u32[]{:S(2)}, u32[]{:S(2)}) collective-permute-start(bf16[400,384]{1,0:T(8,128)(2,1)} %get-tuple-element.52), channel_id=1, source_target_pairs={{0,4},{1,5},{2,6},{3,7},{4,8},{5,9},{6,10},{7,11},{8,12},{9,13},{1... | collective-permute-start | bytes 921608 | tf_op jit(solution)/shard_map/ppermute | solution.py:714
  12.3 15.0 %collective-permute-start.3 = (bf16[400,384]{1,0:T(8,128)(2,1)}, bf16[400,384]{1,0:T(8,128)(2,1)S(1)}, u32[]{:S(2)}, u32[]{:S(2)}) collective-permute-start(bf16[400,384]{1,0:T(8,128)(2,1)} %get-tuple-element.53), channel_id=1, source_target_pairs={{4,0},{5,1},{6,2},{7,3},{8,4},{9,5},{10,6},{11,7},{12,8},{13,9},{1... | collective-permute-start | bytes 921608 | tf_op jit(solution)/shard_map/ppermute | solution.py:714
  13.9 13.4 %collective-permute-start.4 = (bf16[64,384]{1,0:T(8,128)(2,1)S(1)}, bf16[64,384]{1,0:T(8,128)(2,1)S(1)}, u32[]{:S(2)}, u32[]{:S(2)}) collective-permute-start(bf16[64,384]{1,0:T(8,128)(2,1)S(1)} %get-tuple-element.54), channel_id=1, source_target_pairs={{0,4},{1,5},{2,6},{3,7},{4,8},{5,9},{6,10},{7,11},{8,12},{9,13},{1... | collective-permute-start | bytes 147464 | tf_op jit(solution)/shard_map/ppermute | solution.py:714
  18.5 8.8 %collective-permute-start.5 = (bf16[64,384]{1,0:T(8,128)(2,1)S(1)}, bf16[64,384]{1,0:T(8,128)(2,1)S(1)}, u32[]{:S(2)}, u32[]{:S(2)}) collective-permute-start(bf16[64,384]{1,0:T(8,128)(2,1)S(1)} %get-tuple-element.48.c_low), channel_id=1, source_target_pairs={{4,0},{5,1},{6,2},{7,3},{8,4},{9,5},{10,6},{11,7},{12,8},{13,9},{1... | collective-permute-start | bytes 147464 | tf_op jit(solution)/shard_map/ppermute | solution.py:714
  19.8 1.0 copy-start.3
  20.8 1.0 copy-start.4
  21.8 5.5 %copy-start.7 = (f32[16,128]{1,0:T(8,128)S(1)}, f32[16,128]{1,0:T(8,128)}, u32[]{:S(2)}) copy-start(f32[16,128]{1,0:T(8,128)} %get-tuple-element.50.flags) | copy-start | bytes 24580
  47.1 17.6 %copy-start.10 = (f32[80,48,128]{2,1,0:T(8,128)}, f32[80,48,128]{2,1,0:T(8,128)S(1)}, u32[]{:S(2)}) copy-start(f32[80,48,128]{2,1,0:T(8,128)S(1)} %get-tuple-element.62.hidden) | copy-start | bytes 5898244
  47.1 9.1 %collective-permute-start.6 = (bf16[5,48,128]{2,1,0:T(8,128)(2,1)S(1)}, bf16[5,48,128]{2,1,0:T(8,128)(2,1)S(1)}, u32[]{:S(2)}, u32[]{:S(2)}) collective-permute-start(bf16[5,48,128]{2,1,0:T(8,128)(2,1)S(1)} %get-tuple-element.60), channel_id=1, source_target_pairs={{0,4},{1,5},{2,6},{3,7},{4,8},{5,9},{6,10},{7,11},{8,12},{9,13},{1... | collective-permute-start | bytes 184328 | tf_op jit(solution)/shard_map/ppermute | solution.py:714
  51.6 8.0 %collective-permute-start.7 = (bf16[5,48,128]{2,1,0:T(8,128)(2,1)S(1)}, bf16[5,48,128]{2,1,0:T(8,128)(2,1)S(1)}, u32[]{:S(2)}, u32[]{:S(2)}) collective-permute-start(bf16[5,48,128]{2,1,0:T(8,128)(2,1)S(1)} %get-tuple-element.61), channel_id=1, source_target_pairs={{4,0},{5,1},{6,2},{7,3},{8,4},{9,5},{10,6},{11,7},{12,8},{13,9},{1... | collective-permute-start | bytes 184328 | tf_op jit(solution)/shard_map/ppermute | solution.py:714
  72.6 20.3 %all-to-all-start = ((bf16[32,40,128]{2,1,0:T(8,128)(2,1)}), bf16[32,40,128]{2,1,0:T(8,128)(2,1)S(1)}, u32[]{:S(2)}, u32[]{:S(2)}) async-start(bf16[32,40,128]{2,1,0:T(8,128)(2,1)} %bitcast.6), calls=%async_computation | async-start | bytes 655360 | tf_op jit(solution)/shard_map/all_to_all | solution.py:722
  80.4 6.4 %copy-start.11 = (f32[80,48,128]{2,1,0:T(8,128)S(1)}, f32[80,48,128]{2,1,0:T(8,128)}, u32[]{:S(2)}) copy-start(f32[80,48,128]{2,1,0:T(8,128)} %copy-done.10) | copy-start | bytes 5898244
  81.6 18.8 %collective-permute-start.8 = (bf16[10,48,128]{2,1,0:T(8,128)(2,1)S(1)}, bf16[10,48,128]{2,1,0:T(8,128)(2,1)S(1)}, u32[]{:S(2)}, u32[]{:S(2)}) collective-permute-start(bf16[10,48,128]{2,1,0:T(8,128)(2,1)S(1)} %get-tuple-element.77), channel_id=1, source_target_pairs={{0,4},{1,5},{2,6},{3,7},{4,8},{5,9},{6,10},{7,11},{8,12},{9,13},{1... | collective-permute-start | bytes 368648 | tf_op jit(solution)/shard_map/ppermute | solution.py:714
  85.3 15.1 %collective-permute-start.9 = (bf16[10,48,128]{2,1,0:T(8,128)(2,1)S(1)}, bf16[10,48,128]{2,1,0:T(8,128)(2,1)S(1)}, u32[]{:S(2)}, u32[]{:S(2)}) collective-permute-start(bf16[10,48,128]{2,1,0:T(8,128)(2,1)S(1)} %get-tuple-element.78), channel_id=1, source_target_pairs={{4,0},{5,1},{6,2},{7,3},{8,4},{9,5},{10,6},{11,7},{12,8},{13,9},{1... | collective-permute-start | bytes 368648 | tf_op jit(solution)/shard_map/ppermute | solution.py:714
  91.6 1.4 %copy-start.8 = (bf16[1024,1024]{1,0:T(8,128)(2,1)}, bf16[1024,1024]{1,0:T(8,128)(2,1)S(1)}, u32[]{:S(2)}) copy-start(bf16[1024,1024]{1,0:T(8,128)(2,1)S(1)} %get-tuple-element.80.back) | copy-start | bytes 6291460
  93.7 18.7 %all-to-all-start.1 = ((bf16[32,40,128]{2,1,0:T(8,128)(2,1)}), bf16[32,40,128]{2,1,0:T(8,128)(2,1)S(1)}, u32[]{:S(2)}, u32[]{:S(2)}) async-start(bf16[32,40,128]{2,1,0:T(8,128)(2,1)} %sum_kernel.1), calls=%async_computation.1 | async-start | bytes 655360 | tf_op jit(solution)/shard_map/all_to_all | solution.py:728
  100.4 1.6 %copy-start.9 = (bf16[1024,1024]{1,0:T(8,128)(2,1)S(1)}, bf16[1024,1024]{1,0:T(8,128)(2,1)}, u32[]{:S(2)}) copy-start(bf16[1024,1024]{1,0:T(8,128)(2,1)} %copy-done.8) | copy-start | bytes 6291460

commit v16 on v14

--- a/solution.py
+++ b/solution.py
@@ -308,7 +308,7 @@
         for inner in range(4):
             grad_r[4 * block + inner] = gather_sub(parts[:, LANES * inner : LANES * (inner + 1)])
 
-    loop(0, pairs, rect_step, 2)
+    loop(0, pairs, rect_step, 5)
 
 
 def conv_steps(sums, weight, load, tiles, step, first, even, odd):
@@ -406,7 +406,7 @@
             total = gather_sub(parts[:, LANES * inner : LANES * (inner + 1)])
             lowered[4 * block + inner] = (total * keep).astype(BF16)
 
-    loop(0, last + 1, lower_step, 2)
+    loop(0, last + 1, lower_step, 3)
     pairs = hidden.shape[0] // EDGE
     shift = last - pairs + 1
     edges = edge_masks(2)
@@ -421,7 +421,7 @@
             lower, upper = lowered[tile], lowered[tile + 4 * shift]
             low_cols[tile] = pair_columns(*pair_tiles(lower, upper, halves), edges, 2)
 
-    loop(0, pairs, pair_step, 2)
+    loop(0, pairs, pair_step, 5)
     conv_steps(coarse_p, coarse_w, lambda tile: low_cols[tile], 4 * pairs, 32, 4, even, odd)
     pair_anchors = anchor_mask(4)
 
@@ -434,7 +434,7 @@
             rects[coarse] = (smooth * pair_anchors).astype(BF16)
             grad_c[coarse] = (grad_r[coarse] * slope * keep).astype(BF16)
 
-    loop(0, pairs, grad_step, 2)
+    loop(0, pairs, grad_step, 5)
     pack_columns(grad_c, pack_low, pack_high, 2)
 
 
@@ -513,8 +513,8 @@
     def up_step(block):
         spreads = []
         pairs = []
-        for inner in range(4):
-            coarse = 4 * block + inner
+        for inner in range(8):
+            coarse = 4 + 8 * block + inner
             spreads.append(spread_sub(rects[coarse]))
             pairs.append(
                 jnp.concatenate([cot_grid[2 * coarse], cot_grid[2 * coarse + 1]], axis=0)
@@ -523,7 +523,7 @@
             jnp.concatenate(spreads, axis=1), jnp.concatenate(pairs, axis=1), (1, 1)
         )
 
-    loop(1, tiles // 4 - 1, up_step, 2)
+    loop(0, (tiles - 8) // 8, up_step, 2)
     zero = jnp.zeros((C, LANES), BF16)
     for coarse in range(1, 4):
         grad_own[coarse] = zero
@@ -536,13 +536,13 @@
     masks = depth_masks(32, 4)
 
     def weight_step(index):
-        at = [2 + 4 * index + inner for inner in range(4)]
+        at = [2 + 12 * index + inner for inner in range(12)]
         rights = [depth_columns(low_cols[tile], masks, 32) for tile in at]
         coarse_g[0 : 9 * C, :] += dot(
             jnp.concatenate(rights, axis=1), stacks(grad_own, at), (1, 1)
         )
 
-    loop(0, (tiles - 4) // 4, weight_step, 3)
+    loop(0, (tiles - 4) // 12, weight_step)
     rest = flatten_weights(coarse_g, flat)
     flat[9 * C : 12 * C, :] = squeeze_rows(up_g[...], 3 * C).astype(BF16)
     flat[12 * C :, :] = roll(rest, C).astype(BF16)
@@ -575,7 +575,7 @@
                 grad = cot_grid[tile].astype(F32) + part * slope
                 grad_h[tile] = (grad * alive).astype(BF16)
 
-    loop(0, tiles // 4, step, 2)
+    loop(0, tiles // 4, step, 5)
 
 
 def pack_kernel(grad_h, low, high):
@@ -601,7 +601,7 @@
     halves = own_masks()
 
     def fine_step(index):
-        at = [4 + 8 * index + inner for inner in range(8)]
+        at = [4 + 18 * index + inner for inner in range(18)]
         rights = []
         for tile in at:
             lower, upper = grid[tile], grid[tile + shift]
@@ -611,13 +611,13 @@
             jnp.concatenate(rights, axis=1), stacks(grad_own, at), (1, 1)
         )
 
-    loop(0, (tiles - 8) // 8, fine_step)
+    loop(0, (tiles - 8) // 18, fine_step)
 
     def down_step(index):
         lefts = []
         rights = []
-        for inner in range(4):
-            coarse = 4 + 4 * index + inner
+        for inner in range(8):
+            coarse = 4 + 8 * index + inner
             lefts.append(spread_sub(grad_d[coarse]))
             actives = [silu_parts(hidden[2 * coarse + side])[0].astype(BF16) for side in range(2)]
             rights.append(jnp.concatenate(actives, axis=0))
@@ -625,7 +625,7 @@
             jnp.concatenate(lefts, axis=1), jnp.concatenate(rights, axis=1), (1, 1)
         )
 
-    loop(0, (tiles // 2 - 8) // 4, down_step, 2)
+    loop(0, (tiles // 2 - 8) // 8, down_step, 2)
     rest = flatten_weights(fine_g, joined) + early[12 * C :, :].astype(F32)
     joined[9 * C : 18 * C, :] = early[0 : 9 * C, :]
     joined[18 * C : 21 * C, :] = squeeze_rows(down_g[...], 3 * C).astype(BF16)
@@ -853,9 +853,7 @@
         scalars=1,
         flops=8 * 10**9,
     )
-    share, output, slots, edge_left, edge_right = lax.optimization_barrier(
-        (share, output, slots, edge_left, edge_right)
-    )
+    share, output, slots = lax.optimization_barrier((share, output, slots))
     (input_grad,) = call(
         input_kernel,
         (slots, grad_h, edge_left, edge_right, live, fine_back),

time: 115 us -> 110 us (0.957)
  Pallas kernels: 61.9 us -> 57.6 us
  waiting for transfers between devices: 7.64 us -> 9.51 us
  starting transfers between devices: 39.8 us -> 38.4 us
    pallas_call x12, Pallas kernels: 61.9 us -> 57.6 us  [call(): pl.pallas_call(kernel, out_shape=tuple((jax.ShapeDtypeStruct(s, d) for s,...]
    all_to_all x1, waiting for transfers between devices: 0.01 us -> 1.19 us  [reduce_share(): lax.all_to_all(joined.reshape(devices, share, LANES), ('gx', 'gy'), 0, 0)]
    unnamed x28 -> x20, local copies, waits for them, and re-layouts: 2.9 us -> 1.98 us
  transfers between devices with their start and end apart: 12 -> 12, of which waited for: 4 -> 4; matrix products, arithmetic and copies ran while one was open for 0% -> 0% of each run, Pallas kernels for 20% -> 21%
where the time goes in v16:
time: 110 us; the launch traced here: 109 us
  Pallas kernels  57.6 us (52%)
  starting transfers between devices  38.4 us (35%)
  waiting for transfers between devices  9.51 us (9%)
  local copies, waits for them, and re-layouts  1.98 us (2%)
  between operations  1.71 us (2%)
    pallas_call x12, Pallas kernels, call(): pl.pallas_call(kernel, out_shape=tuple((jax.ShapeDtypeStruct(s, d) for s,...  57.6 us
    ppermute x10, starting transfers between devices, send(): return lax.ppermute(array, ('gx', 'gy'), pairs)  25.9 us
    all_to_all x1, starting transfers between devices, reduce_share(): lax.all_to_all(joined.reshape(devices, share, LANES), ('gx', 'gy'), 0, 0)  7 us
    all_to_all x1, starting transfers between devices, spread_share(): full = lax.all_to_all(copies, ('gx', 'gy'), 0, 0)  5.52 us
    ppermute x10, waiting for transfers between devices, send(): return lax.ppermute(array, ('gx', 'gy'), pairs)  5.26 us
    all_to_all x1, waiting for transfers between devices, spread_share(): full = lax.all_to_all(copies, ('gx', 'gy'), 0, 0)  3.05 us
  transfers between devices with their start and end apart: 12, of which 4 were waited for; matrix products, arithmetic and copies ran while one was open for 0% of the time, Pallas kernels for 21%

profile of v16, /device:TPU:0, one launch (start us, length us, event | category | flops | bytes accessed | tf_op | source)
XLA Modules:
  0.0 109.2 jit_solution(6192066904218406302)
XLA Ops:
  1.5 2.9 %prepare_kernel.1 = (f32[16,128]{1,0:T(8,128)}, bf16[400,384]{1,0:T(8,128)(2,1)}, bf16[400,384]{1,0:T(8,128)(2,1)}, bf16[112,512]{1,0:T(8,128)(2,1)}, bf16[112,512]{1,0:T(8,128)(2,1)}) custom-call(s32[16]{0:T(128)} %bitcast.19, s32[1]{0:T(128)} %bitcast.12.count, bf16[16,48,512]{2,1,0:T(8,128)(2,1)} %bitcast.15, bf16[16,48,512]{2,1,0:T(8,128)(2,1)} %bitcast.17), custom_call_target="tpu_custom_call" | custom-call | bytes 2424900 | tf_op jit(solution)/shard_map/prepare_kernel/pallas_call | solution.py:694
  4.4 2.3 %collective-permute-start = (bf16[112,512]{1,0:T(8,128)(2,1)}, bf16[112,512]{1,0:T(8,128)(2,1)S(1)}, u32[]{:S(2)}, u32[]{:S(2)}) collective-permute-start(bf16[112,512]{1,0:T(8,128)(2,1)} %get-tuple-element.44), channel_id=1, source_target_pairs={{0,1},{1,2},{2,3},{4,5},{5,6},{6,7},{8,9},{9,10},{10,11},{12,13},{... | collective-permute-start | bytes 344072 | tf_op jit(solution)/shard_map/ppermute | solution.py:714
  6.7 1.3 %collective-permute-start.1 = (bf16[112,512]{1,0:T(8,128)(2,1)}, bf16[112,512]{1,0:T(8,128)(2,1)S(1)}, u32[]{:S(2)}, u32[]{:S(2)}) collective-permute-start(bf16[112,512]{1,0:T(8,128)(2,1)} %get-tuple-element.45), channel_id=1, source_target_pairs={{1,0},{2,1},{3,2},{5,4},{6,5},{7,6},{9,8},{10,9},{11,10},{13,12},{... | collective-permute-start | bytes 344072 | tf_op jit(solution)/shard_map/ppermute | solution.py:714
  8.0 4.2 %collective-permute-start.2 = (bf16[400,384]{1,0:T(8,128)(2,1)}, bf16[400,384]{1,0:T(8,128)(2,1)S(1)}, u32[]{:S(2)}, u32[]{:S(2)}) collective-permute-start(bf16[400,384]{1,0:T(8,128)(2,1)} %get-tuple-element.50), channel_id=1, source_target_pairs={{0,4},{1,5},{2,6},{3,7},{4,8},{5,9},{6,10},{7,11},{8,12},{9,13},{1... | collective-permute-start | bytes 921608 | tf_op jit(solution)/shard_map/ppermute | solution.py:714
  12.3 1.3 %collective-permute-start.3 = (bf16[400,384]{1,0:T(8,128)(2,1)}, bf16[400,384]{1,0:T(8,128)(2,1)S(1)}, u32[]{:S(2)}, u32[]{:S(2)}) collective-permute-start(bf16[400,384]{1,0:T(8,128)(2,1)} %get-tuple-element.51), channel_id=1, source_target_pairs={{4,0},{5,1},{6,2},{7,3},{8,4},{9,5},{10,6},{11,7},{12,8},{13,9},{1... | collective-permute-start | bytes 921608 | tf_op jit(solution)/shard_map/ppermute | solution.py:714
  13.6 0.0 collective-permute-done.y_left
  13.6 0.3 corner_kernel.1
  13.9 4.5 %collective-permute-start.4 = (bf16[64,384]{1,0:T(8,128)(2,1)S(1)}, bf16[64,384]{1,0:T(8,128)(2,1)S(1)}, u32[]{:S(2)}, u32[]{:S(2)}) collective-permute-start(bf16[64,384]{1,0:T(8,128)(2,1)S(1)} %get-tuple-element.52), channel_id=1, source_target_pairs={{0,4},{1,5},{2,6},{3,7},{4,8},{5,9},{6,10},{7,11},{8,12},{9,13},{1... | collective-permute-start | bytes 147464 | tf_op jit(solution)/shard_map/ppermute | solution.py:714
  18.5 1.3 %collective-permute-start.5 = (bf16[64,384]{1,0:T(8,128)(2,1)S(1)}, bf16[64,384]{1,0:T(8,128)(2,1)S(1)}, u32[]{:S(2)}, u32[]{:S(2)}) collective-permute-start(bf16[64,384]{1,0:T(8,128)(2,1)S(1)} %get-tuple-element.46.c_low), channel_id=1, source_target_pairs={{4,0},{5,1},{6,2},{7,3},{8,4},{9,5},{10,6},{11,7},{12,8},{13,9},{1... | collective-permute-start | bytes 147464 | tf_op jit(solution)/shard_map/ppermute | solution.py:714
  19.8 0.0 copy-start.3
  19.8 1.0 copy-done.3
  20.8 1.0 copy-done.4
  21.8 4.1 %place_kernel.1 = (bf16[144,48,128]{2,1,0:T(8,128)(2,1)S(1)}, bf16[80,48,128]{2,1,0:T(8,128)(2,1)S(1)}, f32[40,48,128]{2,1,0:T(8,128)S(1)}, bf16[144,432]{1,0:T(...) custom-call(s32[16]{0:T(128)S(1)} %bitcast.20, ...), custom_call_target="tpu_custom_call" | custom-call | flops 8000000000 | bytes 6480964 | tf_op jit(solution)/shard_map/place_kernel/pallas_call | solution.py:694
  25.9 1.4 %collective-permute-done.4.c_left = bf16[64,384]{1,0:T(8,128)(2,1)S(1)} collective-permute-done((bf16[64,384]{1,0:T(8,128)(2,1)S(1)}, bf16[64,384]{1,0:T(8,128)(2,1)S(1)}, u32[]{:S(2)}, u32[]{:S(2)}) %collective-permute-start.4) | collective-permute-done | bytes 49184 | tf_op jit(solution)/shard_map/ppermute | solution.py:714
  27.3 19.4 %forward_kernel.1 = (bf16[144,48,128]{2,1,0:T(8,128)(2,1)S(1)}, f32[80,48,128]{2,1,0:T(8,128)S(1)}, bf16[40,144,128]{2,1,0:T(8,128)(2,1)S(1)}, bf16[40,48,128]{2...) custom-call(bf16[144,48,128]{2,1,0:T(8,128)(2,1)S(1)} %get-tuple-ele, ...), custom_call_target="tpu_custom_call" | custom-call | flops 8000000000 | bytes 10312704 | tf_op jit(solution)/shard_map/forward_kernel/pallas_call | solution.py:694
  46.7 4.4 %collective-permute-start.6 = (bf16[5,48,128]{2,1,0:T(8,128)(2,1)S(1)}, bf16[5,48,128]{2,1,0:T(8,128)(2,1)S(1)}, u32[]{:S(2)}, u32[]{:S(2)}) collective-permute-start(bf16[5,48,128]{2,1,0:T(8,128)(2,1)S(1)} %get-tuple-element.58), channel_id=1, source_target_pairs={{0,4},{1,5},{2,6},{3,7},{4,8},{5,9},{6,10},{7,11},{8,12},{9,13},{1... | collective-permute-start | bytes 184328 | tf_op jit(solution)/shard_map/ppermute | solution.py:714
  51.1 1.3 %collective-permute-start.7 = (bf16[5,48,128]{2,1,0:T(8,128)(2,1)S(1)}, bf16[5,48,128]{2,1,0:T(8,128)(2,1)S(1)}, u32[]{:S(2)}, u32[]{:S(2)}) collective-permute-start(bf16[5,48,128]{2,1,0:T(8,128)(2,1)S(1)} %get-tuple-element.59), channel_id=1, source_target_pairs={{4,0},{5,1},{6,2},{7,3},{8,4},{9,5},{10,6},{11,7},{12,8},{13,9},{1... | collective-permute-start | bytes 184328 | tf_op jit(solution)/shard_map/ppermute | solution.py:714
  52.4 2.8 %side_kernel.1.early = bf16[720,128]{1,0:T(8,128)(2,1)S(1)} custom-call(bf16[40,48,128]{2,1,0:T(8,128)(2,1)S(1)} %get-tuple-element.66.rects, bf16[80,48,128]{2,1,0:T(8,128)(2,1)S(1)} %get-tuple-element.61.cot_grid, bf16[40,144,128]{2,1,0:T(8,128)(2,1)S(1)} %get-tuple-element.67.low_cols, bf16[40,48,128]{2,1,0:T(8,128)(2,1)S(1)} %get-tuple-element.57.grad_c), custom_call_target="tpu_custom_call" | custom-call | flops 8000000000 | bytes 3624960 | tf_op jit(solution)/shard_map/side_kernel/pallas_call | solution.py:694
  55.2 3.8 %collective-permute-done.7.from_right = bf16[5,48,128]{2,1,0:T(8,128)(2,1)S(1)} collective-permute-done((bf16[5,48,128]{2,1,0:T(8,128)(2,1)S(1)}, bf16[5,48,128]{2,1,0:T(8,128)(2,1)S(1)}, u32[]{:S(2)}, u32[]{:S(2)}) %collective-permute-start.7) | collective-permute-done | bytes 61472 | tf_op jit(solution)/shard_map/ppermute | solution.py:714
  59.0 4.3 %backward_kernel.1 = (bf16[80,48,128]{2,1,0:T(8,128)(2,1)S(1)}, bf16[40,48,128]{2,1,0:T(8,128)(2,1)S(1)}) custom-call(bf16[40,48,128]{2,1,0:T(8,128)(2,1)S(1)} %get-tuple-element.57.grad_c, bf16[5,48,128]{2,1,0:T(8,128)(2,1)S(1)} %collective-permute-done.6.from_left, bf16[5,48,128]{2,1,0:T(8,128)(2,1)S(1)} %collective-permute-done.7.from_right, ...), custom_call_target="tpu_custom_call" | custom-call | flops 8000000000 | bytes 5207552 | tf_op jit(solution)/shard_map/backward_kernel/pallas_call | solution.py:694
  63.3 6.7 %weight_kernel.1 = bf16[1280,128]{1,0:T(8,128)(2,1)} custom-call(bf16[144,48,128]{2,1,0:T(8,128)(2,1)S(1)} %get-tuple-element.56.grid, bf16[80,48,128]{2,1,0:T(8,128)(2,1)S(1)} %get-tuple-element.73.grad_h, bf16[40,48,128]{2,1,0:T(8,128)(2,1)S(1)} %get-tuple-element.65.grad_d, f32[80,48,128]{2,1,0:T(8,128)S(1)} %get-tuple-element.60.hidden, ...), custom_call_target="tpu_custom_call" | custom-call | flops 12000000000 | bytes 5722112 | tf_op jit(solution)/shard_map/weight_kernel/pallas_call | solution.py:694
  70.0 7.0 %all-to-all-start = ((bf16[32,40,128]{2,1,0:T(8,128)(2,1)}), bf16[32,40,128]{2,1,0:T(8,128)(2,1)S(1)}, u32[]{:S(2)}, u32[]{:S(2)}) async-start(bf16[32,40,128]{2,1,0:T(8,128)(2,1)} %bitcast.6), calls=%async_computation | async-start | bytes 655360 | tf_op jit(solution)/shard_map/all_to_all | solution.py:722
  77.0 1.2 %pack_kernel.1 = (bf16[10,48,128]{2,1,0:T(8,128)(2,1)S(1)}, bf16[10,48,128]{2,1,0:T(8,128)(2,1)S(1)}) custom-call(bf16[80,48,128]{2,1,0:T(8,128)(2,1)S(1)} %get-tuple-element.73.grad_h), custom_call_target="tpu_custom_call" | custom-call | flops 1000000000 | bytes 1228800 | tf_op jit(solution)/shard_map/pack_kernel/pallas_call | solution.py:694
  78.2 3.7 %collective-permute-start.8 = (bf16[10,48,128]{2,1,0:T(8,128)(2,1)S(1)}, bf16[10,48,128]{2,1,0:T(8,128)(2,1)S(1)}, u32[]{:S(2)}, u32[]{:S(2)}) collective-permute-start(bf16[10,48,128]{2,1,0:T(8,128)(2,1)S(1)} %get-tuple-element.74), channel_id=1, source_target_pairs={{0,4},{1,5},{2,6},{3,7},{4,8},{5,9},{6,10},{7,11},{8,12},{9,13},{1... | collective-permute-start | bytes 368648 | tf_op jit(solution)/shard_map/ppermute | solution.py:714
  81.9 1.5 %collective-permute-start.9 = (bf16[10,48,128]{2,1,0:T(8,128)(2,1)S(1)}, bf16[10,48,128]{2,1,0:T(8,128)(2,1)S(1)}, u32[]{:S(2)}, u32[]{:S(2)}) collective-permute-start(bf16[10,48,128]{2,1,0:T(8,128)(2,1)S(1)} %get-tuple-element.75), channel_id=1, source_target_pairs={{4,0},{5,1},{6,2},{7,3},{8,4},{9,5},{10,6},{11,7},{12,8},{13,9},{1... | collective-permute-start | bytes 368648 | tf_op jit(solution)/shard_map/ppermute | solution.py:714
  83.4 4.4 %output_kernel.1 = bf16[16,48,512]{2,1,0:T(8,128)(2,1)} custom-call(s32[16]{0:T(128)S(1)} %bitcast.21, f32[80,48,128]{2,1,0:T(8,128)S(1)} %copy-done.9, bf16[40,48,128]{2,1,0:T(8,128)(2,1)S(1)} %get-tuple-element.66.rects, f32[16,128]{1,0:T(8,128)S(1)} %get-tuple-element.62.live, bf16[96,192]{1,0:T(8,128)(2,1)S(1)} %get-tuple-element.70.up_w), custom_call_target="tpu_custom_call" | custom-call | flops 8000000000 | bytes 3289152 | tf_op jit(solution)/shard_map/output_kernel/pallas_call | solution.py:694
  87.8 1.2 %all-to-all-done.parts = bf16[32,40,128]{2,1,0:T(8,128)(2,1)S(1)} async-done(((bf16[32,40,128]{2,1,0:T(8,128)(2,1)}), bf16[32,40,128]{2,1,0:T(8,128)(2,1)S(1)}, u32[]{:S(2)}, u32[]{:S(2)}) %all-to-all-start) | async-done | bytes 327712 | tf_op jit(solution)/shard_map/all_to_all | solution.py:722
  89.0 0.8 sum_kernel.1
  89.8 5.5 %all-to-all-start.1 = ((bf16[32,40,128]{2,1,0:T(8,128)(2,1)}), bf16[32,40,128]{2,1,0:T(8,128)(2,1)S(1)}, u32[]{:S(2)}, u32[]{:S(2)}) async-start(bf16[32,40,128]{2,1,0:T(8,128)(2,1)} %sum_kernel.1), calls=%async_computation.1 | async-start | bytes 655360 | tf_op jit(solution)/shard_map/all_to_all | solution.py:728
  95.4 8.9 %input_kernel.1 = bf16[16,48,512]{2,1,0:T(8,128)(2,1)} custom-call(s32[16]{0:T(128)S(1)} %bitcast.22, bf16[80,48,128]{2,1,0:T(8,128)(2,1)S(1)} %get-tuple-element.73.grad_h, bf16[10,48,128]{2,1,0:T(8,128)(2,1)S(1)} %collective-permute-done.8.from_left, bf16[10,48,128]{2,1,0:T(8,128)(2,1)S(1)} %collective-permute-done.9.from_right, ...), custom_call_target="tpu_custom_call" | custom-call | flops 8000000000 | bytes 2147904 | tf_op jit(solution)/shard_map/input_kernel/pallas_call | solution.py:694
  104.3 3.1 %all-to-all-done.1 = bf16[32,40,128]{2,1,0:T(8,128)(2,1)S(1)} async-done(((bf16[32,40,128]{2,1,0:T(8,128)(2,1)}), bf16[32,40,128]{2,1,0:T(8,128)(2,1)S(1)}, u32[]{:S(2)}, u32[]{:S(2)}) %all-to-all-start.1) | async-done | bytes 327712 | tf_op jit(solution)/shard_map/all_to_all | solution.py:728
  107.3 1.9 %finish_kernel.1 = (f32[27,48,48]{2,1,0:T(8,128)}, f32[48,8,48]{2,1,0:T(8,128)}, f32[27,48,48]{2,1,0:T(8,128)}, f32[8,48,48]{2,1,0:T(8,128)}) custom-call(bf16[1280,128]{1,0:T(8,128)(2,1)S(1)} %bitcast.14), custom_call_target="tpu_custom_call" | custom-call | bytes 972800 | tf_op jit(solution)/shard_map/finish_kernel/pallas_call | solution.py:694
  (24 shorter events, 0.1 us)
Async XLA Ops:
  0.6 19.2 %copy-start.1 = (bf16[1,1,16,48,512]{4,3,2,1,0:T(8,128)(2,1)S(1)}, bf16[1,1,16,48,512]{4,3,2,1,0:T(8,128)(2,1)}, u32[]{:S(2)}) copy-start(bf16[1,1,16,48,512]{4,3,2,1,0:T(8,128)(2,1)} %param.11) | copy-start | bytes 2359300
  0.6 19.2 %copy-start.2 = (s32[1,1,16]{2,1,0:T(1,128)S(1)}, s32[1,1,16]{2,1,0:T(1,128)}, u32[]{:S(2)}) copy-start(s32[1,1,16]{2,1,0:T(1,128)} %param.9) | copy-start | bytes 196
  0.7 19.2 %copy-start = (bf16[1,1,16,48,512]{4,3,2,1,0:T(8,128)(2,1)S(1)}, bf16[1,1,16,48,512]{4,3,2,1,0:T(8,128)(2,1)}, u32[]{:S(2)}) copy-start(bf16[1,1,16,48,512]{4,3,2,1,0:T(8,128)(2,1)} %param.8) | copy-start | bytes 2359300
  0.7 19.2 %copy-start.6 = (bf16[8,48,48]{2,1,0:T(8,128)(2,1)S(1)}, bf16[8,48,48]{2,1,0:T(8,128)(2,1)}, u32[]{:S(2)}) copy-start(bf16[8,48,48]{2,1,0:T(8,128)(2,1)} %up.1) | copy-start | bytes 110596
  0.7 19.2 %copy-start.5 = (bf16[48,8,48]{2,1,0:T(8,128)(2,1)S(1)}, bf16[48,8,48]{2,1,0:T(8,128)(2,1)}, u32[]{:S(2)}) copy-start(bf16[48,8,48]{2,1,0:T(8,128)(2,1)} %down.1) | copy-start | bytes 110596
  4.4 9.2 %collective-permute-start = (bf16[112,512]{1,0:T(8,128)(2,1)}, bf16[112,512]{1,0:T(8,128)(2,1)S(1)}, u32[]{:S(2)}, u32[]{:S(2)}) collective-permute-start(bf16[112,512]{1,0:T(8,128)(2,1)} %get-tuple-element.44), channel_id=1, source_target_pairs={{0,1},{1,2},{2,3},{4,5},{5,6},{6,7},{8,9},{9,10},{10,11},{12,13},{... | collective-permute-start | bytes 344072 | tf_op jit(solution)/shard_map/ppermute | solution.py:714
  6.7 6.9 %collective-permute-start.1 = (bf16[112,512]{1,0:T(8,128)(2,1)}, bf16[112,512]{1,0:T(8,128)(2,1)S(1)}, u32[]{:S(2)}, u32[]{:S(2)}) collective-permute-start(bf16[112,512]{1,0:T(8,128)(2,1)} %get-tuple-element.45), channel_id=1, source_target_pairs={{1,0},{2,1},{3,2},{5,4},{6,5},{7,6},{9,8},{10,9},{11,10},{13,12},{... | collective-permute-start | bytes 344072 | tf_op jit(solution)/shard_map/ppermute | solution.py:714
  8.0 19.3 %collective-permute-start.2 = (bf16[400,384]{1,0:T(8,128)(2,1)}, bf16[400,384]{1,0:T(8,128)(2,1)S(1)}, u32[]{:S(2)}, u32[]{:S(2)}) collective-permute-start(bf16[400,384]{1,0:T(8,128)(2,1)} %get-tuple-element.50), channel_id=1, source_target_pairs={{0,4},{1,5},{2,6},{3,7},{4,8},{5,9},{6,10},{7,11},{8,12},{9,13},{1... | collective-permute-start | bytes 921608 | tf_op jit(solution)/shard_map/ppermute | solution.py:714
  12.3 15.0 %collective-permute-start.3 = (bf16[400,384]{1,0:T(8,128)(2,1)}, bf16[400,384]{1,0:T(8,128)(2,1)S(1)}, u32[]{:S(2)}, u32[]{:S(2)}) collective-permute-start(bf16[400,384]{1,0:T(8,128)(2,1)} %get-tuple-element.51), channel_id=1, source_target_pairs={{4,0},{5,1},{6,2},{7,3},{8,4},{9,5},{10,6},{11,7},{12,8},{13,9},{1... | collective-permute-start | bytes 921608 | tf_op jit(solution)/shard_map/ppermute | solution.py:714
  13.9 13.4 %collective-permute-start.4 = (bf16[64,384]{1,0:T(8,128)(2,1)S(1)}, bf16[64,384]{1,0:T(8,128)(2,1)S(1)}, u32[]{:S(2)}, u32[]{:S(2)}) collective-permute-start(bf16[64,384]{1,0:T(8,128)(2,1)S(1)} %get-tuple-element.52), channel_id=1, source_target_pairs={{0,4},{1,5},{2,6},{3,7},{4,8},{5,9},{6,10},{7,11},{8,12},{9,13},{1... | collective-permute-start | bytes 147464 | tf_op jit(solution)/shard_map/ppermute | solution.py:714
  18.5 8.8 %collective-permute-start.5 = (bf16[64,384]{1,0:T(8,128)(2,1)S(1)}, bf16[64,384]{1,0:T(8,128)(2,1)S(1)}, u32[]{:S(2)}, u32[]{:S(2)}) collective-permute-start(bf16[64,384]{1,0:T(8,128)(2,1)S(1)} %get-tuple-element.46.c_low), channel_id=1, source_target_pairs={{4,0},{5,1},{6,2},{7,3},{8,4},{9,5},{10,6},{11,7},{12,8},{13,9},{1... | collective-permute-start | bytes 147464 | tf_op jit(solution)/shard_map/ppermute | solution.py:714
  19.8 1.0 copy-start.3
  20.8 1.0 copy-start.4
  21.8 5.5 %copy-start.7 = (f32[16,128]{1,0:T(8,128)S(1)}, f32[16,128]{1,0:T(8,128)}, u32[]{:S(2)}) copy-start(f32[16,128]{1,0:T(8,128)} %get-tuple-element.48.flags) | copy-start | bytes 24580
  46.7 16.6 %copy-start.8 = (f32[80,48,128]{2,1,0:T(8,128)}, f32[80,48,128]{2,1,0:T(8,128)S(1)}, u32[]{:S(2)}) copy-start(f32[80,48,128]{2,1,0:T(8,128)S(1)} %get-tuple-element.60.hidden) | copy-start | bytes 5898244
  46.7 8.5 %collective-permute-start.6 = (bf16[5,48,128]{2,1,0:T(8,128)(2,1)S(1)}, bf16[5,48,128]{2,1,0:T(8,128)(2,1)S(1)}, u32[]{:S(2)}, u32[]{:S(2)}) collective-permute-start(bf16[5,48,128]{2,1,0:T(8,128)(2,1)S(1)} %get-tuple-element.58), channel_id=1, source_target_pairs={{0,4},{1,5},{2,6},{3,7},{4,8},{5,9},{6,10},{7,11},{8,12},{9,13},{1... | collective-permute-start | bytes 184328 | tf_op jit(solution)/shard_map/ppermute | solution.py:714
  51.1 7.9 %collective-permute-start.7 = (bf16[5,48,128]{2,1,0:T(8,128)(2,1)S(1)}, bf16[5,48,128]{2,1,0:T(8,128)(2,1)S(1)}, u32[]{:S(2)}, u32[]{:S(2)}) collective-permute-start(bf16[5,48,128]{2,1,0:T(8,128)(2,1)S(1)} %get-tuple-element.59), channel_id=1, source_target_pairs={{4,0},{5,1},{6,2},{7,3},{8,4},{9,5},{10,6},{11,7},{12,8},{13,9},{1... | collective-permute-start | bytes 184328 | tf_op jit(solution)/shard_map/ppermute | solution.py:714
  70.0 19.0 %all-to-all-start = ((bf16[32,40,128]{2,1,0:T(8,128)(2,1)}), bf16[32,40,128]{2,1,0:T(8,128)(2,1)S(1)}, u32[]{:S(2)}, u32[]{:S(2)}) async-start(bf16[32,40,128]{2,1,0:T(8,128)(2,1)} %bitcast.6), calls=%async_computation | async-start | bytes 655360 | tf_op jit(solution)/shard_map/all_to_all | solution.py:722
  77.0 6.4 %copy-start.9 = (f32[80,48,128]{2,1,0:T(8,128)S(1)}, f32[80,48,128]{2,1,0:T(8,128)}, u32[]{:S(2)}) copy-start(f32[80,48,128]{2,1,0:T(8,128)} %copy-done.8) | copy-start | bytes 5898244
  78.2 17.1 %collective-permute-start.8 = (bf16[10,48,128]{2,1,0:T(8,128)(2,1)S(1)}, bf16[10,48,128]{2,1,0:T(8,128)(2,1)S(1)}, u32[]{:S(2)}, u32[]{:S(2)}) collective-permute-start(bf16[10,48,128]{2,1,0:T(8,128)(2,1)S(1)} %get-tuple-element.74), channel_id=1, source_target_pairs={{0,4},{1,5},{2,6},{3,7},{4,8},{5,9},{6,10},{7,11},{8,12},{9,13},{1... | collective-permute-start | bytes 368648 | tf_op jit(solution)/shard_map/ppermute | solution.py:714
  81.9 13.4 %collective-permute-start.9 = (bf16[10,48,128]{2,1,0:T(8,128)(2,1)S(1)}, bf16[10,48,128]{2,1,0:T(8,128)(2,1)S(1)}, u32[]{:S(2)}, u32[]{:S(2)}) collective-permute-start(bf16[10,48,128]{2,1,0:T(8,128)(2,1)S(1)} %get-tuple-element.75), channel_id=1, source_target_pairs={{4,0},{5,1},{6,2},{7,3},{8,4},{9,5},{10,6},{11,7},{12,8},{13,9},{1... | collective-permute-start | bytes 368648 | tf_op jit(solution)/shard_map/ppermute | solution.py:714
  89.8 17.5 %all-to-all-start.1 = ((bf16[32,40,128]{2,1,0:T(8,128)(2,1)}), bf16[32,40,128]{2,1,0:T(8,128)(2,1)S(1)}, u32[]{:S(2)}, u32[]{:S(2)}) async-start(bf16[32,40,128]{2,1,0:T(8,128)(2,1)} %sum_kernel.1), calls=%async_computation.1 | async-start | bytes 655360 | tf_op jit(solution)/shard_map/all_to_all | solution.py:728

commit v17 on v16

--- a/solution.py
+++ b/solution.py
@@ -342,7 +342,8 @@
         fill(even, jnp.minimum(tile + 8, tiles - 4))
         return multiply(odd, tile + 4, carry)
 
-    lax.fori_loop(0, tiles // 8, body, jnp.zeros((C, LANES), F32))
+    unroll = 3 if tiles % 24 == 0 else 5
+    lax.fori_loop(0, tiles // 8, body, jnp.zeros((C, LANES), F32), unroll=unroll)
 
 
 def forward_kernel(
@@ -501,7 +502,7 @@
                 at = LANES * (2 * inner + half)
                 rows_out[pl.ds(start, C), at : at + LANES] = (value * alive).astype(BF16)
 
-    loop(1, pairs - 1, block_step, 2)
+    loop(1, pairs - 1, block_step, 4)
     to_blocks(slots, rows_out, flat, out)
 
 
@@ -536,13 +537,13 @@
     masks = depth_masks(32, 4)
 
     def weight_step(index):
-        at = [2 + 12 * index + inner for inner in range(12)]
+        at = [2 + 18 * index + inner for inner in range(18)]
         rights = [depth_columns(low_cols[tile], masks, 32) for tile in at]
         coarse_g[0 : 9 * C, :] += dot(
             jnp.concatenate(rights, axis=1), stacks(grad_own, at), (1, 1)
         )
 
-    loop(0, (tiles - 4) // 12, weight_step)
+    loop(0, (tiles - 4) // 18, weight_step)
     rest = flatten_weights(coarse_g, flat)
     flat[9 * C : 12 * C, :] = squeeze_rows(up_g[...], 3 * C).astype(BF16)
     flat[12 * C :, :] = roll(rest, C).astype(BF16)
@@ -601,7 +602,7 @@
     halves = own_masks()
 
     def fine_step(index):
-        at = [4 + 18 * index + inner for inner in range(18)]
+        at = [4 + 36 * index + inner for inner in range(36)]
         rights = []
         for tile in at:
             lower, upper = grid[tile], grid[tile + shift]
@@ -611,7 +612,7 @@
             jnp.concatenate(rights, axis=1), stacks(grad_own, at), (1, 1)
         )
 
-    loop(0, (tiles - 8) // 18, fine_step)
+    loop(0, (tiles - 8) // 36, fine_step)
 
     def down_step(index):
         lefts = []
@@ -651,7 +652,7 @@
                 value * alive
             ).astype(BF16)
 
-    loop(1, tiles // EDGE - 1, block_step, 2)
+    loop(1, tiles // EDGE - 1, block_step, 4)
     to_blocks(slots, rows_out, flat, out)
 
 

time: 110 us -> 106 us (0.964)
  Pallas kernels: 57.6 us -> 52.2 us
  waiting for transfers between devices: 9.51 us -> 11.6 us
    pallas_call x12, Pallas kernels: 57.6 us -> 52.2 us  [call(): pl.pallas_call(kernel, out_shape=tuple((jax.ShapeDtypeStruct(s, d) for s,...]
    all_to_all x1, waiting for transfers between devices: 3.05 us -> 4.44 us  [spread_share(): full = lax.all_to_all(copies, ('gx', 'gy'), 0, 0)]
  transfers between devices with their start and end apart: 12 -> 12, of which waited for: 4 -> 4; matrix products, arithmetic and copies ran while one was open for 0% -> 0% of each run, Pallas kernels for 21% -> 19%
where the time goes in v17:
time: 106 us; the launch traced here: 105 us
  Pallas kernels  52.2 us (49%)
  starting transfers between devices  37.8 us (36%)
  waiting for transfers between devices  11.6 us (11%)
  local copies, waits for them, and re-layouts  1.98 us (2%)
  between operations  1.71 us (2%)
    pallas_call x12, Pallas kernels, call(): pl.pallas_call(kernel, out_shape=tuple((jax.ShapeDtypeStruct(s, d) for s,...  52.2 us
    ppermute x10, starting transfers between devices, send(): return lax.ppermute(array, ('gx', 'gy'), pairs)  25.8 us
    all_to_all x1, starting transfers between devices, reduce_share(): lax.all_to_all(joined.reshape(devices, share, LANES), ('gx', 'gy'), 0, 0)  6.98 us
    ppermute x10, waiting for transfers between devices, send(): return lax.ppermute(array, ('gx', 'gy'), pairs)  5.34 us
    all_to_all x1, starting transfers between devices, spread_share(): full = lax.all_to_all(copies, ('gx', 'gy'), 0, 0)  4.93 us
    all_to_all x1, waiting for transfers between devices, spread_share(): full = lax.all_to_all(copies, ('gx', 'gy'), 0, 0)  4.44 us
  transfers between devices with their start and end apart: 12, of which 4 were waited for; matrix products, arithmetic and copies ran while one was open for 0% of the time, Pallas kernels for 19%

profile of v17, /device:TPU:0, one launch (start us, length us, event | category | flops | bytes accessed | tf_op | source)
XLA Modules:
  0.0 105.2 jit_solution(317638722338004876)
XLA Ops:
  1.5 2.9 %prepare_kernel.1 = (f32[16,128]{1,0:T(8,128)}, bf16[400,384]{1,0:T(8,128)(2,1)}, bf16[400,384]{1,0:T(8,128)(2,1)}, bf16[112,512]{1,0:T(8,128)(2,1)}, bf16[112,512]{1,0:T(8,128)(2,1)}) custom-call(s32[16]{0:T(128)} %bitcast.19, s32[1]{0:T(128)} %bitcast.12.count, bf16[16,48,512]{2,1,0:T(8,128)(2,1)} %bitcast.15, bf16[16,48,512]{2,1,0:T(8,128)(2,1)} %bitcast.17), custom_call_target="tpu_custom_call" | custom-call | bytes 2424900 | tf_op jit(solution)/shard_map/prepare_kernel/pallas_call | solution.py:695
  4.4 2.3 %collective-permute-start = (bf16[112,512]{1,0:T(8,128)(2,1)}, bf16[112,512]{1,0:T(8,128)(2,1)S(1)}, u32[]{:S(2)}, u32[]{:S(2)}) collective-permute-start(bf16[112,512]{1,0:T(8,128)(2,1)} %get-tuple-element.44), channel_id=1, source_target_pairs={{0,1},{1,2},{2,3},{4,5},{5,6},{6,7},{8,9},{9,10},{10,11},{12,13},{... | collective-permute-start | bytes 344072 | tf_op jit(solution)/shard_map/ppermute | solution.py:715
  6.7 1.3 %collective-permute-start.1 = (bf16[112,512]{1,0:T(8,128)(2,1)}, bf16[112,512]{1,0:T(8,128)(2,1)S(1)}, u32[]{:S(2)}, u32[]{:S(2)}) collective-permute-start(bf16[112,512]{1,0:T(8,128)(2,1)} %get-tuple-element.45), channel_id=1, source_target_pairs={{1,0},{2,1},{3,2},{5,4},{6,5},{7,6},{9,8},{10,9},{11,10},{13,12},{... | collective-permute-start | bytes 344072 | tf_op jit(solution)/shard_map/ppermute | solution.py:715
  8.0 4.2 %collective-permute-start.2 = (bf16[400,384]{1,0:T(8,128)(2,1)}, bf16[400,384]{1,0:T(8,128)(2,1)S(1)}, u32[]{:S(2)}, u32[]{:S(2)}) collective-permute-start(bf16[400,384]{1,0:T(8,128)(2,1)} %get-tuple-element.50), channel_id=1, source_target_pairs={{0,4},{1,5},{2,6},{3,7},{4,8},{5,9},{6,10},{7,11},{8,12},{9,13},{1... | collective-permute-start | bytes 921608 | tf_op jit(solution)/shard_map/ppermute | solution.py:715
  12.3 1.3 %collective-permute-start.3 = (bf16[400,384]{1,0:T(8,128)(2,1)}, bf16[400,384]{1,0:T(8,128)(2,1)S(1)}, u32[]{:S(2)}, u32[]{:S(2)}) collective-permute-start(bf16[400,384]{1,0:T(8,128)(2,1)} %get-tuple-element.51), channel_id=1, source_target_pairs={{4,0},{5,1},{6,2},{7,3},{8,4},{9,5},{10,6},{11,7},{12,8},{13,9},{1... | collective-permute-start | bytes 921608 | tf_op jit(solution)/shard_map/ppermute | solution.py:715
  13.6 0.0 collective-permute-done.y_left
  13.6 0.3 corner_kernel.1
  13.9 4.5 %collective-permute-start.4 = (bf16[64,384]{1,0:T(8,128)(2,1)S(1)}, bf16[64,384]{1,0:T(8,128)(2,1)S(1)}, u32[]{:S(2)}, u32[]{:S(2)}) collective-permute-start(bf16[64,384]{1,0:T(8,128)(2,1)S(1)} %get-tuple-element.52), channel_id=1, source_target_pairs={{0,4},{1,5},{2,6},{3,7},{4,8},{5,9},{6,10},{7,11},{8,12},{9,13},{1... | collective-permute-start | bytes 147464 | tf_op jit(solution)/shard_map/ppermute | solution.py:715
  18.5 1.3 %collective-permute-start.5 = (bf16[64,384]{1,0:T(8,128)(2,1)S(1)}, bf16[64,384]{1,0:T(8,128)(2,1)S(1)}, u32[]{:S(2)}, u32[]{:S(2)}) collective-permute-start(bf16[64,384]{1,0:T(8,128)(2,1)S(1)} %get-tuple-element.46.c_low), channel_id=1, source_target_pairs={{4,0},{5,1},{6,2},{7,3},{8,4},{9,5},{10,6},{11,7},{12,8},{13,9},{1... | collective-permute-start | bytes 147464 | tf_op jit(solution)/shard_map/ppermute | solution.py:715
  19.8 0.0 copy-start.3
  19.8 1.0 copy-done.3
  20.8 1.0 copy-done.4
  21.8 4.1 %place_kernel.1 = (bf16[144,48,128]{2,1,0:T(8,128)(2,1)S(1)}, bf16[80,48,128]{2,1,0:T(8,128)(2,1)S(1)}, f32[40,48,128]{2,1,0:T(8,128)S(1)}, bf16[144,432]{1,0:T(...) custom-call(s32[16]{0:T(128)S(1)} %bitcast.20, ...), custom_call_target="tpu_custom_call" | custom-call | flops 8000000000 | bytes 6480964 | tf_op jit(solution)/shard_map/place_kernel/pallas_call | solution.py:695
  25.9 1.4 %collective-permute-done.4.c_left = bf16[64,384]{1,0:T(8,128)(2,1)S(1)} collective-permute-done((bf16[64,384]{1,0:T(8,128)(2,1)S(1)}, bf16[64,384]{1,0:T(8,128)(2,1)S(1)}, u32[]{:S(2)}, u32[]{:S(2)}) %collective-permute-start.4) | collective-permute-done | bytes 49184 | tf_op jit(solution)/shard_map/ppermute | solution.py:715
  27.3 16.6 %forward_kernel.1 = (bf16[144,48,128]{2,1,0:T(8,128)(2,1)S(1)}, f32[80,48,128]{2,1,0:T(8,128)S(1)}, bf16[40,144,128]{2,1,0:T(8,128)(2,1)S(1)}, bf16[40,48,128]{2...) custom-call(bf16[144,48,128]{2,1,0:T(8,128)(2,1)S(1)} %get-tuple-ele, ...), custom_call_target="tpu_custom_call" | custom-call | flops 8000000000 | bytes 10312704 | tf_op jit(solution)/shard_map/forward_kernel/pallas_call | solution.py:695
  43.9 4.4 %collective-permute-start.6 = (bf16[5,48,128]{2,1,0:T(8,128)(2,1)S(1)}, bf16[5,48,128]{2,1,0:T(8,128)(2,1)S(1)}, u32[]{:S(2)}, u32[]{:S(2)}) collective-permute-start(bf16[5,48,128]{2,1,0:T(8,128)(2,1)S(1)} %get-tuple-element.58), channel_id=1, source_target_pairs={{0,4},{1,5},{2,6},{3,7},{4,8},{5,9},{6,10},{7,11},{8,12},{9,13},{1... | collective-permute-start | bytes 184328 | tf_op jit(solution)/shard_map/ppermute | solution.py:715
  48.3 1.5 %collective-permute-start.7 = (bf16[5,48,128]{2,1,0:T(8,128)(2,1)S(1)}, bf16[5,48,128]{2,1,0:T(8,128)(2,1)S(1)}, u32[]{:S(2)}, u32[]{:S(2)}) collective-permute-start(bf16[5,48,128]{2,1,0:T(8,128)(2,1)S(1)} %get-tuple-element.59), channel_id=1, source_target_pairs={{4,0},{5,1},{6,2},{7,3},{8,4},{9,5},{10,6},{11,7},{12,8},{13,9},{1... | collective-permute-start | bytes 184328 | tf_op jit(solution)/shard_map/ppermute | solution.py:715
  49.8 2.6 %side_kernel.1.early = bf16[720,128]{1,0:T(8,128)(2,1)S(1)} custom-call(bf16[40,48,128]{2,1,0:T(8,128)(2,1)S(1)} %get-tuple-element.66.rects, bf16[80,48,128]{2,1,0:T(8,128)(2,1)S(1)} %get-tuple-element.61.cot_grid, bf16[40,144,128]{2,1,0:T(8,128)(2,1)S(1)} %get-tuple-element.67.low_cols, bf16[40,48,128]{2,1,0:T(8,128)(2,1)S(1)} %get-tuple-element.57.grad_c), custom_call_target="tpu_custom_call" | custom-call | flops 8000000000 | bytes 3624960 | tf_op jit(solution)/shard_map/side_kernel/pallas_call | solution.py:695
  52.4 3.9 %collective-permute-done.7.from_right = bf16[5,48,128]{2,1,0:T(8,128)(2,1)S(1)} collective-permute-done((bf16[5,48,128]{2,1,0:T(8,128)(2,1)S(1)}, bf16[5,48,128]{2,1,0:T(8,128)(2,1)S(1)}, u32[]{:S(2)}, u32[]{:S(2)}) %collective-permute-start.7) | collective-permute-done | bytes 61472 | tf_op jit(solution)/shard_map/ppermute | solution.py:715
  56.3 3.5 %backward_kernel.1 = (bf16[80,48,128]{2,1,0:T(8,128)(2,1)S(1)}, bf16[40,48,128]{2,1,0:T(8,128)(2,1)S(1)}) custom-call(bf16[40,48,128]{2,1,0:T(8,128)(2,1)S(1)} %get-tuple-element.57.grad_c, bf16[5,48,128]{2,1,0:T(8,128)(2,1)S(1)} %collective-permute-done.6.from_left, bf16[5,48,128]{2,1,0:T(8,128)(2,1)S(1)} %collective-permute-done.7.from_right, ...), custom_call_target="tpu_custom_call" | custom-call | flops 8000000000 | bytes 5207552 | tf_op jit(solution)/shard_map/backward_kernel/pallas_call | solution.py:695
  59.8 6.8 %weight_kernel.1 = bf16[1280,128]{1,0:T(8,128)(2,1)} custom-call(bf16[144,48,128]{2,1,0:T(8,128)(2,1)S(1)} %get-tuple-element.56.grid, bf16[80,48,128]{2,1,0:T(8,128)(2,1)S(1)} %get-tuple-element.73.grad_h, bf16[40,48,128]{2,1,0:T(8,128)(2,1)S(1)} %get-tuple-element.65.grad_d, f32[80,48,128]{2,1,0:T(8,128)S(1)} %get-tuple-element.60.hidden, ...), custom_call_target="tpu_custom_call" | custom-call | flops 12000000000 | bytes 5722112 | tf_op jit(solution)/shard_map/weight_kernel/pallas_call | solution.py:695
  66.6 7.0 %all-to-all-start = ((bf16[32,40,128]{2,1,0:T(8,128)(2,1)}), bf16[32,40,128]{2,1,0:T(8,128)(2,1)S(1)}, u32[]{:S(2)}, u32[]{:S(2)}) async-start(bf16[32,40,128]{2,1,0:T(8,128)(2,1)} %bitcast.6), calls=%async_computation | async-start | bytes 655360 | tf_op jit(solution)/shard_map/all_to_all | solution.py:723
  73.6 1.2 %pack_kernel.1 = (bf16[10,48,128]{2,1,0:T(8,128)(2,1)S(1)}, bf16[10,48,128]{2,1,0:T(8,128)(2,1)S(1)}) custom-call(bf16[80,48,128]{2,1,0:T(8,128)(2,1)S(1)} %get-tuple-element.73.grad_h), custom_call_target="tpu_custom_call" | custom-call | flops 1000000000 | bytes 1228800 | tf_op jit(solution)/shard_map/pack_kernel/pallas_call | solution.py:695
  74.8 3.7 %collective-permute-start.8 = (bf16[10,48,128]{2,1,0:T(8,128)(2,1)S(1)}, bf16[10,48,128]{2,1,0:T(8,128)(2,1)S(1)}, u32[]{:S(2)}, u32[]{:S(2)}) collective-permute-start(bf16[10,48,128]{2,1,0:T(8,128)(2,1)S(1)} %get-tuple-element.74), channel_id=1, source_target_pairs={{0,4},{1,5},{2,6},{3,7},{4,8},{5,9},{6,10},{7,11},{8,12},{9,13},{1... | collective-permute-start | bytes 368648 | tf_op jit(solution)/shard_map/ppermute | solution.py:715
  78.5 1.3 %collective-permute-start.9 = (bf16[10,48,128]{2,1,0:T(8,128)(2,1)S(1)}, bf16[10,48,128]{2,1,0:T(8,128)(2,1)S(1)}, u32[]{:S(2)}, u32[]{:S(2)}) collective-permute-start(bf16[10,48,128]{2,1,0:T(8,128)(2,1)S(1)} %get-tuple-element.75), channel_id=1, source_target_pairs={{4,0},{5,1},{6,2},{7,3},{8,4},{9,5},{10,6},{11,7},{12,8},{13,9},{1... | collective-permute-start | bytes 368648 | tf_op jit(solution)/shard_map/ppermute | solution.py:715
  79.8 4.0 %output_kernel.1 = bf16[16,48,512]{2,1,0:T(8,128)(2,1)} custom-call(s32[16]{0:T(128)S(1)} %bitcast.21, f32[80,48,128]{2,1,0:T(8,128)S(1)} %copy-done.9, bf16[40,48,128]{2,1,0:T(8,128)(2,1)S(1)} %get-tuple-element.66.rects, f32[16,128]{1,0:T(8,128)S(1)} %get-tuple-element.62.live, bf16[96,192]{1,0:T(8,128)(2,1)S(1)} %get-tuple-element.70.up_w), custom_call_target="tpu_custom_call" | custom-call | flops 8000000000 | bytes 3289152 | tf_op jit(solution)/shard_map/output_kernel/pallas_call | solution.py:695
  83.8 1.8 %all-to-all-done.parts = bf16[32,40,128]{2,1,0:T(8,128)(2,1)S(1)} async-done(((bf16[32,40,128]{2,1,0:T(8,128)(2,1)}), bf16[32,40,128]{2,1,0:T(8,128)(2,1)S(1)}, u32[]{:S(2)}, u32[]{:S(2)}) %all-to-all-start) | async-done | bytes 327712 | tf_op jit(solution)/shard_map/all_to_all | solution.py:723
  85.6 0.8 sum_kernel.1
  86.4 4.9 %all-to-all-start.1 = ((bf16[32,40,128]{2,1,0:T(8,128)(2,1)}), bf16[32,40,128]{2,1,0:T(8,128)(2,1)S(1)}, u32[]{:S(2)}, u32[]{:S(2)}) async-start(bf16[32,40,128]{2,1,0:T(8,128)(2,1)} %sum_kernel.1), calls=%async_computation.1 | async-start | bytes 655360 | tf_op jit(solution)/shard_map/all_to_all | solution.py:729
  91.3 7.5 %input_kernel.1 = bf16[16,48,512]{2,1,0:T(8,128)(2,1)} custom-call(s32[16]{0:T(128)S(1)} %bitcast.22, bf16[80,48,128]{2,1,0:T(8,128)(2,1)S(1)} %get-tuple-element.73.grad_h, bf16[10,48,128]{2,1,0:T(8,128)(2,1)S(1)} %collective-permute-done.8.from_left, bf16[10,48,128]{2,1,0:T(8,128)(2,1)S(1)} %collective-permute-done.9.from_right, ...), custom_call_target="tpu_custom_call" | custom-call | flops 8000000000 | bytes 2147904 | tf_op jit(solution)/shard_map/input_kernel/pallas_call | solution.py:695
  98.9 4.4 %all-to-all-done.1 = bf16[32,40,128]{2,1,0:T(8,128)(2,1)S(1)} async-done(((bf16[32,40,128]{2,1,0:T(8,128)(2,1)}), bf16[32,40,128]{2,1,0:T(8,128)(2,1)S(1)}, u32[]{:S(2)}, u32[]{:S(2)}) %all-to-all-start.1) | async-done | bytes 327712 | tf_op jit(solution)/shard_map/all_to_all | solution.py:729
  103.3 1.9 %finish_kernel.1 = (f32[27,48,48]{2,1,0:T(8,128)}, f32[48,8,48]{2,1,0:T(8,128)}, f32[27,48,48]{2,1,0:T(8,128)}, f32[8,48,48]{2,1,0:T(8,128)}) custom-call(bf16[1280,128]{1,0:T(8,128)(2,1)S(1)} %bitcast.14), custom_call_target="tpu_custom_call" | custom-call | bytes 972800 | tf_op jit(solution)/shard_map/finish_kernel/pallas_call | solution.py:695
  (24 shorter events, 0.1 us)
Async XLA Ops:
  0.6 19.2 %copy-start.1 = (bf16[1,1,16,48,512]{4,3,2,1,0:T(8,128)(2,1)S(1)}, bf16[1,1,16,48,512]{4,3,2,1,0:T(8,128)(2,1)}, u32[]{:S(2)}) copy-start(bf16[1,1,16,48,512]{4,3,2,1,0:T(8,128)(2,1)} %param.11) | copy-start | bytes 2359300
  0.6 19.2 %copy-start.2 = (s32[1,1,16]{2,1,0:T(1,128)S(1)}, s32[1,1,16]{2,1,0:T(1,128)}, u32[]{:S(2)}) copy-start(s32[1,1,16]{2,1,0:T(1,128)} %param.9) | copy-start | bytes 196
  0.7 19.2 %copy-start = (bf16[1,1,16,48,512]{4,3,2,1,0:T(8,128)(2,1)S(1)}, bf16[1,1,16,48,512]{4,3,2,1,0:T(8,128)(2,1)}, u32[]{:S(2)}) copy-start(bf16[1,1,16,48,512]{4,3,2,1,0:T(8,128)(2,1)} %param.8) | copy-start | bytes 2359300
  0.7 19.2 %copy-start.6 = (bf16[8,48,48]{2,1,0:T(8,128)(2,1)S(1)}, bf16[8,48,48]{2,1,0:T(8,128)(2,1)}, u32[]{:S(2)}) copy-start(bf16[8,48,48]{2,1,0:T(8,128)(2,1)} %up.1) | copy-start | bytes 110596
  0.7 19.2 %copy-start.5 = (bf16[48,8,48]{2,1,0:T(8,128)(2,1)S(1)}, bf16[48,8,48]{2,1,0:T(8,128)(2,1)}, u32[]{:S(2)}) copy-start(bf16[48,8,48]{2,1,0:T(8,128)(2,1)} %down.1) | copy-start | bytes 110596
  4.4 9.2 %collective-permute-start = (bf16[112,512]{1,0:T(8,128)(2,1)}, bf16[112,512]{1,0:T(8,128)(2,1)S(1)}, u32[]{:S(2)}, u32[]{:S(2)}) collective-permute-start(bf16[112,512]{1,0:T(8,128)(2,1)} %get-tuple-element.44), channel_id=1, source_target_pairs={{0,1},{1,2},{2,3},{4,5},{5,6},{6,7},{8,9},{9,10},{10,11},{12,13},{... | collective-permute-start | bytes 344072 | tf_op jit(solution)/shard_map/ppermute | solution.py:715
  6.7 6.9 %collective-permute-start.1 = (bf16[112,512]{1,0:T(8,128)(2,1)}, bf16[112,512]{1,0:T(8,128)(2,1)S(1)}, u32[]{:S(2)}, u32[]{:S(2)}) collective-permute-start(bf16[112,512]{1,0:T(8,128)(2,1)} %get-tuple-element.45), channel_id=1, source_target_pairs={{1,0},{2,1},{3,2},{5,4},{6,5},{7,6},{9,8},{10,9},{11,10},{13,12},{... | collective-permute-start | bytes 344072 | tf_op jit(solution)/shard_map/ppermute | solution.py:715
  8.0 19.3 %collective-permute-start.2 = (bf16[400,384]{1,0:T(8,128)(2,1)}, bf16[400,384]{1,0:T(8,128)(2,1)S(1)}, u32[]{:S(2)}, u32[]{:S(2)}) collective-permute-start(bf16[400,384]{1,0:T(8,128)(2,1)} %get-tuple-element.50), channel_id=1, source_target_pairs={{0,4},{1,5},{2,6},{3,7},{4,8},{5,9},{6,10},{7,11},{8,12},{9,13},{1... | collective-permute-start | bytes 921608 | tf_op jit(solution)/shard_map/ppermute | solution.py:715
  12.3 15.0 %collective-permute-start.3 = (bf16[400,384]{1,0:T(8,128)(2,1)}, bf16[400,384]{1,0:T(8,128)(2,1)S(1)}, u32[]{:S(2)}, u32[]{:S(2)}) collective-permute-start(bf16[400,384]{1,0:T(8,128)(2,1)} %get-tuple-element.51), channel_id=1, source_target_pairs={{4,0},{5,1},{6,2},{7,3},{8,4},{9,5},{10,6},{11,7},{12,8},{13,9},{1... | collective-permute-start | bytes 921608 | tf_op jit(solution)/shard_map/ppermute | solution.py:715
  13.9 13.4 %collective-permute-start.4 = (bf16[64,384]{1,0:T(8,128)(2,1)S(1)}, bf16[64,384]{1,0:T(8,128)(2,1)S(1)}, u32[]{:S(2)}, u32[]{:S(2)}) collective-permute-start(bf16[64,384]{1,0:T(8,128)(2,1)S(1)} %get-tuple-element.52), channel_id=1, source_target_pairs={{0,4},{1,5},{2,6},{3,7},{4,8},{5,9},{6,10},{7,11},{8,12},{9,13},{1... | collective-permute-start | bytes 147464 | tf_op jit(solution)/shard_map/ppermute | solution.py:715
  18.5 8.8 %collective-permute-start.5 = (bf16[64,384]{1,0:T(8,128)(2,1)S(1)}, bf16[64,384]{1,0:T(8,128)(2,1)S(1)}, u32[]{:S(2)}, u32[]{:S(2)}) collective-permute-start(bf16[64,384]{1,0:T(8,128)(2,1)S(1)} %get-tuple-element.46.c_low), channel_id=1, source_target_pairs={{4,0},{5,1},{6,2},{7,3},{8,4},{9,5},{10,6},{11,7},{12,8},{13,9},{1... | collective-permute-start | bytes 147464 | tf_op jit(solution)/shard_map/ppermute | solution.py:715
  19.8 1.0 copy-start.3
  20.8 1.0 copy-start.4
  21.8 5.5 %copy-start.7 = (f32[16,128]{1,0:T(8,128)S(1)}, f32[16,128]{1,0:T(8,128)}, u32[]{:S(2)}) copy-start(f32[16,128]{1,0:T(8,128)} %get-tuple-element.48.flags) | copy-start | bytes 24580
  43.9 15.9 %copy-start.8 = (f32[80,48,128]{2,1,0:T(8,128)}, f32[80,48,128]{2,1,0:T(8,128)S(1)}, u32[]{:S(2)}) copy-start(f32[80,48,128]{2,1,0:T(8,128)S(1)} %get-tuple-element.60.hidden) | copy-start | bytes 5898244
  43.9 8.5 %collective-permute-start.6 = (bf16[5,48,128]{2,1,0:T(8,128)(2,1)S(1)}, bf16[5,48,128]{2,1,0:T(8,128)(2,1)S(1)}, u32[]{:S(2)}, u32[]{:S(2)}) collective-permute-start(bf16[5,48,128]{2,1,0:T(8,128)(2,1)S(1)} %get-tuple-element.58), channel_id=1, source_target_pairs={{0,4},{1,5},{2,6},{3,7},{4,8},{5,9},{6,10},{7,11},{8,12},{9,13},{1... | collective-permute-start | bytes 184328 | tf_op jit(solution)/shard_map/ppermute | solution.py:715
  48.3 8.0 %collective-permute-start.7 = (bf16[5,48,128]{2,1,0:T(8,128)(2,1)S(1)}, bf16[5,48,128]{2,1,0:T(8,128)(2,1)S(1)}, u32[]{:S(2)}, u32[]{:S(2)}) collective-permute-start(bf16[5,48,128]{2,1,0:T(8,128)(2,1)S(1)} %get-tuple-element.59), channel_id=1, source_target_pairs={{4,0},{5,1},{6,2},{7,3},{8,4},{9,5},{10,6},{11,7},{12,8},{13,9},{1... | collective-permute-start | bytes 184328 | tf_op jit(solution)/shard_map/ppermute | solution.py:715
  66.6 19.0 %all-to-all-start = ((bf16[32,40,128]{2,1,0:T(8,128)(2,1)}), bf16[32,40,128]{2,1,0:T(8,128)(2,1)S(1)}, u32[]{:S(2)}, u32[]{:S(2)}) async-start(bf16[32,40,128]{2,1,0:T(8,128)(2,1)} %bitcast.6), calls=%async_computation | async-start | bytes 655360 | tf_op jit(solution)/shard_map/all_to_all | solution.py:723
  73.6 6.2 %copy-start.9 = (f32[80,48,128]{2,1,0:T(8,128)S(1)}, f32[80,48,128]{2,1,0:T(8,128)}, u32[]{:S(2)}) copy-start(f32[80,48,128]{2,1,0:T(8,128)} %copy-done.8) | copy-start | bytes 5898244
  74.8 16.5 %collective-permute-start.8 = (bf16[10,48,128]{2,1,0:T(8,128)(2,1)S(1)}, bf16[10,48,128]{2,1,0:T(8,128)(2,1)S(1)}, u32[]{:S(2)}, u32[]{:S(2)}) collective-permute-start(bf16[10,48,128]{2,1,0:T(8,128)(2,1)S(1)} %get-tuple-element.74), channel_id=1, source_target_pairs={{0,4},{1,5},{2,6},{3,7},{4,8},{5,9},{6,10},{7,11},{8,12},{9,13},{1... | collective-permute-start | bytes 368648 | tf_op jit(solution)/shard_map/ppermute | solution.py:715
  78.5 12.9 %collective-permute-start.9 = (bf16[10,48,128]{2,1,0:T(8,128)(2,1)S(1)}, bf16[10,48,128]{2,1,0:T(8,128)(2,1)S(1)}, u32[]{:S(2)}, u32[]{:S(2)}) collective-permute-start(bf16[10,48,128]{2,1,0:T(8,128)(2,1)S(1)} %get-tuple-element.75), channel_id=1, source_target_pairs={{4,0},{5,1},{6,2},{7,3},{8,4},{9,5},{10,6},{11,7},{12,8},{13,9},{1... | collective-permute-start | bytes 368648 | tf_op jit(solution)/shard_map/ppermute | solution.py:715
  86.4 16.9 %all-to-all-start.1 = ((bf16[32,40,128]{2,1,0:T(8,128)(2,1)}), bf16[32,40,128]{2,1,0:T(8,128)(2,1)S(1)}, u32[]{:S(2)}, u32[]{:S(2)}) async-start(bf16[32,40,128]{2,1,0:T(8,128)(2,1)} %sum_kernel.1), calls=%async_computation.1 | async-start | bytes 655360 | tf_op jit(solution)/shard_map/all_to_all | solution.py:729

commit v18 on v17

--- a/solution.py
+++ b/solution.py
@@ -127,7 +127,7 @@
                 parts = [a + b for a, b in zip(parts[::2], parts[1::2])]
             out[group] = parts[0]
 
-    loop(0, low.shape[0], body)
+    loop(0, low.shape[0], body, 5)
 
 
 def own_masks():
@@ -342,7 +342,7 @@
         fill(even, jnp.minimum(tile + 8, tiles - 4))
         return multiply(odd, tile + 4, carry)
 
-    unroll = 3 if tiles % 24 == 0 else 5
+    unroll = 6 if tiles % 48 == 0 else 10 if tiles % 80 == 0 else 5
     lax.fori_loop(0, tiles // 8, body, jnp.zeros((C, LANES), F32), unroll=unroll)
 
 
@@ -407,7 +407,7 @@
             total = gather_sub(parts[:, LANES * inner : LANES * (inner + 1)])
             lowered[4 * block + inner] = (total * keep).astype(BF16)
 
-    loop(0, last + 1, lower_step, 3)
+    loop(0, last + 1, lower_step, 6)
     pairs = hidden.shape[0] // EDGE
     shift = last - pairs + 1
     edges = edge_masks(2)
@@ -524,7 +524,7 @@
             jnp.concatenate(spreads, axis=1), jnp.concatenate(pairs, axis=1), (1, 1)
         )
 
-    loop(0, (tiles - 8) // 8, up_step, 2)
+    loop(0, (tiles - 8) // 8, up_step, 4)
     zero = jnp.zeros((C, LANES), BF16)
     for coarse in range(1, 4):
         grad_own[coarse] = zero
@@ -543,7 +543,7 @@
             jnp.concatenate(rights, axis=1), stacks(grad_own, at), (1, 1)
         )
 
-    loop(0, (tiles - 4) // 18, weight_step)
+    loop(0, (tiles - 4) // 18, weight_step, 2)
     rest = flatten_weights(coarse_g, flat)
     flat[9 * C : 12 * C, :] = squeeze_rows(up_g[...], 3 * C).astype(BF16)
     flat[12 * C :, :] = roll(rest, C).astype(BF16)
@@ -626,7 +626,7 @@
             jnp.concatenate(lefts, axis=1), jnp.concatenate(rights, axis=1), (1, 1)
         )
 
-    loop(0, (tiles // 2 - 8) // 8, down_step, 2)
+    loop(0, (tiles // 2 - 8) // 8, down_step, 4)
     rest = flatten_weights(fine_g, joined) + early[12 * C :, :].astype(F32)
     joined[9 * C : 18 * C, :] = early[0 : 9 * C, :]
     joined[18 * C : 21 * C, :] = squeeze_rows(down_g[...], 3 * C).astype(BF16)

time: 106 us -> 106 us (level)
  transfers between devices with their start and end apart: 12 -> 12, of which waited for: 4 -> 4; matrix products, arithmetic and copies ran while one was open for 0% -> 0% of each run, Pallas kernels for 19% -> 18%
where the time goes in v18:
time: 106 us
  Pallas kernels  52.1 us (49%)
  starting transfers between devices  37.4 us (35%)
  waiting for transfers between devices  12.6 us (12%)
  local copies, waits for them, and re-layouts  1.98 us (2%)
  between operations  1.72 us (2%)
    pallas_call x12, Pallas kernels, call(): pl.pallas_call(kernel, out_shape=tuple((jax.ShapeDtypeStruct(s, d) for s,...  52.1 us
    ppermute x10, starting transfers between devices, send(): return lax.ppermute(array, ('gx', 'gy'), pairs)  25.8 us
    all_to_all x1, starting transfers between devices, reduce_share(): lax.all_to_all(joined.reshape(devices, share, LANES), ('gx', 'gy'), 0, 0)  7 us
    ppermute x10, waiting for transfers between devices, send(): return lax.ppermute(array, ('gx', 'gy'), pairs)  5.85 us
    all_to_all x1, starting transfers between devices, spread_share(): full = lax.all_to_all(copies, ('gx', 'gy'), 0, 0)  4.6 us
    all_to_all x1, waiting for transfers between devices, spread_share(): full = lax.all_to_all(copies, ('gx', 'gy'), 0, 0)  4.4 us
    all_to_all x1, waiting for transfers between devices, reduce_share(): lax.all_to_all(joined.reshape(devices, share, LANES), ('gx', 'gy'), 0, 0)  2.33 us
  transfers between devices with their start and end apart: 12, of which 4 were waited for; matrix products, arithmetic and copies ran while one was open for 0% of the time, Pallas kernels for 18%

profile of v18, /device:TPU:0, one launch (start us, length us, event | category | flops | bytes accessed | tf_op | source)
XLA Modules:
  0.0 105.8 jit_solution(3603610086484364448)
XLA Ops:
  1.5 2.9 %prepare_kernel.1 = (f32[16,128]{1,0:T(8,128)}, bf16[400,384]{1,0:T(8,128)(2,1)}, bf16[400,384]{1,0:T(8,128)(2,1)}, bf16[112,512]{1,0:T(8,128)(2,1)}, bf16[112,512]{1,0:T(8,128)(2,1)}) custom-call(s32[16]{0:T(128)} %bitcast.19, s32[1]{0:T(128)} %bitcast.12.count, bf16[16,48,512]{2,1,0:T(8,128)(2,1)} %bitcast.15, bf16[16,48,512]{2,1,0:T(8,128)(2,1)} %bitcast.17), custom_call_target="tpu_custom_call" | custom-call | bytes 2424900 | tf_op jit(solution)/shard_map/prepare_kernel/pallas_call | solution.py:695
  4.4 2.3 %collective-permute-start = (bf16[112,512]{1,0:T(8,128)(2,1)}, bf16[112,512]{1,0:T(8,128)(2,1)S(1)}, u32[]{:S(2)}, u32[]{:S(2)}) collective-permute-start(bf16[112,512]{1,0:T(8,128)(2,1)} %get-tuple-element.44), channel_id=1, source_target_pairs={{0,1},{1,2},{2,3},{4,5},{5,6},{6,7},{8,9},{9,10},{10,11},{12,13},{... | collective-permute-start | bytes 344072 | tf_op jit(solution)/shard_map/ppermute | solution.py:715
  6.7 1.3 %collective-permute-start.1 = (bf16[112,512]{1,0:T(8,128)(2,1)}, bf16[112,512]{1,0:T(8,128)(2,1)S(1)}, u32[]{:S(2)}, u32[]{:S(2)}) collective-permute-start(bf16[112,512]{1,0:T(8,128)(2,1)} %get-tuple-element.45), channel_id=1, source_target_pairs={{1,0},{2,1},{3,2},{5,4},{6,5},{7,6},{9,8},{10,9},{11,10},{13,12},{... | collective-permute-start | bytes 344072 | tf_op jit(solution)/shard_map/ppermute | solution.py:715
  8.0 4.2 %collective-permute-start.2 = (bf16[400,384]{1,0:T(8,128)(2,1)}, bf16[400,384]{1,0:T(8,128)(2,1)S(1)}, u32[]{:S(2)}, u32[]{:S(2)}) collective-permute-start(bf16[400,384]{1,0:T(8,128)(2,1)} %get-tuple-element.50), channel_id=1, source_target_pairs={{0,4},{1,5},{2,6},{3,7},{4,8},{5,9},{6,10},{7,11},{8,12},{9,13},{1... | collective-permute-start | bytes 921608 | tf_op jit(solution)/shard_map/ppermute | solution.py:715
  12.3 1.3 %collective-permute-start.3 = (bf16[400,384]{1,0:T(8,128)(2,1)}, bf16[400,384]{1,0:T(8,128)(2,1)S(1)}, u32[]{:S(2)}, u32[]{:S(2)}) collective-permute-start(bf16[400,384]{1,0:T(8,128)(2,1)} %get-tuple-element.51), channel_id=1, source_target_pairs={{4,0},{5,1},{6,2},{7,3},{8,4},{9,5},{10,6},{11,7},{12,8},{13,9},{1... | collective-permute-start | bytes 921608 | tf_op jit(solution)/shard_map/ppermute | solution.py:715
  13.6 0.0 collective-permute-done.y_left
  13.6 0.3 corner_kernel.1
  13.9 4.5 %collective-permute-start.4 = (bf16[64,384]{1,0:T(8,128)(2,1)S(1)}, bf16[64,384]{1,0:T(8,128)(2,1)S(1)}, u32[]{:S(2)}, u32[]{:S(2)}) collective-permute-start(bf16[64,384]{1,0:T(8,128)(2,1)S(1)} %get-tuple-element.52), channel_id=1, source_target_pairs={{0,4},{1,5},{2,6},{3,7},{4,8},{5,9},{6,10},{7,11},{8,12},{9,13},{1... | collective-permute-start | bytes 147464 | tf_op jit(solution)/shard_map/ppermute | solution.py:715
  18.5 1.3 %collective-permute-start.5 = (bf16[64,384]{1,0:T(8,128)(2,1)S(1)}, bf16[64,384]{1,0:T(8,128)(2,1)S(1)}, u32[]{:S(2)}, u32[]{:S(2)}) collective-permute-start(bf16[64,384]{1,0:T(8,128)(2,1)S(1)} %get-tuple-element.46.c_low), channel_id=1, source_target_pairs={{4,0},{5,1},{6,2},{7,3},{8,4},{9,5},{10,6},{11,7},{12,8},{13,9},{1... | collective-permute-start | bytes 147464 | tf_op jit(solution)/shard_map/ppermute | solution.py:715
  19.8 0.0 copy-start.3
  19.8 1.0 copy-done.3
  20.8 1.0 copy-done.4
  21.8 4.0 %place_kernel.1 = (bf16[144,48,128]{2,1,0:T(8,128)(2,1)S(1)}, bf16[80,48,128]{2,1,0:T(8,128)(2,1)S(1)}, f32[40,48,128]{2,1,0:T(8,128)S(1)}, bf16[144,432]{1,0:T(...) custom-call(s32[16]{0:T(128)S(1)} %bitcast.20, ...), custom_call_target="tpu_custom_call" | custom-call | flops 8000000000 | bytes 6480964 | tf_op jit(solution)/shard_map/place_kernel/pallas_call | solution.py:695
  25.8 1.4 %collective-permute-done.4.c_left = bf16[64,384]{1,0:T(8,128)(2,1)S(1)} collective-permute-done((bf16[64,384]{1,0:T(8,128)(2,1)S(1)}, bf16[64,384]{1,0:T(8,128)(2,1)S(1)}, u32[]{:S(2)}, u32[]{:S(2)}) %collective-permute-start.4) | collective-permute-done | bytes 49184 | tf_op jit(solution)/shard_map/ppermute | solution.py:715
  27.3 18.0 %forward_kernel.1 = (bf16[144,48,128]{2,1,0:T(8,128)(2,1)S(1)}, f32[80,48,128]{2,1,0:T(8,128)S(1)}, bf16[40,144,128]{2,1,0:T(8,128)(2,1)S(1)}, bf16[40,48,128]{2...) custom-call(bf16[144,48,128]{2,1,0:T(8,128)(2,1)S(1)} %get-tuple-ele, ...), custom_call_target="tpu_custom_call" | custom-call | flops 8000000000 | bytes 10312704 | tf_op jit(solution)/shard_map/forward_kernel/pallas_call | solution.py:695
  45.4 4.4 %collective-permute-start.6 = (bf16[5,48,128]{2,1,0:T(8,128)(2,1)S(1)}, bf16[5,48,128]{2,1,0:T(8,128)(2,1)S(1)}, u32[]{:S(2)}, u32[]{:S(2)}) collective-permute-start(bf16[5,48,128]{2,1,0:T(8,128)(2,1)S(1)} %get-tuple-element.58), channel_id=1, source_target_pairs={{0,4},{1,5},{2,6},{3,7},{4,8},{5,9},{6,10},{7,11},{8,12},{9,13},{1... | collective-permute-start | bytes 184328 | tf_op jit(solution)/shard_map/ppermute | solution.py:715
  49.8 1.5 %collective-permute-start.7 = (bf16[5,48,128]{2,1,0:T(8,128)(2,1)S(1)}, bf16[5,48,128]{2,1,0:T(8,128)(2,1)S(1)}, u32[]{:S(2)}, u32[]{:S(2)}) collective-permute-start(bf16[5,48,128]{2,1,0:T(8,128)(2,1)S(1)} %get-tuple-element.59), channel_id=1, source_target_pairs={{4,0},{5,1},{6,2},{7,3},{8,4},{9,5},{10,6},{11,7},{12,8},{13,9},{1... | collective-permute-start | bytes 184328 | tf_op jit(solution)/shard_map/ppermute | solution.py:715
  51.2 2.1 %side_kernel.1.early = bf16[720,128]{1,0:T(8,128)(2,1)S(1)} custom-call(bf16[40,48,128]{2,1,0:T(8,128)(2,1)S(1)} %get-tuple-element.66.rects, bf16[80,48,128]{2,1,0:T(8,128)(2,1)S(1)} %get-tuple-element.61.cot_grid, bf16[40,144,128]{2,1,0:T(8,128)(2,1)S(1)} %get-tuple-element.67.low_cols, bf16[40,48,128]{2,1,0:T(8,128)(2,1)S(1)} %get-tuple-element.57.grad_c), custom_call_target="tpu_custom_call" | custom-call | flops 8000000000 | bytes 3624960 | tf_op jit(solution)/shard_map/side_kernel/pallas_call | solution.py:695
  53.4 4.4 %collective-permute-done.7.from_right = bf16[5,48,128]{2,1,0:T(8,128)(2,1)S(1)} collective-permute-done((bf16[5,48,128]{2,1,0:T(8,128)(2,1)S(1)}, bf16[5,48,128]{2,1,0:T(8,128)(2,1)S(1)}, u32[]{:S(2)}, u32[]{:S(2)}) %collective-permute-start.7) | collective-permute-done | bytes 61472 | tf_op jit(solution)/shard_map/ppermute | solution.py:715
  57.7 3.5 %backward_kernel.1 = (bf16[80,48,128]{2,1,0:T(8,128)(2,1)S(1)}, bf16[40,48,128]{2,1,0:T(8,128)(2,1)S(1)}) custom-call(bf16[40,48,128]{2,1,0:T(8,128)(2,1)S(1)} %get-tuple-element.57.grad_c, bf16[5,48,128]{2,1,0:T(8,128)(2,1)S(1)} %collective-permute-done.6.from_left, bf16[5,48,128]{2,1,0:T(8,128)(2,1)S(1)} %collective-permute-done.7.from_right, ...), custom_call_target="tpu_custom_call" | custom-call | flops 8000000000 | bytes 5207552 | tf_op jit(solution)/shard_map/backward_kernel/pallas_call | solution.py:695
  61.3 6.5 %weight_kernel.1 = bf16[1280,128]{1,0:T(8,128)(2,1)} custom-call(bf16[144,48,128]{2,1,0:T(8,128)(2,1)S(1)} %get-tuple-element.56.grid, bf16[80,48,128]{2,1,0:T(8,128)(2,1)S(1)} %get-tuple-element.73.grad_h, bf16[40,48,128]{2,1,0:T(8,128)(2,1)S(1)} %get-tuple-element.65.grad_d, f32[80,48,128]{2,1,0:T(8,128)S(1)} %get-tuple-element.60.hidden, ...), custom_call_target="tpu_custom_call" | custom-call | flops 12000000000 | bytes 5722112 | tf_op jit(solution)/shard_map/weight_kernel/pallas_call | solution.py:695
  67.8 7.0 %all-to-all-start = ((bf16[32,40,128]{2,1,0:T(8,128)(2,1)}), bf16[32,40,128]{2,1,0:T(8,128)(2,1)S(1)}, u32[]{:S(2)}, u32[]{:S(2)}) async-start(bf16[32,40,128]{2,1,0:T(8,128)(2,1)} %bitcast.6), calls=%async_computation | async-start | bytes 655360 | tf_op jit(solution)/shard_map/all_to_all | solution.py:723
  74.8 0.6 pack_kernel.1
  75.4 3.7 %collective-permute-start.8 = (bf16[10,48,128]{2,1,0:T(8,128)(2,1)S(1)}, bf16[10,48,128]{2,1,0:T(8,128)(2,1)S(1)}, u32[]{:S(2)}, u32[]{:S(2)}) collective-permute-start(bf16[10,48,128]{2,1,0:T(8,128)(2,1)S(1)} %get-tuple-element.74), channel_id=1, source_target_pairs={{0,4},{1,5},{2,6},{3,7},{4,8},{5,9},{6,10},{7,11},{8,12},{9,13},{1... | collective-permute-start | bytes 368648 | tf_op jit(solution)/shard_map/ppermute | solution.py:715
  79.1 1.3 %collective-permute-start.9 = (bf16[10,48,128]{2,1,0:T(8,128)(2,1)S(1)}, bf16[10,48,128]{2,1,0:T(8,128)(2,1)S(1)}, u32[]{:S(2)}, u32[]{:S(2)}) collective-permute-start(bf16[10,48,128]{2,1,0:T(8,128)(2,1)S(1)} %get-tuple-element.75), channel_id=1, source_target_pairs={{4,0},{5,1},{6,2},{7,3},{8,4},{9,5},{10,6},{11,7},{12,8},{13,9},{1... | collective-permute-start | bytes 368648 | tf_op jit(solution)/shard_map/ppermute | solution.py:715
  80.4 4.0 %output_kernel.1 = bf16[16,48,512]{2,1,0:T(8,128)(2,1)} custom-call(s32[16]{0:T(128)S(1)} %bitcast.21, f32[80,48,128]{2,1,0:T(8,128)S(1)} %copy-done.9, bf16[40,48,128]{2,1,0:T(8,128)(2,1)S(1)} %get-tuple-element.66.rects, f32[16,128]{1,0:T(8,128)S(1)} %get-tuple-element.62.live, bf16[96,192]{1,0:T(8,128)(2,1)S(1)} %get-tuple-element.70.up_w), custom_call_target="tpu_custom_call" | custom-call | flops 8000000000 | bytes 3289152 | tf_op jit(solution)/shard_map/output_kernel/pallas_call | solution.py:695
  84.5 2.3 %all-to-all-done.parts = bf16[32,40,128]{2,1,0:T(8,128)(2,1)S(1)} async-done(((bf16[32,40,128]{2,1,0:T(8,128)(2,1)}), bf16[32,40,128]{2,1,0:T(8,128)(2,1)S(1)}, u32[]{:S(2)}, u32[]{:S(2)}) %all-to-all-start) | async-done | bytes 327712 | tf_op jit(solution)/shard_map/all_to_all | solution.py:723
  86.8 0.8 sum_kernel.1
  87.6 4.6 %all-to-all-start.1 = ((bf16[32,40,128]{2,1,0:T(8,128)(2,1)}), bf16[32,40,128]{2,1,0:T(8,128)(2,1)S(1)}, u32[]{:S(2)}, u32[]{:S(2)}) async-start(bf16[32,40,128]{2,1,0:T(8,128)(2,1)} %sum_kernel.1), calls=%async_computation.1 | async-start | bytes 655360 | tf_op jit(solution)/shard_map/all_to_all | solution.py:729
  92.2 7.3 %input_kernel.1 = bf16[16,48,512]{2,1,0:T(8,128)(2,1)} custom-call(s32[16]{0:T(128)S(1)} %bitcast.22, bf16[80,48,128]{2,1,0:T(8,128)(2,1)S(1)} %get-tuple-element.73.grad_h, bf16[10,48,128]{2,1,0:T(8,128)(2,1)S(1)} %collective-permute-done.8.from_left, bf16[10,48,128]{2,1,0:T(8,128)(2,1)S(1)} %collective-permute-done.9.from_right, ...), custom_call_target="tpu_custom_call" | custom-call | flops 8000000000 | bytes 2147904 | tf_op jit(solution)/shard_map/input_kernel/pallas_call | solution.py:695
  99.6 4.4 %all-to-all-done.1 = bf16[32,40,128]{2,1,0:T(8,128)(2,1)S(1)} async-done(((bf16[32,40,128]{2,1,0:T(8,128)(2,1)}), bf16[32,40,128]{2,1,0:T(8,128)(2,1)S(1)}, u32[]{:S(2)}, u32[]{:S(2)}) %all-to-all-start.1) | async-done | bytes 327712 | tf_op jit(solution)/shard_map/all_to_all | solution.py:729
  104.0 1.9 %finish_kernel.1 = (f32[27,48,48]{2,1,0:T(8,128)}, f32[48,8,48]{2,1,0:T(8,128)}, f32[27,48,48]{2,1,0:T(8,128)}, f32[8,48,48]{2,1,0:T(8,128)}) custom-call(bf16[1280,128]{1,0:T(8,128)(2,1)S(1)} %bitcast.14), custom_call_target="tpu_custom_call" | custom-call | bytes 972800 | tf_op jit(solution)/shard_map/finish_kernel/pallas_call | solution.py:695
  (24 shorter events, 0.1 us)
Async XLA Ops:
  0.6 19.2 %copy-start.1 = (bf16[1,1,16,48,512]{4,3,2,1,0:T(8,128)(2,1)S(1)}, bf16[1,1,16,48,512]{4,3,2,1,0:T(8,128)(2,1)}, u32[]{:S(2)}) copy-start(bf16[1,1,16,48,512]{4,3,2,1,0:T(8,128)(2,1)} %param.11) | copy-start | bytes 2359300
  0.6 19.2 %copy-start.2 = (s32[1,1,16]{2,1,0:T(1,128)S(1)}, s32[1,1,16]{2,1,0:T(1,128)}, u32[]{:S(2)}) copy-start(s32[1,1,16]{2,1,0:T(1,128)} %param.9) | copy-start | bytes 196
  0.7 19.2 %copy-start = (bf16[1,1,16,48,512]{4,3,2,1,0:T(8,128)(2,1)S(1)}, bf16[1,1,16,48,512]{4,3,2,1,0:T(8,128)(2,1)}, u32[]{:S(2)}) copy-start(bf16[1,1,16,48,512]{4,3,2,1,0:T(8,128)(2,1)} %param.8) | copy-start | bytes 2359300
  0.7 19.2 %copy-start.6 = (bf16[8,48,48]{2,1,0:T(8,128)(2,1)S(1)}, bf16[8,48,48]{2,1,0:T(8,128)(2,1)}, u32[]{:S(2)}) copy-start(bf16[8,48,48]{2,1,0:T(8,128)(2,1)} %up.1) | copy-start | bytes 110596
  0.7 19.2 %copy-start.5 = (bf16[48,8,48]{2,1,0:T(8,128)(2,1)S(1)}, bf16[48,8,48]{2,1,0:T(8,128)(2,1)}, u32[]{:S(2)}) copy-start(bf16[48,8,48]{2,1,0:T(8,128)(2,1)} %down.1) | copy-start | bytes 110596
  4.4 9.2 %collective-permute-start = (bf16[112,512]{1,0:T(8,128)(2,1)}, bf16[112,512]{1,0:T(8,128)(2,1)S(1)}, u32[]{:S(2)}, u32[]{:S(2)}) collective-permute-start(bf16[112,512]{1,0:T(8,128)(2,1)} %get-tuple-element.44), channel_id=1, source_target_pairs={{0,1},{1,2},{2,3},{4,5},{5,6},{6,7},{8,9},{9,10},{10,11},{12,13},{... | collective-permute-start | bytes 344072 | tf_op jit(solution)/shard_map/ppermute | solution.py:715
  6.7 6.9 %collective-permute-start.1 = (bf16[112,512]{1,0:T(8,128)(2,1)}, bf16[112,512]{1,0:T(8,128)(2,1)S(1)}, u32[]{:S(2)}, u32[]{:S(2)}) collective-permute-start(bf16[112,512]{1,0:T(8,128)(2,1)} %get-tuple-element.45), channel_id=1, source_target_pairs={{1,0},{2,1},{3,2},{5,4},{6,5},{7,6},{9,8},{10,9},{11,10},{13,12},{... | collective-permute-start | bytes 344072 | tf_op jit(solution)/shard_map/ppermute | solution.py:715
  8.0 19.3 %collective-permute-start.2 = (bf16[400,384]{1,0:T(8,128)(2,1)}, bf16[400,384]{1,0:T(8,128)(2,1)S(1)}, u32[]{:S(2)}, u32[]{:S(2)}) collective-permute-start(bf16[400,384]{1,0:T(8,128)(2,1)} %get-tuple-element.50), channel_id=1, source_target_pairs={{0,4},{1,5},{2,6},{3,7},{4,8},{5,9},{6,10},{7,11},{8,12},{9,13},{1... | collective-permute-start | bytes 921608 | tf_op jit(solution)/shard_map/ppermute | solution.py:715
  12.3 15.0 %collective-permute-start.3 = (bf16[400,384]{1,0:T(8,128)(2,1)}, bf16[400,384]{1,0:T(8,128)(2,1)S(1)}, u32[]{:S(2)}, u32[]{:S(2)}) collective-permute-start(bf16[400,384]{1,0:T(8,128)(2,1)} %get-tuple-element.51), channel_id=1, source_target_pairs={{4,0},{5,1},{6,2},{7,3},{8,4},{9,5},{10,6},{11,7},{12,8},{13,9},{1... | collective-permute-start | bytes 921608 | tf_op jit(solution)/shard_map/ppermute | solution.py:715
  13.9 13.4 %collective-permute-start.4 = (bf16[64,384]{1,0:T(8,128)(2,1)S(1)}, bf16[64,384]{1,0:T(8,128)(2,1)S(1)}, u32[]{:S(2)}, u32[]{:S(2)}) collective-permute-start(bf16[64,384]{1,0:T(8,128)(2,1)S(1)} %get-tuple-element.52), channel_id=1, source_target_pairs={{0,4},{1,5},{2,6},{3,7},{4,8},{5,9},{6,10},{7,11},{8,12},{9,13},{1... | collective-permute-start | bytes 147464 | tf_op jit(solution)/shard_map/ppermute | solution.py:715
  18.5 8.8 %collective-permute-start.5 = (bf16[64,384]{1,0:T(8,128)(2,1)S(1)}, bf16[64,384]{1,0:T(8,128)(2,1)S(1)}, u32[]{:S(2)}, u32[]{:S(2)}) collective-permute-start(bf16[64,384]{1,0:T(8,128)(2,1)S(1)} %get-tuple-element.46.c_low), channel_id=1, source_target_pairs={{4,0},{5,1},{6,2},{7,3},{8,4},{9,5},{10,6},{11,7},{12,8},{13,9},{1... | collective-permute-start | bytes 147464 | tf_op jit(solution)/shard_map/ppermute | solution.py:715
  19.8 1.0 copy-start.3
  20.8 1.0 copy-start.4
  21.8 5.5 %copy-start.7 = (f32[16,128]{1,0:T(8,128)S(1)}, f32[16,128]{1,0:T(8,128)}, u32[]{:S(2)}) copy-start(f32[16,128]{1,0:T(8,128)} %get-tuple-element.48.flags) | copy-start | bytes 24580
  45.4 15.9 %copy-start.8 = (f32[80,48,128]{2,1,0:T(8,128)}, f32[80,48,128]{2,1,0:T(8,128)S(1)}, u32[]{:S(2)}) copy-start(f32[80,48,128]{2,1,0:T(8,128)S(1)} %get-tuple-element.60.hidden) | copy-start | bytes 5898244
  45.4 8.0 %collective-permute-start.6 = (bf16[5,48,128]{2,1,0:T(8,128)(2,1)S(1)}, bf16[5,48,128]{2,1,0:T(8,128)(2,1)S(1)}, u32[]{:S(2)}, u32[]{:S(2)}) collective-permute-start(bf16[5,48,128]{2,1,0:T(8,128)(2,1)S(1)} %get-tuple-element.58), channel_id=1, source_target_pairs={{0,4},{1,5},{2,6},{3,7},{4,8},{5,9},{6,10},{7,11},{8,12},{9,13},{1... | collective-permute-start | bytes 184328 | tf_op jit(solution)/shard_map/ppermute | solution.py:715
  49.8 8.0 %collective-permute-start.7 = (bf16[5,48,128]{2,1,0:T(8,128)(2,1)S(1)}, bf16[5,48,128]{2,1,0:T(8,128)(2,1)S(1)}, u32[]{:S(2)}, u32[]{:S(2)}) collective-permute-start(bf16[5,48,128]{2,1,0:T(8,128)(2,1)S(1)} %get-tuple-element.59), channel_id=1, source_target_pairs={{4,0},{5,1},{6,2},{7,3},{8,4},{9,5},{10,6},{11,7},{12,8},{13,9},{1... | collective-permute-start | bytes 184328 | tf_op jit(solution)/shard_map/ppermute | solution.py:715
  67.8 19.0 %all-to-all-start = ((bf16[32,40,128]{2,1,0:T(8,128)(2,1)}), bf16[32,40,128]{2,1,0:T(8,128)(2,1)S(1)}, u32[]{:S(2)}, u32[]{:S(2)}) async-start(bf16[32,40,128]{2,1,0:T(8,128)(2,1)} %bitcast.6), calls=%async_computation | async-start | bytes 655360 | tf_op jit(solution)/shard_map/all_to_all | solution.py:723
  74.8 5.6 %copy-start.9 = (f32[80,48,128]{2,1,0:T(8,128)S(1)}, f32[80,48,128]{2,1,0:T(8,128)}, u32[]{:S(2)}) copy-start(f32[80,48,128]{2,1,0:T(8,128)} %copy-done.8) | copy-start | bytes 5898244
  75.4 16.8 %collective-permute-start.8 = (bf16[10,48,128]{2,1,0:T(8,128)(2,1)S(1)}, bf16[10,48,128]{2,1,0:T(8,128)(2,1)S(1)}, u32[]{:S(2)}, u32[]{:S(2)}) collective-permute-start(bf16[10,48,128]{2,1,0:T(8,128)(2,1)S(1)} %get-tuple-element.74), channel_id=1, source_target_pairs={{0,4},{1,5},{2,6},{3,7},{4,8},{5,9},{6,10},{7,11},{8,12},{9,13},{1... | collective-permute-start | bytes 368648 | tf_op jit(solution)/shard_map/ppermute | solution.py:715
  79.1 13.1 %collective-permute-start.9 = (bf16[10,48,128]{2,1,0:T(8,128)(2,1)S(1)}, bf16[10,48,128]{2,1,0:T(8,128)(2,1)S(1)}, u32[]{:S(2)}, u32[]{:S(2)}) collective-permute-start(bf16[10,48,128]{2,1,0:T(8,128)(2,1)S(1)} %get-tuple-element.75), channel_id=1, source_target_pairs={{4,0},{5,1},{6,2},{7,3},{8,4},{9,5},{10,6},{11,7},{12,8},{13,9},{1... | collective-permute-start | bytes 368648 | tf_op jit(solution)/shard_map/ppermute | solution.py:715
  87.6 16.4 %all-to-all-start.1 = ((bf16[32,40,128]{2,1,0:T(8,128)(2,1)}), bf16[32,40,128]{2,1,0:T(8,128)(2,1)S(1)}, u32[]{:S(2)}, u32[]{:S(2)}) async-start(bf16[32,40,128]{2,1,0:T(8,128)(2,1)} %sum_kernel.1), calls=%async_computation.1 | async-start | bytes 655360 | tf_op jit(solution)/shard_map/all_to_all | solution.py:729

commit v19 on v18

--- a/solution.py
+++ b/solution.py
@@ -342,7 +342,7 @@
         fill(even, jnp.minimum(tile + 8, tiles - 4))
         return multiply(odd, tile + 4, carry)
 
-    unroll = 6 if tiles % 48 == 0 else 10 if tiles % 80 == 0 else 5
+    unroll = 3 if tiles % 24 == 0 else 10 if tiles % 80 == 0 else 5
     lax.fori_loop(0, tiles // 8, body, jnp.zeros((C, LANES), F32), unroll=unroll)
 
 
@@ -407,7 +407,7 @@
             total = gather_sub(parts[:, LANES * inner : LANES * (inner + 1)])
             lowered[4 * block + inner] = (total * keep).astype(BF16)
 
-    loop(0, last + 1, lower_step, 6)
+    loop(0, last + 1, lower_step, 3)
     pairs = hidden.shape[0] // EDGE
     shift = last - pairs + 1
     edges = edge_masks(2)

time: 106 us -> 105 us (level)
  Pallas kernels: 52.1 us -> 50.3 us
    pallas_call x12, Pallas kernels: 52.1 us -> 50.3 us  [call(): pl.pallas_call(kernel, out_shape=tuple((jax.ShapeDtypeStruct(s, d) for s,...]
where the time goes in v19:
time: 105 us; the launch traced here: 104 us
  Pallas kernels  50.3 us (48%)
  starting transfers between devices  37.4 us (36%)
  waiting for transfers between devices  12.6 us (12%)
  local copies, waits for them, and re-layouts  1.98 us (2%)
  between operations  1.72 us (2%)
    pallas_call x12, Pallas kernels, call(): pl.pallas_call(kernel, out_shape=tuple((jax.ShapeDtypeStruct(s, d) for s,...  50.3 us
    ppermute x10, starting transfers between devices, send(): return lax.ppermute(array, ('gx', 'gy'), pairs)  25.8 us
    all_to_all x1, starting transfers between devices, reduce_share(): lax.all_to_all(joined.reshape(devices, share, LANES), ('gx', 'gy'), 0, 0)  7 us
    ppermute x10, waiting for transfers between devices, send(): return lax.ppermute(array, ('gx', 'gy'), pairs)  5.84 us
    all_to_all x1, starting transfers between devices, spread_share(): full = lax.all_to_all(copies, ('gx', 'gy'), 0, 0)  4.6 us
    all_to_all x1, waiting for transfers between devices, spread_share(): full = lax.all_to_all(copies, ('gx', 'gy'), 0, 0)  4.4 us
    all_to_all x1, waiting for transfers between devices, reduce_share(): lax.all_to_all(joined.reshape(devices, share, LANES), ('gx', 'gy'), 0, 0)  2.33 us
  transfers between devices with their start and end apart: 12, of which 4 were waited for; matrix products, arithmetic and copies ran while one was open for 0% of the time, Pallas kernels for 18%

profile of v19, /device:TPU:0, one launch (start us, length us, event | category | flops | bytes accessed | tf_op | source)
XLA Modules:
  0.0 104.1 jit_solution(6745623536467281228)
XLA Ops:
  1.5 2.9 %prepare_kernel.1 = (f32[16,128]{1,0:T(8,128)}, bf16[400,384]{1,0:T(8,128)(2,1)}, bf16[400,384]{1,0:T(8,128)(2,1)}, bf16[112,512]{1,0:T(8,128)(2,1)}, bf16[112,512]{1,0:T(8,128)(2,1)}) custom-call(s32[16]{0:T(128)} %bitcast.19, s32[1]{0:T(128)} %bitcast.12.count, bf16[16,48,512]{2,1,0:T(8,128)(2,1)} %bitcast.15, bf16[16,48,512]{2,1,0:T(8,128)(2,1)} %bitcast.17), custom_call_target="tpu_custom_call" | custom-call | bytes 2424900 | tf_op jit(solution)/shard_map/prepare_kernel/pallas_call | solution.py:695
  4.4 2.3 %collective-permute-start = (bf16[112,512]{1,0:T(8,128)(2,1)}, bf16[112,512]{1,0:T(8,128)(2,1)S(1)}, u32[]{:S(2)}, u32[]{:S(2)}) collective-permute-start(bf16[112,512]{1,0:T(8,128)(2,1)} %get-tuple-element.44), channel_id=1, source_target_pairs={{0,1},{1,2},{2,3},{4,5},{5,6},{6,7},{8,9},{9,10},{10,11},{12,13},{... | collective-permute-start | bytes 344072 | tf_op jit(solution)/shard_map/ppermute | solution.py:715
  6.7 1.3 %collective-permute-start.1 = (bf16[112,512]{1,0:T(8,128)(2,1)}, bf16[112,512]{1,0:T(8,128)(2,1)S(1)}, u32[]{:S(2)}, u32[]{:S(2)}) collective-permute-start(bf16[112,512]{1,0:T(8,128)(2,1)} %get-tuple-element.45), channel_id=1, source_target_pairs={{1,0},{2,1},{3,2},{5,4},{6,5},{7,6},{9,8},{10,9},{11,10},{13,12},{... | collective-permute-start | bytes 344072 | tf_op jit(solution)/shard_map/ppermute | solution.py:715
  8.0 4.2 %collective-permute-start.2 = (bf16[400,384]{1,0:T(8,128)(2,1)}, bf16[400,384]{1,0:T(8,128)(2,1)S(1)}, u32[]{:S(2)}, u32[]{:S(2)}) collective-permute-start(bf16[400,384]{1,0:T(8,128)(2,1)} %get-tuple-element.50), channel_id=1, source_target_pairs={{0,4},{1,5},{2,6},{3,7},{4,8},{5,9},{6,10},{7,11},{8,12},{9,13},{1... | collective-permute-start | bytes 921608 | tf_op jit(solution)/shard_map/ppermute | solution.py:715
  12.3 1.3 %collective-permute-start.3 = (bf16[400,384]{1,0:T(8,128)(2,1)}, bf16[400,384]{1,0:T(8,128)(2,1)S(1)}, u32[]{:S(2)}, u32[]{:S(2)}) collective-permute-start(bf16[400,384]{1,0:T(8,128)(2,1)} %get-tuple-element.51), channel_id=1, source_target_pairs={{4,0},{5,1},{6,2},{7,3},{8,4},{9,5},{10,6},{11,7},{12,8},{13,9},{1... | collective-permute-start | bytes 921608 | tf_op jit(solution)/shard_map/ppermute | solution.py:715
  13.6 0.0 collective-permute-done.y_left
  13.6 0.3 corner_kernel.1
  13.9 4.5 %collective-permute-start.4 = (bf16[64,384]{1,0:T(8,128)(2,1)S(1)}, bf16[64,384]{1,0:T(8,128)(2,1)S(1)}, u32[]{:S(2)}, u32[]{:S(2)}) collective-permute-start(bf16[64,384]{1,0:T(8,128)(2,1)S(1)} %get-tuple-element.52), channel_id=1, source_target_pairs={{0,4},{1,5},{2,6},{3,7},{4,8},{5,9},{6,10},{7,11},{8,12},{9,13},{1... | collective-permute-start | bytes 147464 | tf_op jit(solution)/shard_map/ppermute | solution.py:715
  18.5 1.3 %collective-permute-start.5 = (bf16[64,384]{1,0:T(8,128)(2,1)S(1)}, bf16[64,384]{1,0:T(8,128)(2,1)S(1)}, u32[]{:S(2)}, u32[]{:S(2)}) collective-permute-start(bf16[64,384]{1,0:T(8,128)(2,1)S(1)} %get-tuple-element.46.c_low), channel_id=1, source_target_pairs={{4,0},{5,1},{6,2},{7,3},{8,4},{9,5},{10,6},{11,7},{12,8},{13,9},{1... | collective-permute-start | bytes 147464 | tf_op jit(solution)/shard_map/ppermute | solution.py:715
  19.8 0.0 copy-start.3
  19.8 1.0 copy-done.3
  20.8 1.0 copy-done.4
  21.8 4.1 %place_kernel.1 = (bf16[144,48,128]{2,1,0:T(8,128)(2,1)S(1)}, bf16[80,48,128]{2,1,0:T(8,128)(2,1)S(1)}, f32[40,48,128]{2,1,0:T(8,128)S(1)}, bf16[144,432]{1,0:T(...) custom-call(s32[16]{0:T(128)S(1)} %bitcast.20, ...), custom_call_target="tpu_custom_call" | custom-call | flops 8000000000 | bytes 6480964 | tf_op jit(solution)/shard_map/place_kernel/pallas_call | solution.py:695
  25.9 1.4 %collective-permute-done.4.c_left = bf16[64,384]{1,0:T(8,128)(2,1)S(1)} collective-permute-done((bf16[64,384]{1,0:T(8,128)(2,1)S(1)}, bf16[64,384]{1,0:T(8,128)(2,1)S(1)}, u32[]{:S(2)}, u32[]{:S(2)}) %collective-permute-start.4) | collective-permute-done | bytes 49184 | tf_op jit(solution)/shard_map/ppermute | solution.py:715
  27.3 16.3 %forward_kernel.1 = (bf16[144,48,128]{2,1,0:T(8,128)(2,1)S(1)}, f32[80,48,128]{2,1,0:T(8,128)S(1)}, bf16[40,144,128]{2,1,0:T(8,128)(2,1)S(1)}, bf16[40,48,128]{2...) custom-call(bf16[144,48,128]{2,1,0:T(8,128)(2,1)S(1)} %get-tuple-ele, ...), custom_call_target="tpu_custom_call" | custom-call | flops 8000000000 | bytes 10312704 | tf_op jit(solution)/shard_map/forward_kernel/pallas_call | solution.py:695
  43.6 4.4 %collective-permute-start.6 = (bf16[5,48,128]{2,1,0:T(8,128)(2,1)S(1)}, bf16[5,48,128]{2,1,0:T(8,128)(2,1)S(1)}, u32[]{:S(2)}, u32[]{:S(2)}) collective-permute-start(bf16[5,48,128]{2,1,0:T(8,128)(2,1)S(1)} %get-tuple-element.58), channel_id=1, source_target_pairs={{0,4},{1,5},{2,6},{3,7},{4,8},{5,9},{6,10},{7,11},{8,12},{9,13},{1... | collective-permute-start | bytes 184328 | tf_op jit(solution)/shard_map/ppermute | solution.py:715
  48.0 1.5 %collective-permute-start.7 = (bf16[5,48,128]{2,1,0:T(8,128)(2,1)S(1)}, bf16[5,48,128]{2,1,0:T(8,128)(2,1)S(1)}, u32[]{:S(2)}, u32[]{:S(2)}) collective-permute-start(bf16[5,48,128]{2,1,0:T(8,128)(2,1)S(1)} %get-tuple-element.59), channel_id=1, source_target_pairs={{4,0},{5,1},{6,2},{7,3},{8,4},{9,5},{10,6},{11,7},{12,8},{13,9},{1... | collective-permute-start | bytes 184328 | tf_op jit(solution)/shard_map/ppermute | solution.py:715
  49.5 2.1 %side_kernel.1.early = bf16[720,128]{1,0:T(8,128)(2,1)S(1)} custom-call(bf16[40,48,128]{2,1,0:T(8,128)(2,1)S(1)} %get-tuple-element.66.rects, bf16[80,48,128]{2,1,0:T(8,128)(2,1)S(1)} %get-tuple-element.61.cot_grid, bf16[40,144,128]{2,1,0:T(8,128)(2,1)S(1)} %get-tuple-element.67.low_cols, bf16[40,48,128]{2,1,0:T(8,128)(2,1)S(1)} %get-tuple-element.57.grad_c), custom_call_target="tpu_custom_call" | custom-call | flops 8000000000 | bytes 3624960 | tf_op jit(solution)/shard_map/side_kernel/pallas_call | solution.py:695
  51.6 4.4 %collective-permute-done.7.from_right = bf16[5,48,128]{2,1,0:T(8,128)(2,1)S(1)} collective-permute-done((bf16[5,48,128]{2,1,0:T(8,128)(2,1)S(1)}, bf16[5,48,128]{2,1,0:T(8,128)(2,1)S(1)}, u32[]{:S(2)}, u32[]{:S(2)}) %collective-permute-start.7) | collective-permute-done | bytes 61472 | tf_op jit(solution)/shard_map/ppermute | solution.py:715
  56.0 3.5 %backward_kernel.1 = (bf16[80,48,128]{2,1,0:T(8,128)(2,1)S(1)}, bf16[40,48,128]{2,1,0:T(8,128)(2,1)S(1)}) custom-call(bf16[40,48,128]{2,1,0:T(8,128)(2,1)S(1)} %get-tuple-element.57.grad_c, bf16[5,48,128]{2,1,0:T(8,128)(2,1)S(1)} %collective-permute-done.6.from_left, bf16[5,48,128]{2,1,0:T(8,128)(2,1)S(1)} %collective-permute-done.7.from_right, ...), custom_call_target="tpu_custom_call" | custom-call | flops 8000000000 | bytes 5207552 | tf_op jit(solution)/shard_map/backward_kernel/pallas_call | solution.py:695
  59.5 6.5 %weight_kernel.1 = bf16[1280,128]{1,0:T(8,128)(2,1)} custom-call(bf16[144,48,128]{2,1,0:T(8,128)(2,1)S(1)} %get-tuple-element.56.grid, bf16[80,48,128]{2,1,0:T(8,128)(2,1)S(1)} %get-tuple-element.73.grad_h, bf16[40,48,128]{2,1,0:T(8,128)(2,1)S(1)} %get-tuple-element.65.grad_d, f32[80,48,128]{2,1,0:T(8,128)S(1)} %get-tuple-element.60.hidden, ...), custom_call_target="tpu_custom_call" | custom-call | flops 12000000000 | bytes 5722112 | tf_op jit(solution)/shard_map/weight_kernel/pallas_call | solution.py:695
  66.0 7.0 %all-to-all-start = ((bf16[32,40,128]{2,1,0:T(8,128)(2,1)}), bf16[32,40,128]{2,1,0:T(8,128)(2,1)S(1)}, u32[]{:S(2)}, u32[]{:S(2)}) async-start(bf16[32,40,128]{2,1,0:T(8,128)(2,1)} %bitcast.6), calls=%async_computation | async-start | bytes 655360 | tf_op jit(solution)/shard_map/all_to_all | solution.py:723
  73.1 0.6 pack_kernel.1
  73.7 3.7 %collective-permute-start.8 = (bf16[10,48,128]{2,1,0:T(8,128)(2,1)S(1)}, bf16[10,48,128]{2,1,0:T(8,128)(2,1)S(1)}, u32[]{:S(2)}, u32[]{:S(2)}) collective-permute-start(bf16[10,48,128]{2,1,0:T(8,128)(2,1)S(1)} %get-tuple-element.74), channel_id=1, source_target_pairs={{0,4},{1,5},{2,6},{3,7},{4,8},{5,9},{6,10},{7,11},{8,12},{9,13},{1... | collective-permute-start | bytes 368648 | tf_op jit(solution)/shard_map/ppermute | solution.py:715
  77.4 1.3 %collective-permute-start.9 = (bf16[10,48,128]{2,1,0:T(8,128)(2,1)S(1)}, bf16[10,48,128]{2,1,0:T(8,128)(2,1)S(1)}, u32[]{:S(2)}, u32[]{:S(2)}) collective-permute-start(bf16[10,48,128]{2,1,0:T(8,128)(2,1)S(1)} %get-tuple-element.75), channel_id=1, source_target_pairs={{4,0},{5,1},{6,2},{7,3},{8,4},{9,5},{10,6},{11,7},{12,8},{13,9},{1... | collective-permute-start | bytes 368648 | tf_op jit(solution)/shard_map/ppermute | solution.py:715
  78.7 4.0 %output_kernel.1 = bf16[16,48,512]{2,1,0:T(8,128)(2,1)} custom-call(s32[16]{0:T(128)S(1)} %bitcast.21, f32[80,48,128]{2,1,0:T(8,128)S(1)} %copy-done.9, bf16[40,48,128]{2,1,0:T(8,128)(2,1)S(1)} %get-tuple-element.66.rects, f32[16,128]{1,0:T(8,128)S(1)} %get-tuple-element.62.live, bf16[96,192]{1,0:T(8,128)(2,1)S(1)} %get-tuple-element.70.up_w), custom_call_target="tpu_custom_call" | custom-call | flops 8000000000 | bytes 3289152 | tf_op jit(solution)/shard_map/output_kernel/pallas_call | solution.py:695
  82.7 2.3 %all-to-all-done.parts = bf16[32,40,128]{2,1,0:T(8,128)(2,1)S(1)} async-done(((bf16[32,40,128]{2,1,0:T(8,128)(2,1)}), bf16[32,40,128]{2,1,0:T(8,128)(2,1)S(1)}, u32[]{:S(2)}, u32[]{:S(2)}) %all-to-all-start) | async-done | bytes 327712 | tf_op jit(solution)/shard_map/all_to_all | solution.py:723
  85.0 0.8 sum_kernel.1
  85.8 4.6 %all-to-all-start.1 = ((bf16[32,40,128]{2,1,0:T(8,128)(2,1)}), bf16[32,40,128]{2,1,0:T(8,128)(2,1)S(1)}, u32[]{:S(2)}, u32[]{:S(2)}) async-start(bf16[32,40,128]{2,1,0:T(8,128)(2,1)} %sum_kernel.1), calls=%async_computation.1 | async-start | bytes 655360 | tf_op jit(solution)/shard_map/all_to_all | solution.py:729
  90.5 7.3 %input_kernel.1 = bf16[16,48,512]{2,1,0:T(8,128)(2,1)} custom-call(s32[16]{0:T(128)S(1)} %bitcast.22, bf16[80,48,128]{2,1,0:T(8,128)(2,1)S(1)} %get-tuple-element.73.grad_h, bf16[10,48,128]{2,1,0:T(8,128)(2,1)S(1)} %collective-permute-done.8.from_left, bf16[10,48,128]{2,1,0:T(8,128)(2,1)S(1)} %collective-permute-done.9.from_right, ...), custom_call_target="tpu_custom_call" | custom-call | flops 8000000000 | bytes 2147904 | tf_op jit(solution)/shard_map/input_kernel/pallas_call | solution.py:695
  97.8 4.4 %all-to-all-done.1 = bf16[32,40,128]{2,1,0:T(8,128)(2,1)S(1)} async-done(((bf16[32,40,128]{2,1,0:T(8,128)(2,1)}), bf16[32,40,128]{2,1,0:T(8,128)(2,1)S(1)}, u32[]{:S(2)}, u32[]{:S(2)}) %all-to-all-start.1) | async-done | bytes 327712 | tf_op jit(solution)/shard_map/all_to_all | solution.py:729
  102.2 1.9 %finish_kernel.1 = (f32[27,48,48]{2,1,0:T(8,128)}, f32[48,8,48]{2,1,0:T(8,128)}, f32[27,48,48]{2,1,0:T(8,128)}, f32[8,48,48]{2,1,0:T(8,128)}) custom-call(bf16[1280,128]{1,0:T(8,128)(2,1)S(1)} %bitcast.14), custom_call_target="tpu_custom_call" | custom-call | bytes 972800 | tf_op jit(solution)/shard_map/finish_kernel/pallas_call | solution.py:695
  (24 shorter events, 0.1 us)
Async XLA Ops:
  0.6 19.2 %copy-start.1 = (bf16[1,1,16,48,512]{4,3,2,1,0:T(8,128)(2,1)S(1)}, bf16[1,1,16,48,512]{4,3,2,1,0:T(8,128)(2,1)}, u32[]{:S(2)}) copy-start(bf16[1,1,16,48,512]{4,3,2,1,0:T(8,128)(2,1)} %param.11) | copy-start | bytes 2359300
  0.6 19.2 %copy-start.2 = (s32[1,1,16]{2,1,0:T(1,128)S(1)}, s32[1,1,16]{2,1,0:T(1,128)}, u32[]{:S(2)}) copy-start(s32[1,1,16]{2,1,0:T(1,128)} %param.9) | copy-start | bytes 196
  0.7 19.2 %copy-start = (bf16[1,1,16,48,512]{4,3,2,1,0:T(8,128)(2,1)S(1)}, bf16[1,1,16,48,512]{4,3,2,1,0:T(8,128)(2,1)}, u32[]{:S(2)}) copy-start(bf16[1,1,16,48,512]{4,3,2,1,0:T(8,128)(2,1)} %param.8) | copy-start | bytes 2359300
  0.7 19.2 %copy-start.6 = (bf16[8,48,48]{2,1,0:T(8,128)(2,1)S(1)}, bf16[8,48,48]{2,1,0:T(8,128)(2,1)}, u32[]{:S(2)}) copy-start(bf16[8,48,48]{2,1,0:T(8,128)(2,1)} %up.1) | copy-start | bytes 110596
  0.7 19.2 %copy-start.5 = (bf16[48,8,48]{2,1,0:T(8,128)(2,1)S(1)}, bf16[48,8,48]{2,1,0:T(8,128)(2,1)}, u32[]{:S(2)}) copy-start(bf16[48,8,48]{2,1,0:T(8,128)(2,1)} %down.1) | copy-start | bytes 110596
  4.4 9.2 %collective-permute-start = (bf16[112,512]{1,0:T(8,128)(2,1)}, bf16[112,512]{1,0:T(8,128)(2,1)S(1)}, u32[]{:S(2)}, u32[]{:S(2)}) collective-permute-start(bf16[112,512]{1,0:T(8,128)(2,1)} %get-tuple-element.44), channel_id=1, source_target_pairs={{0,1},{1,2},{2,3},{4,5},{5,6},{6,7},{8,9},{9,10},{10,11},{12,13},{... | collective-permute-start | bytes 344072 | tf_op jit(solution)/shard_map/ppermute | solution.py:715
  6.7 6.9 %collective-permute-start.1 = (bf16[112,512]{1,0:T(8,128)(2,1)}, bf16[112,512]{1,0:T(8,128)(2,1)S(1)}, u32[]{:S(2)}, u32[]{:S(2)}) collective-permute-start(bf16[112,512]{1,0:T(8,128)(2,1)} %get-tuple-element.45), channel_id=1, source_target_pairs={{1,0},{2,1},{3,2},{5,4},{6,5},{7,6},{9,8},{10,9},{11,10},{13,12},{... | collective-permute-start | bytes 344072 | tf_op jit(solution)/shard_map/ppermute | solution.py:715
  8.0 19.3 %collective-permute-start.2 = (bf16[400,384]{1,0:T(8,128)(2,1)}, bf16[400,384]{1,0:T(8,128)(2,1)S(1)}, u32[]{:S(2)}, u32[]{:S(2)}) collective-permute-start(bf16[400,384]{1,0:T(8,128)(2,1)} %get-tuple-element.50), channel_id=1, source_target_pairs={{0,4},{1,5},{2,6},{3,7},{4,8},{5,9},{6,10},{7,11},{8,12},{9,13},{1... | collective-permute-start | bytes 921608 | tf_op jit(solution)/shard_map/ppermute | solution.py:715
  12.3 15.0 %collective-permute-start.3 = (bf16[400,384]{1,0:T(8,128)(2,1)}, bf16[400,384]{1,0:T(8,128)(2,1)S(1)}, u32[]{:S(2)}, u32[]{:S(2)}) collective-permute-start(bf16[400,384]{1,0:T(8,128)(2,1)} %get-tuple-element.51), channel_id=1, source_target_pairs={{4,0},{5,1},{6,2},{7,3},{8,4},{9,5},{10,6},{11,7},{12,8},{13,9},{1... | collective-permute-start | bytes 921608 | tf_op jit(solution)/shard_map/ppermute | solution.py:715
  13.9 13.4 %collective-permute-start.4 = (bf16[64,384]{1,0:T(8,128)(2,1)S(1)}, bf16[64,384]{1,0:T(8,128)(2,1)S(1)}, u32[]{:S(2)}, u32[]{:S(2)}) collective-permute-start(bf16[64,384]{1,0:T(8,128)(2,1)S(1)} %get-tuple-element.52), channel_id=1, source_target_pairs={{0,4},{1,5},{2,6},{3,7},{4,8},{5,9},{6,10},{7,11},{8,12},{9,13},{1... | collective-permute-start | bytes 147464 | tf_op jit(solution)/shard_map/ppermute | solution.py:715
  18.5 8.8 %collective-permute-start.5 = (bf16[64,384]{1,0:T(8,128)(2,1)S(1)}, bf16[64,384]{1,0:T(8,128)(2,1)S(1)}, u32[]{:S(2)}, u32[]{:S(2)}) collective-permute-start(bf16[64,384]{1,0:T(8,128)(2,1)S(1)} %get-tuple-element.46.c_low), channel_id=1, source_target_pairs={{4,0},{5,1},{6,2},{7,3},{8,4},{9,5},{10,6},{11,7},{12,8},{13,9},{1... | collective-permute-start | bytes 147464 | tf_op jit(solution)/shard_map/ppermute | solution.py:715
  19.8 1.0 copy-start.3
  20.8 1.0 copy-start.4
  21.8 5.5 %copy-start.7 = (f32[16,128]{1,0:T(8,128)S(1)}, f32[16,128]{1,0:T(8,128)}, u32[]{:S(2)}) copy-start(f32[16,128]{1,0:T(8,128)} %get-tuple-element.48.flags) | copy-start | bytes 24580
  43.6 15.9 %copy-start.8 = (f32[80,48,128]{2,1,0:T(8,128)}, f32[80,48,128]{2,1,0:T(8,128)S(1)}, u32[]{:S(2)}) copy-start(f32[80,48,128]{2,1,0:T(8,128)S(1)} %get-tuple-element.60.hidden) | copy-start | bytes 5898244
  43.6 8.0 %collective-permute-start.6 = (bf16[5,48,128]{2,1,0:T(8,128)(2,1)S(1)}, bf16[5,48,128]{2,1,0:T(8,128)(2,1)S(1)}, u32[]{:S(2)}, u32[]{:S(2)}) collective-permute-start(bf16[5,48,128]{2,1,0:T(8,128)(2,1)S(1)} %get-tuple-element.58), channel_id=1, source_target_pairs={{0,4},{1,5},{2,6},{3,7},{4,8},{5,9},{6,10},{7,11},{8,12},{9,13},{1... | collective-permute-start | bytes 184328 | tf_op jit(solution)/shard_map/ppermute | solution.py:715
  48.0 8.0 %collective-permute-start.7 = (bf16[5,48,128]{2,1,0:T(8,128)(2,1)S(1)}, bf16[5,48,128]{2,1,0:T(8,128)(2,1)S(1)}, u32[]{:S(2)}, u32[]{:S(2)}) collective-permute-start(bf16[5,48,128]{2,1,0:T(8,128)(2,1)S(1)} %get-tuple-element.59), channel_id=1, source_target_pairs={{4,0},{5,1},{6,2},{7,3},{8,4},{9,5},{10,6},{11,7},{12,8},{13,9},{1... | collective-permute-start | bytes 184328 | tf_op jit(solution)/shard_map/ppermute | solution.py:715
  66.0 19.0 %all-to-all-start = ((bf16[32,40,128]{2,1,0:T(8,128)(2,1)}), bf16[32,40,128]{2,1,0:T(8,128)(2,1)S(1)}, u32[]{:S(2)}, u32[]{:S(2)}) async-start(bf16[32,40,128]{2,1,0:T(8,128)(2,1)} %bitcast.6), calls=%async_computation | async-start | bytes 655360 | tf_op jit(solution)/shard_map/all_to_all | solution.py:723
  73.0 5.6 %copy-start.9 = (f32[80,48,128]{2,1,0:T(8,128)S(1)}, f32[80,48,128]{2,1,0:T(8,128)}, u32[]{:S(2)}) copy-start(f32[80,48,128]{2,1,0:T(8,128)} %copy-done.8) | copy-start | bytes 5898244
  73.7 16.8 %collective-permute-start.8 = (bf16[10,48,128]{2,1,0:T(8,128)(2,1)S(1)}, bf16[10,48,128]{2,1,0:T(8,128)(2,1)S(1)}, u32[]{:S(2)}, u32[]{:S(2)}) collective-permute-start(bf16[10,48,128]{2,1,0:T(8,128)(2,1)S(1)} %get-tuple-element.74), channel_id=1, source_target_pairs={{0,4},{1,5},{2,6},{3,7},{4,8},{5,9},{6,10},{7,11},{8,12},{9,13},{1... | collective-permute-start | bytes 368648 | tf_op jit(solution)/shard_map/ppermute | solution.py:715
  77.4 13.1 %collective-permute-start.9 = (bf16[10,48,128]{2,1,0:T(8,128)(2,1)S(1)}, bf16[10,48,128]{2,1,0:T(8,128)(2,1)S(1)}, u32[]{:S(2)}, u32[]{:S(2)}) collective-permute-start(bf16[10,48,128]{2,1,0:T(8,128)(2,1)S(1)} %get-tuple-element.75), channel_id=1, source_target_pairs={{4,0},{5,1},{6,2},{7,3},{8,4},{9,5},{10,6},{11,7},{12,8},{13,9},{1... | collective-permute-start | bytes 368648 | tf_op jit(solution)/shard_map/ppermute | solution.py:715
  85.8 16.4 %all-to-all-start.1 = ((bf16[32,40,128]{2,1,0:T(8,128)(2,1)}), bf16[32,40,128]{2,1,0:T(8,128)(2,1)S(1)}, u32[]{:S(2)}, u32[]{:S(2)}) async-start(bf16[32,40,128]{2,1,0:T(8,128)(2,1)} %sum_kernel.1), calls=%async_computation.1 | async-start | bytes 655360 | tf_op jit(solution)/shard_map/all_to_all | solution.py:729
